TPU v7x, 32 devices: a whole 2x2x4 slice. The times are simulated.
32 devices in a mesh: tensor: 4 (over y, core), context: 4 (over z), dp: 2 (over x).
Axes of the slice: x: 2, y: 2, z: 4, core: 2. Of those that a mesh axis runs over, the one named last changes fastest.
Arguments:
- tokens: bfloat16 [4, 2048, 2048], P('dp', 'context'), may hold values from -6 to 6
- segment_ids: int32 [4, 2048], P('dp'), may hold values from 0 to 4, as said below
- norm_gain_1: float32 [2048], replicated, may hold values from 0.25 to 1.75
- w_query: bfloat16 [2048, 2048], P(None, 'tensor'), may hold values from -0.125 to 0.125
- w_key: bfloat16 [2048, 256], P(None, 'tensor'), may hold values from -0.125 to 0.125
- w_value: bfloat16 [2048, 256], P(None, 'tensor'), may hold values from -0.125 to 0.125
- w_output: bfloat16 [2048, 2048], P('tensor'), may hold values from -1.5 to 1.5
- norm_gain_2: float32 [2048], replicated, may hold values from 0.25 to 1.75
- w_gate: bfloat16 [2048, 5632], P(None, 'tensor'), may hold values from -0.125 to 0.125
- w_up: bfloat16 [2048, 5632], P(None, 'tensor'), may hold values from -0.125 to 0.125
- w_down: bfloat16 [5632, 2048], P('tensor'), may hold values from -0.078125 to 0.078125
- cotangent: bfloat16 [4, 2048, 2048], P('dp', 'context'), may hold values from -6 to 6
Outputs:
- layer_out: bfloat16 [4, 2048, 2048], P('dp', 'context')
- grad_tokens: float32 [4, 2048, 2048], P('dp', 'context')
- grad_gain_1: float32 [2048], P(('context', 'dp'))
- grad_query: float32 [2048, 2048], P(('context', 'dp'), 'tensor')
- grad_key: float32 [2048, 256], P(('context', 'dp'), 'tensor')
- grad_value: float32 [2048, 256], P(('context', 'dp'), 'tensor')
- grad_output: float32 [2048, 2048], P('tensor', ('context', 'dp'))
- grad_gain_2: float32 [2048], P(('context', 'dp'))
- grad_gate: float32 [2048, 5632], P(('context', 'dp'), 'tensor')
- grad_up: float32 [2048, 5632], P(('context', 'dp'), 'tensor')
- grad_down: float32 [5632, 2048], P('tensor', ('context', 'dp'))
Inputs may be any that keep to these rules, and one draw needn't show every extreme that they name: Each row of segment_ids starts at 0, never falls, rises by at most one from a token to the next, and ends at 4.
All inputs are finite; a program needn't handle non-finite values.
Results may differ from a plain program's by a relative error of at most 0.02.
Values may be sent and summed in bfloat16 or wider, within the bound.
No kernel may reach another device: no remote copies, remote signals or barrier semaphores. Data moves between devices by JAX's collectives and lax.ppermute only.
A program may use at most 256 MiB of HBM per device.

v0:
```python
import jax
import jax.numpy as jnp
from jax import lax
from jax.sharding import PartitionSpec as P

EPSILON = 1e-05


def doc_positions(segment_ids):
    length = segment_ids.shape[-1]
    token_index = jnp.arange(length, dtype=jnp.int32)
    previous = jnp.concatenate([segment_ids[..., :1] - 1, segment_ids[..., :-1]], -1)
    starts = jnp.where(segment_ids != previous, token_index, 0)
    return token_index - lax.cummax(starts, axis=starts.ndim - 1)


def rope_tables(positions, head_size):
    half_width = head_size // 2
    frequency = 10000.0 ** (-(2.0 * jnp.arange(half_width, dtype=jnp.float32)) / head_size)
    angles = positions.astype(jnp.float32)[..., None] * frequency
    cos_half = jnp.cos(angles)
    sin_half = jnp.sin(angles)
    return (jnp.concatenate([cos_half, cos_half], -1), jnp.concatenate([sin_half, sin_half], -1))


def rotate(vectors, cos_table, sine_table):
    half_width = vectors.shape[-1] // 2
    turned = jnp.concatenate([-vectors[..., half_width:], vectors[..., :half_width]], -1)
    return vectors * cos_table + turned * sine_table


def rotate_back(grads_in, cos_table, sine_table):
    half_width = grads_in.shape[-1] // 2
    scaled = grads_in * sine_table
    return grads_in * cos_table + jnp.concatenate(
        [scaled[..., half_width:], -scaled[..., :half_width]], -1
    )


def local(
    tokens,
    segment_ids,
    norm_gain_1,
    w_query,
    w_key,
    w_value,
    w_output,
    norm_gain_2,
    w_gate,
    w_up,
    w_down,
    cotangent,
):
    seq_count, stretch_len, model_width = tokens.shape
    length = segment_ids.shape[1]
    head_size = w_key.shape[1]
    head_count = w_query.shape[1] // head_size
    row_count = seq_count * stretch_len
    score_scale = head_size ** (-0.5)
    offset = lax.axis_index("context") * stretch_len
    seg_here = lax.dynamic_slice_in_dim(segment_ids, offset, stretch_len, 1)
    positions = lax.dynamic_slice_in_dim(doc_positions(segment_ids), offset, stretch_len, 1)
    cos_table, sine_table = rope_tables(positions.reshape(row_count), head_size)
    query_index = offset + jnp.arange(stretch_len, dtype=jnp.int32)
    key_index = jnp.arange(length, dtype=jnp.int32)

    def allowed_of(seg_row, seg_local):
        return (seg_row[None, :] == seg_local[:, None]) & (
            key_index[None, :] <= query_index[:, None]
        )

    stream = tokens.reshape(row_count, model_width).astype(jnp.float32)
    scale_one = lax.rsqrt(jnp.mean(stream * stream, -1, keepdims=True) + EPSILON)
    normed_one = stream * scale_one
    attn_in = (normed_one * norm_gain_1).astype(jnp.bfloat16)
    query_proj = jnp.dot(attn_in, w_query, preferred_element_type=jnp.float32).reshape(
        row_count, head_count, head_size
    )
    key_proj = jnp.dot(attn_in, w_key, preferred_element_type=jnp.float32)
    value_proj = jnp.dot(attn_in, w_value, preferred_element_type=jnp.float32)
    query_rot = rotate(query_proj, cos_table[:, None, :], sine_table[:, None, :]).astype(
        jnp.bfloat16
    )
    query_heads = query_rot.reshape(seq_count, stretch_len, head_count, head_size).transpose(
        0, 2, 1, 3
    )
    key_here = (
        rotate(key_proj, cos_table, sine_table)
        .astype(jnp.bfloat16)
        .reshape(seq_count, stretch_len, head_size)
    )
    value_here = value_proj.astype(jnp.bfloat16).reshape(seq_count, stretch_len, head_size)
    key_all, value_all = (
        lax.all_gather(key_here, "context", axis=1, tiled=True),
        lax.all_gather(value_here, "context", axis=1, tiled=True),
    )

    def attend_seq(seq_item):
        query_set, keys_seq, values_seq, seg_row, seg_local = seq_item
        allowed = allowed_of(seg_row, seg_local)

        def attend_head(query_one):
            scores = (
                jnp.dot(query_one, keys_seq.T, preferred_element_type=jnp.float32) * score_scale
            )
            scores = jnp.where(allowed, scores, -1e30)
            row_max = jnp.max(scores, -1, keepdims=True)
            exp_scores = jnp.exp(scores - row_max)
            row_total = jnp.sum(exp_scores, -1, keepdims=True)
            attn_probs = (exp_scores / row_total).astype(jnp.bfloat16)
            head_out = jnp.dot(attn_probs, values_seq, preferred_element_type=jnp.float32)
            return (head_out, (row_max + jnp.log(row_total))[:, 0])

        return lax.map(attend_head, query_set)

    attn_heads, log_totals = lax.map(
        attend_seq, (query_heads, key_all, value_all, segment_ids, seg_here)
    )
    attn_cat = (
        attn_heads.transpose(0, 2, 1, 3)
        .reshape(row_count, head_count * head_size)
        .astype(jnp.bfloat16)
    )
    attn_total = lax.psum(jnp.dot(attn_cat, w_output, preferred_element_type=jnp.float32), "tensor")
    residual = stream + attn_total
    scale_two = lax.rsqrt(jnp.mean(residual * residual, -1, keepdims=True) + EPSILON)
    normed_two = residual * scale_two
    mlp_in = (normed_two * norm_gain_2).astype(jnp.bfloat16)
    gate_pre = jnp.dot(mlp_in, w_gate, preferred_element_type=jnp.float32)
    up_proj = jnp.dot(mlp_in, w_up, preferred_element_type=jnp.float32)
    sigmoid_gate = jax.nn.sigmoid(gate_pre)
    hidden = (gate_pre * sigmoid_gate * up_proj).astype(jnp.bfloat16)
    mlp_total = lax.psum(
        jnp.dot(hidden, w_down, preferred_element_type=jnp.float32).astype(jnp.bfloat16), "tensor"
    ).astype(jnp.float32)
    layer_out = (
        (residual + mlp_total).astype(jnp.bfloat16).reshape(seq_count, stretch_len, model_width)
    )
    grad_rows = cotangent.reshape(row_count, model_width)
    d_hidden = jnp.dot(grad_rows, w_down.T, preferred_element_type=jnp.float32)
    d_gate = (d_hidden * up_proj * sigmoid_gate * (1.0 + gate_pre * (1.0 - sigmoid_gate))).astype(
        jnp.bfloat16
    )
    d_up = (d_hidden * gate_pre * sigmoid_gate).astype(jnp.bfloat16)
    grad_down = jnp.dot(hidden.T, grad_rows, preferred_element_type=jnp.float32)
    grad_gate = jnp.dot(mlp_in.T, d_gate, preferred_element_type=jnp.float32)
    grad_up = jnp.dot(mlp_in.T, d_up, preferred_element_type=jnp.float32)
    mlp_back = jnp.dot(d_gate, w_gate.T, preferred_element_type=jnp.float32) + jnp.dot(
        d_up, w_up.T, preferred_element_type=jnp.float32
    )
    d_mlp_in = lax.psum(mlp_back, "tensor")
    grad_gain_2 = jnp.sum(d_mlp_in * normed_two, 0)
    scaled_two = d_mlp_in * norm_gain_2
    d_residual = grad_rows.astype(jnp.float32) + scale_two * (
        scaled_two - normed_two * jnp.mean(scaled_two * normed_two, -1, keepdims=True)
    )
    d_res_low = d_residual.astype(jnp.bfloat16)
    grad_output = jnp.dot(attn_cat.T, d_res_low, preferred_element_type=jnp.float32)
    d_attn = jnp.dot(d_res_low, w_output.T, preferred_element_type=jnp.float32).astype(jnp.bfloat16)
    d_attn_heads = d_attn.reshape(seq_count, stretch_len, head_count, head_size).transpose(
        0, 2, 1, 3
    )
    key_use, value_use = (key_all, value_all)

    def back_seq(seq_item):
        query_set, d_set, lse_set, keys_seq, values_seq, seg_row, seg_local = seq_item
        allowed = allowed_of(seg_row, seg_local)

        def back_head(acc_pair, head_item):
            key_acc, value_acc = acc_pair
            query_one, d_one, lse_one = head_item
            scores = (
                jnp.dot(query_one, keys_seq.T, preferred_element_type=jnp.float32) * score_scale
            )
            attn_probs = jnp.exp(jnp.where(allowed, scores - lse_one[:, None], -1e30))
            probs_low = attn_probs.astype(jnp.bfloat16)
            d_probs = jnp.dot(d_one, values_seq.T, preferred_element_type=jnp.float32)
            centre = jnp.sum(attn_probs * d_probs, -1, keepdims=True)
            d_scores = (attn_probs * (d_probs - centre) * score_scale).astype(jnp.bfloat16)
            d_query_one = jnp.dot(d_scores, keys_seq, preferred_element_type=jnp.float32)
            key_acc = key_acc + jnp.dot(d_scores.T, query_one, preferred_element_type=jnp.float32)
            value_acc = value_acc + jnp.dot(probs_low.T, d_one, preferred_element_type=jnp.float32)
            return ((key_acc, value_acc), d_query_one)

        zero_rows = jnp.zeros((length, head_size), jnp.float32)
        (key_acc, value_acc), d_query_set = lax.scan(
            back_head, (zero_rows, zero_rows), (query_set, d_set, lse_set)
        )
        return (key_acc, value_acc, d_query_set)

    key_grad_all, value_grad_all, d_query_heads = lax.map(
        back_seq, (query_heads, d_attn_heads, log_totals, key_use, value_use, segment_ids, seg_here)
    )
    key_grad, value_grad = (
        lax.psum_scatter(
            key_grad_all.astype(jnp.bfloat16), "context", scatter_dimension=1, tiled=True
        ).astype(jnp.float32),
        lax.psum_scatter(
            value_grad_all.astype(jnp.bfloat16), "context", scatter_dimension=1, tiled=True
        ).astype(jnp.float32),
    )
    d_query_rows = d_query_heads.transpose(0, 2, 1, 3).reshape(row_count, head_count, head_size)
    d_query = (
        rotate_back(d_query_rows, cos_table[:, None, :], sine_table[:, None, :])
        .astype(jnp.bfloat16)
        .reshape(row_count, head_count * head_size)
    )
    d_key = rotate_back(key_grad.reshape(row_count, head_size), cos_table, sine_table).astype(
        jnp.bfloat16
    )
    d_value = value_grad.reshape(row_count, head_size).astype(jnp.bfloat16)
    grad_query = jnp.dot(attn_in.T, d_query, preferred_element_type=jnp.float32)
    grad_key = jnp.dot(attn_in.T, d_key, preferred_element_type=jnp.float32)
    grad_value = jnp.dot(attn_in.T, d_value, preferred_element_type=jnp.float32)
    attn_back = jnp.dot(d_query, w_query.T, preferred_element_type=jnp.float32)
    attn_back = attn_back + jnp.dot(d_key, w_key.T, preferred_element_type=jnp.float32)
    attn_back = attn_back + jnp.dot(d_value, w_value.T, preferred_element_type=jnp.float32)
    d_attn_in = lax.psum(attn_back.astype(jnp.bfloat16), "tensor").astype(jnp.float32)
    grad_gain_1 = jnp.sum(d_attn_in * normed_one, 0)
    scaled_one = d_attn_in * norm_gain_1
    grad_tokens = d_residual + scale_one * (
        scaled_one - normed_one * jnp.mean(scaled_one * normed_one, -1, keepdims=True)
    )
    grad_tokens = grad_tokens.reshape(seq_count, stretch_len, model_width)
    query_sum, key_sum, value_sum, gate_sum, upper_sum, first_sum, second_sum = (
        lax.psum_scatter(
            grad_query.astype(jnp.bfloat16), ("context", "dp"), scatter_dimension=0, tiled=True
        ).astype(jnp.float32),
        lax.psum_scatter(
            grad_key.astype(jnp.bfloat16), ("context", "dp"), scatter_dimension=0, tiled=True
        ).astype(jnp.float32),
        lax.psum_scatter(
            grad_value.astype(jnp.bfloat16), ("context", "dp"), scatter_dimension=0, tiled=True
        ).astype(jnp.float32),
        lax.psum_scatter(
            grad_gate.astype(jnp.bfloat16), ("context", "dp"), scatter_dimension=0, tiled=True
        ).astype(jnp.float32),
        lax.psum_scatter(
            grad_up.astype(jnp.bfloat16), ("context", "dp"), scatter_dimension=0, tiled=True
        ).astype(jnp.float32),
        lax.psum_scatter(
            grad_gain_1.astype(jnp.bfloat16), ("context", "dp"), scatter_dimension=0, tiled=True
        ).astype(jnp.float32),
        lax.psum_scatter(
            grad_gain_2.astype(jnp.bfloat16), ("context", "dp"), scatter_dimension=0, tiled=True
        ).astype(jnp.float32),
    )
    output_sum, down_sum = (
        lax.psum_scatter(
            grad_output.astype(jnp.bfloat16), ("context", "dp"), scatter_dimension=1, tiled=True
        ).astype(jnp.float32),
        lax.psum_scatter(
            grad_down.astype(jnp.bfloat16), ("context", "dp"), scatter_dimension=1, tiled=True
        ).astype(jnp.float32),
    )
    return (
        layer_out,
        grad_tokens,
        first_sum,
        query_sum,
        key_sum,
        value_sum,
        output_sum,
        second_sum,
        gate_sum,
        upper_sum,
        down_sum,
    )


def solution(mesh):
    in_specs = (
        P("dp", "context", None),
        P("dp", None),
        P(),
        P(None, "tensor"),
        P(None, "tensor"),
        P(None, "tensor"),
        P("tensor", None),
        P(),
        P(None, "tensor"),
        P(None, "tensor"),
        P("tensor", None),
        P("dp", "context", None),
    )
    out_specs = (
        P("dp", "context", None),
        P("dp", "context", None),
        P(("context", "dp")),
        P(("context", "dp"), "tensor"),
        P(("context", "dp"), "tensor"),
        P(("context", "dp"), "tensor"),
        P("tensor", ("context", "dp")),
        P(("context", "dp")),
        P(("context", "dp"), "tensor"),
        P(("context", "dp"), "tensor"),
        P("tensor", ("context", "dp")),
    )
    return jax.shard_map(local, mesh=mesh, in_specs=in_specs, out_specs=out_specs, check_vma=False)
```

profile of v0, /device:TPU:0, one launch (start us, length us, event | category | flops | bytes accessed | tf_op | source)
XLA Modules:
  0.0 1555.8 jit_solution(14008734385442270222)
XLA Ops:
  10.3 3.1 fusion.43
  14.7 3.9 copy.45
  18.6 3.3 fusion.45
  40.9 24.5 %all_gather.6 = bf16[2,2048,64]{2,1,0:T(8,128)(2,1)S(1)} all-gather(bf16[2,512,64]{2,1,0:T(8,128)(2,1)} %bitcast.300), channel_id=1, replica_groups=mesh['tensor'=4,'context'=4,'dp'=2] {'context'}, dimensions={1}, use_global_device_ids=true | all-gather | bytes 655360 | tf_op jit(solution)/shard_map/all_gather | solution.py:94
  65.4 22.4 %all_gather.7 = bf16[2,2048,64]{2,1,0:T(8,128)(2,1)} all-gather(bf16[2,512,64]{2,1,0:T(8,128)(2,1)S(1)} %bitcast.299), channel_id=1, replica_groups=mesh['tensor'=4,'context'=4,'dp'=2] {'context'}, dimensions={1}, use_global_device_ids=true | all-gather | bytes 655360 | tf_op jit(solution)/shard_map/all_gather | solution.py:95
  87.8 4.0 copy.46
  91.8 90.1 %while.65 = (s32[]{:T(128)}, bf16[2,8,512,64]{2,3,1,0:T(8,128)(2,1)}, f32[2,8,512]{2,1,0:T(8,128)S(1)}, bf16[2,8,512,64]{3,2,1,0:T(8,128)(2,1)}, bf16[2,2048,64]...) while((s32[]{:T(128)}, ...), condition=%wide.region_8.9_spmd.clone.clone, body=%wide.region_3.8_spmd.clone.sunk.clone | while | flops 279969792 | bytes 17930652 | solution.py:116
  96.2 38.8 %while.64 = (s32[]{:T(128)}, bf16[8,512,64]{1,2,0:T(8,128)(2,1)}, f32[8,512]{1,0:T(8,128)S(1)}, bf16[8,512,64]{2,1,0:T(8,128)(2,1)}, bf16[2048,64]{1,0:T(8,128)(...) while((s32[]{:T(128)}, bf16[8,512,64]{1,2,0:T(8,128)(2,1)}, ...), condition=%wide.region_7.7_spmd.clone, body=%wide.region_4.6_spmd.clone.sunk | while | flops 279969280 | bytes 14721189 | solution.py:114
  141.3 38.8 %while.64 = (s32[]{:T(128)}, bf16[8,512,64]{1,2,0:T(8,128)(2,1)}, f32[8,512]{1,0:T(8,128)S(1)}, bf16[8,512,64]{2,1,0:T(8,128)(2,1)}, bf16[2048,64]{1,0:T(8,128)(...) while((s32[]{:T(128)}, bf16[8,512,64]{1,2,0:T(8,128)(2,1)}, ...), condition=%wide.region_7.7_spmd.clone, body=%wide.region_4.6_spmd.clone.sunk | while | flops 279969280 | bytes 14721189 | solution.py:114
  185.4 5.8 fusion.76
  191.3 151.7 %all-reduce.8.cloned.1.call-done = f32[1024,2048]{1,0:T(8,128)} async-done(((f32[1024,2048]{1,0:T(8,128)}), f32[1024,2048]{1,0:T(8,128)}) %all-reduce.8.cloned.1.call-update) | async-done | bytes 8388624 | tf_op jit(solution)/shard_map/psum | solution.py:124
  343.0 5.7 multiply_reduce_fusion.3
  352.0 11.8 fusion.78
  363.8 10.4 fusion.77
  374.2 14.7 multiply_convert_fusion.2
  388.9 10.6 fusion.79
  399.5 10.8 convolution_add_fusion.2
  410.4 153.1 %all-reduce.10.cloned.1.call-done = f32[1024,2048]{1,0:T(8,128)} async-done(((f32[1024,2048]{1,0:T(8,128)}), f32[1024,2048]{1,0:T(8,128)}) %all-reduce.10.cloned.1.call-update) | async-done | bytes 8388624 | tf_op jit(solution)/shard_map/psum | solution.py:151
  563.5 7.8 multiply_reduce_fusion.1
  572.9 4.6 multiply_add_fusion
  577.5 3.4 copy-done.8
  580.9 3.3 fusion.54
  587.3 148.7 %while.67 = (s32[]{:T(128)}, bf16[2,2048,64]{1,2,0:T(8,128)(2,1)}, bf16[2,2048,64]{1,2,0:T(8,128)(2,1)}, f32[2,8,512,64]{2,3,1,0:T(8,128)}, bf16[2,8,512,64]{3,2...) while((s32[]{:T(128)}, bf16[2,2048,64]{1,2,0:T(8,128)(2,1)}, ...), condition=%wide.region_18.19_spmd.clone.clone, body=%wide.region_14.18_spmd.clone.sunk.clone | while | flops 685244416 | bytes 47936032 | solution.py:191
  588.9 3.4 constant_dynamic-slice_fusion.21
  597.1 61.4 %while.66 = (s32[]{:T(128)}, f32[2048,64]{0,1:T(8,128)S(1)}, f32[2048,64]{0,1:T(8,128)S(1)}, f32[8,512,64]{1,2,0:T(8,128)}, bf16[8,512,64]{2,1,0:T(8,128)(2,1)},...) while((s32[]{:T(128)}, f32[2048,64]{0,1:T(8,128)S(1)}, ...), condition=%wide.region_17.17_spmd.clone, body=%wide.region_15.16_spmd.clone.sunk | while | flops 685243904 | bytes 35289268 | solution.py:186
  663.3 3.4 constant_dynamic-slice_fusion.21
  671.5 61.4 %while.66 = (s32[]{:T(128)}, f32[2048,64]{0,1:T(8,128)S(1)}, f32[2048,64]{0,1:T(8,128)S(1)}, f32[8,512,64]{1,2,0:T(8,128)}, bf16[8,512,64]{2,1,0:T(8,128)(2,1)},...) while((s32[]{:T(128)}, f32[2048,64]{0,1:T(8,128)S(1)}, ...), condition=%wide.region_17.17_spmd.clone, body=%wide.region_15.16_spmd.clone.sunk | while | flops 685243904 | bytes 35289268 | solution.py:186
  737.9 20.1 %reduce-scatter.12.cloned.1.call-done = bf16[2,512,64]{1,2,0:T(8,128)(2,1)} async-done(((bf16[2,2048,64]{1,2,0:T(8,128)(2,1)}), bf16[2,512,64]{1,2,0:T(8,128)(2,1)}) %reduce-scatter.12.cloned.1.call-update) | async-done | bytes 131088 | tf_op jit(solution)/shard_map/reduce_scatter | solution.py:198
  758.0 3.8 fusion.47
  762.3 18.4 %reduce-scatter.10.cloned.1.call-done = bf16[2,512,64]{1,2,0:T(8,128)(2,1)} async-done(((bf16[2,2048,64]{1,2,0:T(8,128)(2,1)}), bf16[2,512,64]{1,2,0:T(8,128)(2,1)}) %reduce-scatter.10.cloned.1.call-update) | async-done | bytes 131088 | tf_op jit(solution)/shard_map/reduce_scatter | solution.py:195
  781.7 3.8 fusion.46
  785.6 7.1 convolution_convert_fusion.4
  797.7 3.7 convolution_convert_fusion.5
  801.5 11.0 convolution_convert_fusion.3
  819.5 3.3 add_convert_fusion
  823.0 10.5 convolution_convert_fusion
  833.6 11.0 convolution_convert_fusion.1
  844.7 11.0 convolution_convert_fusion.2
  859.0 49.9 %reduce-scatter.16.cloned.1.call-done = bf16[256,64]{0,1:T(8,128)(2,1)} async-done(((bf16[2048,64]{0,1:T(8,128)(2,1)}), bf16[256,64]{0,1:T(8,128)(2,1)}) %reduce-scatter.16.cloned.1.call-update) | async-done | bytes 32784 | tf_op jit(solution)/shard_map/reduce_scatter | solution.py:229
  910.3 69.6 %reduce-scatter.20.cloned.1.call-done = bf16[512,256]{1,0:T(8,128)(2,1)} async-done(((bf16[512,2048]{1,0:T(8,128)(2,1)}), bf16[512,256]{1,0:T(8,128)(2,1)}) %reduce-scatter.20.cloned.1.call-update) | async-done | bytes 262160 | tf_op jit(solution)/shard_map/reduce_scatter | solution.py:249
  981.7 68.4 %reduce-scatter.14.cloned.1.call-done = bf16[256,512]{1,0:T(8,128)(2,1)} async-done(((bf16[2048,512]{1,0:T(8,128)(2,1)}), bf16[256,512]{1,0:T(8,128)(2,1)}) %reduce-scatter.14.cloned.1.call-update) | async-done | bytes 262160 | tf_op jit(solution)/shard_map/reduce_scatter | solution.py:226
  1051.9 153.6 %all-reduce.12.cloned.1.call-done = (bf16[1024,2048]{1,0:T(8,128)(2,1)}, bf16[1024,2048]{1,0:T(8,128)(2,1)}) async-done(((bf16[1024,2048]{1,0:T(8,128)(2,1)}, bf16[1024,2048]{1,0:T(8,128)(2,1)}), (bf16[1024,2048]{1,0:T(8,128)(2,1)}, bf16[1024,2048]{1,0:T(8,128)(2,1)})) %all-reduce.12.cloned.1.call-update) | async-done | bytes 8388624 | tf_op jit(solution)/shard_map/psum | solution.py:133
  1205.5 5.0 fusion.39
  1210.5 23.0 %all-reduce.2 = (bf16[2048]{0:T(1024)(128)(2,1)S(1)}, bf16[2048]{0:T(1024)(128)(2,1)S(1)}) all-reduce(bf16[2048]{0:T(1024)(128)(2,1)S(1)} %get-tuple-element.410, bf16[2048]{0:T(1024)(128)(2,1)S(1)} %copy-done.43), channel_id=4, replica_groups=mesh['tensor'=4,'context'=4,'dp'=2] {'context','dp'}, use_global_device_ids=true, to_apply=%region_24.25.clone | all-reduce | flops 4096 | bytes 16384
  1234.2 17.5 %fusion.38 = (f32[1024,2048]{1,0:T(8,128)}, bf16[1024,2048]{1,0:T(8,128)(2,1)}) fusion(f32[1024,2048]{1,0:T(8,128)} %copy-done.8, bf16[1024,2048]{1,0:T(8,128)(2,1)} %get-tuple-element.503, bf16[2,512,2048]{2,1,0:T(8,128)(2,1)} %param.20, f32[1024]{0:T(1024)S(1)} %broadcast_multiply_fusion.1, f32[2048]{0:T(1024)S(1)} %copy-done.38, f32[1024]{0:T(1024)S(1)} %bitcast.311, ...), kind=kLoop, calls=%fused_computation.64 | loop fusion | flops 23068672 | bytes 41959424 | tf_op jit(solution)/shard_map/add | solution.py:221
  1251.7 68.0 %reduce-scatter.26.cloned.1.call-done = bf16[1408,256]{1,0:T(8,128)(2,1)} async-done(((bf16[1408,2048]{1,0:T(8,128)(2,1)}), bf16[1408,256]{1,0:T(8,128)(2,1)}) %reduce-scatter.26.cloned.1.call-update) | async-done | bytes 720912 | tf_op jit(solution)/shard_map/reduce_scatter | solution.py:252
  1322.0 111.1 %reduce-scatter.24.cloned.1.call-done = bf16[256,1408]{1,0:T(8,128)(2,1)} async-done(((bf16[2048,1408]{1,0:T(8,128)(2,1)}), bf16[256,1408]{1,0:T(8,128)(2,1)}) %reduce-scatter.24.cloned.1.call-update) | async-done | bytes 720912 | tf_op jit(solution)/shard_map/reduce_scatter | solution.py:238
  1435.4 111.0 %reduce-scatter.22.cloned.1.call-done = bf16[256,1408]{1,0:T(8,128)(2,1)} async-done(((bf16[2048,1408]{1,0:T(8,128)(2,1)}), bf16[256,1408]{1,0:T(8,128)(2,1)}) %reduce-scatter.22.cloned.1.call-update) | async-done | bytes 720912 | tf_op jit(solution)/shard_map/reduce_scatter | solution.py:235
  (459 shorter events, 296.1 us)
Async XLA Ops:
  7.2 178.3 %copy-start = (bf16[512,2048]{1,0:T(8,128)(2,1)S(1)}, bf16[512,2048]{1,0:T(8,128)(2,1)}, u32[]{:S(2)}) copy-start(bf16[512,2048]{1,0:T(8,128)(2,1)} %param.26) | copy-start | bytes 6291460
  7.2 6.3 copy-start.33
  7.2 335.8 %all-reduce.8.cloned.1.call-start = ((), (), s32[]{:S(2)}) async-start(), calls=%async_computation.9 | async-start | bytes 16777216 | tf_op jit(solution)/shard_map/psum | solution.py:124
  7.3 26.9 %copy-start.44 = (f32[32]{0:T(128)}, f32[32]{0:T(128)S(1)}, u32[]{:S(2)}) copy-start(f32[32]{0:T(128)S(1)} %multiply_power_fusion) | copy-start | bytes 388
  10.3 8.3 copy-start.37
  13.4 15.1 copy-start.40
  14.6 7.3 copy-start.42
  18.6 5.4 copy-start.22
  26.4 3.7 copy-start.3
  40.9 50.9 %copy-start.35 = (f32[2,8,512]{2,1,0:T(8,128)S(1)}, f32[2,8,512]{2,1,0:T(8,128)}, u32[]{:S(2)}) copy-start(f32[2,8,512]{2,1,0:T(8,128)} %custom-call.7) | copy-start | bytes 98308
  40.9 50.9 %copy-start.36 = (s32[2,512]{1,0:T(2,128)S(1)}, s32[2,512]{1,0:T(2,128)}, u32[]{:S(2)}) copy-start(s32[2,512]{1,0:T(2,128)} %constant_dynamic-slice_fusion.6) | copy-start | bytes 12292
  101.0 3.1 copy-start.10
  110.7 3.1 copy-start.10
  115.6 3.1 copy-start.10
  120.4 3.1 copy-start.10
  125.3 3.1 copy-start.10
  130.1 3.1 copy-start.10
  150.9 3.1 copy-start.10
  165.5 3.1 copy-start.10
  191.3 157.5 %copy-start.39 = (f32[2048]{0:T(1024)S(1)}, f32[2048]{0:T(1024)}, u32[]{:S(2)}) copy-start(f32[2048]{0:T(1024)} %param.27) | copy-start | bytes 24580
  191.3 372.2 %all-reduce.10.cloned.1.call-start = ((), (), s32[]{:S(2)}) async-start(), calls=%async_computation.10 | async-start | bytes 16777216 | tf_op jit(solution)/shard_map/psum | solution.py:151
  348.7 3.3 copy-start.2
  352.0 11.8 copy-start.16
  363.8 10.4 copy-start.14
  388.9 10.7 copy-start.47
  410.3 347.7 %reduce-scatter.12.cloned.1.call-start = ((), (), s32[]{:S(2)}) async-start(), calls=%async_computation.12 | async-start | bytes 655360 | tf_op jit(solution)/shard_map/reduce_scatter | solution.py:198
  563.5 8.2 copy-start.9
  563.5 9.4 copy-start.15
  577.5 3.4 copy-start.8
  587.3 150.1 %copy-start.45 = (f32[32]{0:T(128)S(1)}, f32[32]{0:T(128)}, u32[]{:S(2)}) copy-start(f32[32]{0:T(128)} %copy-done.44) | copy-start | bytes 388
  658.5 3.2 copy-start.5
  732.8 3.2 copy-start.5
  736.1 45.6 %copy-start.24 = (f32[1024,32]{0,1:T(8,128)S(1)}, f32[1024,32]{0,1:T(8,128)}, u32[]{:S(2)}) copy-start(f32[1024,32]{0,1:T(8,128)} %copy-done.23) | copy-start | bytes 393220
  736.1 44.6 %reduce-scatter.10.cloned.1.call-start = ((), (), s32[]{:S(2)}) async-start(), calls=%async_computation.11 | async-start | bytes 655360 | tf_op jit(solution)/shard_map/reduce_scatter | solution.py:195
  736.7 120.9 %reduce-scatter.18.cloned.1.call-start = ((), (), s32[]{:S(2)}) async-start(), calls=%async_computation.15 | async-start | bytes 294912 | tf_op jit(solution)/shard_map/reduce_scatter | solution.py:232
  761.8 23.8 %copy-start.28 = (bf16[64,8,2,512]{3,1,2,0:T(8,128)(2,1)S(1)}, bf16[64,8,2,512]{3,1,2,0:T(8,128)(2,1)}, u32[]{:S(2)}) copy-start(bf16[64,8,2,512]{3,1,2,0:T(8,128)(2,1)} %copy-done.27) | copy-start | bytes 3145732
  761.9 147.0 %reduce-scatter.16.cloned.1.call-start = ((), (), s32[]{:S(2)}) async-start(), calls=%async_computation.14 | async-start | bytes 294912 | tf_op jit(solution)/shard_map/reduce_scatter | solution.py:229
  785.6 194.3 %reduce-scatter.20.cloned.1.call-start = ((), (), s32[]{:S(2)}) async-start(), calls=%async_computation.16 | async-start | bytes 2359296 | tf_op jit(solution)/shard_map/reduce_scatter | solution.py:249
  792.7 257.4 %reduce-scatter.14.cloned.1.call-start = ((), (), s32[]{:S(2)}) async-start(), calls=%async_computation.13 | async-start | bytes 2359296 | tf_op jit(solution)/shard_map/reduce_scatter | solution.py:226
  801.5 404.1 %all-reduce.12.cloned.1.call-start = ((), (), s32[]{:S(2)}) async-start(), calls=%async_computation.20 | async-start | bytes 16777216 | tf_op jit(solution)/shard_map/psum | solution.py:133
  801.5 11.0 copy-start.11
  822.8 496.9 %reduce-scatter.26.cloned.1.call-start = ((), (), s32[]{:S(2)}) async-start(), calls=%async_computation.19 | async-start | bytes 6488064 | tf_op jit(solution)/shard_map/reduce_scatter | solution.py:252
  833.6 599.6 %reduce-scatter.24.cloned.1.call-start = ((), (), s32[]{:S(2)}) async-start(), calls=%async_computation.18 | async-start | bytes 6488064 | tf_op jit(solution)/shard_map/reduce_scatter | solution.py:238
  844.6 701.8 %reduce-scatter.22.cloned.1.call-start = ((), (), s32[]{:S(2)}) async-start(), calls=%async_computation.17 | async-start | bytes 6488064 | tf_op jit(solution)/shard_map/reduce_scatter | solution.py:235
  855.7 349.8 %copy-start.38 = (f32[2048]{0:T(1024)S(1)}, f32[2048]{0:T(1024)}, u32[]{:S(2)}) copy-start(f32[2048]{0:T(1024)} %param.22) | copy-start | bytes 24580
  855.7 349.8 %copy-start.41 = (f32[1,4,2,128]{3,1,2,0:T(4,128)S(1)}, f32[1,4,2,128]{3,1,2,0:T(4,128)}, u32[]{:S(2)}) copy-start(f32[1,4,2,128]{3,1,2,0:T(4,128)} %copy-done.40) | copy-start | bytes 12292
  1205.5 5.0 copy-start.43
  1234.2 314.5 %copy-start.1 = (bf16[512,2048]{1,0:T(8,128)(2,1)S(1)}, bf16[512,2048]{1,0:T(8,128)(2,1)}, u32[]{:S(2)}) copy-start(bf16[512,2048]{1,0:T(8,128)(2,1)} %param.26) | copy-start | bytes 6291460
  (29 other events, 56.6 us)
Sparse Core Ops, SparseCore 0:
  191.4 151.5 all-reduce.7
  410.4 152.9 all-reduce.9
  736.2 21.7 reduce-scatter.11
  760.7 19.9 reduce-scatter.9
  784.4 59.9 reduce-scatter.17
  848.1 60.7 reduce-scatter.15
  912.4 67.4 reduce-scatter.19
  983.4 66.6 reduce-scatter.13
  1053.3 152.2 all-reduce.11
  1209.0 110.6 reduce-scatter.25
  1323.4 109.7 reduce-scatter.23
  1436.6 109.7 reduce-scatter.21
where the time goes:
time: 1570 us; the launch traced here: 1560 us
  waiting for transfers between devices  976 us (62%)
  matrix products  320 us (20%)
  other arithmetic  95.6 us (6%)
  local copies, waits for them, and re-layouts  76.7 us (5%)
  blocking collectives  70 us (4%)
  between operations  15.8 us (1%)
    psum x1, waiting for transfers between devices, local(): lax.psum(jnp.dot(hidden, w_down, preferred_element_type=jnp.float32).asty...  154 us
    psum x1, waiting for transfers between devices, local(): d_mlp_in = lax.psum(mlp_back, 'tensor')  153 us
    psum x1, waiting for transfers between devices, local(): lax.psum(jnp.dot(attn_cat, w_output, preferred_element_type=jnp.float32),...  152 us
    reduce_scatter x1, waiting for transfers between devices, local(): lax.psum_scatter(grad_up.astype(jnp.bfloat16), ('context', 'dp'), scatter...  111 us
    reduce_scatter x1, waiting for transfers between devices, local(): lax.psum_scatter(grad_gate.astype(jnp.bfloat16), ('context', 'dp'), scatt...  111 us
    reduce_scatter x1, waiting for transfers between devices, local(): lax.psum_scatter(grad_output.astype(jnp.bfloat16), ('context', 'dp'), sca...  69.6 us
    reduce_scatter x1, waiting for transfers between devices, local(): lax.psum_scatter(grad_query.astype(jnp.bfloat16), ('context', 'dp'), scat...  68.4 us
    reduce_scatter x1, waiting for transfers between devices, local(): lax.psum_scatter(grad_down.astype(jnp.bfloat16), ('context', 'dp'), scatt...  68 us
  transfers between devices with their start and end apart: 12, of which 11 were waited for; matrix products, arithmetic and copies ran while one was open for 7% of the time, Pallas kernels for 0%

commit v1 on v0

v1 whole, which is shorter than its diff:
```python
import functools

import jax
import jax.numpy as jnp
from jax import lax
from jax.experimental import pallas as pl
from jax.experimental.pallas import tpu as pltpu
from jax.sharding import PartitionSpec as P

EPSILON = 1e-05
BF16 = jnp.bfloat16
F32 = jnp.float32
FAR = 1e30
AUX = 8
ONES_AT = 5
BLOCK = 256


def params():
    return pltpu.CompilerParams(vmem_limit_bytes=56 * 2**20)


def dot(left, right, dims):
    return lax.dot_general(left, right, (dims, ((), ())), preferred_element_type=F32)


NN, NT, TN = ((1,), (0,)), ((1,), (1,)), ((0,), (0,))


def turn(rows, cos_rows, sine_rows, sign):
    half = rows.shape[0] // 2
    first, second = rows[:half], rows[half:]
    return jnp.concatenate(
        [first * cos_rows - sign * second * sine_rows, second * cos_rows + sign * first * sine_rows], 0
    )


def project_kernel(x_ref, gain_ref, wq_ref, wkv_ref, cos_ref, sin_ref, h_ref, q_ref, kv_ref):
    x = x_ref[...].astype(F32)
    scale = lax.rsqrt(jnp.mean(x * x, -1, keepdims=True) + EPSILON)
    h = (x * scale * gain_ref[...]).astype(BF16)
    h_ref[...] = h
    cos_rows, sine_rows = cos_ref[...], sin_ref[...]
    head = kv_ref.shape[0] // 2
    score_scale = head ** (-0.5)
    q = dot(h, wq_ref[...], NN).T
    for at in range(0, q.shape[0], head):
        q_ref[at : at + head] = (turn(q[at : at + head], cos_rows, sine_rows, 1.0) * score_scale).astype(BF16)
    kv = dot(h, wkv_ref[...], NN).T
    kv_ref[:head] = turn(kv[:head], cos_rows, sine_rows, 1.0).astype(BF16)
    kv_ref[head:] = kv[head:].astype(BF16)


def project(x, gain, w_query, w_kv, cos_rows, sine_rows):
    rows, width = x.shape
    step = min(rows, 256)
    wide, both = w_query.shape[1], w_kv.shape[1]
    half = cos_rows.shape[0]
    whole = lambda shape: pl.BlockSpec(shape, lambda i: (0, 0))
    return pl.pallas_call(
        project_kernel,
        grid=(rows // step,),
        in_specs=[
            pl.BlockSpec((step, width), lambda i: (i, 0)),
            whole((1, width)),
            whole((width, wide)),
            whole((width, both)),
            pl.BlockSpec((half, step), lambda i: (0, i)),
            pl.BlockSpec((half, step), lambda i: (0, i)),
        ],
        out_specs=[
            pl.BlockSpec((step, width), lambda i: (i, 0)),
            pl.BlockSpec((wide, step), lambda i: (0, i)),
            pl.BlockSpec((both, step), lambda i: (0, i)),
        ],
        out_shape=[
            jax.ShapeDtypeStruct((rows, width), BF16),
            jax.ShapeDtypeStruct((wide, rows), BF16),
            jax.ShapeDtypeStruct((both, rows), BF16),
        ],
        compiler_params=params(),
        cost_estimate=pl.CostEstimate(
            flops=2 * rows * width * (wide + both), bytes_accessed=4 * rows * width + 2 * width * (wide + both), transcendentals=0
        ),
    )(x, gain, w_query, w_kv, cos_rows, sine_rows)


def pieces(value):
    high = value.astype(BF16).astype(F32)
    middle = (value - high).astype(BF16).astype(F32)
    low = value - high - middle
    return high, middle, low


def key_rows(kv, seg):
    head, count = kv.shape[0] // 2, kv.shape[1]
    row = lax.broadcasted_iota(jnp.int32, (2 * AUX, count), 0)
    extra = jnp.where(row < ONES_AT, jnp.where(seg == row, 0.0, -FAR), jnp.where(row < AUX, 1.0, 0.0))
    rest = jnp.zeros((head - 2 * AUX, count), F32)
    return jnp.concatenate([kv[:head].astype(F32), extra, rest], 0)


def value_rows(kv, fill):
    head, count = kv.shape[0] // 2, kv.shape[1]
    row = lax.broadcasted_iota(jnp.int32, (fill, count), 0)
    return jnp.concatenate([kv[head:].astype(F32), jnp.where(row < 3, 1.0, 0.0)], 0)


def causal(scores):
    key_at = lax.broadcasted_iota(jnp.int32, scores.shape, 0)
    query_at = lax.broadcasted_iota(jnp.int32, scores.shape, 1)
    return jnp.where(key_at <= query_at, scores, -FAR)


def attend_kernel(far_count, at_ref, q_ref, seg_ref, *refs):
    kv_refs = refs[: far_count + 1]
    qa_ref, o_ref, full_ref = refs[far_count + 1 : far_count + 4]
    ka_ref, va_ref, m_ref, acc_ref = refs[far_count + 4 :]
    me = at_ref[0]
    head, count = q_ref.shape

    @pl.when(pl.program_id(0) == 0)
    def _():
        for d, kv_ref in enumerate(kv_refs):
            kv = kv_ref[...]
            ka_ref[d] = key_rows(kv, seg_ref[d : d + 1]).T.astype(BF16)
            va_ref[d] = value_rows(kv, 2 * AUX).astype(BF16)

    row = lax.broadcasted_iota(jnp.int32, (2 * AUX, count), 0)
    same = jnp.where((seg_ref[0:1] == row) & (row < ONES_AT), 1.0, 0.0)
    q = q_ref[...].astype(F32)
    rest = jnp.zeros((head - 2 * AUX, count), F32)
    qa = jnp.concatenate([q, same, rest], 0).astype(BF16)

    scores = causal(dot(ka_ref[0], qa, NN))
    m = jnp.max(scores, 0, keepdims=True)
    probs = jnp.exp(scores - m).astype(BF16)
    m_ref[...] = m
    acc_ref[...] = dot(va_ref[0], probs, NN)
    for d in range(1, far_count + 1):

        @pl.when(d <= me)
        def _(d=d):
            scores = dot(ka_ref[d], qa, NN)
            before = m_ref[...]
            m = jnp.maximum(before, jnp.max(scores, 0, keepdims=True))
            probs = jnp.exp(scores - m).astype(BF16)
            m_ref[...] = m
            acc_ref[...] = acc_ref[...] * jnp.exp(before - m) + dot(va_ref[d], probs, NN)

    acc = acc_ref[...]
    total = acc[head : head + 1]
    out = acc[:head] / total
    full_ref[...] = out
    o_ref[...] = out.astype(BF16)
    high, middle, low = pieces(-(m_ref[...] + jnp.log(total)))
    extra = jnp.where(
        row == ONES_AT, high, jnp.where(row == ONES_AT + 1, middle, jnp.where(row == ONES_AT + 2, low, same))
    )
    qa_ref[...] = jnp.concatenate([q, extra, rest], 0).astype(BF16)


def attend(me, q, kvs, segs, item):
    far_count = len(kvs) - 1
    both = kvs[0].shape[0]
    head = both // 2
    wide, count = q.shape[0], segs.shape[-1]
    heads = wide // head
    return pl.pallas_call(
        functools.partial(attend_kernel, far_count),
        grid_spec=pltpu.PrefetchScalarGridSpec(
            num_scalar_prefetch=1,
            grid=(heads,),
            in_specs=[
                pl.BlockSpec((head, count), lambda h, at: (h, item)),
                pl.BlockSpec((None, far_count + 1, count), lambda h, at: (item, 0, 0)),
            ]
            + [pl.BlockSpec((both, count), lambda h, at: (0, item))] * (far_count + 1),
            out_specs=[
                pl.BlockSpec((None, both, count), lambda h, at: (h, 0, 0)),
                pl.BlockSpec((head, count), lambda h, at: (h, 0)),
                pl.BlockSpec((head, count), lambda h, at: (h, 0)),
            ],
            scratch_shapes=[
                pltpu.VMEM((far_count + 1, count, both), BF16),
                pltpu.VMEM((far_count + 1, head + 2 * AUX, count), BF16),
                pltpu.VMEM((1, count), F32),
                pltpu.VMEM((head + 2 * AUX, count), F32),
            ],
        ),
        out_shape=[
            jax.ShapeDtypeStruct((heads, both, count), BF16),
            jax.ShapeDtypeStruct((wide, count), BF16),
            jax.ShapeDtypeStruct((wide, count), F32),
        ],
        compiler_params=params(),
        cost_estimate=pl.CostEstimate(
            flops=16 * wide * count * count * (far_count + 1), bytes_accessed=12 * wide * count, transcendentals=0
        ),
    )(me, q, segs, *kvs)


def back_kernel(far_count, at_ref, qa_ref, do_ref, full_ref, seg_ref, cos_ref, sin_ref, *refs):
    kv_refs = refs[: far_count + 1]
    dq_ref = refs[far_count + 1]
    out_refs = refs[far_count + 2 : 2 * far_count + 3]
    ka_ref, kt_ref, va_ref, dk_ref, dv_ref, dq_acc = refs[2 * far_count + 3 :]
    me = at_ref[0]
    head, count = do_ref.shape
    step = pl.program_id(0)

    @pl.when(step == 0)
    def _():
        for d, kv_ref in enumerate(kv_refs):
            kv = kv_ref[...]
            ka_ref[d] = key_rows(kv, seg_ref[d : d + 1]).T.astype(BF16)
            kt_ref[d] = kv[:head]
            va_ref[d] = value_rows(kv, head).T.astype(BF16)
        dk_ref[...] = jnp.zeros_like(dk_ref)
        dv_ref[...] = jnp.zeros_like(dv_ref)

    qa = qa_ref[...]
    do = do_ref[...].astype(F32)
    high, middle, low = pieces(-jnp.sum(do * full_ref[...], 0, keepdims=True))
    row = lax.broadcasted_iota(jnp.int32, (2 * AUX, count), 0)
    extra = jnp.where(row == 0, high, jnp.where(row == 1, middle, jnp.where(row == 2, low, 0.0)))
    rest = jnp.zeros((head - 2 * AUX, count), F32)
    da = jnp.concatenate([do, extra, rest], 0).astype(BF16)
    for d in range(far_count + 1):

        def part(d=d):
            scores = dot(ka_ref[d], qa, NN)
            probs = jnp.exp(causal(scores) if d == 0 else scores)
            d_scores = (probs * dot(va_ref[d], da, NN)).astype(BF16)
            dv_ref[d] += dot(probs.astype(BF16), da[:head], NT)
            dk_ref[d] += dot(d_scores, qa[:head], NT)
            update = dot(kt_ref[d], d_scores, NN)
            if d == 0:
                dq_acc[...] = update
            else:
                dq_acc[...] += update

        if d == 0:
            part()
        else:
            pl.when(d <= me)(part)
    score_scale = head ** (-0.5)
    dq_ref[...] = turn(dq_acc[...] * score_scale, cos_ref[...], sin_ref[...], -1.0).astype(BF16)

    @pl.when(step == pl.num_programs(0) - 1)
    def _():
        for d, out_ref in enumerate(out_refs):
            out_ref[...] = jnp.concatenate([dk_ref[d], dv_ref[d]], 1).T.astype(out_ref.dtype)


def attend_back(me, qa, do, full, kvs, segs, cos_rows, sine_rows, item):
    far_count = len(kvs) - 1
    heads, both, count = qa.shape
    head = both // 2
    wide, half = heads * head, cos_rows.shape[0]
    return pl.pallas_call(
        functools.partial(back_kernel, far_count),
        grid_spec=pltpu.PrefetchScalarGridSpec(
            num_scalar_prefetch=1,
            grid=(heads,),
            in_specs=[
                pl.BlockSpec((None, both, count), lambda h, at: (h, 0, 0)),
                pl.BlockSpec((head, count), lambda h, at: (h, 0)),
                pl.BlockSpec((head, count), lambda h, at: (h, 0)),
                pl.BlockSpec((None, far_count + 1, count), lambda h, at: (item, 0, 0)),
                pl.BlockSpec((half, count), lambda h, at: (0, item)),
                pl.BlockSpec((half, count), lambda h, at: (0, item)),
            ]
            + [pl.BlockSpec((both, count), lambda h, at: (0, item))] * (far_count + 1),
            out_specs=[pl.BlockSpec((head, count), lambda h, at: (h, 0))]
            + [pl.BlockSpec((both, count), lambda h, at: (0, 0))] * (far_count + 1),
            scratch_shapes=[
                pltpu.VMEM((far_count + 1, count, both), BF16),
                pltpu.VMEM((far_count + 1, head, count), BF16),
                pltpu.VMEM((far_count + 1, count, both), BF16),
                pltpu.VMEM((far_count + 1, count, head), F32),
                pltpu.VMEM((far_count + 1, count, head), F32),
                pltpu.VMEM((head, count), F32),
            ],
        ),
        out_shape=[jax.ShapeDtypeStruct((wide, count), BF16), jax.ShapeDtypeStruct((both, count), F32)]
        + [jax.ShapeDtypeStruct((both, count), BF16)] * far_count,
        compiler_params=params(),
        cost_estimate=pl.CostEstimate(
            flops=40 * wide * count * count * (far_count + 1), bytes_accessed=12 * wide * count, transcendentals=0
        ),
    )(me, qa, do, full, segs, cos_rows, sine_rows, *kvs)


def grad_kernel(count, form, has_recv, split, *refs):
    refs = refs[1:]
    lefts, rights = refs[:count], refs[count : 2 * count]
    at = 2 * count
    total = None
    for left, right in zip(lefts, rights):
        term = dot(left[...], right[...], form)
        total = term if total is None else total + term
    if has_recv:
        total = total + refs[at][...].astype(F32)
        at += 1
    if not split:
        refs[at][...] = total.astype(BF16)
        return
    send, keep = refs[at], refs[at + 1]
    first = pl.program_id(0) < split

    @pl.when(first)
    def _():
        send[...] = total.astype(BF16)

    @pl.when(jnp.logical_not(first))
    def _():
        keep[...] = total.astype(BF16)


def grad_blocks(table, wide_set, narrow_set, natural, recv=None, split=0):
    n = table.shape[0]
    count = len(wide_set)
    tokens, width = wide_set[0].shape
    blk = BLOCK
    wide_spec = pl.BlockSpec((tokens, blk), lambda i, t: (0, t[i]))
    narrow_spec = [pl.BlockSpec(a.shape, lambda i, t: (0, 0)) for a in narrow_set]
    if natural:
        ins, specs, form = list(wide_set) + list(narrow_set), [wide_spec] * count + narrow_spec, TN
        block = (blk, narrow_set[0].shape[1])
    else:
        ins, specs, form = list(narrow_set) + list(wide_set), narrow_spec + [wide_spec] * count, NN
        block = (narrow_set[0].shape[0], blk)
    full = (None,) + block
    if recv is not None:
        ins.append(recv)
        specs.append(pl.BlockSpec(full, lambda i, t: (lax.rem(i + split, n), 0, 0)))
    if split:
        out_specs = [
            pl.BlockSpec(full, lambda i, t: (jnp.minimum(i, split - 1), 0, 0)),
            pl.BlockSpec(full, lambda i, t: (jnp.maximum(i - split, 0), 0, 0)),
        ]
        out_shape = [jax.ShapeDtypeStruct((split,) + block, BF16), jax.ShapeDtypeStruct((n - split,) + block, BF16)]
    else:
        out_specs = pl.BlockSpec(full, lambda i, t: (i, 0, 0))
        out_shape = jax.ShapeDtypeStruct((n,) + block, BF16)
    size = n * block[0] * block[1]
    return pl.pallas_call(
        functools.partial(grad_kernel, count, form, recv is not None, split),
        grid_spec=pltpu.PrefetchScalarGridSpec(
            num_scalar_prefetch=1, grid=(n,), in_specs=specs, out_specs=out_specs
        ),
        out_shape=out_shape,
        compiler_params=params(),
        cost_estimate=pl.CostEstimate(
            flops=2 * count * tokens * size, bytes_accessed=2 * size, transcendentals=0
        ),
    )(table, *ins)


class Scatter:
    def __init__(self, stages, sizes):
        self.stages, self.sizes = stages, sizes
        ctx, dp = lax.axis_index("context"), lax.axis_index("dp")
        blocks = []
        for p in range(2 ** len(stages)):
            c, d = ctx, dp
            for j, (axis, bit) in enumerate(stages):
                if p >> (len(stages) - 1 - j) & 1:
                    if axis == "context":
                        c = c ^ (1 << bit)
                    else:
                        d = d ^ (1 << bit)
            blocks.append(c * sizes["dp"] + d)
        self.table = jnp.stack(blocks).astype(jnp.int32)

    def swap(self, j, x):
        axis, bit = self.stages[j]
        return lax.ppermute(x, axis, [(i, i ^ (1 << bit)) for i in range(self.sizes[axis])])

    def run(self, wide_set, narrow_set, natural):
        n = self.table.shape[0]
        theirs = grad_blocks(self.table[n // 2 :], wide_set, narrow_set, natural)
        recv = self.swap(0, theirs)
        half = n // 2
        order = jnp.concatenate([self.table[half // 2 : half], self.table[: half // 2]])
        send, keep = grad_blocks(order, wide_set, narrow_set, natural, recv, half // 2)
        for j in range(1, len(self.stages)):
            recv = self.swap(j, send)
            if j == len(self.stages) - 1:
                return (keep.astype(F32) + recv.astype(F32))[0]
            half = keep.shape[0] // 2
            total = keep.astype(F32) + recv.astype(F32)
            send, keep = total[half:].astype(BF16), total[:half]


def swap(x, axis, size, bit):
    return lax.ppermute(x, axis, [(i, i ^ (1 << bit)) for i in range(size)])


def rows_at(x, at, count):
    return lax.dynamic_slice_in_dim(x, at, count, 0)


def local(sizes, tokens, segment_ids, norm_gain_1, w_query, w_key, w_value, w_output, norm_gain_2, w_gate, w_up, w_down, cotangent):
    seqs, stretch, width = tokens.shape
    length = segment_ids.shape[1]
    rows = seqs * stretch
    head = w_key.shape[1]
    n_tensor, n_context, n_dp = sizes["tensor"], sizes["context"], sizes["dp"]
    me_t, me_c = lax.axis_index("tensor"), lax.axis_index("context")
    core, high = me_t % 2, me_t // 2
    half, quarter = stretch // 2, stretch // 4
    offset = me_c * stretch

    seg_here = lax.dynamic_slice_in_dim(segment_ids, offset, stretch, 1)
    start = jnp.zeros(seg_here.shape, jnp.int32)
    for number in range(1, ONES_AT):
        before = jnp.sum((segment_ids < number).astype(jnp.int32), 1, keepdims=True)
        start = jnp.where(seg_here == number, before, start)
    positions = (offset + jnp.arange(stretch, dtype=jnp.int32))[None, :] - start
    frequency = 10000.0 ** (-(2.0 * jnp.arange(head // 2, dtype=F32)) / head)
    angles = frequency[:, None] * positions.reshape(1, rows).astype(F32)
    cos_rows, sine_rows = jnp.cos(angles), jnp.sin(angles)
    padded = jnp.concatenate([jnp.zeros((seqs, (n_context - 1) * stretch), jnp.int32), segment_ids], 1)
    segs = jnp.stack(
        [
            lax.dynamic_slice_in_dim(padded, offset + (n_context - 1 - d) * stretch, stretch, 1)
            for d in range(n_context)
        ],
        1,
    )
    at = jnp.reshape(me_c, (1,)).astype(jnp.int32)

    x_rows = tokens.reshape(rows, width)
    ct_rows = cotangent.reshape(rows, width)
    gain_1, gain_2 = norm_gain_1.reshape(1, width), norm_gain_2.reshape(1, width)
    w_kv = jnp.concatenate([w_key, w_value], 1)
    h1, q_t, kv_t = project(x_rows, gain_1, w_query, w_kv, cos_rows, sine_rows)
    kvs = [kv_t] + [
        lax.ppermute(kv_t, "context", [(i, i + d) for i in range(n_context - d)]) for d in range(1, n_context)
    ]
    d_hidden = [dot(ct_rows[s * stretch : (s + 1) * stretch], w_down, NT) for s in range(seqs)]

    def scatter(make):
        theirs = make((1 - core) * half, half).astype(BF16)
        got = swap(theirs, "tensor", n_tensor, 0)
        mine = make(core * half, half) + got.astype(F32)
        away = rows_at(mine, (1 - high) * quarter, quarter).astype(BF16)
        got = swap(away, "tensor", n_tensor, 1)
        return rows_at(mine, high * quarter, quarter) + got.astype(F32)

    def gather(part):
        got = swap(part, "tensor", n_tensor, 1)
        block = jnp.zeros((half, width), part.dtype)
        block = lax.dynamic_update_slice(block, part, (high * quarter, 0))
        block = lax.dynamic_update_slice(block, got, ((1 - high) * quarter, 0))
        got = swap(block, "tensor", n_tensor, 0)
        full = jnp.zeros((stretch, width), part.dtype)
        full = lax.dynamic_update_slice(full, block, (core * half, 0))
        return lax.dynamic_update_slice(full, got, ((1 - core) * half, 0))

    def quarter_of(x, s):
        return rows_at(x, s * stretch + core * half + high * quarter, quarter)

    seq = []
    for s in range(seqs):
        qa, o_t, full_o = attend(at, q_t, kvs, segs, s)
        part = scatter(
            lambda start, count: dot(lax.dynamic_slice_in_dim(o_t, start, count, 1), w_output, TN)
        )
        residual = quarter_of(x_rows, s).astype(F32) + part
        scale_2 = lax.rsqrt(jnp.mean(residual * residual, -1, keepdims=True) + EPSILON)
        normed_2 = residual * scale_2
        h2 = gather((normed_2 * gain_2).astype(BF16))
        seq.append(dict(qa=qa, o_t=o_t, full_o=full_o, residual=residual, scale_2=scale_2, normed_2=normed_2, h2=h2))
    for s in range(seqs):
        item = seq[s]
        gate = dot(item["h2"], w_gate, NN)
        up = dot(item["h2"], w_up, NN)
        sig = jax.nn.sigmoid(gate)
        item["hidden"] = (gate * sig * up).astype(BF16)
        item["d_gate"] = (d_hidden[s] * up * sig * (1.0 + gate * (1.0 - sig))).astype(BF16)
        item["d_up"] = (d_hidden[s] * gate * sig).astype(BF16)

    of = lambda name: [item[name] for item in seq]
    cts = [ct_rows[s * stretch : (s + 1) * stretch] for s in range(seqs)]
    blocks = n_context * n_dp
    fast = width // blocks == BLOCK and n_dp == 2 and n_context == 4
    if fast:
        x_first = Scatter([("dp", 0), ("context", 0), ("context", 1)], sizes)
        z_first = Scatter([("context", 0), ("dp", 0), ("context", 1)], sizes)
        down_sum = x_first.run(cts, of("hidden"), True).T
        gate_sum = x_first.run(of("h2"), of("d_gate"), True)
        up_sum = x_first.run(of("h2"), of("d_up"), True)
    else:

        def plain(left, right, dim):
            total = sum(dot(a, b, TN) for a, b in zip(left, right))
            return lax.psum_scatter(
                total.astype(BF16), ("context", "dp"), scatter_dimension=dim, tiled=True
            ).astype(F32)

        down_sum = plain(of("hidden"), cts, 1)
        gate_sum = plain(of("h2"), of("d_gate"), 0)
        up_sum = plain(of("h2"), of("d_up"), 0)

    for s in range(seqs):
        item = seq[s]
        back = scatter(
            lambda start, count: dot(rows_at(item["d_gate"], start, count), w_gate, NT)
            + dot(rows_at(item["d_up"], start, count), w_up, NT)
        )
        item["gain"] = jnp.sum(back * item["normed_2"], 0)
        scaled = back * gain_2
        item["d_res"] = quarter_of(ct_rows, s).astype(F32) + item["scale_2"] * (
            scaled - item["normed_2"] * jnp.mean(scaled * item["normed_2"], -1, keepdims=True)
        )
        item["d_low"] = gather(item["d_res"].astype(BF16))
        part = scatter(lambda start, count: dot(rows_at(item["hidden"], start, count), w_down, NN))
        item["out"] = gather((item["residual"] + part).astype(BF16))

    for s in range(seqs):
        item = seq[s]
        do_t = dot(w_output, item["d_low"], NT).astype(BF16)
        item["dq_t"], *item["dkvs"] = attend_back(
            at, item["qa"], do_t, item["full_o"], kvs, segs, cos_rows, sine_rows, s
        )
    dkv = jnp.concatenate([item["dkvs"][0] for item in seq], 1)
    for d in range(1, n_context):
        sent = jnp.concatenate([item["dkvs"][d] for item in seq], 1)
        dkv = dkv + lax.ppermute(sent, "context", [(i + d, i) for i in range(n_context - d)]).astype(F32)
    dkv_t = jnp.concatenate([turn(dkv[:head], cos_rows, sine_rows, -1.0), dkv[head:]], 0).astype(BF16)
    for s in range(seqs):
        item = seq[s]
        item["dqkv_t"] = jnp.concatenate([item["dq_t"], dkv_t[:, s * stretch : (s + 1) * stretch]], 0)
        item["h1"] = h1[s * stretch : (s + 1) * stretch]
    wide = w_query.shape[1]
    if fast:
        output_sum = z_first.run(of("d_low"), of("o_t"), False)
        mixed = z_first.run(of("h1"), of("dqkv_t"), False).T
    else:
        output_sum = lax.psum_scatter(
            sum(dot(a, b, NN) for a, b in zip(of("o_t"), of("d_low"))).astype(BF16),
            ("context", "dp"), scatter_dimension=1, tiled=True,
        ).astype(F32)
        mixed = lax.psum_scatter(
            sum(dot(b, a, NN).T for a, b in zip(of("h1"), of("dqkv_t"))).astype(BF16),
            ("context", "dp"), scatter_dimension=0, tiled=True,
        ).astype(F32)
    query_sum, key_sum, value_sum = mixed[:, :wide], mixed[:, wide : wide + head], mixed[:, wide + head :]

    w_all = jnp.concatenate([w_query, w_kv], 1)
    gains = []
    for s in range(seqs):
        item = seq[s]
        back = scatter(
            lambda start, count: dot(
                lax.dynamic_slice_in_dim(item["dqkv_t"], start, count, 1), w_all, ((0,), (1,))
            )
        )
        stream = quarter_of(x_rows, s).astype(F32)
        scale_1 = lax.rsqrt(jnp.mean(stream * stream, -1, keepdims=True) + EPSILON)
        normed_1 = stream * scale_1
        gains.append(jnp.sum(back * normed_1, 0))
        scaled = back * gain_1
        grad = item["d_res"] + scale_1 * (scaled - normed_1 * jnp.mean(scaled * normed_1, -1, keepdims=True))
        item["grad"] = gather(grad.astype(BF16))
    layer_out = jnp.stack(of("out"))
    grad_tokens = jnp.stack(of("grad")).astype(F32)

    gain_sum = jnp.stack([sum(gains), sum(of("gain"))])
    for axis in ("tensor", "context", "dp"):
        bit = 0
        while 1 << bit < sizes[axis]:
            gain_sum = gain_sum + swap(gain_sum, axis, sizes[axis], bit)
            bit += 1
    per = width // blocks
    gain_sum = lax.dynamic_slice_in_dim(gain_sum, (me_c * n_dp + lax.axis_index("dp")) * per, per, 1)
    return (
        layer_out,
        grad_tokens,
        gain_sum[0],
        query_sum,
        key_sum,
        value_sum,
        output_sum,
        gain_sum[1],
        gate_sum,
        up_sum,
        down_sum,
    )


def solution(mesh):
    in_specs = (
        P("dp", "context", None),
        P("dp", None),
        P(),
        P(None, "tensor"),
        P(None, "tensor"),
        P(None, "tensor"),
        P("tensor", None),
        P(),
        P(None, "tensor"),
        P(None, "tensor"),
        P("tensor", None),
        P("dp", "context", None),
    )
    out_specs = (
        P("dp", "context", None),
        P("dp", "context", None),
        P(("context", "dp")),
        P(("context", "dp"), "tensor"),
        P(("context", "dp"), "tensor"),
        P(("context", "dp"), "tensor"),
        P("tensor", ("context", "dp")),
        P(("context", "dp")),
        P(("context", "dp"), "tensor"),
        P(("context", "dp"), "tensor"),
        P("tensor", ("context", "dp")),
    )
    run = functools.partial(local, dict(mesh.shape))
    return jax.shard_map(run, mesh=mesh, in_specs=in_specs, out_specs=out_specs, check_vma=False)
```

time: 1570 us -> 703 us (0.45)
  waiting for transfers between devices: 976 us -> 261 us
  matrix products: 320 us -> 93.9 us
  Pallas kernels: 0 us -> 120 us
  starting transfers between devices: 1.07 us -> 111 us
  blocking collectives: 70 us -> 0 us
  other arithmetic: 95.6 us -> 51.5 us
  local copies, waits for them, and re-layouts: 76.7 us -> 53.9 us
    reduce_scatter x9 -> x0, waiting for transfers between devices: 517 us -> none  [the longest x1 111 us: local(): lax.psum_scatter(grad_up.astype(jnp.bfloat16), ('context', 'dp'), scatter...]
    psum x3 -> x0, waiting for transfers between devices: 458 us -> none  [the longest x1 154 us: local(): lax.psum(jnp.dot(hidden, w_down, preferred_element_type=jnp.float32).asty...]
    ppermute x0 -> x58, waiting for transfers between devices: none -> 261 us  [the longest x37 131 us: swap(): return lax.ppermute(x, axis, [(i, i ^ 1 << bit) for i in range(size)])]
    dot_general x133 -> x28, matrix products: 320 us -> 93.9 us  [dot(): lax.dot_general(left, right, (dims, ((), ())), preferred_element_type=F32)]
    pallas_call x0 -> x15, Pallas kernels: none -> 120 us  [the longest x10 75.1 us: grad_blocks(): pl.pallas_call(functools.partial(grad_kernel, count, form, recv is not No...]
    ppermute x0 -> x58, starting transfers between devices: none -> 111 us  [the longest x15 70.5 us: swap(): lax.ppermute(x, axis, [(i, i ^ 1 << bit) for i in range(self.sizes[axis])])]
    all_gather x2 -> x0, blocking collectives: 46.9 us -> none  [the longest x1 24.5 us: local(): lax.all_gather(key_here, 'context', axis=1, tiled=True)]
    convert_element_type x32 -> x1, other arithmetic: 33.9 us -> 5.53 us  [local(): grad_tokens = jnp.stack(of('grad')).astype(F32)]
  transfers between devices with their start and end apart: 12 -> 58, of which waited for: 11 -> 24; matrix products, arithmetic and copies ran while one was open for 7% -> 24% of each run, Pallas kernels for 0% -> 14%
where the time goes in v1:
time: 703 us; the launch traced here: 693 us
  waiting for transfers between devices  261 us (37%)
  Pallas kernels  120 us (17%)
  starting transfers between devices  111 us (16%)
  matrix products  93.9 us (13%)
  local copies, waits for them, and re-layouts  53.9 us (8%)
  other arithmetic  51.5 us (7%)
    ppermute x37, waiting for transfers between devices, swap(): return lax.ppermute(x, axis, [(i, i ^ 1 << bit) for i in range(size)])  131 us
    ppermute x15, waiting for transfers between devices, swap(): lax.ppermute(x, axis, [(i, i ^ 1 << bit) for i in range(self.sizes[axis])])  103 us
    dot_general x28, matrix products, dot(): lax.dot_general(left, right, (dims, ((), ())), preferred_element_type=F32)  93.9 us
    pallas_call x10, Pallas kernels, grad_blocks(): pl.pallas_call(functools.partial(grad_kernel, count, form, recv is not No...  75.1 us
    ppermute x15, starting transfers between devices, swap(): lax.ppermute(x, axis, [(i, i ^ 1 << bit) for i in range(self.sizes[axis])])  70.5 us
    ppermute x3, waiting for transfers between devices, local(): lax.ppermute(sent, 'context', [(i + d, i) for i in range(n_context - d)])  27 us
    ppermute x37, starting transfers between devices, swap(): return lax.ppermute(x, axis, [(i, i ^ 1 << bit) for i in range(size)])  24.6 us
    pallas_call x2, Pallas kernels, attend_back(): pl.pallas_call(functools.partial(back_kernel, far_count), grid_spec=pltpu...  20.5 us
  transfers between devices with their start and end apart: 58, of which 24 were waited for; matrix products, arithmetic and copies ran while one was open for 24% of the time, Pallas kernels for 14%

profile of v1, /device:TPU:0, one launch (start us, length us, event | category | flops | bytes accessed | tf_op | source)
XLA Modules:
  0.0 693.2 jit_solution(4915972402708351920)
XLA Ops:
  7.6 8.2 %shard_map.203 = (bf16[1024,2048]{1,0:T(8,128)(2,1)}, bf16[512,1024]{1,0:T(8,128)(2,1)}, bf16[128,1024]{1,0:T(8,128)(2,1)}) custom-call(bf16[1024,2048]{1,0:T(8,128)(2,1)} %bitcast.91, f32[1,2048]{1,0:T(1,128)} %bitcast.102, bf16[2048,512]{1,0:T(8,128)(2,1)} %wq_ref.1, bf16[2048,128]{1,0:T(8,128)(2,1)} %pad_maximum_fusion.4.wkv_ref, ...), custom_call_target="tpu_custom_call" | custom-call | flops 2684354560 | bytes 11010048 | tf_op jit(solution)/shard_map/pallas_call | solution.py:60
  15.8 5.2 collective-permute-start
  26.9 7.7 %fusion.108 = f32[512,1408]{1,0:T(8,128)} fusion(bf16[1408,2048]{1,0:T(8,128)(2,1)} %param.22, bf16[2,512,2048]{2,1,0:T(8,128)(2,1)S(1)} %copy-done.13), kind=kOutput, calls=%fused_computation.256 | convolution fusion | flops 2952790016 | bytes 10747904 | tf_op jit(solution)/shard_map/dot_general | solution.py:24
  34.5 5.0 fusion.109
  43.7 7.9 %shard_map.204 = (bf16[8,128,512]{2,1,0:T(8,128)(2,1)}, bf16[512,512]{1,0:T(8,128)(2,1)}, f32[512,512]{1,0:T(8,128)}) custom-call(s32[1]{0:T(128)} %bitcast.1.at_ref, bf16[512,1024]{1,0:T(8,128)(2,1)} %get-tuple-element.40.q_ref, s32[2,4,512]{2,1,0:T(4,128)} %pad_add_fusion.seg_ref, bf16[128,1024]{1,0:T(8,128)(2,1)} %get-tuple-element.41.refs_0_, ...), custom_call_target="tpu_custom_call" | custom-call | flops 8589934592 | bytes 3145728 | tf_op jit(solution)/shard_map/pallas_call | solution.py:169
  53.4 7.9 %shard_map.205 = (bf16[8,128,512]{2,1,0:T(8,128)(2,1)}, bf16[512,512]{1,0:T(8,128)(2,1)}, f32[512,512]{1,0:T(8,128)}) custom-call(s32[1]{0:T(128)} %bitcast.1.at_ref, bf16[512,1024]{1,0:T(8,128)(2,1)} %get-tuple-element.40.q_ref, s32[2,4,512]{2,1,0:T(4,128)} %pad_add_fusion.seg_ref, bf16[128,1024]{1,0:T(8,128)(2,1)} %get-tuple-element.41.refs_0_, ...), custom_call_target="tpu_custom_call" | custom-call | flops 8589934592 | bytes 3145728 | tf_op jit(solution)/shard_map/pallas_call | solution.py:169
  73.8 9.4 %collective-permute-done.4 = bf16[128,2048]{1,0:T(8,128)(2,1)S(1)} collective-permute-done((bf16[128,2048]{1,0:T(8,128)(2,1)S(1)}, bf16[128,2048]{1,0:T(8,128)(2,1)S(1)}, u32[]{:S(2)}, u32[]{:S(2)}) %collective-permute-start.4) | collective-permute-done | bytes 524320 | tf_op jit(solution)/shard_map/ppermute | solution.py:398
  83.2 10.3 %collective-permute-done.12 = bf16[128,2048]{1,0:T(8,128)(2,1)S(1)} collective-permute-done((bf16[128,2048]{1,0:T(8,128)(2,1)S(1)}, bf16[128,2048]{1,0:T(8,128)(2,1)S(1)}, u32[]{:S(2)}, u32[]{:S(2)}) %collective-permute-start.12) | collective-permute-done | bytes 524320 | tf_op jit(solution)/shard_map/ppermute | solution.py:398
  98.1 12.5 %collective-permute-done.13 = bf16[128,2048]{1,0:T(8,128)(2,1)S(1)} collective-permute-done((bf16[128,2048]{1,0:T(8,128)(2,1)S(1)}, bf16[128,2048]{1,0:T(8,128)(2,1)S(1)}, u32[]{:S(2)}, u32[]{:S(2)}) %collective-permute-start.13) | collective-permute-done | bytes 524320 | tf_op jit(solution)/shard_map/ppermute | solution.py:398
  111.8 8.2 %collective-permute-done.5 = bf16[128,2048]{1,0:T(8,128)(2,1)S(1)} collective-permute-done((bf16[128,2048]{1,0:T(8,128)(2,1)S(1)}, bf16[128,2048]{1,0:T(8,128)(2,1)S(1)}, u32[]{:S(2)}, u32[]{:S(2)}) %collective-permute-start.5) | collective-permute-done | bytes 524320 | tf_op jit(solution)/shard_map/ppermute | solution.py:398
  125.3 6.1 multiply_convert_fusion
  141.2 5.9 multiply_convert_fusion.2
  149.0 8.0 %shard_map.216 = bf16[4,256,1408]{2,1,0:T(8,128)(2,1)} custom-call(s32[4]{0:T(128)} %add_add_fusion.3.refs_0_, bf16[512,2048]{1,0:T(8,128)(2,1)} %get-tuple-element.125.refs_1_, bf16[512,2048]{1,0:T(8,128)(2,1)} %get-tuple-element.124.refs_2_, bf16[512,1408]{1,0:T(8,128)(2,1)} %copy-done.72, bf16[512,1408]{1,0:T(8,128)(2,1)} %get-tuple-element.123.refs_4_), custom_call_target="tpu_custom_call" | custom-call | flops 2952790016 | bytes 2883584 | tf_op jit(solution)/shard_map/pallas_call | solution.py:348
  158.5 8.4 %shard_map.214 = bf16[4,256,1408]{2,1,0:T(8,128)(2,1)} custom-call(s32[4]{0:T(128)} %add_add_fusion.3.refs_0_, bf16[512,2048]{1,0:T(8,128)(2,1)} %copy-done.30, bf16[512,2048]{1,0:T(8,128)(2,1)} %copy-done.31, bf16[512,1408]{1,0:T(8,128)(2,1)} %get-tuple-element.118.refs_3_, bf16[512,1408]{1,0:T(8,128)(2,1)} %get-tuple-element.121.refs_4_), custom_call_target="tpu_custom_call" | custom-call | flops 2952790016 | bytes 2883584 | tf_op jit(solution)/shard_map/pallas_call | solution.py:348
  167.5 6.1 fusion.1
  178.4 5.6 fusion
  189.6 8.1 %shard_map.212 = bf16[4,256,1408]{2,1,0:T(8,128)(2,1)} custom-call(s32[4]{0:T(128)} %add_add_fusion.3.refs_0_, bf16[512,2048]{1,0:T(8,128)(2,1)} %copy-done.30, bf16[512,2048]{1,0:T(8,128)(2,1)} %copy-done.31, bf16[512,1408]{1,0:T(8,128)(2,1)} %get-tuple-element.119.refs_3_, bf16[512,1408]{1,0:T(8,128)(2,1)} %copy-done.68), custom_call_target="tpu_custom_call" | custom-call | flops 2952790016 | bytes 2883584 | tf_op jit(solution)/shard_map/pallas_call | solution.py:348
  198.2 5.9 convert_add_fusion.5
  205.8 5.2 convert_add_fusion.6
  220.6 9.7 %collective-permute-done.20 = bf16[128,2048]{1,0:T(8,128)(2,1)S(1)} collective-permute-done((bf16[128,2048]{1,0:T(8,128)(2,1)S(1)}, bf16[128,2048]{1,0:T(8,128)(2,1)S(1)}, u32[]{:S(2)}, u32[]{:S(2)}) %collective-permute-start.20) | collective-permute-done | bytes 524320 | tf_op jit(solution)/shard_map/ppermute | solution.py:398
  245.2 7.6 %collective-permute-done.16 = bf16[128,2048]{1,0:T(8,128)(2,1)S(1)} collective-permute-done((bf16[128,2048]{1,0:T(8,128)(2,1)S(1)}, bf16[128,2048]{1,0:T(8,128)(2,1)S(1)}, u32[]{:S(2)}, u32[]{:S(2)}) %collective-permute-start.16) | collective-permute-done | bytes 524320 | tf_op jit(solution)/shard_map/ppermute | solution.py:398
  254.7 9.4 %collective-permute-done.25 = bf16[128,2048]{1,0:T(8,128)(2,1)S(1)} collective-permute-done((bf16[128,2048]{1,0:T(8,128)(2,1)S(1)}, bf16[128,2048]{1,0:T(8,128)(2,1)S(1)}, u32[]{:S(2)}, u32[]{:S(2)}) %collective-permute-start.25) | collective-permute-done | bytes 524320 | tf_op jit(solution)/shard_map/ppermute | solution.py:398
  265.6 9.7 %collective-permute-done.21 = bf16[128,2048]{1,0:T(8,128)(2,1)S(1)} collective-permute-done((bf16[128,2048]{1,0:T(8,128)(2,1)S(1)}, bf16[128,2048]{1,0:T(8,128)(2,1)S(1)}, u32[]{:S(2)}, u32[]{:S(2)}) %collective-permute-start.21) | collective-permute-done | bytes 524320 | tf_op jit(solution)/shard_map/ppermute | solution.py:398
  277.7 8.8 %collective-permute-done.9 = bf16[128,2048]{1,0:T(8,128)(2,1)S(1)} collective-permute-done((bf16[128,2048]{1,0:T(8,128)(2,1)S(1)}, bf16[128,2048]{1,0:T(8,128)(2,1)S(1)}, u32[]{:S(2)}, u32[]{:S(2)}) %collective-permute-start.9) | collective-permute-done | bytes 524320 | tf_op jit(solution)/shard_map/ppermute | solution.py:398
  287.4 9.3 %collective-permute-done.17 = bf16[128,2048]{1,0:T(8,128)(2,1)S(1)} collective-permute-done((bf16[128,2048]{1,0:T(8,128)(2,1)S(1)}, bf16[128,2048]{1,0:T(8,128)(2,1)S(1)}, u32[]{:S(2)}, u32[]{:S(2)}) %collective-permute-start.17) | collective-permute-done | bytes 524320 | tf_op jit(solution)/shard_map/ppermute | solution.py:398
  302.9 9.0 %shard_map.217 = (bf16[2,256,1408]{2,1,0:T(8,128)(2,1)}, bf16[2,256,1408]{2,1,0:T(8,128)(2,1)}) custom-call(s32[4]{0:T(128)} %add_add_fusion.2.refs_0_, bf16[512,2048]{1,0:T(8,128)(2,1)} %get-tuple-element.125.refs_1_, bf16[512,2048]{1,0:T(8,128)(2,1)} %get-tuple-element.124.refs_2_, bf16[512,1408]{1,0:T(8,128)(2,1)} %copy-done.72, ...), custom_call_target="tpu_custom_call" | custom-call | flops 2952790016 | bytes 2883584 | tf_op jit(solution)/shard_map/pallas_call | solution.py:348
  312.0 9.1 %shard_map.215 = (bf16[2,256,1408]{2,1,0:T(8,128)(2,1)}, bf16[2,256,1408]{2,1,0:T(8,128)(2,1)}) custom-call(s32[4]{0:T(128)} %add_add_fusion.2.refs_0_, bf16[512,2048]{1,0:T(8,128)(2,1)} %copy-done.30, bf16[512,2048]{1,0:T(8,128)(2,1)} %copy-done.31, bf16[512,1408]{1,0:T(8,128)(2,1)} %get-tuple-element.118.refs_3_, ...), custom_call_target="tpu_custom_call" | custom-call | flops 2952790016 | bytes 2883584 | tf_op jit(solution)/shard_map/pallas_call | solution.py:348
  321.1 24.7 %collective-permute-done.49.refs_5_ = bf16[4,256,1408]{2,1,0:T(8,128)(2,1)} collective-permute-done((bf16[4,256,1408]{2,1,0:T(8,128)(2,1)}, bf16[4,256,1408]{2,1,0:T(8,128)(2,1)}, u32[]{:S(2)}, u32[]{:S(2)}) %collective-permute-start.49) | collective-permute-done | bytes 2883616 | tf_op jit(solution)/shard_map/ppermute | solution.py:379
  345.8 10.0 %collective-permute-start.56 = (bf16[2,256,1408]{2,1,0:T(8,128)(2,1)}, bf16[2,256,1408]{2,1,0:T(8,128)(2,1)}, u32[]{:S(2)}, u32[]{:S(2)}) collective-permute-start(bf16[2,256,1408]{2,1,0:T(8,128)(2,1)} %get-tuple-element.68), channel_id=1, source_target_pairs={{0,2},{2,0},{4,6},{6,4},{1,3},{3,1},{5,7},{7,5},{8,10},{10,8},{12,... | collective-permute-start | bytes 4325384 | tf_op jit(solution)/shard_map/ppermute | solution.py:379
  355.7 8.9 %shard_map.213 = (bf16[2,256,1408]{2,1,0:T(8,128)(2,1)}, bf16[2,256,1408]{2,1,0:T(8,128)(2,1)}) custom-call(s32[4]{0:T(128)} %add_add_fusion.2.refs_0_, bf16[512,2048]{1,0:T(8,128)(2,1)} %copy-done.30, bf16[512,2048]{1,0:T(8,128)(2,1)} %copy-done.31, bf16[512,1408]{1,0:T(8,128)(2,1)} %get-tuple-element.119.refs_3_, bf16[512,1408]{1,0:T(8,128)(2,1)} %copy-done.68, ...), custom_call_target="tpu_custom_call" | custom-call | flops 2952790016 | bytes 2883584 | tf_op jit(solution)/shard_map/pallas_call | solution.py:348
  371.6 10.3 %shard_map.207 = (bf16[512,512]{1,0:T(8,128)(2,1)}, f32[128,512]{1,0:T(8,128)}, bf16[128,512]{1,0:T(8,128)(2,1)}, bf16[128,512]{1,0:T(8,128)(2,1)}, bf16[128,512]{1,0:T(8,128)(2,1)}) custom-call(s32[1]{0:T(128)} %bitcast.1.at_ref, bf16[8,128,512]{2,1,0:T(8,128)(2,1)} %get-tuple-element.48.qa_ref, bf16[512,512]{1,0:T(8,128)(2,1)} %fusion.12.do_ref, ...), custom_call_target="tpu_custom_call" | custom-call | flops 21474836480 | bytes 3145728 | tf_op jit(solution)/shard_map/pallas_call | solution.py:261
  381.9 10.3 %shard_map.206 = (bf16[512,512]{1,0:T(8,128)(2,1)}, f32[128,512]{1,0:T(8,128)}, bf16[128,512]{1,0:T(8,128)(2,1)}, bf16[128,512]{1,0:T(8,128)(2,1)}, bf16[128,512]{1,0:T(8,128)(2,1)}) custom-call(s32[1]{0:T(128)} %bitcast.1.at_ref, bf16[8,128,512]{2,1,0:T(8,128)(2,1)} %get-tuple-element.44.qa_ref, bf16[512,512]{1,0:T(8,128)(2,1)} %fusion.11.do_ref, ...), custom_call_target="tpu_custom_call" | custom-call | flops 21474836480 | bytes 3145728 | tf_op jit(solution)/shard_map/pallas_call | solution.py:261
  394.7 5.4 shard_map.210
  408.5 15.4 %collective-permute-done.27 = bf16[128,1024]{1,0:T(8,128)(2,1)S(1)} collective-permute-done((bf16[128,1024]{1,0:T(8,128)(2,1)S(1)}, bf16[128,1024]{1,0:T(8,128)(2,1)S(1)}, u32[]{:S(2)}, u32[]{:S(2)}) %collective-permute-start.27) | collective-permute-done | bytes 262176 | tf_op jit(solution)/shard_map/ppermute | solution.py:532
  423.9 22.6 %collective-permute-start.50 = (bf16[2,256,1408]{2,1,0:T(8,128)(2,1)}, bf16[2,256,1408]{2,1,0:T(8,128)(2,1)}, u32[]{:S(2)}, u32[]{:S(2)}) collective-permute-start(bf16[2,256,1408]{2,1,0:T(8,128)(2,1)} %get-tuple-element.64), channel_id=1, source_target_pairs={{0,2},{2,0},{4,6},{6,4},{1,3},{3,1},{5,7},{7,5},{8,10},{10,8},{12,... | collective-permute-start | bytes 4325384 | tf_op jit(solution)/shard_map/ppermute | solution.py:379
  446.5 6.5 collective-permute-done.28
  453.1 14.4 %collective-permute-start.46 = (bf16[4,512,256]{2,1,0:T(8,128)(2,1)}, bf16[4,512,256]{2,1,0:T(8,128)(2,1)S(1)}, u32[]{:S(2)}, u32[]{:S(2)}) collective-permute-start(bf16[4,512,256]{2,1,0:T(8,128)(2,1)} %shard_map.210), channel_id=1, source_target_pairs={{0,2},{2,0},{4,6},{6,4},{1,3},{3,1},{5,7},{7,5},{8,10},{10,8},{12,... | collective-permute-start | bytes 3145736 | tf_op jit(solution)/shard_map/ppermute | solution.py:379
  467.5 5.1 collective-permute-done.29
  475.3 5.9 shard_map.208
  485.5 26.6 %collective-permute-done.46.refs_5_ = bf16[4,512,256]{2,1,0:T(8,128)(2,1)S(1)} collective-permute-done((bf16[4,512,256]{2,1,0:T(8,128)(2,1)}, bf16[4,512,256]{2,1,0:T(8,128)(2,1)S(1)}, u32[]{:S(2)}, u32[]{:S(2)}) %collective-permute-start.46) | collective-permute-done | bytes 1048608 | tf_op jit(solution)/shard_map/ppermute | solution.py:379
  513.2 5.9 shard_map.211
  525.4 14.4 %collective-permute-start.57 = (bf16[1,256,1408]{2,1,0:T(8,128)(2,1)}, bf16[1,256,1408]{2,1,0:T(8,128)(2,1)}, u32[]{:S(2)}, u32[]{:S(2)}) collective-permute-start(bf16[1,256,1408]{2,1,0:T(8,128)(2,1)} %slice.185), channel_id=1, source_target_pairs={{0,4},{2,6},{4,0},{6,2},{1,5},{3,7},{5,1},{7,3},{8,12},{10,14},{12... | collective-permute-start | bytes 2162696 | tf_op jit(solution)/shard_map/ppermute | solution.py:379
  554.8 6.4 shard_map.209
  561.4 6.9 %collective-permute-done.31 = bf16[128,2048]{1,0:T(8,128)(2,1)} collective-permute-done((bf16[128,2048]{1,0:T(8,128)(2,1)}, bf16[128,2048]{1,0:T(8,128)(2,1)}, u32[]{:S(2)}, u32[]{:S(2)}) %collective-permute-start.31) | collective-permute-done | bytes 524320 | tf_op jit(solution)/shard_map/ppermute | solution.py:398
  581.5 11.1 %collective-permute-done.40 = f32[2,2048]{1,0:T(2,128)S(1)} collective-permute-done((f32[2,2048]{1,0:T(2,128)S(1)}, f32[2,2048]{1,0:T(2,128)S(1)}, u32[]{:S(2)}, u32[]{:S(2)}) %collective-permute-start.40) | collective-permute-done | bytes 16416 | tf_op jit(solution)/shard_map/ppermute | solution.py:398
  593.2 51.8 %collective-permute-done.48 = bf16[1,512,256]{2,1,0:T(8,128)(2,1)S(1)} collective-permute-done((bf16[1,512,256]{2,1,0:T(8,128)(2,1)}, bf16[1,512,256]{2,1,0:T(8,128)(2,1)S(1)}, u32[]{:S(2)}, u32[]{:S(2)}) %collective-permute-start.48) | collective-permute-done | bytes 262176 | tf_op jit(solution)/shard_map/ppermute | solution.py:379
  668.4 5.2 collective-permute-done.36
  687.5 5.5 maximum_convert_fusion
  (424 shorter events, 203.1 us)
Async XLA Ops:
  15.8 26.9 %collective-permute-start = (bf16[128,1024]{1,0:T(8,128)(2,1)}, bf16[128,1024]{1,0:T(8,128)(2,1)S(1)}, u32[]{:S(2)}, u32[]{:S(2)}) collective-permute-start(bf16[128,1024]{1,0:T(8,128)(2,1)} %get-tuple-element.41.refs_0_), channel_id=1, source_target_pairs={{0,2},{2,4},{4,6},{1,3},{3,5},{5,7},{8,10},{10,12},{12,14},{9,11},... | collective-permute-start | bytes 786440 | tf_op jit(solution)/shard_map/ppermute | solution.py:441
  21.0 21.7 %collective-permute-start.1 = (bf16[128,1024]{1,0:T(8,128)(2,1)}, bf16[128,1024]{1,0:T(8,128)(2,1)S(1)}, u32[]{:S(2)}, u32[]{:S(2)}) collective-permute-start(bf16[128,1024]{1,0:T(8,128)(2,1)} %get-tuple-element.41.refs_0_), channel_id=1, source_target_pairs={{0,4},{2,6},{1,5},{3,7},{8,12},{10,14},{9,13},{11,15},{16,20},{18,... | collective-permute-start | bytes 786440 | tf_op jit(solution)/shard_map/ppermute | solution.py:441
  25.5 17.2 %collective-permute-start.2 = (bf16[128,1024]{1,0:T(8,128)(2,1)}, bf16[128,1024]{1,0:T(8,128)(2,1)S(1)}, u32[]{:S(2)}, u32[]{:S(2)}) collective-permute-start(bf16[128,1024]{1,0:T(8,128)(2,1)} %get-tuple-element.41.refs_0_), channel_id=1, source_target_pairs={{0,6},{1,7},{8,14},{9,15},{16,22},{17,23},{24,30},{25,31}} | collective-permute-start | bytes 786440 | tf_op jit(solution)/shard_map/ppermute | solution.py:441
  68.4 14.9 %collective-permute-start.4 = (bf16[128,2048]{1,0:T(8,128)(2,1)S(1)}, bf16[128,2048]{1,0:T(8,128)(2,1)S(1)}, u32[]{:S(2)}, u32[]{:S(2)}) collective-permute-start(bf16[128,2048]{1,0:T(8,128)(2,1)S(1)} %dynamic-slice_convert_fusion.7), channel_id=1, source_target_pairs={{0,16},{8,24},{16,0},{24,8},{1,17},{9,25},{17,1},{25,9},{2,18},{10... | collective-permute-start | bytes 1572872 | tf_op jit(solution)/shard_map/ppermute | solution.py:398
  70.8 22.8 %collective-permute-start.12 = (bf16[128,2048]{1,0:T(8,128)(2,1)S(1)}, bf16[128,2048]{1,0:T(8,128)(2,1)S(1)}, u32[]{:S(2)}, u32[]{:S(2)}) collective-permute-start(bf16[128,2048]{1,0:T(8,128)(2,1)S(1)} %dynamic-slice_convert_fusion.5), channel_id=1, source_target_pairs={{0,16},{8,24},{16,0},{24,8},{1,17},{9,25},{17,1},{25,9},{2,18},{10... | collective-permute-start | bytes 1572872 | tf_op jit(solution)/shard_map/ppermute | solution.py:398
  95.7 14.9 %collective-permute-start.13 = (bf16[128,2048]{1,0:T(8,128)(2,1)S(1)}, bf16[128,2048]{1,0:T(8,128)(2,1)S(1)}, u32[]{:S(2)}, u32[]{:S(2)}) collective-permute-start(bf16[128,2048]{1,0:T(8,128)(2,1)S(1)} %get-tuple-element.115), channel_id=1, source_target_pairs={{0,16},{8,24},{16,0},{24,8},{1,17},{9,25},{17,1},{25,9},{2,18},{10... | collective-permute-start | bytes 1572872 | tf_op jit(solution)/shard_map/ppermute | solution.py:398
  97.6 22.4 %collective-permute-start.5 = (bf16[128,2048]{1,0:T(8,128)(2,1)S(1)}, bf16[128,2048]{1,0:T(8,128)(2,1)S(1)}, u32[]{:S(2)}, u32[]{:S(2)}) collective-permute-start(bf16[128,2048]{1,0:T(8,128)(2,1)S(1)} %get-tuple-element.109), channel_id=1, source_target_pairs={{0,16},{8,24},{16,0},{24,8},{1,17},{9,25},{17,1},{25,9},{2,18},{10... | collective-permute-start | bytes 1572872 | tf_op jit(solution)/shard_map/ppermute | solution.py:398
  120.1 17.5 %collective-permute-start.6 = (bf16[256,2048]{1,0:T(8,128)(2,1)S(1)}, bf16[256,2048]{1,0:T(8,128)(2,1)S(1)}, u32[]{:S(2)}, u32[]{:S(2)}) collective-permute-start(bf16[256,2048]{1,0:T(8,128)(2,1)S(1)} %constant_dynamic-update-slice_fusion.22), channel_id=1, source_target_pairs={{0,8},{8,0},{16,24},{24,16},{1,9},{9,1},{17,25},{25,17},{2,10},{10... | collective-permute-start | bytes 3145736 | tf_op jit(solution)/shard_map/ppermute | solution.py:398
  157.0 145.4 %collective-permute-start.55 = (bf16[4,256,1408]{2,1,0:T(8,128)(2,1)}, bf16[4,256,1408]{2,1,0:T(8,128)(2,1)}, u32[]{:S(2)}, u32[]{:S(2)}) collective-permute-start(bf16[4,256,1408]{2,1,0:T(8,128)(2,1)} %shard_map.216), channel_id=1, source_target_pairs={{0,1},{1,0},{2,3},{3,2},{4,5},{5,4},{6,7},{7,6},{8,9},{9,8},{10,11... | collective-permute-start | bytes 8650760 | tf_op jit(solution)/shard_map/ppermute | solution.py:379
  166.9 145.0 %collective-permute-start.52 = (bf16[4,256,1408]{2,1,0:T(8,128)(2,1)}, bf16[4,256,1408]{2,1,0:T(8,128)(2,1)}, u32[]{:S(2)}, u32[]{:S(2)}) collective-permute-start(bf16[4,256,1408]{2,1,0:T(8,128)(2,1)} %shard_map.214), channel_id=1, source_target_pairs={{0,1},{1,0},{2,3},{3,2},{4,5},{5,4},{6,7},{7,6},{8,9},{9,8},{10,11... | collective-permute-start | bytes 8650760 | tf_op jit(solution)/shard_map/ppermute | solution.py:379
  173.7 24.0 %collective-permute-start.23 = (bf16[256,2048]{1,0:T(8,128)(2,1)}, bf16[256,2048]{1,0:T(8,128)(2,1)}, u32[]{:S(2)}, u32[]{:S(2)}) collective-permute-start(bf16[256,2048]{1,0:T(8,128)(2,1)} %fusion.1), channel_id=1, source_target_pairs={{0,8},{8,0},{16,24},{24,16},{1,9},{9,1},{17,25},{25,17},{2,10},{10... | collective-permute-start | bytes 3145736 | tf_op jit(solution)/shard_map/ppermute | solution.py:398
  184.0 20.2 %collective-permute-start.19 = (bf16[256,2048]{1,0:T(8,128)(2,1)}, bf16[256,2048]{1,0:T(8,128)(2,1)}, u32[]{:S(2)}, u32[]{:S(2)}) collective-permute-start(bf16[256,2048]{1,0:T(8,128)(2,1)} %fusion), channel_id=1, source_target_pairs={{0,8},{8,0},{16,24},{24,16},{1,9},{9,1},{17,25},{25,17},{2,10},{10... | collective-permute-start | bytes 3145736 | tf_op jit(solution)/shard_map/ppermute | solution.py:398
  184.5 26.7 %collective-permute-start.7 = (bf16[256,2048]{1,0:T(8,128)(2,1)S(1)}, bf16[256,2048]{1,0:T(8,128)(2,1)S(1)}, u32[]{:S(2)}, u32[]{:S(2)}) collective-permute-start(bf16[256,2048]{1,0:T(8,128)(2,1)S(1)} %convolution_convert_fusion.5), channel_id=1, source_target_pairs={{0,8},{8,0},{16,24},{24,16},{1,9},{9,1},{17,25},{25,17},{2,10},{10... | collective-permute-start | bytes 3145736 | tf_op jit(solution)/shard_map/ppermute | solution.py:398
  197.7 15.9 %collective-permute-start.15 = (bf16[256,2048]{1,0:T(8,128)(2,1)S(1)}, bf16[256,2048]{1,0:T(8,128)(2,1)S(1)}, u32[]{:S(2)}, u32[]{:S(2)}) collective-permute-start(bf16[256,2048]{1,0:T(8,128)(2,1)S(1)} %convolution_convert_fusion.4), channel_id=1, source_target_pairs={{0,8},{8,0},{16,24},{24,16},{1,9},{9,1},{17,25},{25,17},{2,10},{10... | collective-permute-start | bytes 3145736 | tf_op jit(solution)/shard_map/ppermute | solution.py:398
  204.3 14.9 %collective-permute-start.24 = (bf16[128,2048]{1,0:T(8,128)(2,1)S(1)}, bf16[128,2048]{1,0:T(8,128)(2,1)S(1)}, u32[]{:S(2)}, u32[]{:S(2)}) collective-permute-start(bf16[128,2048]{1,0:T(8,128)(2,1)S(1)} %dynamic-slice_convert_fusion.2), channel_id=1, source_target_pairs={{0,16},{8,24},{16,0},{24,8},{1,17},{9,25},{17,1},{25,9},{2,18},{10... | collective-permute-start | bytes 1572872 | tf_op jit(solution)/shard_map/ppermute | solution.py:398
  211.2 19.2 %collective-permute-start.20 = (bf16[128,2048]{1,0:T(8,128)(2,1)S(1)}, bf16[128,2048]{1,0:T(8,128)(2,1)S(1)}, u32[]{:S(2)}, u32[]{:S(2)}) collective-permute-start(bf16[128,2048]{1,0:T(8,128)(2,1)S(1)} %dynamic-slice_convert_fusion.3), channel_id=1, source_target_pairs={{0,16},{8,24},{16,0},{24,8},{1,17},{9,25},{17,1},{25,9},{2,18},{10... | collective-permute-start | bytes 1572872 | tf_op jit(solution)/shard_map/ppermute | solution.py:398
  213.6 28.0 %collective-permute-start.8 = (bf16[128,2048]{1,0:T(8,128)(2,1)S(1)}, bf16[128,2048]{1,0:T(8,128)(2,1)S(1)}, u32[]{:S(2)}, u32[]{:S(2)}) collective-permute-start(bf16[128,2048]{1,0:T(8,128)(2,1)S(1)} %dynamic-slice_convert_fusion.6), channel_id=1, source_target_pairs={{0,16},{8,24},{16,0},{24,8},{1,17},{9,25},{17,1},{25,9},{2,18},{10... | collective-permute-start | bytes 1572872 | tf_op jit(solution)/shard_map/ppermute | solution.py:398
  219.1 33.7 %collective-permute-start.16 = (bf16[128,2048]{1,0:T(8,128)(2,1)S(1)}, bf16[128,2048]{1,0:T(8,128)(2,1)S(1)}, u32[]{:S(2)}, u32[]{:S(2)}) collective-permute-start(bf16[128,2048]{1,0:T(8,128)(2,1)S(1)} %dynamic-slice_convert_fusion.4), channel_id=1, source_target_pairs={{0,16},{8,24},{16,0},{24,8},{1,17},{9,25},{17,1},{25,9},{2,18},{10... | collective-permute-start | bytes 1572872 | tf_op jit(solution)/shard_map/ppermute | solution.py:398
  233.7 30.4 %collective-permute-start.25 = (bf16[128,2048]{1,0:T(8,128)(2,1)S(1)}, bf16[128,2048]{1,0:T(8,128)(2,1)S(1)}, u32[]{:S(2)}, u32[]{:S(2)}) collective-permute-start(bf16[128,2048]{1,0:T(8,128)(2,1)S(1)} %get-tuple-element.101), channel_id=1, source_target_pairs={{0,16},{8,24},{16,0},{24,8},{1,17},{9,25},{17,1},{25,9},{2,18},{10... | collective-permute-start | bytes 1572872 | tf_op jit(solution)/shard_map/ppermute | solution.py:398
  241.6 33.7 %collective-permute-start.21 = (bf16[128,2048]{1,0:T(8,128)(2,1)S(1)}, bf16[128,2048]{1,0:T(8,128)(2,1)S(1)}, u32[]{:S(2)}, u32[]{:S(2)}) collective-permute-start(bf16[128,2048]{1,0:T(8,128)(2,1)S(1)} %get-tuple-element.104), channel_id=1, source_target_pairs={{0,16},{8,24},{16,0},{24,8},{1,17},{9,25},{17,1},{25,9},{2,18},{10... | collective-permute-start | bytes 1572872 | tf_op jit(solution)/shard_map/ppermute | solution.py:398
  252.8 33.7 %collective-permute-start.9 = (bf16[128,2048]{1,0:T(8,128)(2,1)S(1)}, bf16[128,2048]{1,0:T(8,128)(2,1)S(1)}, u32[]{:S(2)}, u32[]{:S(2)}) collective-permute-start(bf16[128,2048]{1,0:T(8,128)(2,1)S(1)} %get-tuple-element.107), channel_id=1, source_target_pairs={{0,16},{8,24},{16,0},{24,8},{1,17},{9,25},{17,1},{25,9},{2,18},{10... | collective-permute-start | bytes 1572872 | tf_op jit(solution)/shard_map/ppermute | solution.py:398
  264.1 81.7 %collective-permute-start.49 = (bf16[4,256,1408]{2,1,0:T(8,128)(2,1)}, bf16[4,256,1408]{2,1,0:T(8,128)(2,1)}, u32[]{:S(2)}, u32[]{:S(2)}) collective-permute-start(bf16[4,256,1408]{2,1,0:T(8,128)(2,1)} %shard_map.212), channel_id=1, source_target_pairs={{0,1},{1,0},{2,3},{3,2},{4,5},{5,4},{6,7},{7,6},{8,9},{9,8},{10,11... | collective-permute-start | bytes 8650760 | tf_op jit(solution)/shard_map/ppermute | solution.py:379
  275.3 21.4 %collective-permute-start.17 = (bf16[128,2048]{1,0:T(8,128)(2,1)S(1)}, bf16[128,2048]{1,0:T(8,128)(2,1)S(1)}, u32[]{:S(2)}, u32[]{:S(2)}) collective-permute-start(bf16[128,2048]{1,0:T(8,128)(2,1)S(1)} %get-tuple-element.113), channel_id=1, source_target_pairs={{0,16},{8,24},{16,0},{24,8},{1,17},{9,25},{17,1},{25,9},{2,18},{10... | collective-permute-start | bytes 1572872 | tf_op jit(solution)/shard_map/ppermute | solution.py:398
  286.5 78.1 %collective-permute-start.26 = (bf16[256,2048]{1,0:T(8,128)(2,1)S(1)}, bf16[256,2048]{1,0:T(8,128)(2,1)}, u32[]{:S(2)}, u32[]{:S(2)}) collective-permute-start(bf16[256,2048]{1,0:T(8,128)(2,1)S(1)} %constant_dynamic-update-slice_fusion.6), channel_id=1, source_target_pairs={{0,8},{8,0},{16,24},{24,16},{1,9},{9,1},{17,25},{25,17},{2,10},{10... | collective-permute-start | bytes 3145736 | tf_op jit(solution)/shard_map/ppermute | solution.py:398
  296.7 71.5 %collective-permute-start.22 = (bf16[256,2048]{1,0:T(8,128)(2,1)}, bf16[256,2048]{1,0:T(8,128)(2,1)}, u32[]{:S(2)}, u32[]{:S(2)}) collective-permute-start(bf16[256,2048]{1,0:T(8,128)(2,1)} %constant_dynamic-update-slice_fusion.10), channel_id=1, source_target_pairs={{0,8},{8,0},{16,24},{24,16},{1,9},{9,1},{17,25},{25,17},{2,10},{10... | collective-permute-start | bytes 3145736 | tf_op jit(solution)/shard_map/ppermute | solution.py:398
  302.3 97.9 %collective-permute-start.10 = (bf16[256,2048]{1,0:T(8,128)(2,1)}, bf16[256,2048]{1,0:T(8,128)(2,1)}, u32[]{:S(2)}, u32[]{:S(2)}) collective-permute-start(bf16[256,2048]{1,0:T(8,128)(2,1)} %constant_dynamic-update-slice_fusion.18), channel_id=1, source_target_pairs={{0,8},{8,0},{16,24},{24,16},{1,9},{9,1},{17,25},{25,17},{2,10},{10... | collective-permute-start | bytes 3145736 | tf_op jit(solution)/shard_map/ppermute | solution.py:398
  311.9 91.2 %collective-permute-start.18 = (bf16[256,2048]{1,0:T(8,128)(2,1)}, bf16[256,2048]{1,0:T(8,128)(2,1)}, u32[]{:S(2)}, u32[]{:S(2)}) collective-permute-start(bf16[256,2048]{1,0:T(8,128)(2,1)} %copy-done.19), channel_id=1, source_target_pairs={{0,8},{8,0},{16,24},{24,16},{1,9},{9,1},{17,25},{25,17},{2,10},{10... | collective-permute-start | bytes 3145736 | tf_op jit(solution)/shard_map/ppermute | solution.py:398
  345.8 173.2 %collective-permute-start.56 = (bf16[2,256,1408]{2,1,0:T(8,128)(2,1)}, bf16[2,256,1408]{2,1,0:T(8,128)(2,1)}, u32[]{:S(2)}, u32[]{:S(2)}) collective-permute-start(bf16[2,256,1408]{2,1,0:T(8,128)(2,1)} %get-tuple-element.68), channel_id=1, source_target_pairs={{0,2},{2,0},{4,6},{6,4},{1,3},{3,1},{5,7},{7,5},{8,10},{10,8},{12,... | collective-permute-start | bytes 4325384 | tf_op jit(solution)/shard_map/ppermute | solution.py:379
  364.7 156.2 %collective-permute-start.53 = (bf16[2,256,1408]{2,1,0:T(8,128)(2,1)}, bf16[2,256,1408]{2,1,0:T(8,128)(2,1)}, u32[]{:S(2)}, u32[]{:S(2)}) collective-permute-start(bf16[2,256,1408]{2,1,0:T(8,128)(2,1)} %get-tuple-element.66), channel_id=1, source_target_pairs={{0,2},{2,0},{4,6},{6,4},{1,3},{3,1},{5,7},{7,5},{8,10},{10,8},{12,... | collective-permute-start | bytes 4325384 | tf_op jit(solution)/shard_map/ppermute | solution.py:379
  393.2 30.8 %collective-permute-start.27 = (bf16[128,1024]{1,0:T(8,128)(2,1)S(1)}, bf16[128,1024]{1,0:T(8,128)(2,1)S(1)}, u32[]{:S(2)}, u32[]{:S(2)}) collective-permute-start(bf16[128,1024]{1,0:T(8,128)(2,1)S(1)} %pad_maximum_fusion.5), channel_id=1, source_target_pairs={{2,0},{4,2},{6,4},{3,1},{5,3},{7,5},{10,8},{12,10},{14,12},{11,9},... | collective-permute-start | bytes 786440 | tf_op jit(solution)/shard_map/ppermute | solution.py:532
  400.3 52.8 %collective-permute-start.28 = (bf16[128,1024]{1,0:T(8,128)(2,1)S(1)}, bf16[128,1024]{1,0:T(8,128)(2,1)S(1)}, u32[]{:S(2)}, u32[]{:S(2)}) collective-permute-start(bf16[128,1024]{1,0:T(8,128)(2,1)S(1)} %pad_maximum_fusion.6), channel_id=1, source_target_pairs={{4,0},{6,2},{5,1},{7,3},{12,8},{14,10},{13,9},{15,11},{20,16},{22,... | collective-permute-start | bytes 786440 | tf_op jit(solution)/shard_map/ppermute | solution.py:532
  403.1 69.5 %collective-permute-start.29 = (bf16[128,1024]{1,0:T(8,128)(2,1)S(1)}, bf16[128,1024]{1,0:T(8,128)(2,1)S(1)}, u32[]{:S(2)}, u32[]{:S(2)}) collective-permute-start(bf16[128,1024]{1,0:T(8,128)(2,1)S(1)} %pad_maximum_fusion.7), channel_id=1, source_target_pairs={{6,0},{7,1},{14,8},{15,9},{22,16},{23,17},{30,24},{31,25}} | collective-permute-start | bytes 786440 | tf_op jit(solution)/shard_map/ppermute | solution.py:532
  423.9 122.8 %collective-permute-start.50 = (bf16[2,256,1408]{2,1,0:T(8,128)(2,1)}, bf16[2,256,1408]{2,1,0:T(8,128)(2,1)}, u32[]{:S(2)}, u32[]{:S(2)}) collective-permute-start(bf16[2,256,1408]{2,1,0:T(8,128)(2,1)} %get-tuple-element.64), channel_id=1, source_target_pairs={{0,2},{2,0},{4,6},{6,4},{1,3},{3,1},{5,7},{7,5},{8,10},{10,8},{12,... | collective-permute-start | bytes 4325384 | tf_op jit(solution)/shard_map/ppermute | solution.py:379
  453.1 59.0 %collective-permute-start.46 = (bf16[4,512,256]{2,1,0:T(8,128)(2,1)}, bf16[4,512,256]{2,1,0:T(8,128)(2,1)S(1)}, u32[]{:S(2)}, u32[]{:S(2)}) collective-permute-start(bf16[4,512,256]{2,1,0:T(8,128)(2,1)} %shard_map.210), channel_id=1, source_target_pairs={{0,2},{2,0},{4,6},{6,4},{1,3},{3,1},{5,7},{7,5},{8,10},{10,8},{12,... | collective-permute-start | bytes 3145736 | tf_op jit(solution)/shard_map/ppermute | solution.py:379
  481.2 70.8 %collective-permute-start.43 = (bf16[4,640,256]{2,1,0:T(8,128)(2,1)}, bf16[4,640,256]{2,1,0:T(8,128)(2,1)}, u32[]{:S(2)}, u32[]{:S(2)}) collective-permute-start(bf16[4,640,256]{2,1,0:T(8,128)(2,1)} %shard_map.208), channel_id=1, source_target_pairs={{0,2},{2,0},{4,6},{6,4},{1,3},{3,1},{5,7},{7,5},{8,10},{10,8},{12,... | collective-permute-start | bytes 3932168 | tf_op jit(solution)/shard_map/ppermute | solution.py:379
  519.0 24.0 %collective-permute-start.30 = (bf16[256,2048]{1,0:T(8,128)(2,1)}, bf16[256,2048]{1,0:T(8,128)(2,1)S(1)}, u32[]{:S(2)}, u32[]{:S(2)}) collective-permute-start(bf16[256,2048]{1,0:T(8,128)(2,1)} %convolution_convert_fusion.3), channel_id=1, source_target_pairs={{0,8},{8,0},{16,24},{24,16},{1,9},{9,1},{17,25},{25,17},{2,10},{10... | collective-permute-start | bytes 3145736 | tf_op jit(solution)/shard_map/ppermute | solution.py:398
  520.9 30.0 %collective-permute-start.47 = (bf16[2,512,256]{2,1,0:T(8,128)(2,1)S(1)}, bf16[2,512,256]{2,1,0:T(8,128)(2,1)S(1)}, u32[]{:S(2)}, u32[]{:S(2)}) collective-permute-start(bf16[2,512,256]{2,1,0:T(8,128)(2,1)S(1)} %copy-done.60), channel_id=1, source_target_pairs={{0,1},{1,0},{2,3},{3,2},{4,5},{5,4},{6,7},{7,6},{8,9},{9,8},{10,11... | collective-permute-start | bytes 1572872 | tf_op jit(solution)/shard_map/ppermute | solution.py:379
  525.4 125.7 %collective-permute-start.57 = (bf16[1,256,1408]{2,1,0:T(8,128)(2,1)}, bf16[1,256,1408]{2,1,0:T(8,128)(2,1)}, u32[]{:S(2)}, u32[]{:S(2)}) collective-permute-start(bf16[1,256,1408]{2,1,0:T(8,128)(2,1)} %slice.185), channel_id=1, source_target_pairs={{0,4},{2,6},{4,0},{6,2},{1,5},{3,7},{5,1},{7,3},{8,12},{10,14},{12... | collective-permute-start | bytes 2162696 | tf_op jit(solution)/shard_map/ppermute | solution.py:379
  543.1 18.2 %collective-permute-start.35 = (bf16[128,2048]{1,0:T(8,128)(2,1)}, bf16[128,2048]{1,0:T(8,128)(2,1)}, u32[]{:S(2)}, u32[]{:S(2)}) collective-permute-start(bf16[128,2048]{1,0:T(8,128)(2,1)} %dynamic-slice_convert_fusion), channel_id=1, source_target_pairs={{0,16},{8,24},{16,0},{24,8},{1,17},{9,25},{17,1},{25,9},{2,18},{10... | collective-permute-start | bytes 1572872 | tf_op jit(solution)/shard_map/ppermute | solution.py:398
  546.7 21.7 %collective-permute-start.31 = (bf16[128,2048]{1,0:T(8,128)(2,1)}, bf16[128,2048]{1,0:T(8,128)(2,1)}, u32[]{:S(2)}, u32[]{:S(2)}) collective-permute-start(bf16[128,2048]{1,0:T(8,128)(2,1)} %dynamic-slice_convert_fusion.1), channel_id=1, source_target_pairs={{0,16},{8,24},{16,0},{24,8},{1,17},{9,25},{17,1},{25,9},{2,18},{10... | collective-permute-start | bytes 1572872 | tf_op jit(solution)/shard_map/ppermute | solution.py:398
  550.9 102.0 %collective-permute-start.54 = (bf16[1,256,1408]{2,1,0:T(8,128)(2,1)}, bf16[1,256,1408]{2,1,0:T(8,128)(2,1)}, u32[]{:S(2)}, u32[]{:S(2)}) collective-permute-start(bf16[1,256,1408]{2,1,0:T(8,128)(2,1)} %slice.186), channel_id=1, source_target_pairs={{0,4},{2,6},{4,0},{6,2},{1,5},{3,7},{5,1},{7,3},{8,12},{10,14},{12... | collective-permute-start | bytes 2162696 | tf_op jit(solution)/shard_map/ppermute | solution.py:379
  552.0 104.2 %collective-permute-start.51 = (bf16[1,256,1408]{2,1,0:T(8,128)(2,1)}, bf16[1,256,1408]{2,1,0:T(8,128)(2,1)}, u32[]{:S(2)}, u32[]{:S(2)}) collective-permute-start(bf16[1,256,1408]{2,1,0:T(8,128)(2,1)} %slice.187), channel_id=1, source_target_pairs={{0,4},{2,6},{4,0},{6,2},{1,5},{3,7},{5,1},{7,3},{8,12},{10,14},{12... | collective-permute-start | bytes 2162696 | tf_op jit(solution)/shard_map/ppermute | solution.py:379
  561.2 83.7 %collective-permute-start.48 = (bf16[1,512,256]{2,1,0:T(8,128)(2,1)}, bf16[1,512,256]{2,1,0:T(8,128)(2,1)S(1)}, u32[]{:S(2)}, u32[]{:S(2)}) collective-permute-start(bf16[1,512,256]{2,1,0:T(8,128)(2,1)} %slice.189), channel_id=1, source_target_pairs={{0,4},{2,6},{4,0},{6,2},{1,5},{3,7},{5,1},{7,3},{8,12},{10,14},{12... | collective-permute-start | bytes 786440 | tf_op jit(solution)/shard_map/ppermute | solution.py:379
  592.7 68.7 %collective-permute-start.44 = (bf16[2,640,256]{2,1,0:T(8,128)(2,1)}, bf16[2,640,256]{2,1,0:T(8,128)(2,1)}, u32[]{:S(2)}, u32[]{:S(2)}) collective-permute-start(bf16[2,640,256]{2,1,0:T(8,128)(2,1)} %get-tuple-element.60), channel_id=1, source_target_pairs={{0,1},{1,0},{2,3},{3,2},{4,5},{5,4},{6,7},{7,6},{8,9},{9,8},{10,11... | collective-permute-start | bytes 1966088 | tf_op jit(solution)/shard_map/ppermute | solution.py:379
  649.6 15.2 %collective-permute-start.32 = (bf16[128,2048]{1,0:T(8,128)(2,1)}, bf16[128,2048]{1,0:T(8,128)(2,1)}, u32[]{:S(2)}, u32[]{:S(2)}) collective-permute-start(bf16[128,2048]{1,0:T(8,128)(2,1)} %get-tuple-element.97), channel_id=1, source_target_pairs={{0,16},{8,24},{16,0},{24,8},{1,17},{9,25},{17,1},{25,9},{2,18},{10... | collective-permute-start | bytes 1572872 | tf_op jit(solution)/shard_map/ppermute | solution.py:398
  651.1 22.4 %collective-permute-start.36 = (bf16[128,2048]{1,0:T(8,128)(2,1)}, bf16[128,2048]{1,0:T(8,128)(2,1)}, u32[]{:S(2)}, u32[]{:S(2)}) collective-permute-start(bf16[128,2048]{1,0:T(8,128)(2,1)} %get-tuple-element.99), channel_id=1, source_target_pairs={{0,16},{8,24},{16,0},{24,8},{1,17},{9,25},{17,1},{25,9},{2,18},{10... | collective-permute-start | bytes 1572872 | tf_op jit(solution)/shard_map/ppermute | solution.py:398
  662.8 14.5 %collective-permute-start.45 = (bf16[1,640,256]{2,1,0:T(8,128)(2,1)S(1)}, bf16[1,640,256]{2,1,0:T(8,128)(2,1)S(1)}, u32[]{:S(2)}, u32[]{:S(2)}) collective-permute-start(bf16[1,640,256]{2,1,0:T(8,128)(2,1)S(1)} %slice.188), channel_id=1, source_target_pairs={{0,4},{2,6},{4,0},{6,2},{1,5},{3,7},{5,1},{7,3},{8,12},{10,14},{12... | collective-permute-start | bytes 983048 | tf_op jit(solution)/shard_map/ppermute | solution.py:379
  666.7 16.0 %collective-permute-start.33 = (bf16[256,2048]{1,0:T(8,128)(2,1)}, bf16[256,2048]{1,0:T(8,128)(2,1)}, u32[]{:S(2)}, u32[]{:S(2)}) collective-permute-start(bf16[256,2048]{1,0:T(8,128)(2,1)} %constant_dynamic-update-slice_fusion.2), channel_id=1, source_target_pairs={{0,8},{8,0},{16,24},{24,16},{1,9},{9,1},{17,25},{25,17},{2,10},{10... | collective-permute-start | bytes 3145736 | tf_op jit(solution)/shard_map/ppermute | solution.py:398
  (100 other events, 1190.7 us)

commit v2 on v1

v2 whole, which is shorter than its diff:
```python
import functools

import jax
import jax.numpy as jnp
from jax import lax
from jax.experimental import pallas as pl
from jax.experimental.pallas import tpu as pltpu
from jax.sharding import PartitionSpec as P

EPSILON = 1e-05
BF16 = jnp.bfloat16
F32 = jnp.float32
FAR = 1e30
AUX = 8
ONES_AT = 5
BLOCK = 256


COST = pl.CostEstimate(flops=1024, bytes_accessed=1024, transcendentals=0)


def params():
    return pltpu.CompilerParams(vmem_limit_bytes=56 * 2**20)


def dot(left, right, dims):
    return lax.dot_general(left, right, (dims, ((), ())), preferred_element_type=F32)


NN, NT, TN, TT = ((1,), (0,)), ((1,), (1,)), ((0,), (0,)), ((0,), (1,))


def turn(rows, cos_rows, sine_rows, sign):
    half = rows.shape[0] // 2
    first, second = rows[:half], rows[half:]
    return jnp.concatenate(
        [first * cos_rows - sign * second * sine_rows, second * cos_rows + sign * first * sine_rows], 0
    )


def project_kernel(at_ref, x_ref, gain_ref, wq_ref, wkv_ref, cos_ref, sin_ref, h_ref, q_ref, kv_ref):
    x = x_ref[...].astype(F32)
    scale = lax.rsqrt(jnp.mean(x * x, -1, keepdims=True) + EPSILON)
    h = (x * scale * gain_ref[...]).astype(BF16)
    part = h.shape[0] // 2
    swapped = at_ref[2] * part
    h_ref[pl.ds(pl.multiple_of(swapped, part), part)] = h[:part]
    h_ref[pl.ds(pl.multiple_of(part - swapped, part), part)] = h[part:]
    cos_rows, sine_rows = cos_ref[...], sin_ref[...]
    head = kv_ref.shape[0] // 2
    score_scale = head ** (-0.5)
    q = dot(h, wq_ref[...], NN).T
    for at in range(0, q.shape[0], head):
        q_ref[at : at + head] = (turn(q[at : at + head], cos_rows, sine_rows, 1.0) * score_scale).astype(BF16)
    kv = dot(wkv_ref[...], h, NT)
    kv_ref[:head] = turn(kv[:head], cos_rows, sine_rows, 1.0).astype(BF16)
    kv_ref[head:] = kv[head:].astype(BF16)


def project(at, x, gain, w_query, w_kv, cos_rows, sine_rows, stretch):
    rows, width = x.shape
    step = stretch // 2
    wide, both = w_query.shape[1], w_kv.shape[0]
    half = cos_rows.shape[0]
    whole = lambda shape: pl.BlockSpec(shape, lambda i, at: (0, 0))
    return pl.pallas_call(
        project_kernel,
        grid_spec=pltpu.PrefetchScalarGridSpec(
            num_scalar_prefetch=1,
            grid=(rows // step,),
            in_specs=[
                pl.BlockSpec((step, width), lambda i, at: (i, 0)),
                whole((1, width)),
                whole((width, wide)),
                whole((both, width)),
                pl.BlockSpec((half, step), lambda i, at: (0, i)),
                pl.BlockSpec((half, step), lambda i, at: (0, i)),
            ],
            out_specs=[
                pl.BlockSpec((step, width), lambda i, at: (i + at[1] - 2 * at[1] * lax.rem(i, 2), 0)),
                pl.BlockSpec((wide, step), lambda i, at: (0, i)),
                pl.BlockSpec((both, step), lambda i, at: (0, i)),
            ],
        ),
        out_shape=[
            jax.ShapeDtypeStruct((rows, width), BF16),
            jax.ShapeDtypeStruct((wide, rows), BF16),
            jax.ShapeDtypeStruct((both, rows), BF16),
        ],
        compiler_params=params(),
        cost_estimate=COST,
    )(at, x, gain, w_query, w_kv, cos_rows, sine_rows)


def pieces(value):
    high = value.astype(BF16).astype(F32)
    middle = (value - high).astype(BF16).astype(F32)
    low = value - high - middle
    return high, middle, low


def key_rows(kv, seg):
    head, count = kv.shape[0] // 2, kv.shape[1]
    row = lax.broadcasted_iota(jnp.int32, (2 * AUX, count), 0)
    extra = jnp.where(row < ONES_AT, jnp.where(seg == row, 0.0, -FAR), jnp.where(row < AUX, 1.0, 0.0))
    rest = jnp.zeros((head - 2 * AUX, count), F32)
    return jnp.concatenate([kv[:head].astype(F32), extra, rest], 0)


def value_rows(kv, fill):
    head, count = kv.shape[0] // 2, kv.shape[1]
    row = lax.broadcasted_iota(jnp.int32, (fill, count), 0)
    return jnp.concatenate([kv[head:].astype(F32), jnp.where(row < 3, 1.0, 0.0)], 0)


def places(at_ref, count):
    quarter = count // 4
    mine = 2 * at_ref[1] + at_ref[2]
    return [pl.ds(pl.multiple_of((b ^ mine) * quarter, quarter), quarter) for b in range(4)]


def causal(scores):
    key_at = lax.broadcasted_iota(jnp.int32, scores.shape, 0)
    query_at = lax.broadcasted_iota(jnp.int32, scores.shape, 1)
    return jnp.where(key_at <= query_at, scores, -FAR)


def attend_kernel(far_count, at_ref, q_ref, seg_ref, *refs):
    kv_refs = refs[: far_count + 1]
    qa_ref, o_ref, full_ref = refs[far_count + 1 : far_count + 4]
    ka_ref, va_ref = refs[far_count + 4 :]
    me = at_ref[0]
    head = kv_refs[0].shape[0] // 2
    count = q_ref.shape[1]

    @pl.when(pl.program_id(0) == 0)
    def _():
        for d, kv_ref in enumerate(kv_refs):
            kv = kv_ref[...]
            ka_ref[d] = key_rows(kv, seg_ref[d : d + 1]).T.astype(BF16)
            va_ref[d] = value_rows(kv, 2 * AUX).astype(BF16)

    row = lax.broadcasted_iota(jnp.int32, (2 * AUX, count), 0)
    same = jnp.where((seg_ref[0:1] == row) & (row < ONES_AT), 1.0, 0.0)
    rest = jnp.zeros((head - 2 * AUX, count), F32)

    def heads(blocks):
        for h in range(q_ref.shape[0] // head):
            q = q_ref[h * head : (h + 1) * head].astype(F32)
            qa = jnp.concatenate([q, same, rest], 0).astype(BF16)
            scores = [dot(ka_ref[d], qa, NN) for d in range(blocks)]
            scores[0] = causal(scores[0])
            m = jnp.max(scores[0], 0, keepdims=True)
            for d in range(1, blocks):
                m = jnp.maximum(m, jnp.max(scores[d], 0, keepdims=True))
            acc = None
            for d in range(blocks):
                term = dot(va_ref[d], jnp.exp(scores[d] - m).astype(BF16), NN)
                acc = term if acc is None else acc + term
            total = acc[head : head + 1]
            out = acc[:head] / total
            for b, place in enumerate(places(at_ref, count)):
                quarter = out[:, b * (count // 4) : (b + 1) * (count // 4)]
                full_ref[h * head : (h + 1) * head, place] = quarter
                o_ref[h * head : (h + 1) * head, place] = quarter.astype(BF16)
            high, middle, low = pieces(-(m + jnp.log(total)))
            extra = jnp.where(
                row == ONES_AT, high, jnp.where(row == ONES_AT + 1, middle, jnp.where(row == ONES_AT + 2, low, same))
            )
            qa_ref[h] = jnp.concatenate([q, extra, rest], 0).astype(BF16)

    for blocks in range(1, far_count + 2):
        pl.when(me == blocks - 1)(functools.partial(heads, blocks))


def attend(me, q, kvs, segs, item, group=2):
    far_count = len(kvs) - 1
    both = kvs[0].shape[0]
    head = both // 2
    wide, count = q.shape[0], segs.shape[-1]
    heads = wide // head
    return pl.pallas_call(
        functools.partial(attend_kernel, far_count),
        grid_spec=pltpu.PrefetchScalarGridSpec(
            num_scalar_prefetch=1,
            grid=(heads // group,),
            in_specs=[
                pl.BlockSpec((group * head, count), lambda h, at: (h, item)),
                pl.BlockSpec((None, far_count + 1, count), lambda h, at: (item, 0, 0)),
            ]
            + [pl.BlockSpec((both, count), lambda h, at: (0, item))] * (far_count + 1),
            out_specs=[
                pl.BlockSpec((group, both, count), lambda h, at: (h, 0, 0)),
                pl.BlockSpec((group * head, count), lambda h, at: (h, 0)),
                pl.BlockSpec((group * head, count), lambda h, at: (h, 0)),
            ],
            scratch_shapes=[
                pltpu.VMEM((far_count + 1, count, both), BF16),
                pltpu.VMEM((far_count + 1, head + 2 * AUX, count), BF16),
            ],
        ),
        out_shape=[
            jax.ShapeDtypeStruct((heads, both, count), BF16),
            jax.ShapeDtypeStruct((wide, count), BF16),
            jax.ShapeDtypeStruct((wide, count), F32),
        ],
        compiler_params=params(),
        cost_estimate=COST,
    )(me, q, segs, *kvs)


def back_kernel(far_count, at_ref, qa_ref, do_ref, full_ref, seg_ref, cos_ref, sin_ref, *refs):
    kv_refs = refs[: far_count + 1]
    dq_ref, keep_ref, send_ref = refs[far_count + 1 : far_count + 4]
    ka_ref, kt_ref, va_ref, dk_ref, dv_ref, dq_acc = refs[far_count + 4 :]
    me = at_ref[0]
    head, count = do_ref.shape
    step = pl.program_id(0)

    @pl.when(step == 0)
    def _():
        for d, kv_ref in enumerate(kv_refs):
            kv = kv_ref[...]
            ka_ref[d] = key_rows(kv, seg_ref[d : d + 1]).T.astype(BF16)
            kt_ref[d] = kv[:head]
            va_ref[d] = value_rows(kv, head).T.astype(BF16)
        dk_ref[...] = jnp.zeros_like(dk_ref)
        dv_ref[...] = jnp.zeros_like(dv_ref)

    qa = qa_ref[...]
    here = places(at_ref, count)
    do = jnp.concatenate([do_ref[:, place] for place in here], 1).astype(F32)
    full = jnp.concatenate([full_ref[:, place] for place in here], 1)
    high, middle, low = pieces(-jnp.sum(do * full, 0, keepdims=True))
    row = lax.broadcasted_iota(jnp.int32, (2 * AUX, count), 0)
    extra = jnp.where(row == 0, high, jnp.where(row == 1, middle, jnp.where(row == 2, low, 0.0)))
    rest = jnp.zeros((head - 2 * AUX, count), F32)
    da = jnp.concatenate([do, extra, rest], 0).astype(BF16)
    for d in range(far_count + 1):

        def part(d=d):
            scores = dot(ka_ref[d], qa, NN)
            probs = jnp.exp(causal(scores) if d == 0 else scores)
            d_scores = (probs * dot(va_ref[d], da, NN)).astype(BF16)
            dv_ref[d] += dot(probs.astype(BF16), da[:head], NT)
            dk_ref[d] += dot(d_scores, qa[:head], NT)
            update = dot(kt_ref[d], d_scores, NN)
            if d == 0:
                dq_acc[...] = update
            else:
                dq_acc[...] += update

        if d == 0:
            part()
        else:
            pl.when(d <= me)(part)
    score_scale = head ** (-0.5)
    dq = turn(dq_acc[...] * score_scale, cos_ref[...], sin_ref[...], -1.0).astype(BF16)
    for b, place in enumerate(here):
        dq_ref[:, place] = dq[:, b * (count // 4) : (b + 1) * (count // 4)]

    @pl.when(step == pl.num_programs(0) - 1)
    def _():
        keep_ref[...] = jnp.zeros_like(keep_ref)
        send_ref[...] = jnp.zeros_like(send_ref)
        keep_ref[0] = jnp.concatenate([dk_ref[0], dv_ref[0]], 1).T.astype(BF16)
        for d in range(1, far_count + 1):

            @pl.when(d <= me)
            def _(d=d):
                part = jnp.concatenate([dk_ref[d], dv_ref[d]], 1).T.astype(BF16)
                place = (me - d) ^ me

                @pl.when(place % 2 == 0)
                def _():
                    keep_ref[place // 2] = part

                @pl.when(place % 2 == 1)
                def _():
                    send_ref[place // 2] = part


def attend_back(me, qa, do, full, kvs, segs, cos_rows, sine_rows, item):
    far_count = len(kvs) - 1
    heads, both, count = qa.shape
    head = both // 2
    wide, half = heads * head, cos_rows.shape[0]
    return pl.pallas_call(
        functools.partial(back_kernel, far_count),
        grid_spec=pltpu.PrefetchScalarGridSpec(
            num_scalar_prefetch=1,
            grid=(heads,),
            in_specs=[
                pl.BlockSpec((None, both, count), lambda h, at: (h, 0, 0)),
                pl.BlockSpec((head, count), lambda h, at: (h, 0)),
                pl.BlockSpec((head, count), lambda h, at: (h, 0)),
                pl.BlockSpec((None, far_count + 1, count), lambda h, at: (item, 0, 0)),
                pl.BlockSpec((half, count), lambda h, at: (0, item)),
                pl.BlockSpec((half, count), lambda h, at: (0, item)),
            ]
            + [pl.BlockSpec((both, count), lambda h, at: (0, item))] * (far_count + 1),
            out_specs=[pl.BlockSpec((head, count), lambda h, at: (h, 0))]
            + [pl.BlockSpec(((far_count + 1) // 2, both, count), lambda h, at: (0, 0, 0))] * 2,
            scratch_shapes=[
                pltpu.VMEM((far_count + 1, count, both), BF16),
                pltpu.VMEM((far_count + 1, head, count), BF16),
                pltpu.VMEM((far_count + 1, count, both), BF16),
                pltpu.VMEM((far_count + 1, count, head), F32),
                pltpu.VMEM((far_count + 1, count, head), F32),
                pltpu.VMEM((head, count), F32),
            ],
        ),
        out_shape=[jax.ShapeDtypeStruct((wide, count), BF16)]
        + [jax.ShapeDtypeStruct(((far_count + 1) // 2, both, count), BF16)] * 2,
        compiler_params=params(),
        cost_estimate=COST,
    )(me, qa, do, full, segs, cos_rows, sine_rows, *kvs)


def merge_kernel(at_ref, own_ref, recv_ref, cos_ref, sin_ref, out_ref):
    head, count = out_ref.shape[0] // 2, out_ref.shape[1]
    total = own_ref[...].astype(F32) + recv_ref[...].astype(F32)
    turned = turn(total[:head], cos_ref[...], sin_ref[...], -1.0)
    out = jnp.concatenate([turned, total[head:]], 0).astype(BF16)
    for b, place in enumerate(places(at_ref, count)):
        out_ref[:, place] = out[:, b * (count // 4) : (b + 1) * (count // 4)]


def merge(at, own, received, cos_rows, sine_rows):
    seqs, both, count = own.shape
    half = cos_rows.shape[0]
    block = pl.BlockSpec((None, both, count), lambda s, at: (s, 0, 0))
    table = pl.BlockSpec((half, count), lambda s, at: (0, s))
    return pl.pallas_call(
        merge_kernel,
        grid_spec=pltpu.PrefetchScalarGridSpec(
            num_scalar_prefetch=1,
            grid=(seqs,),
            in_specs=[block, block, table, table],
            out_specs=block,
        ),
        out_shape=jax.ShapeDtypeStruct(own.shape, BF16),
        compiler_params=params(),
        cost_estimate=COST,
    )(at, own, received, cos_rows, sine_rows)


def product(order, pieces, *items):
    total = order.mark(sum(dot(a, b, form) for a, b, form in items).astype(BF16))
    half = total.shape[0] // 2
    return cut(total[half:], pieces), total[:half]


def cut(x, pieces):
    size = x.shape[0] // pieces
    return [x[j * size : (j + 1) * size] for j in range(pieces)]


def unfold_kernel(near_ref, *refs):
    *far_refs, w_ref, out_ref, full_ref = refs
    half = near_ref.shape[0]
    full_ref[:half] = near_ref[...]
    piece = far_refs[0].shape[0]
    for j, far_ref in enumerate(far_refs):
        full_ref[half + j * piece : half + (j + 1) * piece] = far_ref[...]
    out_ref[...] = dot(w_ref[...], full_ref[...], NT).astype(BF16)


def unfold(near, far, w):
    rows, width = 2 * near.shape[0], near.shape[1]
    return pl.pallas_call(
        unfold_kernel,
        out_shape=[
            jax.ShapeDtypeStruct((w.shape[0], rows), BF16),
            jax.ShapeDtypeStruct((rows, width), BF16),
        ],
        compiler_params=params(),
        cost_estimate=COST,
    )(near, *far, w)


def grad_kernel(groups, has_recv, split, table_ref, *refs):
    out = []
    for form, pairs in groups:
        total = None
        for narrow, wide in pairs:
            both = jnp.concatenate([refs[wide][...], refs[wide + 1][...]], 1)
            if form == TN:
                term = dot(both, refs[narrow][...], TN)
            else:
                term = dot(refs[narrow][...], both, NN)
            total = term if total is None else total + term
        out.append(total)
    at = len(refs) - (2 if split else 1) - (1 if has_recv else 0)
    recv = None
    if has_recv:
        recv, at = refs[at], at + 1

    def put(ref):
        if groups[0][0] == TN:
            rows = out[0].shape[0] // 2
            for j in range(2):
                block = out[0][j * rows : (j + 1) * rows]
                ref[j] = (block if recv is None else block + recv[j].astype(F32)).astype(BF16)
            return
        row = 0
        for total in out:
            count, wide = total.shape[0], total.shape[1] // 2
            for j in range(2):
                block = total[:, j * wide : (j + 1) * wide]
                if recv is not None:
                    block = block + recv[j, row : row + count].astype(F32)
                ref[j, row : row + count] = block.astype(BF16)
            row += count

    if not split:
        put(refs[at])
        return
    first = pl.program_id(0) < split // 2
    pl.when(first)(lambda: put(refs[at]))
    pl.when(jnp.logical_not(first))(lambda: put(refs[at + 1]))


def grad_blocks(table, form, sets, recv=None, split=0):
    n = table.shape[0]
    ins, specs, groups = [], [], []
    for wide_set, narrow_set in sets:
        pairs = []
        for wide, narrow in zip(wide_set, narrow_set):
            pairs.append((len(ins), len(ins) + 1))
            ins += [narrow, wide, wide]
            specs.append(pl.BlockSpec(narrow.shape, lambda i, t: (0, 0)))
            for j in range(2):
                specs.append(pl.BlockSpec((wide.shape[0], BLOCK), lambda i, t, j=j: (0, t[2 * i + j])))
        groups.append((form, pairs))
    if form == TN:
        block = (BLOCK, sets[0][1][0].shape[1])
    else:
        block = (sum(narrow_set[0].shape[0] for _, narrow_set in sets), BLOCK)
    two = (2,) + block
    if recv is not None:
        ins.append(recv)
        specs.append(pl.BlockSpec(two, lambda i, t: (lax.rem(i + split // 2, n // 2), 0, 0)))
    if split:
        out_specs = [
            pl.BlockSpec(two, lambda i, t: (jnp.minimum(i, split // 2 - 1), 0, 0)),
            pl.BlockSpec(two, lambda i, t: (jnp.maximum(i - split // 2, 0), 0, 0)),
        ]
        out_shape = [jax.ShapeDtypeStruct((split,) + block, BF16), jax.ShapeDtypeStruct((n - split,) + block, BF16)]
    else:
        out_specs = pl.BlockSpec(two, lambda i, t: (i, 0, 0))
        out_shape = jax.ShapeDtypeStruct((n,) + block, BF16)
    return pl.pallas_call(
        functools.partial(grad_kernel, groups, recv is not None, split),
        grid_spec=pltpu.PrefetchScalarGridSpec(num_scalar_prefetch=1, grid=(n // 2,), in_specs=specs, out_specs=out_specs),
        out_shape=out_shape,
        compiler_params=params(),
        cost_estimate=COST,
    )(table, *ins)


class Order:
    def __init__(self):
        self.last = None

    def take_all(self, xs):
        if self.last is not None:
            xs = lax.optimization_barrier((self.last, *xs))[1:]
        return xs

    def take(self, *xs):
        xs = self.take_all(xs)
        return xs if len(xs) > 1 else xs[0]

    def mark(self, x):
        self.last = x
        return x


class Scatter:
    def __init__(self, stages, sizes, form, fast):
        self.stages, self.sizes, self.form, self.fast = stages, sizes, form, fast
        ctx, dp = lax.axis_index("context"), lax.axis_index("dp")
        blocks = []
        for p in range(2 ** len(stages)):
            c, d = ctx, dp
            for j, (axis, bit) in enumerate(stages):
                if p >> (len(stages) - 1 - j) & 1:
                    if axis == "context":
                        c = c ^ (1 << bit)
                    else:
                        d = d ^ (1 << bit)
            blocks.append(c * sizes["dp"] + d)
        self.away = jnp.stack(blocks[4:]).astype(jnp.int32)
        self.near = jnp.stack([blocks[p] for p in (2, 3, 0, 1)]).astype(jnp.int32)

    def send(self, j, x):
        axis, bit = self.stages[j]
        self.got = swap(x, axis, self.sizes[axis], bit)

    def first(self, order, sets):
        if self.fast:
            wide = order.take(*sets[0][0])
            self.sets = [(list(wide), sets[0][1])] + sets[1:]
            self.send(0, order.mark(grad_blocks(self.away, self.form, self.sets)))

    def second(self, order):
        if self.fast:
            send, self.keep = grad_blocks(self.near, self.form, self.sets, order.take(self.got), 2)
            self.send(1, order.mark(send))

    def third(self, order):
        if self.fast:
            recv = order.take(self.got)
            send = (self.keep[1].astype(F32) + recv[1].astype(F32)).astype(BF16)
            self.rest = self.keep[0].astype(F32) + recv[0].astype(F32)
            self.send(2, order.mark(send))

    def final(self, order):
        if self.fast:
            return order.mark(self.rest + order.take(self.got).astype(F32))


def place_kernel(at_ref, near_ref, far_ref, out_ref):
    p = pl.program_id(1)

    @pl.when(p < 2)
    def _():
        out_ref[...] = near_ref[...].astype(out_ref.dtype)

    @pl.when(p >= 2)
    def _():
        out_ref[...] = far_ref[...].astype(out_ref.dtype)


def place(at, near, far, dtype):
    seqs, half, width = near.shape
    quarter = half // 2
    block = (None, quarter, width)
    return pl.pallas_call(
        place_kernel,
        grid_spec=pltpu.PrefetchScalarGridSpec(
            num_scalar_prefetch=1,
            grid=(seqs, 4),
            in_specs=[
                pl.BlockSpec(block, lambda s, p, at: (s, jnp.minimum(p, 1), 0)),
                pl.BlockSpec(block, lambda s, p, at: (s, jnp.maximum(p - 2, 0), 0)),
            ],
            out_specs=pl.BlockSpec(block, lambda s, p, at: (s, p ^ (2 * at[1] + at[2]), 0)),
        ),
        out_shape=jax.ShapeDtypeStruct((seqs, 2 * half, width), dtype),
        compiler_params=params(),
        cost_estimate=COST,
    )(at, near, far)


def sealed(fn, *args):
    def never(*args):
        return jax.tree.map(lambda leaf: jnp.zeros(leaf.shape, leaf.dtype), jax.eval_shape(fn, *args))

    return lax.cond(lax.axis_index("tensor") >= 0, fn, never, *args)


def swap(x, axis, size, bit):
    return lax.ppermute(x, axis, [(i, i ^ (1 << bit)) for i in range(size)])


def rows_at(x, at, count):
    return lax.dynamic_slice_in_dim(x, at, count, 0)


def local(sizes, tokens, segment_ids, norm_gain_1, w_query, w_key, w_value, w_output, norm_gain_2, w_gate, w_up, w_down, cotangent):
    seqs, stretch, width = tokens.shape
    rows = seqs * stretch
    head = w_key.shape[1]
    wide = w_query.shape[1]
    n_tensor, n_context, n_dp = sizes["tensor"], sizes["context"], sizes["dp"]
    me_t, me_c = lax.axis_index("tensor"), lax.axis_index("context")
    core, high = me_t % 2, me_t // 2
    mine = 2 * core + high
    half, quarter = stretch // 2, stretch // 4
    offset = me_c * stretch
    order = Order()
    each = range(seqs)

    seg_here = lax.dynamic_slice_in_dim(segment_ids, offset, stretch, 1)
    start = jnp.zeros(seg_here.shape, jnp.int32)
    for number in range(1, ONES_AT):
        before = jnp.sum((segment_ids < number).astype(jnp.int32), 1, keepdims=True)
        start = jnp.where(seg_here == number, before, start)
    positions = (offset + jnp.arange(stretch, dtype=jnp.int32))[None, :] - start
    frequency = 10000.0 ** (-(2.0 * jnp.arange(head // 2, dtype=F32)) / head)
    angles = frequency[:, None] * positions.reshape(1, rows).astype(F32)
    cos_rows, sine_rows = jnp.cos(angles), jnp.sin(angles)
    padded = jnp.concatenate([jnp.zeros((seqs, (n_context - 1) * stretch), jnp.int32), segment_ids], 1)
    segs = jnp.stack(
        [
            lax.dynamic_slice_in_dim(padded, offset + (n_context - 1 - d) * stretch, stretch, 1)
            for d in range(n_context)
        ],
        1,
    )
    at = jnp.stack([me_c, core, high]).astype(jnp.int32)

    x_rows = tokens.reshape(rows, width)
    ct_rows = cotangent.reshape(rows, width)
    gain_1, gain_2 = norm_gain_1.reshape(1, width), norm_gain_2.reshape(1, width)
    w_kv = jnp.concatenate([w_key.T, w_value.T], 0)
    h1, q_t, kv_t = project(at, x_rows, gain_1, w_query, w_kv, cos_rows, sine_rows, stretch)
    order.mark(kv_t)
    kvs = [kv_t] + [
        lax.ppermute(kv_t, "context", [(i, i + d) for i in range(n_context - d)]) for d in range(1, n_context)
    ]

    def own_order(x, s):
        return jnp.concatenate([rows_at(x, s * stretch + (p ^ mine) * quarter, quarter) for p in range(4)], 0)

    def fold(pair):
        sends, keep = pair
        return [swap(x, "tensor", n_tensor, 0) for x in sends], keep

    def join(pieces):
        return jnp.concatenate(order.take_all(pieces), 0)

    def fold_more(kept, got):
        total = kept.astype(F32) + got.astype(F32)
        send = total[quarter:].astype(BF16)
        return swap(order.mark(send), "tensor", n_tensor, 1), total[:quarter]

    def core_swap(x):
        return swap(x, "tensor", n_tensor, 0)

    def fold_now(total):
        near = total[:, :half].astype(F32) + core_swap(total[:, half:]).astype(F32)
        return near[:, quarter:].astype(BF16), near[:, :quarter]

    def spread(part):
        return swap(part, "tensor", n_tensor, 1)

    def spread_more(part, got, pieces):
        got = order.take(got)
        block = order.mark(jnp.concatenate([part, got], 0))
        return [swap(x, "tensor", n_tensor, 0) for x in cut(block, pieces)], block

    cts, d_hidden = [], []
    for s in each:
        cts.append(own_order(order.take(ct_rows), s))
        d_hidden.append(order.mark(dot(cts[s], w_down, NT)))

    stream = [rows_at(x_rows, s * stretch + mine * quarter, quarter).astype(F32) for s in each]
    ct_own = [rows_at(ct_rows, s * stretch + mine * quarter, quarter).astype(F32) for s in each]

    qa, o_t, full_o = [None] * seqs, [None] * seqs, [None] * seqs
    got_o, kept_o = [None] * seqs, [None] * seqs
    residual, scale_2, normed_2, h2_own, got_h = ([None] * seqs for _ in range(5))

    def after_attention(s):
        total = kept_o[s] + order.take(got_o[s]).astype(F32)
        residual[s] = stream[s] + total
        scale_2[s] = lax.rsqrt(jnp.mean(residual[s] * residual[s], -1, keepdims=True) + EPSILON)
        normed_2[s] = residual[s] * scale_2[s]
        h2_own[s] = order.mark((normed_2[s] * gain_2).astype(BF16))
        got_h[s] = spread(h2_own[s])

    for s in each:
        qa[s], o_t[s], full_o[s] = attend(at, order.take(q_t), kvs, segs, s)
        order.mark(o_t[s])
        if s:
            after_attention(s - 1)
        got, kept = fold(product(order, 1, (order.take(o_t[s]), w_output, TN)))
        got_o[s], kept_o[s] = fold_more(kept, join(got))

    hidden, d_gate, d_up, h2 = ([None] * seqs for _ in range(4))
    got_b, kept_b = [None] * seqs, [None] * seqs

    def whole(part, got):
        got, block = spread_more(part, got, 1)
        return order.mark(jnp.concatenate([block, *order.take_all(got)], 0))

    def back_partial(s, pieces):
        left, right = order.take(d_gate[s], d_up[s])
        got, kept = fold(product(order, pieces, (left, w_gate, NT), (right, w_up, NT)))
        got_b[s], kept_b[s] = fold_more(kept, join(got))

    d_res, d_low_own, got_d, gains_2 = ([None] * seqs for _ in range(4))

    def after_back(s):
        back = kept_b[s] + order.take(got_b[s]).astype(F32)
        gains_2[s] = jnp.sum(back * normed_2[s], 0)
        scaled = back * gain_2
        d_res[s] = ct_own[s] + scale_2[s] * (
            scaled - normed_2[s] * jnp.mean(scaled * normed_2[s], -1, keepdims=True)
        )
        d_low_own[s] = order.mark(d_res[s].astype(BF16))
        got_d[s] = spread(d_low_own[s])

    blocks = n_context * n_dp
    fast = width // blocks == BLOCK and n_dp == 2 and n_context == 4
    x_first = [("dp", 0), ("context", 0), ("context", 1)]
    z_first = [("context", 0), ("dp", 0), ("context", 1)]
    down_job = Scatter(x_first, sizes, TN, fast)
    gate_job = Scatter(x_first, sizes, TN, fast)
    up_job = Scatter(z_first, sizes, TN, fast)
    mix_job = Scatter(x_first, sizes, NN, fast)
    kv_job = Scatter(x_first, sizes, NN, fast)

    downs = []
    for s in each:
        h2[s] = whole(h2_own[s], got_h[s])
        gate = order.mark(dot(h2[s], w_gate, NN))
        if s + 1 < seqs:
            after_attention(s + 1)
        if s:
            after_back(s - 1)
        up = dot(order.take(h2[s]), w_up, NN)
        sig = jax.nn.sigmoid(gate)
        hidden[s] = (gate * sig * up).astype(BF16)
        d_gate[s] = (d_hidden[s] * up * sig * (1.0 + gate * (1.0 - sig))).astype(BF16)
        d_up[s] = order.mark((d_hidden[s] * gate * sig).astype(BF16))
        if s + 1 < seqs:
            back_partial(s, 1)
        downs.append(order.mark(dot(order.take(hidden[s]), w_down, NN).astype(BF16)))

    d_low, dq_t, dkvs = [None] * seqs, [None] * seqs, [None] * seqs

    do_t = [None] * seqs

    def unfolded(s):
        def run(part, got):
            block = jnp.concatenate([part, got], 0)
            return unfold(block, [core_swap(block)], w_output)

        do_t[s], d_low[s] = sealed(run, d_low_own[s], order.take(got_d[s]))
        order.mark(do_t[s])

    def back_sealed(s):
        def run(left, right):
            return fold_now((dot(left, w_gate, NT) + dot(right, w_up, NT)).astype(BF16)[None])

        send, kept = sealed(run, *order.take(d_gate[s], d_up[s]))
        got_b[s], kept_b[s] = swap(order.mark(send)[0], "tensor", n_tensor, 1), kept[0]

    def attention_back(s):
        dq_t[s], *dkvs[s] = attend_back(
            at, qa[s], order.take(do_t[s]), full_o[s], kvs, segs, cos_rows, sine_rows, s
        )
        order.mark(dq_t[s])

    def gather_natural(part):
        part = order.mark(part)
        return part, swap(part, "tensor", n_tensor, 1)

    def gather_more(part, got):
        block = order.mark(jnp.concatenate([part, order.take(got)], 1))
        return block, order.mark(sealed(core_swap, block))

    def natural(block, far, dtype):
        return order.mark(place(at, block, order.take(far), dtype))

    last = seqs - 1
    down_job.first(order, [(cts, hidden)])
    unfolded(0)
    back_sealed(last)
    up_job.first(order, [(h2, d_up)])
    attention_back(0)
    after_back(last)
    gate_job.first(order, [(h2, d_gate)])
    unfolded(last)
    down_job.second(order)
    send, kept_out = sealed(lambda *parts: fold_now(jnp.stack(parts)), *order.take_all(downs))
    got_out = swap(order.mark(send), "tensor", n_tensor, 1)
    attention_back(last)

    h1s = [h1[s * stretch : (s + 1) * stretch] for s in each]
    send = order.mark(jnp.stack([dkvs[s][1] for s in each]))
    got_kv = swap(send, "context", n_context, 0)
    kept_kv = jnp.stack([dkvs[s][0] for s in each])
    out_own = (jnp.stack(residual) + kept_out + order.take(got_out).astype(F32)).astype(BF16)
    out_part = gather_natural(out_own)
    up_job.second(order)
    mix_job.first(order, [(d_low, o_t), (h1s, dq_t)])
    got_kv = order.take(got_kv)
    send = order.mark((kept_kv[:, 1].astype(F32) + got_kv[:, 1].astype(F32)).astype(BF16))
    kept_kv = (kept_kv[:, 0].astype(F32) + got_kv[:, 0].astype(F32)).astype(BF16)
    got_kv = swap(send, "context", n_context, 1)
    gate_job.second(order)
    layer_out = natural(*gather_more(*out_part), BF16)
    down_job.third(order)
    dkv_t = order.mark(merge(at, kept_kv, order.take(got_kv), cos_rows, sine_rows))
    dkv_ts = [dkv_t[s] for s in each]
    def input_partial(*parts):
        rows_q, rows_kv = jnp.concatenate(parts[:seqs], 1), jnp.concatenate(parts[seqs:], 1)
        total = dot(rows_q, w_query, TT) + dot(rows_kv, w_kv, TN)
        return fold_now(total.astype(BF16).reshape(seqs, stretch, width))

    send, kept_x = sealed(input_partial, *dq_t, *order.take_all(dkv_ts))
    got_x = swap(order.mark(send), "tensor", n_tensor, 1)
    up_job.third(order)
    kv_job.first(order, [(h1s, dkv_ts)])
    mix_job.second(order)
    gate_job.third(order)

    back = kept_x + order.take(got_x).astype(F32)
    streams = jnp.stack(stream)
    scale_1 = lax.rsqrt(jnp.mean(streams * streams, -1, keepdims=True) + EPSILON)
    normed_1 = streams * scale_1
    gains_1 = jnp.sum(back * normed_1, (0, 1))
    scaled = back * gain_1
    grad = jnp.stack(d_res) + scale_1 * (scaled - normed_1 * jnp.mean(scaled * normed_1, -1, keepdims=True))
    grad_part = gather_natural(grad.astype(BF16))
    hops = [(axis, bit) for axis in ("tensor", "context", "dp") for bit in range((sizes[axis] - 1).bit_length())]
    gain_sum = jnp.stack([gains_1, sum(gains_2)])

    def hop():
        axis, bit = hops.pop(0)
        return order.mark(gain_sum + order.take(swap(gain_sum, axis, sizes[axis], bit)))

    down_sum = down_job.final(order)
    gain_sum = hop()
    up_sum = up_job.final(order)
    gain_sum = hop()
    kv_job.second(order)
    mix_job.third(order)
    grad_tokens = natural(*gather_more(*grad_part), F32)
    kv_job.third(order)
    gain_sum = hop()
    gate_sum = gate_job.final(order)
    while hops:
        gain_sum = hop()
    per = width // blocks
    gain_sum = lax.dynamic_slice_in_dim(gain_sum, (me_c * n_dp + lax.axis_index("dp")) * per, per, 1)

    if fast:
        down_sum = down_sum.T
        kv_sum = kv_job.final(order)
        mixed = mix_job.final(order)
        output_sum, query_sum = mixed[:wide], mixed[wide:].T
        key_sum, value_sum = kv_sum[:head].T, kv_sum[head:].T
    else:

        def plain(left, right, dim):
            total = sum(dot(a, b, TN) for a, b in zip(left, right))
            return lax.psum_scatter(
                total.astype(BF16), ("context", "dp"), scatter_dimension=dim, tiled=True
            ).astype(F32)

        down_sum = plain(hidden, cts, 1)
        gate_sum = plain(h2, d_gate, 0)
        up_sum = plain(h2, d_up, 0)
        output_sum = plain([a.T for a in o_t], d_low, 1)
        query_sum = plain(h1s, [a.T for a in dq_t], 0)
        kv_sum = plain(h1s, [a.T for a in dkv_ts], 0)
        key_sum, value_sum = kv_sum[:, :head], kv_sum[:, head:]
    return (
        layer_out,
        grad_tokens,
        gain_sum[0],
        query_sum,
        key_sum,
        value_sum,
        output_sum,
        gain_sum[1],
        gate_sum,
        up_sum,
        down_sum,
    )


def solution(mesh):
    in_specs = (
        P("dp", "context", None),
        P("dp", None),
        P(),
        P(None, "tensor"),
        P(None, "tensor"),
        P(None, "tensor"),
        P("tensor", None),
        P(),
        P(None, "tensor"),
        P(None, "tensor"),
        P("tensor", None),
        P("dp", "context", None),
    )
    out_specs = (
        P("dp", "context", None),
        P("dp", "context", None),
        P(("context", "dp")),
        P(("context", "dp"), "tensor"),
        P(("context", "dp"), "tensor"),
        P(("context", "dp"), "tensor"),
        P("tensor", ("context", "dp")),
        P(("context", "dp")),
        P(("context", "dp"), "tensor"),
        P(("context", "dp"), "tensor"),
        P("tensor", ("context", "dp")),
    )
    run = functools.partial(local, dict(mesh.shape))
    return jax.shard_map(run, mesh=mesh, in_specs=in_specs, out_specs=out_specs, check_vma=False)
```

time: 703 us -> 582 us (0.83)
  waiting for transfers between devices: 261 us -> 144 us
  local copies, waits for them, and re-layouts: 53.9 us -> 28.6 us
  Pallas kernels: 120 us -> 142 us
  matrix products: 93.9 us -> 73.3 us
  other arithmetic: 51.5 us -> 62.5 us
  starting transfers between devices: 111 us -> 121 us
    ppermute x18 -> x0, waiting for transfers between devices: 130 us -> none  [the longest x15 103 us: swap(): lax.ppermute(x, axis, [(i, i ^ 1 << bit) for i in range(self.sizes[axis])])]
    ppermute x37 -> x46, starting transfers between devices: 24.6 us -> 110 us  [swap(): return lax.ppermute(x, axis, [(i, i ^ 1 << bit) for i in range(size)])]
    ppermute x18 -> x0, starting transfers between devices: 75.1 us -> none  [the longest x15 70.5 us: swap(): lax.ppermute(x, axis, [(i, i ^ 1 << bit) for i in range(self.sizes[axis])])]
    pallas_call x11 -> x16, Pallas kernels: 83.3 us -> 106 us  [the longest x10 71.4 us: grad_blocks(): pl.pallas_call(functools.partial(grad_kernel, groups, recv is not None, s...]
    dynamic_update_slice x24 -> x0, local copies, waits for them, and re-layouts: 21.2 us -> none  [the longest x8 10.3 us: gather(): return lax.dynamic_update_slice(full, got, ((1 - core) * half, 0))]
    dot_general x28 -> x16, matrix products: 93.9 us -> 73.3 us  [dot(): lax.dot_general(left, right, (dims, ((), ())), preferred_element_type=F32)]
    convert_element_type x1 -> x12, other arithmetic: 5.53 us -> 22.1 us  [the longest x5 10 us: third(): send = (self.keep[1].astype(F32) + recv[1].astype(F32)).astype(BF16)]
    ppermute x37 -> x46, waiting for transfers between devices: 131 us -> 144 us  [swap(): return lax.ppermute(x, axis, [(i, i ^ 1 << bit) for i in range(size)])]
  transfers between devices with their start and end apart: 58 -> 49, of which waited for: 24 -> 25; matrix products, arithmetic and copies ran while one was open for 24% -> 20% of each run, Pallas kernels for 14% -> 21%
where the time goes in v2:
time: 582 us; the launch traced here: 574 us
  waiting for transfers between devices  144 us (25%)
  Pallas kernels  142 us (24%)
  starting transfers between devices  121 us (21%)
  matrix products  73.3 us (13%)
  other arithmetic  62.5 us (11%)
  local copies, waits for them, and re-layouts  28.6 us (5%)
    ppermute x46, waiting for transfers between devices, swap(): return lax.ppermute(x, axis, [(i, i ^ 1 << bit) for i in range(size)])  144 us
    ppermute x46, starting transfers between devices, swap(): return lax.ppermute(x, axis, [(i, i ^ 1 << bit) for i in range(size)])  110 us
    dot_general x16, matrix products, dot(): lax.dot_general(left, right, (dims, ((), ())), preferred_element_type=F32)  73.3 us
    pallas_call x10, Pallas kernels, grad_blocks(): pl.pallas_call(functools.partial(grad_kernel, groups, recv is not None, s...  71.4 us
    pallas_call x2, Pallas kernels, attend_back(): pl.pallas_call(functools.partial(back_kernel, far_count), grid_spec=pltpu...  21.6 us
    pallas_call x2, Pallas kernels, place(): pl.pallas_call(place_kernel, grid_spec=pltpu.PrefetchScalarGridSpec(num_s...  15.6 us
    pallas_call x2, Pallas kernels, attend(): pl.pallas_call(functools.partial(attend_kernel, far_count), grid_spec=plt...  14.4 us
  transfers between devices with their start and end apart: 49, of which 25 were waited for; matrix products, arithmetic and copies ran while one was open for 20% of the time, Pallas kernels for 21%

profile of v2, /device:TPU:0, one launch (start us, length us, event | category | flops | bytes accessed | tf_op | source)
XLA Modules:
  0.0 573.9 jit_solution(15759697763143454207)
XLA Ops:
  5.4 9.0 %shard_map.203 = (bf16[1024,2048]{1,0:T(8,128)(2,1)}, bf16[512,1024]{1,0:T(8,128)(2,1)}, bf16[128,1024]{1,0:T(8,128)(2,1)}) custom-call(s32[3]{0:T(128)} %pad_add_fusion.1.at_ref, bf16[1024,2048]{1,0:T(8,128)(2,1)} %bitcast.108, f32[1,2048]{1,0:T(1,128)} %bitcast.135, bf16[2048,512]{1,0:T(8,128)(2,1)} %wq_ref.1, ...), custom_call_target="tpu_custom_call" | custom-call | flops 1024 | bytes 1024 | tf_op jit(solution)/shard_map/pallas_call | solution.py:66
  14.4 4.9 collective-permute-start.7
  19.3 4.5 collective-permute-start.8
  26.9 8.4 %fusion.33 = f32[512,1408]{1,0:T(8,128)} fusion(bf16[1408,2048]{1,0:T(8,128)(2,1)} %param.36, bf16[128,2048]{1,0:T(8,128)(2,1)S(1)} %get-tuple-element.326, bf16[128,2048]{1,0:T(8,128)(2,1)S(1)} %get-tuple-element.327, bf16[128,2048]{1,0:T(8,128)(2,1)S(1)} %get-tuple-element.328, bf16[128,2048]{1,0:T(8,128)(2,1)S(1)} %get-tuple-element.325), kind=kOutput, calls=%fused_computation.164 | convolution fusion | flops 2961178624 | bytes 10747904 | tf_op jit(solution)/shard_map/dot_general | solution.py:27
  37.0 8.4 %fusion.32 = f32[512,1408]{1,0:T(8,128)} fusion(bf16[1408,2048]{1,0:T(8,128)(2,1)} %param.36, bf16[128,2048]{1,0:T(8,128)(2,1)S(1)} %get-tuple-element.322, bf16[128,2048]{1,0:T(8,128)(2,1)S(1)} %get-tuple-element.323, bf16[128,2048]{1,0:T(8,128)(2,1)S(1)} %get-tuple-element.324, bf16[128,2048]{1,0:T(8,128)(2,1)S(1)} %get-tuple-element.321), kind=kOutput, calls=%fused_computation.163 | convolution fusion | flops 2961178624 | bytes 10747904 | tf_op jit(solution)/shard_map/dot_general | solution.py:27
  47.7 7.1 %shard_map.204 = (bf16[8,128,512]{2,1,0:T(8,128)(2,1)}, bf16[512,512]{1,0:T(8,128)(2,1)}, f32[512,512]{1,0:T(8,128)}) custom-call(s32[3]{0:T(128)} %pad_add_fusion.1.at_ref, bf16[512,1024]{1,0:T(8,128)(2,1)} %get-tuple-element.186.q_ref, s32[2,4,512]{2,1,0:T(4,128)} %pad_add_fusion.seg_ref, bf16[128,1024]{1,0:T(8,128)(2,1)} %get-tuple-element.178.refs_0_, ...), custom_call_target="tpu_custom_call" | custom-call | flops 1024 | bytes 1024 | tf_op jit(solution)/shard_map/pallas_call | solution.py:182
  61.9 7.3 %shard_map.205 = (bf16[8,128,512]{2,1,0:T(8,128)(2,1)}, bf16[512,512]{1,0:T(8,128)(2,1)}, f32[512,512]{1,0:T(8,128)}) custom-call(s32[3]{0:T(128)} %pad_add_fusion.1.at_ref, bf16[512,1024]{1,0:T(8,128)(2,1)} %get-tuple-element.186.q_ref, s32[2,4,512]{2,1,0:T(4,128)} %pad_add_fusion.seg_ref, bf16[128,1024]{1,0:T(8,128)(2,1)} %get-tuple-element.178.refs_0_, ...), custom_call_target="tpu_custom_call" | custom-call | flops 1024 | bytes 1024 | tf_op jit(solution)/shard_map/pallas_call | solution.py:182
  69.2 5.2 collective-permute-done.11
  80.5 11.3 %collective-permute-done.13 = bf16[128,2048]{1,0:T(8,128)(2,1)S(1)} collective-permute-done((bf16[128,2048]{1,0:T(8,128)(2,1)S(1)}, bf16[128,2048]{1,0:T(8,128)(2,1)S(1)}, u32[]{:S(2)}, u32[]{:S(2)}) %collective-permute-start.13) | collective-permute-done | bytes 524320 | tf_op jit(solution)/shard_map/ppermute | solution.py:565
  94.6 5.0 fusion.31
  99.8 6.5 %collective-permute-done.15 = bf16[128,2048]{1,0:T(8,128)(2,1)S(1)} collective-permute-done((bf16[128,2048]{1,0:T(8,128)(2,1)S(1)}, bf16[128,2048]{1,0:T(8,128)(2,1)S(1)}, u32[]{:S(2)}, u32[]{:S(2)}) %collective-permute-start.15) | collective-permute-done | bytes 524320 | tf_op jit(solution)/shard_map/ppermute | solution.py:565
  109.0 6.2 %multiply_convert_fusion.5 = (bf16[512,1408]{1,0:T(8,128)(2,1)S(1)}, bf16[512,1408]{1,0:T(8,128)(2,1)S(1)}, bf16[512,1408]{1,0:T(8,128)(2,1)S(1)}) fusion(f32[512,1408]{1,0:T(8,128)} %fusion.31, f32[512,1408]{1,0:T(8,128)S(1)} %copy-done.83, bf16[512,2048]{1,0:T(8,128)(2,1)S(1)} %pad_maximum_fusion.3.refs_1_.refs_2_, bf16[2048,1408]{1,0:T(8,128)(2,1)S(1)} %bitcast.146), kind=kOutput, calls=%fused_computation.38 | convolution fusion | flops 2964324352 | bytes 17956864 | tf_op jit(solution)/shard_map/dot_general | solution.py:27
  127.6 4.6 convolution_convert_fusion.3
  132.2 5.8 %collective-permute-done.17 = bf16[128,2048]{1,0:T(8,128)(2,1)S(1)} collective-permute-done((bf16[128,2048]{1,0:T(8,128)(2,1)S(1)}, bf16[128,2048]{1,0:T(8,128)(2,1)S(1)}, u32[]{:S(2)}, u32[]{:S(2)}) %collective-permute-start.17) | collective-permute-done | bytes 524320 | tf_op jit(solution)/shard_map/ppermute | solution.py:565
  145.5 6.0 %fusion.30 = f32[512,1408]{1,0:T(8,128)S(1)} fusion(bf16[2048,1408]{1,0:T(8,128)(2,1)} %param.34, bf16[256,2048]{1,0:T(8,128)(2,1)} %collective-permute-done.18, bf16[128,2048]{1,0:T(8,128)(2,1)S(1)} %copy-done.60, bf16[128,2048]{1,0:T(8,128)(2,1)S(1)} %copy-done.30), kind=kOutput, calls=%fused_computation.161 | convolution fusion | flops 2959081472 | bytes 10747904 | tf_op jit(solution)/shard_map/dot_general | solution.py:27
  152.9 5.4 collective-permute-done.19
  161.5 5.5 multiply_convert_fusion
  167.1 4.9 convolution_convert_fusion.2
  172.0 7.8 %shard_map.206 = bf16[4,256,1408]{2,1,0:T(8,128)(2,1)} custom-call(s32[4]{0:T(128)} %add_add_fusion.1.table_ref, bf16[512,1408]{1,0:T(8,128)(2,1)} %copy-done.25, bf16[512,2048]{1,0:T(8,128)(2,1)} %get-tuple-element.204.refs_1_.refs_2_, bf16[512,2048]{1,0:T(8,128)(2,1)} %get-tuple-element.204.refs_1_.refs_2_, bf16[512,1408]{1,0:T(8,128)(2,1)} %copy-done.26, ...), custom_call_target="tpu_custom_call" | custom-call | flops 1024 | bytes 1024 | tf_op jit(solution)/shard_map/pallas_call | solution.py:453
  182.8 11.9 %collective-permute-done.20 = bf16[128,2048]{1,0:T(8,128)(2,1)S(1)} collective-permute-done((bf16[128,2048]{1,0:T(8,128)(2,1)}, bf16[128,2048]{1,0:T(8,128)(2,1)S(1)}, u32[]{:S(2)}, u32[]{:S(2)}) %collective-permute-start.20) | collective-permute-done | bytes 524320 | tf_op jit(solution)/shard_map/ppermute | solution.py:565
  194.7 8.7 %conditional.7 = ((bf16[512,512]{1,0:T(8,128)(2,1)}, bf16[512,2048]{1,0:T(8,128)(2,1)S(1)})) conditional(s32[]{:T(128)} %convert_element_type.330, () %tuple.147, (bf16[128,2048]{1,0:T(8,128)(2,1)}, bf16[128,2048]{1,0:T(8,128)(2,1)S(1)}, bf16[512,2048]{1,0:T(8,128)(2,1)}) %tuple.149), branch_computations={%region_7.8_spmd, %region_8.9_spmd} | conditional | flops 1024 | bytes 23069828 | solution.py:561
  203.4 14.9 %conditional.8 = (bf16[1,128,2048]{2,1,0:T(8,128)(2,1)}, f32[128,2048]{1,0:T(8,128)}) conditional(s32[]{:T(128)} %convert_element_type.330, () %tuple.146, (bf16[512,1408]{1,0:T(8,128)(2,1)}, bf16[2048,1408]{1,0:T(8,128)(2,1)}, bf16[512,1408]{1,0:T(8,128)(2,1)}, bf16[2048,1408]{1,0:T(8,128)(2,1)}) %tuple.151), branch_computations={%region_9.10_spmd, %region_10.11_spmd} | conditional | flops 5909250048 | bytes 67371120 | solution.py:561
  203.4 6.1 %fusion.39 = f32[512,2048]{1,0:T(8,128)S(1)} fusion(bf16[512,1408]{1,0:T(8,128)(2,1)} %get-tuple-element.48, bf16[2048,1408]{1,0:T(8,128)(2,1)} %get-tuple-element.49), kind=kOutput, calls=%fused_computation.170 | convolution fusion | flops 2952790016 | bytes 11403264 | tf_op jit(solution)/shard_map/cond/branch_1_fun/dot_general | solution.py:27
  220.5 7.9 %shard_map.207 = bf16[4,256,1408]{2,1,0:T(8,128)(2,1)} custom-call(s32[4]{0:T(128)} %add_add_fusion.2.table_ref, bf16[512,1408]{1,0:T(8,128)(2,1)} %copy-done.20, bf16[512,2048]{1,0:T(8,128)(2,1)} %copy-done, bf16[512,2048]{1,0:T(8,128)(2,1)} %copy-done, bf16[512,1408]{1,0:T(8,128)(2,1)} %get-tuple-element.209.refs_3_, bf16[512,2048]{1,0:T(8,128)(2,1)} %copy-done.1, ...), custom_call_target="tpu_custom_call" | custom-call | flops 1024 | bytes 1024 | tf_op jit(solution)/shard_map/pallas_call | solution.py:453
  230.1 10.9 %shard_map.208 = (bf16[512,512]{1,0:T(8,128)(2,1)}, bf16[2,128,512]{2,1,0:T(8,128)(2,1)}, bf16[2,128,512]{2,1,0:T(8,128)(2,1)}) custom-call(s32[3]{0:T(128)} %pad_add_fusion.1.at_ref, bf16[8,128,512]{2,1,0:T(8,128)(2,1)} %get-tuple-element.211.qa_ref, bf16[512,512]{1,0:T(8,128)(2,1)S(1)} %copy-done.48, f32[512,512]{1,0:T(8,128)} %get-tuple-element.216.full_ref, ...), custom_call_target="tpu_custom_call" | custom-call | flops 1024 | bytes 1024 | tf_op jit(solution)/shard_map/pallas_call | solution.py:288
  247.0 7.3 %shard_map.209 = bf16[4,256,1408]{2,1,0:T(8,128)(2,1)} custom-call(s32[4]{0:T(128)} %add_add_fusion.1.table_ref, bf16[512,1408]{1,0:T(8,128)(2,1)} %copy-done.19, bf16[512,2048]{1,0:T(8,128)(2,1)} %copy-done, bf16[512,2048]{1,0:T(8,128)(2,1)} %copy-done, bf16[512,1408]{1,0:T(8,128)(2,1)S(1)} %copy-done.21, bf16[512,2048]{1,0:T(8,128)(2,1)} %copy-done.1, ...), custom_call_target="tpu_custom_call" | custom-call | flops 1024 | bytes 1024 | tf_op jit(solution)/shard_map/pallas_call | solution.py:453
  255.5 4.7 collective-permute-done.22
  260.2 10.2 %conditional.9 = ((bf16[512,512]{1,0:T(8,128)(2,1)}, bf16[512,2048]{1,0:T(8,128)(2,1)})) conditional(s32[]{:T(128)} %convert_element_type.330, () %tuple.145, (bf16[128,2048]{1,0:T(8,128)(2,1)}, bf16[128,2048]{1,0:T(8,128)(2,1)}, bf16[512,2048]{1,0:T(8,128)(2,1)}) %tuple.157), branch_computations={%region_12.13_spmd, %region_13.14_spmd} | conditional | flops 1024 | bytes 23069828 | solution.py:561
  270.5 9.8 %shard_map.210 = (bf16[2,256,1408]{2,1,0:T(8,128)(2,1)}, bf16[2,256,1408]{2,1,0:T(8,128)(2,1)}) custom-call(s32[4]{0:T(128)} %add_add_fusion.table_ref, bf16[512,1408]{1,0:T(8,128)(2,1)} %copy-done.25, bf16[512,2048]{1,0:T(8,128)(2,1)} %get-tuple-element.204.refs_1_.refs_2_, bf16[512,2048]{1,0:T(8,128)(2,1)} %get-tuple-element.204.refs_1_.refs_2_, ...), custom_call_target="tpu_custom_call" | custom-call | flops 1024 | bytes 1024 | tf_op jit(solution)/shard_map/pallas_call | solution.py:453
  280.3 6.5 %conditional.10 = (bf16[2,128,2048]{2,1,0:T(8,128)(2,1)}, f32[2,128,2048]{2,1,0:T(8,128)S(1)}) conditional(s32[]{:T(128)} %convert_element_type.330, () %tuple.134, (bf16[512,2048]{1,0:T(8,128)(2,1)S(1)}, bf16[512,2048]{1,0:T(8,128)(2,1)S(1)}) %tuple.248), branch_computations={%region_14.15_spmd, %region_15.16_spmd} | conditional | flops 8388608 | bytes 31457336 | solution.py:561
  289.6 6.2 %collective-permute-start.29 = (bf16[2,256,1408]{2,1,0:T(8,128)(2,1)}, bf16[2,256,1408]{2,1,0:T(8,128)(2,1)}, u32[]{:S(2)}, u32[]{:S(2)}) collective-permute-start(bf16[2,256,1408]{2,1,0:T(8,128)(2,1)} %get-tuple-element.224), channel_id=1, source_target_pairs={{0,2},{2,0},{4,6},{6,4},{1,3},{3,1},{5,7},{7,5},{8,10},{10,8},{12,... | collective-permute-start | bytes 4325384 | tf_op jit(solution)/shard_map/ppermute | solution.py:565
  295.8 10.7 %shard_map.211 = (bf16[512,512]{1,0:T(8,128)(2,1)}, bf16[2,128,512]{2,1,0:T(8,128)(2,1)}, bf16[2,128,512]{2,1,0:T(8,128)(2,1)}) custom-call(s32[3]{0:T(128)} %pad_add_fusion.1.at_ref, bf16[8,128,512]{2,1,0:T(8,128)(2,1)} %get-tuple-element.229.qa_ref, bf16[512,512]{1,0:T(8,128)(2,1)S(1)} %copy-done.49, f32[512,512]{1,0:T(8,128)} %get-tuple-element.232.full_ref, ...), custom_call_target="tpu_custom_call" | custom-call | flops 1024 | bytes 1024 | tf_op jit(solution)/shard_map/pallas_call | solution.py:288
  308.3 5.9 %collective-permute-start.26 = (bf16[2,2,128,512]{3,2,0,1:T(8,128)(2,1)}, bf16[2,2,128,512]{3,2,0,1:T(8,128)(2,1)}, u32[]{:S(2)}, u32[]{:S(2)}) collective-permute-start(bf16[2,2,128,512]{3,2,0,1:T(8,128)(2,1)} %pad_maximum_fusion.11), channel_id=1, source_target_pairs={{0,2},{2,0},{4,6},{6,4},{1,3},{3,1},{5,7},{7,5},{8,10},{10,8},{12,... | collective-permute-start | bytes 1572872 | tf_op jit(solution)/shard_map/ppermute | solution.py:565
  321.5 9.2 %shard_map.212 = (bf16[2,256,1408]{2,1,0:T(8,128)(2,1)}, bf16[2,256,1408]{2,1,0:T(8,128)(2,1)}) custom-call(s32[4]{0:T(128)} %add_add_fusion.3.table_ref, bf16[512,1408]{1,0:T(8,128)(2,1)} %copy-done.20, bf16[512,2048]{1,0:T(8,128)(2,1)} %copy-done, bf16[512,2048]{1,0:T(8,128)(2,1)} %copy-done, bf16[512,1408]{1,0:T(8,128)(2,1)S(1)} %copy-done.23, ...), custom_call_target="tpu_custom_call" | custom-call | flops 1024 | bytes 1024 | tf_op jit(solution)/shard_map/pallas_call | solution.py:453
  330.7 6.3 %shard_map.213 = bf16[4,1024,256]{2,1,0:T(8,128)(2,1)} custom-call(s32[4]{0:T(128)} %add_add_fusion.1.table_ref, bf16[512,512]{1,0:T(8,128)(2,1)} %get-tuple-element.184.refs_0_, bf16[512,2048]{1,0:T(8,128)(2,1)S(1)} %get-tuple-element.241.refs_1_.refs_2_, bf16[512,2048]{1,0:T(8,128)(2,1)S(1)} %get-tuple-element.241.refs_1_.refs_2_, ...), custom_call_target="tpu_custom_call" | custom-call | flops 1024 | bytes 1024 | tf_op jit(solution)/shard_map/pallas_call | solution.py:453
  341.3 8.8 %shard_map.214 = (bf16[2,256,1408]{2,1,0:T(8,128)(2,1)}, bf16[2,256,1408]{2,1,0:T(8,128)(2,1)}) custom-call(s32[4]{0:T(128)} %add_add_fusion.table_ref, bf16[512,1408]{1,0:T(8,128)(2,1)} %copy-done.19, bf16[512,2048]{1,0:T(8,128)(2,1)} %copy-done, bf16[512,2048]{1,0:T(8,128)(2,1)} %copy-done, bf16[512,1408]{1,0:T(8,128)(2,1)S(1)} %copy-done.22, ...), custom_call_target="tpu_custom_call" | custom-call | flops 1024 | bytes 1024 | tf_op jit(solution)/shard_map/pallas_call | solution.py:453
  356.5 4.5 conditional.11
  361.0 32.3 %collective-permute-start.30 = (bf16[2,128,512]{2,1,0:T(8,128)(2,1)S(1)}, bf16[2,128,512]{2,1,0:T(8,128)(2,1)S(1)}, u32[]{:S(2)}, u32[]{:S(2)}) collective-permute-start(bf16[2,128,512]{2,1,0:T(8,128)(2,1)S(1)} %get-tuple-element.332), channel_id=1, source_target_pairs={{0,4},{2,6},{4,0},{6,2},{1,5},{3,7},{5,1},{7,3},{8,12},{10,14},{12... | collective-permute-start | bytes 786440 | tf_op jit(solution)/shard_map/ppermute | solution.py:565
  393.3 7.7 %shard_map.215 = bf16[2,512,2048]{2,1,0:T(8,128)(2,1)} custom-call(s32[3]{0:T(128)} %pad_add_fusion.1.at_ref, bf16[2,256,2048]{2,1,0:T(8,128)(2,1)} %pad_maximum_fusion.5.near_ref, bf16[2,256,2048]{2,1,0:T(8,128)(2,1)} %get-tuple-element.370.far_ref), custom_call_target="tpu_custom_call" | custom-call | flops 1024 | bytes 1024 | tf_op jit(solution)/shard_map/pallas_call | solution.py:540
  407.8 10.2 %conditional.12 = (bf16[2,128,2048]{2,1,0:T(8,128)(2,1)}, f32[2,128,2048]{2,1,0:T(8,128)S(1)}) conditional(s32[]{:T(128)} %convert_element_type.330, () %tuple.169, (bf16[512,512]{1,0:T(8,128)(2,1)S(1)}, bf16[512,512]{1,0:T(8,128)(2,1)S(1)}, bf16[2048,512]{1,0:T(8,128)(2,1)S(1)}, bf16[128,512]{1,0:T(8,128)(2,1)S(1)}, ...), branch_computations={%region_19.20_spmd, %region_20.21_spmd} | conditional | flops 2694316032 | bytes 52166712 | solution.py:561
  421.7 31.1 %collective-permute-start.37 = (bf16[256,1408]{1,0:T(8,128)(2,1)}, bf16[256,1408]{1,0:T(8,128)(2,1)}, u32[]{:S(2)}, u32[]{:S(2)}) collective-permute-start(bf16[256,1408]{1,0:T(8,128)(2,1)} %fusion.15), channel_id=1, source_target_pairs={{0,4},{2,6},{4,0},{6,2},{1,5},{3,7},{5,1},{7,3},{8,12},{10,14},{12... | collective-permute-start | bytes 2162696 | tf_op jit(solution)/shard_map/ppermute | solution.py:565
  456.6 7.6 %shard_map.218 = (bf16[2,1024,256]{2,1,0:T(8,128)(2,1)}, bf16[2,1024,256]{2,1,0:T(8,128)(2,1)}) custom-call(s32[4]{0:T(128)} %add_add_fusion.table_ref, bf16[512,512]{1,0:T(8,128)(2,1)} %get-tuple-element.184.refs_0_, bf16[512,2048]{1,0:T(8,128)(2,1)S(1)} %get-tuple-element.241.refs_1_.refs_2_, bf16[512,2048]{1,0:T(8,128)(2,1)S(1)} %get-tuple-element.241.refs_1_.refs_2_, ...), custom_call_target="tpu_custom_call" | custom-call | flops 1024 | bytes 1024 | tf_op jit(solution)/shard_map/pallas_call | solution.py:453
  472.9 10.5 %collective-permute-done.37 = bf16[256,1408]{1,0:T(8,128)(2,1)} collective-permute-done((bf16[256,1408]{1,0:T(8,128)(2,1)}, bf16[256,1408]{1,0:T(8,128)(2,1)}, u32[]{:S(2)}, u32[]{:S(2)}) %collective-permute-start.37) | collective-permute-done | bytes 720928 | tf_op jit(solution)/shard_map/ppermute | solution.py:565
  487.7 7.0 %collective-permute-done.38 = f32[2,2048]{1,0:T(2,128)S(1)} collective-permute-done((f32[2,2048]{1,0:T(2,128)S(1)}, f32[2,2048]{1,0:T(2,128)S(1)}, u32[]{:S(2)}, u32[]{:S(2)}) %collective-permute-start.38) | collective-permute-done | bytes 16416 | tf_op jit(solution)/shard_map/ppermute | solution.py:565
  500.5 19.1 %collective-permute-done.40 = bf16[2,1024,256]{2,1,0:T(8,128)(2,1)} collective-permute-done((bf16[2,1024,256]{2,1,0:T(8,128)(2,1)}, bf16[2,1024,256]{2,1,0:T(8,128)(2,1)}, u32[]{:S(2)}, u32[]{:S(2)}) %collective-permute-start.40) | collective-permute-done | bytes 1048608 | tf_op jit(solution)/shard_map/ppermute | solution.py:565
  526.1 7.9 %shard_map.220 = f32[2,512,2048]{2,1,0:T(8,128)} custom-call(s32[3]{0:T(128)} %pad_add_fusion.1.at_ref, bf16[2,256,2048]{2,1,0:T(8,128)(2,1)S(1)} %pad_maximum_fusion.7.near_ref, bf16[2,256,2048]{2,1,0:T(8,128)(2,1)} %get-tuple-element.371.far_ref), custom_call_target="tpu_custom_call" | custom-call | flops 1024 | bytes 1024 | tf_op jit(solution)/shard_map/pallas_call | solution.py:540
  546.4 14.2 %collective-permute-done.47 = bf16[128,256]{1,0:T(8,128)(2,1)S(1)} collective-permute-done((bf16[128,256]{1,0:T(8,128)(2,1)S(1)}, bf16[128,256]{1,0:T(8,128)(2,1)S(1)}, u32[]{:S(2)}, u32[]{:S(2)}) %collective-permute-start.47) | collective-permute-done | bytes 65568 | tf_op jit(solution)/shard_map/ppermute | solution.py:565
  562.1 8.5 %collective-permute-done.48 = bf16[1024,256]{1,0:T(8,128)(2,1)S(1)} collective-permute-done((bf16[1024,256]{1,0:T(8,128)(2,1)S(1)}, bf16[1024,256]{1,0:T(8,128)(2,1)S(1)}, u32[]{:S(2)}, u32[]{:S(2)}) %collective-permute-start.48) | collective-permute-done | bytes 524320 | tf_op jit(solution)/shard_map/ppermute | solution.py:565
  (387 shorter events, 200.3 us)
Async XLA Ops:
  14.4 31.8 %collective-permute-start.7 = (bf16[128,1024]{1,0:T(8,128)(2,1)}, bf16[128,1024]{1,0:T(8,128)(2,1)S(1)}, u32[]{:S(2)}, u32[]{:S(2)}) collective-permute-start(bf16[128,1024]{1,0:T(8,128)(2,1)} %get-tuple-element.178.refs_0_), channel_id=1, source_target_pairs={{0,2},{2,4},{4,6},{1,3},{3,5},{5,7},{8,10},{10,12},{12,14},{9,11},... | collective-permute-start | bytes 786440 | tf_op jit(solution)/shard_map/ppermute | solution.py:612
  19.3 26.9 %collective-permute-start.8 = (bf16[128,1024]{1,0:T(8,128)(2,1)}, bf16[128,1024]{1,0:T(8,128)(2,1)S(1)}, u32[]{:S(2)}, u32[]{:S(2)}) collective-permute-start(bf16[128,1024]{1,0:T(8,128)(2,1)} %get-tuple-element.178.refs_0_), channel_id=1, source_target_pairs={{0,4},{2,6},{1,5},{3,7},{8,12},{10,14},{9,13},{11,15},{16,20},{18,... | collective-permute-start | bytes 786440 | tf_op jit(solution)/shard_map/ppermute | solution.py:612
  23.8 22.4 %collective-permute-start.9 = (bf16[128,1024]{1,0:T(8,128)(2,1)}, bf16[128,1024]{1,0:T(8,128)(2,1)S(1)}, u32[]{:S(2)}, u32[]{:S(2)}) collective-permute-start(bf16[128,1024]{1,0:T(8,128)(2,1)} %get-tuple-element.178.refs_0_), channel_id=1, source_target_pairs={{0,6},{1,7},{8,14},{9,15},{16,22},{17,23},{24,30},{25,31}} | collective-permute-start | bytes 786440 | tf_op jit(solution)/shard_map/ppermute | solution.py:612
  57.2 2.7 collective-permute-start.10
  60.3 14.0 %collective-permute-start.11 = (bf16[128,2048]{1,0:T(8,128)(2,1)S(1)}, bf16[128,2048]{1,0:T(8,128)(2,1)S(1)}, u32[]{:S(2)}, u32[]{:S(2)}) collective-permute-start(bf16[128,2048]{1,0:T(8,128)(2,1)S(1)} %slice.331), channel_id=1, source_target_pairs={{0,16},{8,24},{16,0},{24,8},{1,17},{9,25},{17,1},{25,9},{2,18},{10... | collective-permute-start | bytes 1572872 | tf_op jit(solution)/shard_map/ppermute | solution.py:565
  77.3 2.7 collective-permute-start.12
  77.4 14.3 %collective-permute-start.13 = (bf16[128,2048]{1,0:T(8,128)(2,1)S(1)}, bf16[128,2048]{1,0:T(8,128)(2,1)S(1)}, u32[]{:S(2)}, u32[]{:S(2)}) collective-permute-start(bf16[128,2048]{1,0:T(8,128)(2,1)S(1)} %multiply_convert_fusion.7), channel_id=1, source_target_pairs={{0,16},{8,24},{16,0},{24,8},{1,17},{9,25},{17,1},{25,9},{2,18},{10... | collective-permute-start | bytes 1572872 | tf_op jit(solution)/shard_map/ppermute | solution.py:565
  91.9 2.7 collective-permute-start.14
  92.0 14.3 %collective-permute-start.15 = (bf16[128,2048]{1,0:T(8,128)(2,1)S(1)}, bf16[128,2048]{1,0:T(8,128)(2,1)S(1)}, u32[]{:S(2)}, u32[]{:S(2)}) collective-permute-start(bf16[128,2048]{1,0:T(8,128)(2,1)S(1)} %slice.330), channel_id=1, source_target_pairs={{0,16},{8,24},{16,0},{24,8},{1,17},{9,25},{17,1},{25,9},{2,18},{10... | collective-permute-start | bytes 1572872 | tf_op jit(solution)/shard_map/ppermute | solution.py:565
  123.6 2.7 collective-permute-start.16
  123.7 14.3 %collective-permute-start.17 = (bf16[128,2048]{1,0:T(8,128)(2,1)S(1)}, bf16[128,2048]{1,0:T(8,128)(2,1)S(1)}, u32[]{:S(2)}, u32[]{:S(2)}) collective-permute-start(bf16[128,2048]{1,0:T(8,128)(2,1)S(1)} %multiply_convert_fusion.6), channel_id=1, source_target_pairs={{0,16},{8,24},{16,0},{24,8},{1,17},{9,25},{17,1},{25,9},{2,18},{10... | collective-permute-start | bytes 1572872 | tf_op jit(solution)/shard_map/ppermute | solution.py:565
  139.2 6.2 %collective-permute-start.18 = (bf16[256,2048]{1,0:T(8,128)(2,1)}, bf16[256,2048]{1,0:T(8,128)(2,1)}, u32[]{:S(2)}, u32[]{:S(2)}) collective-permute-start(bf16[256,2048]{1,0:T(8,128)(2,1)} %pad_maximum_fusion.9), channel_id=1, source_target_pairs={{0,8},{8,0},{16,24},{24,16},{1,9},{9,1},{17,25},{25,17},{2,10},{10... | collective-permute-start | bytes 3145736 | tf_op jit(solution)/shard_map/ppermute | solution.py:565
  143.8 14.4 %collective-permute-start.19 = (bf16[128,2048]{1,0:T(8,128)(2,1)S(1)}, bf16[128,2048]{1,0:T(8,128)(2,1)S(1)}, u32[]{:S(2)}, u32[]{:S(2)}) collective-permute-start(bf16[128,2048]{1,0:T(8,128)(2,1)S(1)} %copy-done.70), channel_id=1, source_target_pairs={{0,16},{8,24},{16,0},{24,8},{1,17},{9,25},{17,1},{25,9},{2,18},{10... | collective-permute-start | bytes 1572872 | tf_op jit(solution)/shard_map/ppermute | solution.py:565
  179.8 90.7 %collective-permute-start.23 = (bf16[4,256,1408]{2,1,0:T(8,128)(2,1)}, bf16[4,256,1408]{2,1,0:T(8,128)(2,1)}, u32[]{:S(2)}, u32[]{:S(2)}) collective-permute-start(bf16[4,256,1408]{2,1,0:T(8,128)(2,1)} %shard_map.206), channel_id=1, source_target_pairs={{0,1},{1,0},{2,3},{3,2},{4,5},{5,4},{6,7},{7,6},{8,9},{9,8},{10,11... | collective-permute-start | bytes 8650760 | tf_op jit(solution)/shard_map/ppermute | solution.py:565
  181.2 13.5 %collective-permute-start.20 = (bf16[128,2048]{1,0:T(8,128)(2,1)}, bf16[128,2048]{1,0:T(8,128)(2,1)S(1)}, u32[]{:S(2)}, u32[]{:S(2)}) collective-permute-start(bf16[128,2048]{1,0:T(8,128)(2,1)} %get-tuple-element.305), channel_id=1, source_target_pairs={{0,16},{8,24},{16,0},{24,8},{1,17},{9,25},{17,1},{25,9},{2,18},{10... | collective-permute-start | bytes 1572872 | tf_op jit(solution)/shard_map/ppermute | solution.py:565
  196.0 2.7 collective-permute-start.2
  213.3 2.7 collective-permute-start.5
  218.3 22.7 %collective-permute-start.21 = (bf16[128,2048]{1,0:T(8,128)(2,1)}, bf16[128,2048]{1,0:T(8,128)(2,1)}, u32[]{:S(2)}, u32[]{:S(2)}) collective-permute-start(bf16[128,2048]{1,0:T(8,128)(2,1)} %bitcast.23), channel_id=1, source_target_pairs={{0,16},{8,24},{16,0},{24,8},{1,17},{9,25},{17,1},{25,9},{2,18},{10... | collective-permute-start | bytes 1572872 | tf_op jit(solution)/shard_map/ppermute | solution.py:565
  228.4 93.1 %collective-permute-start.25 = (bf16[4,256,1408]{2,1,0:T(8,128)(2,1)}, bf16[4,256,1408]{2,1,0:T(8,128)(2,1)}, u32[]{:S(2)}, u32[]{:S(2)}) collective-permute-start(bf16[4,256,1408]{2,1,0:T(8,128)(2,1)} %shard_map.207), channel_id=1, source_target_pairs={{0,2},{2,0},{4,6},{6,4},{1,3},{3,1},{5,7},{7,5},{8,10},{10,8},{12,... | collective-permute-start | bytes 8650760 | tf_op jit(solution)/shard_map/ppermute | solution.py:565
  246.5 13.7 %collective-permute-start.22 = (bf16[128,2048]{1,0:T(8,128)(2,1)}, bf16[128,2048]{1,0:T(8,128)(2,1)}, u32[]{:S(2)}, u32[]{:S(2)}) collective-permute-start(bf16[128,2048]{1,0:T(8,128)(2,1)} %get-tuple-element.303), channel_id=1, source_target_pairs={{0,16},{8,24},{16,0},{24,8},{1,17},{9,25},{17,1},{25,9},{2,18},{10... | collective-permute-start | bytes 1572872 | tf_op jit(solution)/shard_map/ppermute | solution.py:565
  254.3 87.0 %collective-permute-start.27 = (bf16[4,256,1408]{2,1,0:T(8,128)(2,1)}, bf16[4,256,1408]{2,1,0:T(8,128)(2,1)}, u32[]{:S(2)}, u32[]{:S(2)}) collective-permute-start(bf16[4,256,1408]{2,1,0:T(8,128)(2,1)} %shard_map.209), channel_id=1, source_target_pairs={{0,1},{1,0},{2,3},{3,2},{4,5},{5,4},{6,7},{7,6},{8,9},{9,8},{10,11... | collective-permute-start | bytes 8650760 | tf_op jit(solution)/shard_map/ppermute | solution.py:565
  280.4 4.2 collective-permute-start.4
  286.8 27.4 %collective-permute-start.24 = (bf16[2,128,2048]{2,1,0:T(8,128)(2,1)}, bf16[2,128,2048]{2,1,0:T(8,128)(2,1)S(1)}, u32[]{:S(2)}, u32[]{:S(2)}) collective-permute-start(bf16[2,128,2048]{2,1,0:T(8,128)(2,1)} %get-tuple-element.230), channel_id=1, source_target_pairs={{0,16},{8,24},{16,0},{24,8},{1,17},{9,25},{17,1},{25,9},{2,18},{10... | collective-permute-start | bytes 3145736 | tf_op jit(solution)/shard_map/ppermute | solution.py:565
  289.6 111.5 %collective-permute-start.29 = (bf16[2,256,1408]{2,1,0:T(8,128)(2,1)}, bf16[2,256,1408]{2,1,0:T(8,128)(2,1)}, u32[]{:S(2)}, u32[]{:S(2)}) collective-permute-start(bf16[2,256,1408]{2,1,0:T(8,128)(2,1)} %get-tuple-element.224), channel_id=1, source_target_pairs={{0,2},{2,0},{4,6},{6,4},{1,3},{3,1},{5,7},{7,5},{8,10},{10,8},{12,... | collective-permute-start | bytes 4325384 | tf_op jit(solution)/shard_map/ppermute | solution.py:565
  308.3 30.6 %collective-permute-start.26 = (bf16[2,2,128,512]{3,2,0,1:T(8,128)(2,1)}, bf16[2,2,128,512]{3,2,0,1:T(8,128)(2,1)}, u32[]{:S(2)}, u32[]{:S(2)}) collective-permute-start(bf16[2,2,128,512]{3,2,0,1:T(8,128)(2,1)} %pad_maximum_fusion.11), channel_id=1, source_target_pairs={{0,2},{2,0},{4,6},{6,4},{1,3},{3,1},{5,7},{7,5},{8,10},{10,8},{12,... | collective-permute-start | bytes 1572872 | tf_op jit(solution)/shard_map/ppermute | solution.py:565
  317.4 35.9 %collective-permute-start.28 = (bf16[2,128,2048]{2,1,0:T(8,128)(2,1)}, bf16[2,128,2048]{2,1,0:T(8,128)(2,1)}, u32[]{:S(2)}, u32[]{:S(2)}) collective-permute-start(bf16[2,128,2048]{2,1,0:T(8,128)(2,1)} %fusion.12), channel_id=1, source_target_pairs={{0,16},{8,24},{16,0},{24,8},{1,17},{9,25},{17,1},{25,9},{2,18},{10... | collective-permute-start | bytes 3145736 | tf_op jit(solution)/shard_map/ppermute | solution.py:565
  337.0 119.1 %collective-permute-start.32 = (bf16[4,1024,256]{2,1,0:T(8,128)(2,1)}, bf16[4,1024,256]{2,1,0:T(8,128)(2,1)}, u32[]{:S(2)}, u32[]{:S(2)}) collective-permute-start(bf16[4,1024,256]{2,1,0:T(8,128)(2,1)} %shard_map.213), channel_id=1, source_target_pairs={{0,1},{1,0},{2,3},{3,2},{4,5},{5,4},{6,7},{7,6},{8,9},{9,8},{10,11... | collective-permute-start | bytes 6291464 | tf_op jit(solution)/shard_map/ppermute | solution.py:565
  338.8 80.5 %collective-permute-start.31 = (bf16[2,256,1408]{2,1,0:T(8,128)(2,1)}, bf16[2,256,1408]{2,1,0:T(8,128)(2,1)}, u32[]{:S(2)}, u32[]{:S(2)}) collective-permute-start(bf16[2,256,1408]{2,1,0:T(8,128)(2,1)} %get-tuple-element.238), channel_id=1, source_target_pairs={{0,1},{1,0},{2,3},{3,2},{4,5},{5,4},{6,7},{7,6},{8,9},{9,8},{10,11... | collective-permute-start | bytes 4325384 | tf_op jit(solution)/shard_map/ppermute | solution.py:565
  350.2 114.1 %collective-permute-start.33 = (bf16[2,256,1408]{2,1,0:T(8,128)(2,1)}, bf16[2,256,1408]{2,1,0:T(8,128)(2,1)}, u32[]{:S(2)}, u32[]{:S(2)}) collective-permute-start(bf16[2,256,1408]{2,1,0:T(8,128)(2,1)} %get-tuple-element.247), channel_id=1, source_target_pairs={{0,2},{2,0},{4,6},{6,4},{1,3},{3,1},{5,7},{7,5},{8,10},{10,8},{12,... | collective-permute-start | bytes 4325384 | tf_op jit(solution)/shard_map/ppermute | solution.py:565
  356.5 4.5 collective-permute-start
  361.0 42.5 %collective-permute-start.30 = (bf16[2,128,512]{2,1,0:T(8,128)(2,1)S(1)}, bf16[2,128,512]{2,1,0:T(8,128)(2,1)S(1)}, u32[]{:S(2)}, u32[]{:S(2)}) collective-permute-start(bf16[2,128,512]{2,1,0:T(8,128)(2,1)S(1)} %get-tuple-element.332), channel_id=1, source_target_pairs={{0,4},{2,6},{4,0},{6,2},{1,5},{3,7},{5,1},{7,3},{8,12},{10,14},{12... | collective-permute-start | bytes 786440 | tf_op jit(solution)/shard_map/ppermute | solution.py:565
  403.3 66.1 %collective-permute-start.35 = (bf16[256,1408]{1,0:T(8,128)(2,1)}, bf16[256,1408]{1,0:T(8,128)(2,1)}, u32[]{:S(2)}, u32[]{:S(2)}) collective-permute-start(bf16[256,1408]{1,0:T(8,128)(2,1)} %fusion.14), channel_id=1, source_target_pairs={{0,4},{2,6},{4,0},{6,2},{1,5},{3,7},{5,1},{7,3},{8,12},{10,14},{12... | collective-permute-start | bytes 2162696 | tf_op jit(solution)/shard_map/ppermute | solution.py:565
  411.7 4.2 collective-permute-start.6
  418.0 49.2 %collective-permute-start.34 = (bf16[2,128,2048]{2,1,0:T(8,128)(2,1)}, bf16[2,128,2048]{2,1,0:T(8,128)(2,1)S(1)}, u32[]{:S(2)}, u32[]{:S(2)}) collective-permute-start(bf16[2,128,2048]{2,1,0:T(8,128)(2,1)} %get-tuple-element.257), channel_id=1, source_target_pairs={{0,16},{8,24},{16,0},{24,8},{1,17},{9,25},{17,1},{25,9},{2,18},{10... | collective-permute-start | bytes 3145736 | tf_op jit(solution)/shard_map/ppermute | solution.py:565
  421.7 61.7 %collective-permute-start.37 = (bf16[256,1408]{1,0:T(8,128)(2,1)}, bf16[256,1408]{1,0:T(8,128)(2,1)}, u32[]{:S(2)}, u32[]{:S(2)}) collective-permute-start(bf16[256,1408]{1,0:T(8,128)(2,1)} %fusion.15), channel_id=1, source_target_pairs={{0,4},{2,6},{4,0},{6,2},{1,5},{3,7},{5,1},{7,3},{8,12},{10,14},{12... | collective-permute-start | bytes 2162696 | tf_op jit(solution)/shard_map/ppermute | solution.py:565
  456.1 39.3 %collective-permute-start.39 = (bf16[4,128,256]{2,1,0:T(8,128)(2,1)}, bf16[4,128,256]{2,1,0:T(8,128)(2,1)}, u32[]{:S(2)}, u32[]{:S(2)}) collective-permute-start(bf16[4,128,256]{2,1,0:T(8,128)(2,1)} %shard_map.217), channel_id=1, source_target_pairs={{0,1},{1,0},{2,3},{3,2},{4,5},{5,4},{6,7},{7,6},{8,9},{9,8},{10,11... | collective-permute-start | bytes 786440 | tf_op jit(solution)/shard_map/ppermute | solution.py:565
  464.2 55.3 %collective-permute-start.40 = (bf16[2,1024,256]{2,1,0:T(8,128)(2,1)}, bf16[2,1024,256]{2,1,0:T(8,128)(2,1)}, u32[]{:S(2)}, u32[]{:S(2)}) collective-permute-start(bf16[2,1024,256]{2,1,0:T(8,128)(2,1)} %get-tuple-element.262), channel_id=1, source_target_pairs={{0,2},{2,0},{4,6},{6,4},{1,3},{3,1},{5,7},{7,5},{8,10},{10,8},{12,... | collective-permute-start | bytes 3145736 | tf_op jit(solution)/shard_map/ppermute | solution.py:565
  467.9 4.7 collective-permute-start.36
  469.4 52.1 %collective-permute-start.41 = (bf16[2,128,2048]{2,1,0:T(8,128)(2,1)S(1)}, bf16[2,128,2048]{2,1,0:T(8,128)(2,1)S(1)}, u32[]{:S(2)}, u32[]{:S(2)}) collective-permute-start(bf16[2,128,2048]{2,1,0:T(8,128)(2,1)S(1)} %fusion.13), channel_id=1, source_target_pairs={{0,16},{8,24},{16,0},{24,8},{1,17},{9,25},{17,1},{25,9},{2,18},{10... | collective-permute-start | bytes 3145736 | tf_op jit(solution)/shard_map/ppermute | solution.py:565
  472.6 62.4 %collective-permute-start.44 = (bf16[256,1408]{1,0:T(8,128)(2,1)}, bf16[256,1408]{1,0:T(8,128)(2,1)}, u32[]{:S(2)}, u32[]{:S(2)}) collective-permute-start(bf16[256,1408]{1,0:T(8,128)(2,1)} %fusion.16), channel_id=1, source_target_pairs={{0,4},{2,6},{4,0},{6,2},{1,5},{3,7},{5,1},{7,3},{8,12},{10,14},{12... | collective-permute-start | bytes 2162696 | tf_op jit(solution)/shard_map/ppermute | solution.py:565
  483.4 11.4 %collective-permute-start.38 = (f32[2,2048]{1,0:T(2,128)S(1)}, f32[2,2048]{1,0:T(2,128)S(1)}, u32[]{:S(2)}, u32[]{:S(2)}) collective-permute-start(f32[2,2048]{1,0:T(2,128)S(1)} %fusion.29), channel_id=1, source_target_pairs={{0,16},{8,24},{16,0},{24,8},{1,17},{9,25},{17,1},{25,9},{2,18},{10... | collective-permute-start | bytes 49160 | tf_op jit(solution)/shard_map/ppermute | solution.py:565
  498.9 35.2 %collective-permute-start.42 = (bf16[2,128,256]{2,1,0:T(8,128)(2,1)}, bf16[2,128,256]{2,1,0:T(8,128)(2,1)}, u32[]{:S(2)}, u32[]{:S(2)}) collective-permute-start(bf16[2,128,256]{2,1,0:T(8,128)(2,1)} %get-tuple-element.271), channel_id=1, source_target_pairs={{0,2},{2,0},{4,6},{6,4},{1,3},{3,1},{5,7},{7,5},{8,10},{10,8},{12,... | collective-permute-start | bytes 393224 | tf_op jit(solution)/shard_map/ppermute | solution.py:565
  521.7 4.4 collective-permute-start.1
  526.1 8.9 %collective-permute-start.43 = (f32[2,2048]{1,0:T(2,128)S(1)}, f32[2,2048]{1,0:T(2,128)S(1)}, u32[]{:S(2)}, u32[]{:S(2)}) collective-permute-start(f32[2,2048]{1,0:T(2,128)S(1)} %copy-done.79), channel_id=1, source_target_pairs={{0,2},{2,0},{4,6},{6,4},{1,3},{3,1},{5,7},{7,5},{8,10},{10,8},{12,... | collective-permute-start | bytes 49160 | tf_op jit(solution)/shard_map/ppermute | solution.py:565
  535.0 4.7 collective-permute-start.45
  539.7 6.0 %collective-permute-start.46 = (f32[2,2048]{1,0:T(2,128)S(1)}, f32[2,2048]{1,0:T(2,128)S(1)}, u32[]{:S(2)}, u32[]{:S(2)}) collective-permute-start(f32[2,2048]{1,0:T(2,128)S(1)} %add.440), channel_id=1, source_target_pairs={{0,1},{1,0},{2,3},{3,2},{4,5},{5,4},{6,7},{7,6},{8,9},{9,8},{10,11... | collective-permute-start | bytes 49160 | tf_op jit(solution)/shard_map/ppermute | solution.py:565
  542.8 17.8 %collective-permute-start.47 = (bf16[128,256]{1,0:T(8,128)(2,1)S(1)}, bf16[128,256]{1,0:T(8,128)(2,1)S(1)}, u32[]{:S(2)}, u32[]{:S(2)}) collective-permute-start(bf16[128,256]{1,0:T(8,128)(2,1)S(1)} %fusion.21), channel_id=1, source_target_pairs={{0,4},{2,6},{4,0},{6,2},{1,5},{3,7},{5,1},{7,3},{8,12},{10,14},{12... | collective-permute-start | bytes 196616 | tf_op jit(solution)/shard_map/ppermute | solution.py:565
  543.8 26.8 %collective-permute-start.48 = (bf16[1024,256]{1,0:T(8,128)(2,1)S(1)}, bf16[1024,256]{1,0:T(8,128)(2,1)S(1)}, u32[]{:S(2)}, u32[]{:S(2)}) collective-permute-start(bf16[1024,256]{1,0:T(8,128)(2,1)S(1)} %copy-done.69), channel_id=1, source_target_pairs={{0,4},{2,6},{4,0},{6,2},{1,5},{3,7},{5,1},{7,3},{8,12},{10,14},{12... | collective-permute-start | bytes 1572872 | tf_op jit(solution)/shard_map/ppermute | solution.py:565
  (97 other events, 1058.8 us)

commit v3 on v2

--- a/solution.py
+++ b/solution.py
@@ -16,7 +16,11 @@
 BLOCK = 256
 
 
-COST = pl.CostEstimate(flops=1024, bytes_accessed=1024, transcendentals=0)
+def cost(us=0):
+    return pl.CostEstimate(flops=int(us * 1.15e9) + 1024, bytes_accessed=1024, transcendentals=0)
+
+
+COST = cost()
 
 
 def params():
@@ -356,18 +360,16 @@
     return [x[j * size : (j + 1) * size] for j in range(pieces)]
 
 
-def unfold_kernel(near_ref, *refs):
-    *far_refs, w_ref, out_ref, full_ref = refs
-    half = near_ref.shape[0]
-    full_ref[:half] = near_ref[...]
-    piece = far_refs[0].shape[0]
-    for j, far_ref in enumerate(far_refs):
-        full_ref[half + j * piece : half + (j + 1) * piece] = far_ref[...]
+def unfold_kernel(*refs):
+    *part_refs, w_ref, out_ref, full_ref = refs
+    size = part_refs[0].shape[0]
+    for j, ref in enumerate(part_refs):
+        full_ref[j * size : (j + 1) * size] = ref[...]
     out_ref[...] = dot(w_ref[...], full_ref[...], NT).astype(BF16)
 
 
-def unfold(near, far, w):
-    rows, width = 2 * near.shape[0], near.shape[1]
+def unfold(parts, w):
+    rows, width = len(parts) * parts[0].shape[0], parts[0].shape[1]
     return pl.pallas_call(
         unfold_kernel,
         out_shape=[
@@ -376,7 +378,7 @@
         ],
         compiler_params=params(),
         cost_estimate=COST,
-    )(near, *far, w)
+    )(*parts, w)
 
 
 def grad_kernel(groups, has_recv, split, table_ref, *refs):
@@ -421,17 +423,19 @@
     pl.when(jnp.logical_not(first))(lambda: put(refs[at + 1]))
 
 
-def grad_blocks(table, form, sets, recv=None, split=0):
+def grad_blocks(table, form, sets, recv=None, split=0, us=0):
     n = table.shape[0]
     ins, specs, groups = [], [], []
     for wide_set, narrow_set in sets:
         pairs = []
-        for wide, narrow in zip(wide_set, narrow_set):
+        for s, (wide, narrow) in enumerate(zip(wide_set, narrow_set)):
             pairs.append((len(ins), len(ins) + 1))
             ins += [narrow, wide, wide]
             specs.append(pl.BlockSpec(narrow.shape, lambda i, t: (0, 0)))
+            tokens = narrow.shape[0 if form == TN else 1]
+            item = s if wide.shape[0] > tokens else 0
             for j in range(2):
-                specs.append(pl.BlockSpec((wide.shape[0], BLOCK), lambda i, t, j=j: (0, t[2 * i + j])))
+                specs.append(pl.BlockSpec((tokens, BLOCK), lambda i, t, j=j, item=item: (item, t[2 * i + j])))
         groups.append((form, pairs))
     if form == TN:
         block = (BLOCK, sets[0][1][0].shape[1])
@@ -455,8 +459,43 @@
         grid_spec=pltpu.PrefetchScalarGridSpec(num_scalar_prefetch=1, grid=(n // 2,), in_specs=specs, out_specs=out_specs),
         out_shape=out_shape,
         compiler_params=params(),
-        cost_estimate=COST,
+        cost_estimate=cost(us),
     )(table, *ins)
+
+
+def add_send_kernel(keep_ref, recv_ref, send_ref, rest_ref):
+    send_ref[...] = (keep_ref[1].astype(F32) + recv_ref[1].astype(F32)).astype(BF16)
+    rest_ref[...] = keep_ref[0].astype(F32) + recv_ref[0].astype(F32)
+
+
+def add_send(keep, recv, us):
+    shape = keep.shape[1:]
+    return pl.pallas_call(
+        add_send_kernel,
+        out_shape=[jax.ShapeDtypeStruct(shape, BF16), jax.ShapeDtypeStruct(shape, F32)],
+        compiler_params=params(),
+        cost_estimate=cost(us),
+    )(keep, recv)
+
+
+def add_last_kernel(turned, rest_ref, got_ref, *out_refs):
+    row = 0
+    for (count, flip), out_ref in zip(turned, out_refs):
+        total = rest_ref[row : row + count] + got_ref[row : row + count].astype(F32)
+        out_ref[...] = total.T if flip else total
+        row += count
+
+
+def add_last(rest, got, turned, us):
+    wide = rest.shape[1]
+    return pl.pallas_call(
+        functools.partial(add_last_kernel, turned),
+        out_shape=[
+            jax.ShapeDtypeStruct((wide, count) if flip else (count, wide), F32) for count, flip in turned
+        ],
+        compiler_params=params(),
+        cost_estimate=cost(us),
+    )(rest, got)
 
 
 class Order:
@@ -475,6 +514,13 @@
     def mark(self, x):
         self.last = x
         return x
+
+
+def sealed(fn, *args):
+    def never(*args):
+        return jax.tree.map(lambda leaf: jnp.zeros(leaf.shape, leaf.dtype), jax.eval_shape(fn, *args))
+
+    return lax.cond(lax.axis_index("tensor") >= 0, fn, never, *args)
 
 
 class Scatter:
@@ -498,67 +544,50 @@
         axis, bit = self.stages[j]
         self.got = swap(x, axis, self.sizes[axis], bit)
 
-    def first(self, order, sets):
+    def first(self, order, sets, us=0):
         if self.fast:
             wide = order.take(*sets[0][0])
             self.sets = [(list(wide), sets[0][1])] + sets[1:]
-            self.send(0, order.mark(grad_blocks(self.away, self.form, self.sets)))
-
-    def second(self, order):
+            self.send(0, order.mark(grad_blocks(self.away, self.form, self.sets, us=us)))
+
+    def second(self, order, us=0):
         if self.fast:
-            send, self.keep = grad_blocks(self.near, self.form, self.sets, order.take(self.got), 2)
+            send, self.keep = grad_blocks(self.near, self.form, self.sets, order.take(self.got), 2, us)
             self.send(1, order.mark(send))
 
-    def third(self, order):
+    def third(self, order, us=0):
         if self.fast:
-            recv = order.take(self.got)
-            send = (self.keep[1].astype(F32) + recv[1].astype(F32)).astype(BF16)
-            self.rest = self.keep[0].astype(F32) + recv[0].astype(F32)
+            send, self.rest = add_send(self.keep, order.take(self.got), us)
             self.send(2, order.mark(send))
 
-    def final(self, order):
+    def final(self, order, turned, us=0):
         if self.fast:
-            return order.mark(self.rest + order.take(self.got).astype(F32))
-
-
-def place_kernel(at_ref, near_ref, far_ref, out_ref):
-    p = pl.program_id(1)
-
-    @pl.when(p < 2)
-    def _():
-        out_ref[...] = near_ref[...].astype(out_ref.dtype)
-
-    @pl.when(p >= 2)
-    def _():
-        out_ref[...] = far_ref[...].astype(out_ref.dtype)
-
-
-def place(at, near, far, dtype):
-    seqs, half, width = near.shape
-    quarter = half // 2
-    block = (None, quarter, width)
+            out = add_last(self.rest, order.take(self.got), turned, us)
+            order.mark(out[0])
+            return out if len(out) > 1 else out[0]
+
+
+def place_kernel(at_ref, *refs):
+    *part_refs, out_ref = refs
+    quarter = part_refs[0].shape[0]
+    mine = 2 * at_ref[1] + at_ref[2]
+    for p, ref in enumerate(part_refs):
+        where = pl.ds(pl.multiple_of((p ^ mine) * quarter, quarter), quarter)
+        out_ref[where] = ref[...].astype(out_ref.dtype)
+
+
+def place(at, parts, dtype, us):
+    seqs, quarter, width = parts[0].shape
+    spec = lambda rows: pl.BlockSpec((None, rows, width), lambda s, at: (s, 0, 0))
     return pl.pallas_call(
         place_kernel,
         grid_spec=pltpu.PrefetchScalarGridSpec(
-            num_scalar_prefetch=1,
-            grid=(seqs, 4),
-            in_specs=[
-                pl.BlockSpec(block, lambda s, p, at: (s, jnp.minimum(p, 1), 0)),
-                pl.BlockSpec(block, lambda s, p, at: (s, jnp.maximum(p - 2, 0), 0)),
-            ],
-            out_specs=pl.BlockSpec(block, lambda s, p, at: (s, p ^ (2 * at[1] + at[2]), 0)),
+            num_scalar_prefetch=1, grid=(seqs,), in_specs=[spec(quarter)] * 4, out_specs=spec(4 * quarter)
         ),
-        out_shape=jax.ShapeDtypeStruct((seqs, 2 * half, width), dtype),
+        out_shape=jax.ShapeDtypeStruct((seqs, 4 * quarter, width), dtype),
         compiler_params=params(),
-        cost_estimate=COST,
-    )(at, near, far)
-
-
-def sealed(fn, *args):
-    def never(*args):
-        return jax.tree.map(lambda leaf: jnp.zeros(leaf.shape, leaf.dtype), jax.eval_shape(fn, *args))
-
-    return lax.cond(lax.axis_index("tensor") >= 0, fn, never, *args)
+        cost_estimate=cost(us),
+    )(at, *parts)
 
 
 def swap(x, axis, size, bit):
@@ -630,6 +659,11 @@
     def core_swap(x):
         return swap(x, "tensor", n_tensor, 0)
 
+    def core_swaps(first, second):
+        first = core_swap(first)
+        first, second = lax.optimization_barrier((first, second))
+        return first, core_swap(second)
+
     def fold_now(total):
         near = total[:, :half].astype(F32) + core_swap(total[:, half:]).astype(F32)
         return near[:, quarter:].astype(BF16), near[:, :quarter]
@@ -677,22 +711,29 @@
         got, block = spread_more(part, got, 1)
         return order.mark(jnp.concatenate([block, *order.take_all(got)], 0))
 
-    def back_partial(s, pieces):
-        left, right = order.take(d_gate[s], d_up[s])
-        got, kept = fold(product(order, pieces, (left, w_gate, NT), (right, w_up, NT)))
-        got_b[s], kept_b[s] = fold_more(kept, join(got))
+    def back_sealed(s):
+        def run(left, right):
+            return fold_now((dot(left, w_gate, NT) + dot(right, w_up, NT)).astype(BF16)[None])
+
+        send, kept = sealed(run, *order.take(d_gate[s], d_up[s]))
+        got_b[s], kept_b[s] = swap(order.mark(send)[0], "tensor", n_tensor, 1), kept[0]
 
     d_res, d_low_own, got_d, gains_2 = ([None] * seqs for _ in range(4))
 
+    def norm_back(scaled_grad, normed, scale, gain):
+        scaled = scaled_grad * gain
+        return scale * (scaled - normed * jnp.mean(scaled * normed, -1, keepdims=True))
+
     def after_back(s):
-        back = kept_b[s] + order.take(got_b[s]).astype(F32)
-        gains_2[s] = jnp.sum(back * normed_2[s], 0)
-        scaled = back * gain_2
-        d_res[s] = ct_own[s] + scale_2[s] * (
-            scaled - normed_2[s] * jnp.mean(scaled * normed_2[s], -1, keepdims=True)
+        def run(kept, got, normed, scale, own):
+            back = kept + got.astype(F32)
+            grad = own + norm_back(back, normed, scale, gain_2)
+            return grad.astype(BF16), grad, jnp.sum(back * normed, 0)
+
+        d_low_own[s], d_res[s], gains_2[s] = sealed(
+            run, kept_b[s], order.take(got_b[s]), normed_2[s], scale_2[s], ct_own[s]
         )
-        d_low_own[s] = order.mark(d_res[s].astype(BF16))
-        got_d[s] = spread(d_low_own[s])
+        got_d[s] = spread(order.mark(d_low_own[s]))
 
     blocks = n_context * n_dp
     fast = width // blocks == BLOCK and n_dp == 2 and n_context == 4
@@ -705,21 +746,30 @@
     kv_job = Scatter(x_first, sizes, NN, fast)
 
     downs = []
+
+    def feed_forward(rows, d_rows):
+        gate, up = dot(rows, w_gate, NN), dot(rows, w_up, NN)
+        sig = jax.nn.sigmoid(gate)
+        return (
+            (gate * sig * up).astype(BF16),
+            (d_rows * up * sig * (1.0 + gate * (1.0 - sig))).astype(BF16),
+            (d_rows * gate * sig).astype(BF16),
+        )
+
+    def add_down(s):
+        run = lambda rows: dot(rows, w_down, NN).astype(BF16)
+        downs.append(order.mark(sealed(run, order.take(hidden[s]))))
+
     for s in each:
         h2[s] = whole(h2_own[s], got_h[s])
-        gate = order.mark(dot(h2[s], w_gate, NN))
+        if s:
+            after_back(s - 1)
+        hidden[s], d_gate[s], d_up[s] = sealed(feed_forward, order.take(h2[s]), d_hidden[s])
+        order.mark(d_up[s])
         if s + 1 < seqs:
             after_attention(s + 1)
-        if s:
-            after_back(s - 1)
-        up = dot(order.take(h2[s]), w_up, NN)
-        sig = jax.nn.sigmoid(gate)
-        hidden[s] = (gate * sig * up).astype(BF16)
-        d_gate[s] = (d_hidden[s] * up * sig * (1.0 + gate * (1.0 - sig))).astype(BF16)
-        d_up[s] = order.mark((d_hidden[s] * gate * sig).astype(BF16))
-        if s + 1 < seqs:
-            back_partial(s, 1)
-        downs.append(order.mark(dot(order.take(hidden[s]), w_down, NN).astype(BF16)))
+            back_sealed(s)
+            add_down(s)
 
     d_low, dq_t, dkvs = [None] * seqs, [None] * seqs, [None] * seqs
 
@@ -727,18 +777,10 @@
 
     def unfolded(s):
         def run(part, got):
-            block = jnp.concatenate([part, got], 0)
-            return unfold(block, [core_swap(block)], w_output)
+            return unfold([part, got, *core_swaps(part, got)], w_output)
 
         do_t[s], d_low[s] = sealed(run, d_low_own[s], order.take(got_d[s]))
         order.mark(do_t[s])
-
-    def back_sealed(s):
-        def run(left, right):
-            return fold_now((dot(left, w_gate, NT) + dot(right, w_up, NT)).astype(BF16)[None])
-
-        send, kept = sealed(run, *order.take(d_gate[s], d_up[s]))
-        got_b[s], kept_b[s] = swap(order.mark(send)[0], "tensor", n_tensor, 1), kept[0]
 
     def attention_back(s):
         dq_t[s], *dkvs[s] = attend_back(
@@ -746,96 +788,91 @@
         )
         order.mark(dq_t[s])
 
-    def gather_natural(part):
-        part = order.mark(part)
-        return part, swap(part, "tensor", n_tensor, 1)
-
-    def gather_more(part, got):
-        block = order.mark(jnp.concatenate([part, order.take(got)], 1))
-        return block, order.mark(sealed(core_swap, block))
-
-    def natural(block, far, dtype):
-        return order.mark(place(at, block, order.take(far), dtype))
+    def place_all(part, got, dtype, us=0):
+        far = sealed(core_swaps, part, order.take(got))
+        return order.mark(place(at, [part, got, *far], dtype, us))
 
     last = seqs - 1
     down_job.first(order, [(cts, hidden)])
+    back_sealed(last)
     unfolded(0)
-    back_sealed(last)
     up_job.first(order, [(h2, d_up)])
-    attention_back(0)
     after_back(last)
-    gate_job.first(order, [(h2, d_gate)])
-    unfolded(last)
-    down_job.second(order)
+    gate_job.first(order, [(h2, d_gate)], 12)
+    add_down(last)
     send, kept_out = sealed(lambda *parts: fold_now(jnp.stack(parts)), *order.take_all(downs))
     got_out = swap(order.mark(send), "tensor", n_tensor, 1)
+    attention_back(0)
+    unfolded(last)
+    down_job.second(order, 6)
+    up_job.second(order)
+
+    def out_rows(got, kept, *rows):
+        return (jnp.stack(rows) + kept + got.astype(F32)).astype(BF16)
+
+    out_own = order.mark(sealed(out_rows, order.take(got_out), kept_out, *residual))
+    got_out = spread(out_own)
     attention_back(last)
 
-    h1s = [h1[s * stretch : (s + 1) * stretch] for s in each]
-    send = order.mark(jnp.stack([dkvs[s][1] for s in each]))
-    got_kv = swap(send, "context", n_context, 0)
-    kept_kv = jnp.stack([dkvs[s][0] for s in each])
-    out_own = (jnp.stack(residual) + kept_out + order.take(got_out).astype(F32)).astype(BF16)
-    out_part = gather_natural(out_own)
-    up_job.second(order)
-    mix_job.first(order, [(d_low, o_t), (h1s, dq_t)])
-    got_kv = order.take(got_kv)
-    send = order.mark((kept_kv[:, 1].astype(F32) + got_kv[:, 1].astype(F32)).astype(BF16))
-    kept_kv = (kept_kv[:, 0].astype(F32) + got_kv[:, 0].astype(F32)).astype(BF16)
-    got_kv = swap(send, "context", n_context, 1)
+    keep_send = [x for s in each for x in dkvs[s]]
+    kept_kv, send = sealed(lambda *xs: (jnp.stack(xs[0::2]), jnp.stack(xs[1::2])), *keep_send)
+    got_kv = swap(order.mark(send), "context", n_context, 0)
+    layer_out = place_all(out_own, got_out, BF16)
+    mix_job.first(order, [(d_low, o_t), ([h1] * seqs, dq_t)])
+
+    def add_kv(kept, got):
+        total = kept.astype(F32) + got.astype(F32)
+        return total[:, 0].astype(BF16), total[:, 1].astype(BF16)
+
+    kept_kv, send = sealed(add_kv, kept_kv, order.take(got_kv))
+    got_kv = swap(order.mark(send), "context", n_context, 1)
     gate_job.second(order)
-    layer_out = natural(*gather_more(*out_part), BF16)
-    down_job.third(order)
-    dkv_t = order.mark(merge(at, kept_kv, order.take(got_kv), cos_rows, sine_rows))
-    dkv_ts = [dkv_t[s] for s in each]
-    def input_partial(*parts):
-        rows_q, rows_kv = jnp.concatenate(parts[:seqs], 1), jnp.concatenate(parts[seqs:], 1)
+    down_job.third(order, 2)
+    up_job.third(order, 12)
+
+    def input_partial(kept, got, *parts):
+        both = merge(at, kept, got, cos_rows, sine_rows)
+        rows_q, rows_kv = jnp.concatenate(parts, 1), jnp.concatenate([both[s] for s in each], 1)
         total = dot(rows_q, w_query, TT) + dot(rows_kv, w_kv, TN)
-        return fold_now(total.astype(BF16).reshape(seqs, stretch, width))
-
-    send, kept_x = sealed(input_partial, *dq_t, *order.take_all(dkv_ts))
+        return *fold_now(total.astype(BF16).reshape(seqs, stretch, width)), *[both[s] for s in each]
+
+    send, kept_x, *dkv_ts = sealed(input_partial, kept_kv, order.take(got_kv), *dq_t)
     got_x = swap(order.mark(send), "tensor", n_tensor, 1)
-    up_job.third(order)
-    kv_job.first(order, [(h1s, dkv_ts)])
+    down_sum = down_job.final(order, [(BLOCK, True)], 2)
+    kv_job.first(order, [([h1] * seqs, dkv_ts)])
     mix_job.second(order)
-    gate_job.third(order)
-
-    back = kept_x + order.take(got_x).astype(F32)
-    streams = jnp.stack(stream)
-    scale_1 = lax.rsqrt(jnp.mean(streams * streams, -1, keepdims=True) + EPSILON)
-    normed_1 = streams * scale_1
-    gains_1 = jnp.sum(back * normed_1, (0, 1))
-    scaled = back * gain_1
-    grad = jnp.stack(d_res) + scale_1 * (scaled - normed_1 * jnp.mean(scaled * normed_1, -1, keepdims=True))
-    grad_part = gather_natural(grad.astype(BF16))
-    hops = [(axis, bit) for axis in ("tensor", "context", "dp") for bit in range((sizes[axis] - 1).bit_length())]
-    gain_sum = jnp.stack([gains_1, sum(gains_2)])
-
-    def hop():
-        axis, bit = hops.pop(0)
-        return order.mark(gain_sum + order.take(swap(gain_sum, axis, sizes[axis], bit)))
-
-    down_sum = down_job.final(order)
-    gain_sum = hop()
-    up_sum = up_job.final(order)
-    gain_sum = hop()
-    kv_job.second(order)
+    up_sum = up_job.final(order, [(BLOCK, False)], 4)
+
+    def input_grad(kept, got, sums_0, sums_1, *parts):
+        back = kept + got.astype(F32)
+        streams, res = jnp.stack(parts[:seqs]), jnp.stack(parts[seqs:])
+        scale = lax.rsqrt(jnp.mean(streams * streams, -1, keepdims=True) + EPSILON)
+        normed = streams * scale
+        grad = res + norm_back(back, normed, scale, gain_1)
+        return grad.astype(BF16), jnp.stack([jnp.sum(back * normed, (0, 1)), sums_0 + sums_1])
+
+    grad_own, gain_sum = sealed(input_grad, kept_x, order.take(got_x), *gains_2, *stream, *d_res)
+    got_grad = spread(order.mark(grad_own))
+    gate_job.third(order, 4)
+    kv_job.second(order, 8)
+
+    def all_sum(total):
+        for axis in ("tensor", "context", "dp"):
+            for bit in range((sizes[axis] - 1).bit_length()):
+                total = total + swap(total, axis, sizes[axis], bit)
+        return total
+
+    gain_sum = order.mark(sealed(all_sum, order.take(gain_sum)))
     mix_job.third(order)
-    grad_tokens = natural(*gather_more(*grad_part), F32)
+    gate_sum = gate_job.final(order, [(BLOCK, False)])
     kv_job.third(order)
-    gain_sum = hop()
-    gate_sum = gate_job.final(order)
-    while hops:
-        gain_sum = hop()
+    grad_tokens = place_all(grad_own, got_grad, F32, 6)
     per = width // blocks
     gain_sum = lax.dynamic_slice_in_dim(gain_sum, (me_c * n_dp + lax.axis_index("dp")) * per, per, 1)
 
     if fast:
-        down_sum = down_sum.T
-        kv_sum = kv_job.final(order)
-        mixed = mix_job.final(order)
-        output_sum, query_sum = mixed[:wide], mixed[wide:].T
-        key_sum, value_sum = kv_sum[:head].T, kv_sum[head:].T
+        key_sum, value_sum = kv_job.final(order, [(head, True), (head, True)])
+        output_sum, query_sum = mix_job.final(order, [(wide, False), (wide, True)])
     else:
 
         def plain(left, right, dim):
@@ -848,6 +885,7 @@
         gate_sum = plain(h2, d_gate, 0)
         up_sum = plain(h2, d_up, 0)
         output_sum = plain([a.T for a in o_t], d_low, 1)
+        h1s = [h1[s * stretch : (s + 1) * stretch] for s in each]
         query_sum = plain(h1s, [a.T for a in dq_t], 0)
         kv_sum = plain(h1s, [a.T for a in dkv_ts], 0)
         key_sum, value_sum = kv_sum[:, :head], kv_sum[:, head:]

time: 582 us -> 551 us (0.947)
  starting transfers between devices: 121 us -> 91.2 us
  waiting for transfers between devices: 144 us -> 119 us
  Pallas kernels: 142 us -> 164 us
  matrix products: 73.3 us -> 81.6 us
  other arithmetic: 62.5 us -> 54.9 us
    ppermute x46 -> x50, starting transfers between devices: 110 us -> 80.4 us  [swap(): return lax.ppermute(x, axis, [(i, i ^ 1 << bit) for i in range(size)])]
    pallas_call x0 -> x10, Pallas kernels: none -> 27.6 us  [the longest x5 14.5 us: add_send(): pl.pallas_call(add_send_kernel, out_shape=[jax.ShapeDtypeStruct(shape, BF...]
    ppermute x46 -> x50, waiting for transfers between devices: 144 us -> 119 us  [swap(): return lax.ppermute(x, axis, [(i, i ^ 1 << bit) for i in range(size)])]
    add x11 -> x6, other arithmetic: 9.66 us -> 0.06 us  [the longest x5 0.05 us: all_sum(): total = total + swap(total, axis, sizes[axis], bit)]
    dot_general x16, matrix products: 73.3 us -> 81.6 us  [dot(): lax.dot_general(left, right, (dims, ((), ())), preferred_element_type=F32)]
    convert_element_type x10 -> x6, other arithmetic: 21.8 us -> 15.7 us  [the longest x2 4.89 us: run(): return (grad.astype(BF16), grad, jnp.sum(back * normed, 0))]
    unnamed x179 -> x123, local copies, waits for them, and re-layouts: 7.81 us -> 12.4 us
  transfers between devices with their start and end apart: 49 -> 53, of which waited for: 25 -> 27; matrix products, arithmetic and copies ran while one was open for 20% -> 22% of each run, Pallas kernels for 21% -> 25%
where the time goes in v3:
time: 551 us; the launch traced here: 543 us
  Pallas kernels  164 us (30%)
  waiting for transfers between devices  119 us (22%)
  starting transfers between devices  91.2 us (17%)
  matrix products  81.6 us (15%)
  other arithmetic  54.9 us (10%)
  local copies, waits for them, and re-layouts  30.3 us (5%)
    ppermute x50, waiting for transfers between devices, swap(): return lax.ppermute(x, axis, [(i, i ^ 1 << bit) for i in range(size)])  119 us
    dot_general x16, matrix products, dot(): lax.dot_general(left, right, (dims, ((), ())), preferred_element_type=F32)  81.6 us
    ppermute x50, starting transfers between devices, swap(): return lax.ppermute(x, axis, [(i, i ^ 1 << bit) for i in range(size)])  80.4 us
    pallas_call x10, Pallas kernels, grad_blocks(): pl.pallas_call(functools.partial(grad_kernel, groups, recv is not None, s...  70.4 us
    pallas_call x2, Pallas kernels, attend_back(): pl.pallas_call(functools.partial(back_kernel, far_count), grid_spec=pltpu...  21 us
    pallas_call x5, Pallas kernels, add_send(): pl.pallas_call(add_send_kernel, out_shape=[jax.ShapeDtypeStruct(shape, BF...  14.5 us
    pallas_call x2, Pallas kernels, attend(): pl.pallas_call(functools.partial(attend_kernel, far_count), grid_spec=plt...  14.2 us
    pallas_call x5, Pallas kernels, add_last(): pl.pallas_call(functools.partial(add_last_kernel, turned), out_shape=[jax...  13 us
  transfers between devices with their start and end apart: 53, of which 27 were waited for; matrix products, arithmetic and copies ran while one was open for 22% of the time, Pallas kernels for 25%

profile of v3, /device:TPU:0, one launch (start us, length us, event | category | flops | bytes accessed | tf_op | source)
XLA Modules:
  0.0 543.3 jit_solution(11713081339873386285)
XLA Ops:
  4.3 8.8 %shard_map.203 = (bf16[1024,2048]{1,0:T(8,128)(2,1)}, bf16[512,1024]{1,0:T(8,128)(2,1)}, bf16[128,1024]{1,0:T(8,128)(2,1)}) custom-call(s32[3]{0:T(128)S(1)} %pad_add_fusion.1.at_ref, bf16[1024,2048]{1,0:T(8,128)(2,1)} %bitcast.117, f32[1,2048]{1,0:T(1,128)} %bitcast.140, bf16[2048,512]{1,0:T(8,128)(2,1)} %wq_ref.1, ...), custom_call_target="tpu_custom_call" | custom-call | flops 1024 | bytes 1024 | tf_op jit(solution)/shard_map/pallas_call | solution.py:70
  13.1 4.9 collective-permute-start.17
  26.9 7.8 %fusion.31 = f32[512,1408]{1,0:T(8,128)} fusion(bf16[1408,2048]{1,0:T(8,128)(2,1)} %param.60, bf16[128,2048]{1,0:T(8,128)(2,1)S(1)} %get-tuple-element.594, bf16[128,2048]{1,0:T(8,128)(2,1)S(1)} %get-tuple-element.595, bf16[128,2048]{1,0:T(8,128)(2,1)S(1)} %get-tuple-element.596, bf16[128,2048]{1,0:T(8,128)(2,1)S(1)} %get-tuple-element.593), kind=kOutput, calls=%fused_computation.147 | convolution fusion | flops 2961178624 | bytes 10747904 | tf_op jit(solution)/shard_map/dot_general | solution.py:31
  36.4 8.6 %fusion.30 = f32[512,1408]{1,0:T(8,128)} fusion(bf16[1408,2048]{1,0:T(8,128)(2,1)} %param.60, bf16[128,2048]{1,0:T(8,128)(2,1)S(1)} %get-tuple-element.590, bf16[128,2048]{1,0:T(8,128)(2,1)S(1)} %get-tuple-element.591, bf16[128,2048]{1,0:T(8,128)(2,1)S(1)} %get-tuple-element.592, bf16[128,2048]{1,0:T(8,128)(2,1)S(1)} %get-tuple-element.589), kind=kOutput, calls=%fused_computation.146 | convolution fusion | flops 2961178624 | bytes 10747904 | tf_op jit(solution)/shard_map/dot_general | solution.py:31
  47.1 7.2 %shard_map.204 = (bf16[8,128,512]{2,1,0:T(8,128)(2,1)}, bf16[512,512]{1,0:T(8,128)(2,1)}, f32[512,512]{1,0:T(8,128)}) custom-call(s32[3]{0:T(128)S(1)} %pad_add_fusion.1.at_ref, bf16[512,1024]{1,0:T(8,128)(2,1)} %get-tuple-element.413.q_ref, s32[2,4,512]{2,1,0:T(4,128)} %pad_add_fusion.seg_ref, bf16[128,1024]{1,0:T(8,128)(2,1)} %get-tuple-element.405.refs_0_, ...), custom_call_target="tpu_custom_call" | custom-call | flops 1024 | bytes 1024 | tf_op jit(solution)/shard_map/pallas_call | solution.py:186
  61.5 6.9 %shard_map.205 = (bf16[8,128,512]{2,1,0:T(8,128)(2,1)}, bf16[512,512]{1,0:T(8,128)(2,1)}, f32[512,512]{1,0:T(8,128)}) custom-call(s32[3]{0:T(128)S(1)} %pad_add_fusion.1.at_ref, bf16[512,1024]{1,0:T(8,128)(2,1)} %get-tuple-element.413.q_ref, s32[2,4,512]{2,1,0:T(4,128)} %pad_add_fusion.seg_ref, bf16[128,1024]{1,0:T(8,128)(2,1)} %get-tuple-element.405.refs_0_, ...), custom_call_target="tpu_custom_call" | custom-call | flops 1024 | bytes 1024 | tf_op jit(solution)/shard_map/pallas_call | solution.py:186
  68.5 5.5 %collective-permute-done.21 = bf16[128,2048]{1,0:T(8,128)(2,1)S(1)} collective-permute-done((bf16[128,2048]{1,0:T(8,128)(2,1)S(1)}, bf16[128,2048]{1,0:T(8,128)(2,1)S(1)}, u32[]{:S(2)}, u32[]{:S(2)}) %collective-permute-start.21) | collective-permute-done | bytes 524320 | tf_op jit(solution)/shard_map/ppermute | solution.py:594
  84.1 9.1 %collective-permute-done.23 = bf16[128,2048]{1,0:T(8,128)(2,1)S(1)} collective-permute-done((bf16[128,2048]{1,0:T(8,128)(2,1)S(1)}, bf16[128,2048]{1,0:T(8,128)(2,1)S(1)}, u32[]{:S(2)}, u32[]{:S(2)}) %collective-permute-start.23) | collective-permute-done | bytes 524320 | tf_op jit(solution)/shard_map/ppermute | solution.py:594
  97.6 10.8 %conditional.19 = (bf16[512,1408]{1,0:T(8,128)(2,1)S(1)}, bf16[512,1408]{1,0:T(8,128)(2,1)S(1)}, bf16[512,1408]{1,0:T(8,128)(2,1)S(1)}) conditional(s32[]{:T(128)} %convert_element_type.187, () %tuple.222, (bf16[512,2048]{1,0:T(8,128)(2,1)S(1)}, bf16[2048,1408]{1,0:T(8,128)(2,1)}, bf16[2048,1408]{1,0:T(8,128)(2,1)}, f32[512,1408]{1,0:T(8,128)S(1)}) %tuple.404), branch_computations={%region_5.6_spmd, %region_6.7_spmd} | conditional | flops 5917114368 | bytes 51773492 | solution.py:523
  97.6 6.1 %fusion.37 = f32[512,1408]{1,0:T(8,128)S(1)} fusion(bf16[512,2048]{1,0:T(8,128)(2,1)S(1)} %get-tuple-element.175, bf16[2048,1408]{1,0:T(8,128)(2,1)} %get-tuple-element.177), kind=kOutput, calls=%fused_computation.151 | convolution fusion | flops 2952790016 | bytes 10747904 | tf_op jit(solution)/shard_map/cond/branch_1_fun/dot_general | solution.py:31
  114.2 12.3 %conditional.20 = (bf16[1,128,2048]{2,1,0:T(8,128)(2,1)}, f32[128,2048]{1,0:T(8,128)}) conditional(s32[]{:T(128)} %convert_element_type.187, () %tuple.230, (bf16[512,1408]{1,0:T(8,128)(2,1)S(1)}, bf16[2048,1408]{1,0:T(8,128)(2,1)S(1)}, bf16[512,1408]{1,0:T(8,128)(2,1)S(1)}, bf16[2048,1408]{1,0:T(8,128)(2,1)}) %tuple.403), branch_computations={%region_8.9_spmd, %region_9.10_spmd} | conditional | flops 5909250048 | bytes 61603924 | solution.py:523
  126.5 7.9 %conditional.21 = (bf16[512,2048]{1,0:T(8,128)(2,1)}) conditional(s32[]{:T(128)} %convert_element_type.187, () %tuple.229, (bf16[512,1408]{1,0:T(8,128)(2,1)}, bf16[1408,2048]{1,0:T(8,128)(2,1)}) %tuple.387), branch_computations={%region_10.11_spmd, %region_11.12_spmd} | conditional | flops 2953838592 | bytes 9306120 | solution.py:523
  126.5 7.9 %convolution_convert_fusion = bf16[512,2048]{1,0:T(8,128)(2,1)} fusion(bf16[512,1408]{1,0:T(8,128)(2,1)} %get-tuple-element.183, bf16[1408,2048]{1,0:T(8,128)(2,1)} %get-tuple-element.184), kind=kOutput, calls=%fused_computation.9 | convolution fusion | flops 2953838592 | bytes 9306112 | tf_op jit(solution)/shard_map/cond/branch_1_fun/dot_general | solution.py:31
  147.7 7.8 %collective-permute-done.28 = bf16[128,2048]{1,0:T(8,128)(2,1)S(1)} collective-permute-done((bf16[128,2048]{1,0:T(8,128)(2,1)}, bf16[128,2048]{1,0:T(8,128)(2,1)S(1)}, u32[]{:S(2)}, u32[]{:S(2)}) %collective-permute-start.28) | collective-permute-done | bytes 524320 | tf_op jit(solution)/shard_map/ppermute | solution.py:594
  162.3 13.4 %conditional.23 = (bf16[512,1408]{1,0:T(8,128)(2,1)}, bf16[512,1408]{1,0:T(8,128)(2,1)}, bf16[512,1408]{1,0:T(8,128)(2,1)}) conditional(s32[]{:T(128)} %convert_element_type.187, () %tuple.244, (bf16[512,2048]{1,0:T(8,128)(2,1)}, bf16[2048,1408]{1,0:T(8,128)(2,1)}, bf16[2048,1408]{1,0:T(8,128)(2,1)}, f32[512,1408]{1,0:T(8,128)}) %tuple.246), branch_computations={%region_16.17_spmd, %region_17.18_spmd} | conditional | flops 5917114368 | bytes 71696488 | solution.py:523
  162.3 7.3 %fusion.39 = f32[512,1408]{1,0:T(8,128)S(1)} fusion(bf16[512,2048]{1,0:T(8,128)(2,1)} %get-tuple-element.193, bf16[2048,1408]{1,0:T(8,128)(2,1)} %get-tuple-element.195), kind=kOutput, calls=%fused_computation.153 | convolution fusion | flops 2952790016 | bytes 10747904 | tf_op jit(solution)/shard_map/cond/branch_1_fun/dot_general | solution.py:31
  169.6 6.1 %multiply_convert_fusion.3 = (bf16[512,1408]{1,0:T(8,128)(2,1)}, bf16[512,1408]{1,0:T(8,128)(2,1)}, bf16[512,1408]{1,0:T(8,128)(2,1)}) fusion(f32[512,1408]{1,0:T(8,128)S(1)} %copy-done.73, f32[512,1408]{1,0:T(8,128)S(1)} %fusion.39, bf16[512,2048]{1,0:T(8,128)(2,1)S(1)} %copy-done.1, bf16[2048,1408]{1,0:T(8,128)(2,1)S(1)} %copy-done.70), kind=kOutput, calls=%fused_computation.19 | convolution fusion | flops 2964324352 | bytes 17956864 | tf_op jit(solution)/shard_map/cond/branch_1_fun/dot_general | solution.py:31
  175.7 7.8 %shard_map.206 = bf16[4,256,1408]{2,1,0:T(8,128)(2,1)} custom-call(s32[4]{0:T(128)} %add_add_fusion.table_ref, bf16[512,1408]{1,0:T(8,128)(2,1)} %copy-done.15, bf16[512,2048]{1,0:T(8,128)(2,1)} %get-tuple-element.436.refs_1_.refs_2_, bf16[512,2048]{1,0:T(8,128)(2,1)} %get-tuple-element.436.refs_1_.refs_2_, bf16[512,1408]{1,0:T(8,128)(2,1)} %get-tuple-element.452.refs_3_, ...), custom_call_target="tpu_custom_call" | custom-call | flops 1024 | bytes 1024 | tf_op jit(solution)/shard_map/pallas_call | solution.py:457
  186.0 16.3 %conditional.24 = (bf16[1,128,2048]{2,1,0:T(8,128)(2,1)}, f32[128,2048]{1,0:T(8,128)}) conditional(s32[]{:T(128)} %convert_element_type.187, () %tuple.243, (bf16[512,1408]{1,0:T(8,128)(2,1)}, bf16[2048,1408]{1,0:T(8,128)(2,1)}, bf16[512,1408]{1,0:T(8,128)(2,1)}, bf16[2048,1408]{1,0:T(8,128)(2,1)}) %tuple.249), branch_computations={%region_18.19_spmd, %region_19.20_spmd} | conditional | flops 5909250048 | bytes 61603924 | solution.py:523
  186.0 6.0 %fusion.40 = f32[512,2048]{1,0:T(8,128)S(1)} fusion(bf16[512,1408]{1,0:T(8,128)(2,1)} %get-tuple-element.197, bf16[2048,1408]{1,0:T(8,128)(2,1)} %get-tuple-element.198), kind=kOutput, calls=%fused_computation.154 | convolution fusion | flops 2952790016 | bytes 11403264 | tf_op jit(solution)/shard_map/cond/branch_1_fun/dot_general | solution.py:31
  192.0 5.0 fusion.4
  203.9 9.9 %conditional.25 = ((bf16[512,512]{1,0:T(8,128)(2,1)}, bf16[512,2048]{1,0:T(8,128)(2,1)})) conditional(s32[]{:T(128)} %convert_element_type.187, () %tuple.237, (bf16[128,2048]{1,0:T(8,128)(2,1)}, bf16[128,2048]{1,0:T(8,128)(2,1)}, bf16[512,2048]{1,0:T(8,128)(2,1)}) %tuple.251), branch_computations={%region_20.21_spmd, %region_21.22_spmd} | conditional | flops 1024 | bytes 8389776 | solution.py:523
  213.7 7.3 %shard_map.207 = bf16[4,256,1408]{2,1,0:T(8,128)(2,1)} custom-call(s32[4]{0:T(128)} %add_add_fusion.1.table_ref, bf16[512,1408]{1,0:T(8,128)(2,1)S(1)} %get-tuple-element.425.refs_0_, bf16[512,2048]{1,0:T(8,128)(2,1)S(1)} %pad_maximum_fusion.7.refs_1_.refs_2_, bf16[512,2048]{1,0:T(8,128)(2,1)S(1)} %pad_maximum_fusion.7.refs_1_.refs_2_, ...), custom_call_target="tpu_custom_call" | custom-call | flops 1024 | bytes 1024 | tf_op jit(solution)/shard_map/pallas_call | solution.py:457
  227.6 7.8 %shard_map.208 = bf16[4,256,1408]{2,1,0:T(8,128)(2,1)} custom-call(s32[4]{0:T(128)} %add_add_fusion.table_ref, bf16[512,1408]{1,0:T(8,128)(2,1)} %copy-done.16, bf16[512,2048]{1,0:T(8,128)(2,1)S(1)} %pad_maximum_fusion.7.refs_1_.refs_2_, bf16[512,2048]{1,0:T(8,128)(2,1)S(1)} %pad_maximum_fusion.7.refs_1_.refs_2_, ...), custom_call_target="tpu_custom_call" | custom-call | flops 13800001536 | bytes 1024 | tf_op jit(solution)/shard_map/pallas_call | solution.py:457
  237.0 7.8 %conditional.27 = (bf16[512,2048]{1,0:T(8,128)(2,1)}) conditional(s32[]{:T(128)} %convert_element_type.187, () %tuple.235, (bf16[512,1408]{1,0:T(8,128)(2,1)}, bf16[1408,2048]{1,0:T(8,128)(2,1)}) %tuple.257), branch_computations={%region_26.27_spmd, %region_27.28_spmd} | conditional | flops 2953838592 | bytes 9306120 | solution.py:523
  237.0 7.8 %convolution_convert_fusion.1 = bf16[512,2048]{1,0:T(8,128)(2,1)} fusion(bf16[512,1408]{1,0:T(8,128)(2,1)} %get-tuple-element.214, bf16[1408,2048]{1,0:T(8,128)(2,1)} %get-tuple-element.215), kind=kOutput, calls=%fused_computation.37 | convolution fusion | flops 2953838592 | bytes 9306112 | tf_op jit(solution)/shard_map/cond/branch_1_fun/dot_general | solution.py:31
  244.8 9.5 %conditional.28 = (bf16[2,128,2048]{2,1,0:T(8,128)(2,1)}, f32[2,128,2048]{2,1,0:T(8,128)}) conditional(s32[]{:T(128)} %convert_element_type.187, () %tuple.228, (bf16[512,2048]{1,0:T(8,128)(2,1)}, bf16[512,2048]{1,0:T(8,128)(2,1)}) %tuple.258), branch_computations={%region_28.29_spmd, %region_29.30_spmd} | conditional | flops 8388608 | bytes 48234608 | solution.py:523
  255.9 10.5 %shard_map.209 = (bf16[512,512]{1,0:T(8,128)(2,1)}, bf16[2,128,512]{2,1,0:T(8,128)(2,1)}, bf16[2,128,512]{2,1,0:T(8,128)(2,1)}) custom-call(s32[3]{0:T(128)S(1)} %pad_add_fusion.1.at_ref, bf16[8,128,512]{2,1,0:T(8,128)(2,1)} %get-tuple-element.454.qa_ref, bf16[512,512]{1,0:T(8,128)(2,1)} %get-tuple-element.456.do_ref, ...), custom_call_target="tpu_custom_call" | custom-call | flops 1024 | bytes 1024 | tf_op jit(solution)/shard_map/pallas_call | solution.py:292
  266.5 9.8 %conditional.29 = ((bf16[512,512]{1,0:T(8,128)(2,1)}, bf16[512,2048]{1,0:T(8,128)(2,1)})) conditional(s32[]{:T(128)} %convert_element_type.187, () %tuple.259, (bf16[128,2048]{1,0:T(8,128)(2,1)}, bf16[128,2048]{1,0:T(8,128)(2,1)}, bf16[512,2048]{1,0:T(8,128)(2,1)}) %tuple.262), branch_computations={%region_30.31_spmd, %region_31.32_spmd} | conditional | flops 1024 | bytes 8389776 | solution.py:523
  276.3 9.5 %shard_map.210 = (bf16[2,256,1408]{2,1,0:T(8,128)(2,1)}, bf16[2,256,1408]{2,1,0:T(8,128)(2,1)}) custom-call(s32[4]{0:T(128)} %add_add_fusion.3.table_ref, bf16[512,1408]{1,0:T(8,128)(2,1)} %copy-done.15, bf16[512,2048]{1,0:T(8,128)(2,1)} %get-tuple-element.436.refs_1_.refs_2_, bf16[512,2048]{1,0:T(8,128)(2,1)} %get-tuple-element.436.refs_1_.refs_2_, ...), custom_call_target="tpu_custom_call" | custom-call | flops 6900000768 | bytes 1024 | tf_op jit(solution)/shard_map/pallas_call | solution.py:457
  285.8 6.0 %collective-permute-start.38 = (bf16[2,256,1408]{2,1,0:T(8,128)(2,1)}, bf16[2,256,1408]{2,1,0:T(8,128)(2,1)}, u32[]{:S(2)}, u32[]{:S(2)}) collective-permute-start(bf16[2,256,1408]{2,1,0:T(8,128)(2,1)} %get-tuple-element.462), channel_id=1, source_target_pairs={{0,2},{2,0},{4,6},{6,4},{1,3},{3,1},{5,7},{7,5},{8,10},{10,8},{12,... | collective-permute-start | bytes 4325384 | tf_op jit(solution)/shard_map/ppermute | solution.py:594
  292.5 8.7 %shard_map.211 = (bf16[2,256,1408]{2,1,0:T(8,128)(2,1)}, bf16[2,256,1408]{2,1,0:T(8,128)(2,1)}) custom-call(s32[4]{0:T(128)} %add_add_fusion.2.table_ref, bf16[512,1408]{1,0:T(8,128)(2,1)S(1)} %get-tuple-element.425.refs_0_, bf16[512,2048]{1,0:T(8,128)(2,1)S(1)} %pad_maximum_fusion.7.refs_1_.refs_2_, ...), custom_call_target="tpu_custom_call" | custom-call | flops 1024 | bytes 1024 | tf_op jit(solution)/shard_map/pallas_call | solution.py:457
  306.7 10.5 %shard_map.212 = (bf16[512,512]{1,0:T(8,128)(2,1)}, bf16[2,128,512]{2,1,0:T(8,128)(2,1)}, bf16[2,128,512]{2,1,0:T(8,128)(2,1)}) custom-call(s32[3]{0:T(128)S(1)} %pad_add_fusion.1.at_ref, bf16[8,128,512]{2,1,0:T(8,128)(2,1)} %get-tuple-element.467.qa_ref, bf16[512,512]{1,0:T(8,128)(2,1)} %get-tuple-element.468.do_ref, ...), custom_call_target="tpu_custom_call" | custom-call | flops 1024 | bytes 1024 | tf_op jit(solution)/shard_map/pallas_call | solution.py:292
  319.5 5.7 %collective-permute-start.36 = (bf16[2,2,128,512]{3,2,1,0:T(8,128)(2,1)}, bf16[2,2,128,512]{3,2,1,0:T(8,128)(2,1)}, u32[]{:S(2)}, u32[]{:S(2)}) collective-permute-start(bf16[2,2,128,512]{3,2,1,0:T(8,128)(2,1)} %get-tuple-element.473), channel_id=1, source_target_pairs={{0,2},{2,0},{4,6},{6,4},{1,3},{3,1},{5,7},{7,5},{8,10},{10,8},{12,... | collective-permute-start | bytes 1572872 | tf_op jit(solution)/shard_map/ppermute | solution.py:594
  325.1 5.3 collective-permute-done.35.refs_1_
  330.5 5.8 %conditional.32 = (bf16[2,128,2048]{2,1,0:T(8,128)(2,1)}, bf16[2,128,2048]{2,1,0:T(8,128)(2,1)}) conditional(s32[]{:T(128)} %convert_element_type.187, () %tuple.267, (bf16[2,128,2048]{2,1,0:T(8,128)(2,1)S(1)}, bf16[2,128,2048]{2,1,0:T(8,128)(2,1)}) %tuple.272), branch_computations={%region_36.37_spmd, %region_37.38_spmd} | conditional | bytes 8388704 | solution.py:523
  340.6 6.2 %shard_map.214 = bf16[4,1024,256]{2,1,0:T(8,128)(2,1)} custom-call(s32[4]{0:T(128)} %add_add_fusion.table_ref, bf16[512,512]{1,0:T(8,128)(2,1)} %get-tuple-element.411.refs_0_, bf16[512,2048]{1,0:T(8,128)(2,1)S(1)} %copy-done.2, bf16[512,2048]{1,0:T(8,128)(2,1)S(1)} %copy-done.2, bf16[512,512]{1,0:T(8,128)(2,1)} %get-tuple-element.416.refs_3_, ...), custom_call_target="tpu_custom_call" | custom-call | flops 1024 | bytes 1024 | tf_op jit(solution)/shard_map/pallas_call | solution.py:457
  349.6 29.2 %collective-permute-start.40 = (bf16[2,128,512]{2,1,0:T(8,128)(2,1)}, bf16[2,128,512]{2,1,0:T(8,128)(2,1)S(1)}, u32[]{:S(2)}, u32[]{:S(2)}) collective-permute-start(bf16[2,128,512]{2,1,0:T(8,128)(2,1)} %get-tuple-element.489), channel_id=1, source_target_pairs={{0,4},{2,6},{4,0},{6,2},{1,5},{3,7},{5,1},{7,3},{8,12},{10,14},{12... | collective-permute-start | bytes 786440 | tf_op jit(solution)/shard_map/ppermute | solution.py:594
  378.8 8.7 %shard_map.215 = (bf16[2,256,1408]{2,1,0:T(8,128)(2,1)}, bf16[2,256,1408]{2,1,0:T(8,128)(2,1)}) custom-call(s32[4]{0:T(128)} %add_add_fusion.3.table_ref, bf16[512,1408]{1,0:T(8,128)(2,1)S(1)} %copy-done.17, bf16[512,2048]{1,0:T(8,128)(2,1)S(1)} %pad_maximum_fusion.7.refs_1_.refs_2_, bf16[512,2048]{1,0:T(8,128)(2,1)S(1)} %pad_maximum_fusion.7.refs_1_.refs_2_, ...), custom_call_target="tpu_custom_call" | custom-call | flops 1024 | bytes 1024 | tf_op jit(solution)/shard_map/pallas_call | solution.py:457
  397.3 13.8 %conditional.34 = (bf16[2,128,2048]{2,1,0:T(8,128)(2,1)}, f32[2,128,2048]{2,1,0:T(8,128)S(1)}, bf16[128,512]{1,0:T(8,128)(2,1)S(1)}, bf16[128,512]{1,0:T(8,128)(2,1)}) conditional(s32[]{:T(128)} %convert_element_type.187, () %tuple.281, (bf16[512,512]{1,0:T(8,128)(2,1)S(1)}, bf16[512,512]{1,0:T(8,128)(2,1)S(1)}, bf16[2048,512]{1,0:T(8,128)(2,1)S(1)}, ...), branch_computations={%region_40.41_spmd, %region_41.42_spmd} | conditional | flops 2694317056 | bytes 54264988 | solution.py:523
  414.6 20.8 %collective-permute-done.41.got_ref = bf16[256,1408]{1,0:T(8,128)(2,1)} collective-permute-done((bf16[256,1408]{1,0:T(8,128)(2,1)}, bf16[256,1408]{1,0:T(8,128)(2,1)}, u32[]{:S(2)}, u32[]{:S(2)}) %collective-permute-start.41) | collective-permute-done | bytes 720928 | tf_op jit(solution)/shard_map/ppermute | solution.py:594
  443.8 7.3 %shard_map.220 = (bf16[2,1024,256]{2,1,0:T(8,128)(2,1)}, bf16[2,1024,256]{2,1,0:T(8,128)(2,1)}) custom-call(s32[4]{0:T(128)} %add_add_fusion.3.table_ref, bf16[512,512]{1,0:T(8,128)(2,1)} %get-tuple-element.411.refs_0_, bf16[512,2048]{1,0:T(8,128)(2,1)S(1)} %copy-done.3, bf16[512,2048]{1,0:T(8,128)(2,1)S(1)} %copy-done.3, ...), custom_call_target="tpu_custom_call" | custom-call | flops 1024 | bytes 1024 | tf_op jit(solution)/shard_map/pallas_call | solution.py:457
  459.2 5.0 conditional.35
  474.1 32.2 %conditional.36 = (f32[2,2048]{1,0:T(2,128)S(1)}) conditional(s32[]{:T(128)} %convert_element_type.187, () %tuple.293, f32[2,2048]{1,0:T(2,128)S(1)} %get-tuple-element.523), branch_computations={%region_47.48_spmd, %region_48.49_spmd} | conditional | flops 20480 | bytes 573648 | solution.py:523
  476.4 12.3 %collective-permute-done.7 = f32[2,2048]{1,0:T(2,128)S(1)} collective-permute-done((f32[2,2048]{1,0:T(2,128)S(1)}, f32[2,2048]{1,0:T(2,128)S(1)}, u32[]{:S(2)}, u32[]{:S(2)}) %collective-permute-start.7) | collective-permute-done | bytes 16416 | tf_op jit(solution)/shard_map/cond/branch_1_fun/ppermute | solution.py:594
  496.1 6.3 %collective-permute-done.9 = f32[2,2048]{1,0:T(2,128)S(1)} collective-permute-done((f32[2,2048]{1,0:T(2,128)S(1)}, f32[2,2048]{1,0:T(2,128)S(1)}, u32[]{:S(2)}, u32[]{:S(2)}) %collective-permute-start.9) | collective-permute-done | bytes 16416 | tf_op jit(solution)/shard_map/cond/branch_1_fun/ppermute | solution.py:594
  518.6 5.8 %conditional.37 = (bf16[2,128,2048]{2,1,0:T(8,128)(2,1)}, bf16[2,128,2048]{2,1,0:T(8,128)(2,1)}) conditional(s32[]{:T(128)} %convert_element_type.187, () %tuple.290, (bf16[2,128,2048]{2,1,0:T(8,128)(2,1)}, bf16[2,128,2048]{2,1,0:T(8,128)(2,1)S(1)}) %tuple.299), branch_computations={%region_49.50_spmd, %region_50.51_spmd} | conditional | bytes 8388704 | solution.py:523
  524.4 5.6 %shard_map.227 = f32[2,512,2048]{2,1,0:T(8,128)} custom-call(s32[3]{0:T(128)S(1)} %pad_add_fusion.1.at_ref, bf16[2,128,2048]{2,1,0:T(8,128)(2,1)} %get-tuple-element.513.refs_0_, bf16[2,128,2048]{2,1,0:T(8,128)(2,1)S(1)} %collective-permute-done.45.refs_1_, bf16[2,128,2048]{2,1,0:T(8,128)(2,1)} %get-tuple-element.530.refs_2_, ...), custom_call_target="tpu_custom_call" | custom-call | flops 6900000768 | bytes 1024 | tf_op jit(solution)/shard_map/pallas_call | solution.py:582
  (357 shorter events, 269.8 us)
Async XLA Ops:
  13.1 32.5 %collective-permute-start.17 = (bf16[128,1024]{1,0:T(8,128)(2,1)}, bf16[128,1024]{1,0:T(8,128)(2,1)S(1)}, u32[]{:S(2)}, u32[]{:S(2)}) collective-permute-start(bf16[128,1024]{1,0:T(8,128)(2,1)} %get-tuple-element.405.refs_0_), channel_id=1, source_target_pairs={{0,2},{2,4},{4,6},{1,3},{3,5},{5,7},{8,10},{10,12},{12,14},{9,11},... | collective-permute-start | bytes 786440 | tf_op jit(solution)/shard_map/ppermute | solution.py:641
  18.1 27.6 %collective-permute-start.18 = (bf16[128,1024]{1,0:T(8,128)(2,1)}, bf16[128,1024]{1,0:T(8,128)(2,1)S(1)}, u32[]{:S(2)}, u32[]{:S(2)}) collective-permute-start(bf16[128,1024]{1,0:T(8,128)(2,1)} %get-tuple-element.405.refs_0_), channel_id=1, source_target_pairs={{0,4},{2,6},{1,5},{3,7},{8,12},{10,14},{9,13},{11,15},{16,20},{18,... | collective-permute-start | bytes 786440 | tf_op jit(solution)/shard_map/ppermute | solution.py:641
  22.6 23.1 %collective-permute-start.19 = (bf16[128,1024]{1,0:T(8,128)(2,1)}, bf16[128,1024]{1,0:T(8,128)(2,1)S(1)}, u32[]{:S(2)}, u32[]{:S(2)}) collective-permute-start(bf16[128,1024]{1,0:T(8,128)(2,1)} %get-tuple-element.405.refs_0_), channel_id=1, source_target_pairs={{0,6},{1,7},{8,14},{9,15},{16,22},{17,23},{24,30},{25,31}} | collective-permute-start | bytes 786440 | tf_op jit(solution)/shard_map/ppermute | solution.py:641
  56.8 2.7 collective-permute-start.20
  59.9 14.0 %collective-permute-start.21 = (bf16[128,2048]{1,0:T(8,128)(2,1)S(1)}, bf16[128,2048]{1,0:T(8,128)(2,1)S(1)}, u32[]{:S(2)}, u32[]{:S(2)}) collective-permute-start(bf16[128,2048]{1,0:T(8,128)(2,1)S(1)} %slice.174), channel_id=1, source_target_pairs={{0,16},{8,24},{16,0},{24,8},{1,17},{9,25},{17,1},{25,9},{2,18},{10... | collective-permute-start | bytes 1572872 | tf_op jit(solution)/shard_map/ppermute | solution.py:594
  78.8 2.7 collective-permute-start.22
  78.9 14.3 %collective-permute-start.23 = (bf16[128,2048]{1,0:T(8,128)(2,1)S(1)}, bf16[128,2048]{1,0:T(8,128)(2,1)S(1)}, u32[]{:S(2)}, u32[]{:S(2)}) collective-permute-start(bf16[128,2048]{1,0:T(8,128)(2,1)S(1)} %get-tuple-element.569), channel_id=1, source_target_pairs={{0,16},{8,24},{16,0},{24,8},{1,17},{9,25},{17,1},{25,9},{2,18},{10... | collective-permute-start | bytes 1572872 | tf_op jit(solution)/shard_map/ppermute | solution.py:594
  93.3 2.9 collective-permute-start.24
  93.4 15.0 %collective-permute-start.25 = (bf16[128,2048]{1,0:T(8,128)(2,1)}, bf16[128,2048]{1,0:T(8,128)(2,1)}, u32[]{:S(2)}, u32[]{:S(2)}) collective-permute-start(bf16[128,2048]{1,0:T(8,128)(2,1)} %slice.173), channel_id=1, source_target_pairs={{0,16},{8,24},{16,0},{24,8},{1,17},{9,25},{17,1},{25,9},{2,18},{10... | collective-permute-start | bytes 1572872 | tf_op jit(solution)/shard_map/ppermute | solution.py:594
  112.7 21.7 %collective-permute-start.26 = (bf16[128,2048]{1,0:T(8,128)(2,1)}, bf16[128,2048]{1,0:T(8,128)(2,1)}, u32[]{:S(2)}, u32[]{:S(2)}) collective-permute-start(bf16[128,2048]{1,0:T(8,128)(2,1)} %get-tuple-element.565), channel_id=1, source_target_pairs={{0,16},{8,24},{16,0},{24,8},{1,17},{9,25},{17,1},{25,9},{2,18},{10... | collective-permute-start | bytes 1572872 | tf_op jit(solution)/shard_map/ppermute | solution.py:594
  121.5 2.7 collective-permute-start.14
  136.6 7.9 %collective-permute-start.27 = (bf16[256,2048]{1,0:T(8,128)(2,1)}, bf16[256,2048]{1,0:T(8,128)(2,1)}, u32[]{:S(2)}, u32[]{:S(2)}) collective-permute-start(bf16[256,2048]{1,0:T(8,128)(2,1)} %pad_maximum_fusion.10), channel_id=1, source_target_pairs={{0,8},{8,0},{16,24},{24,16},{1,9},{9,1},{17,25},{25,17},{2,10},{10... | collective-permute-start | bytes 3145736 | tf_op jit(solution)/shard_map/ppermute | solution.py:594
  141.1 14.4 %collective-permute-start.28 = (bf16[128,2048]{1,0:T(8,128)(2,1)}, bf16[128,2048]{1,0:T(8,128)(2,1)S(1)}, u32[]{:S(2)}, u32[]{:S(2)}) collective-permute-start(bf16[128,2048]{1,0:T(8,128)(2,1)} %bitcast.43), channel_id=1, source_target_pairs={{0,16},{8,24},{16,0},{24,8},{1,17},{9,25},{17,1},{25,9},{2,18},{10... | collective-permute-start | bytes 1572872 | tf_op jit(solution)/shard_map/ppermute | solution.py:594
  183.5 92.8 %collective-permute-start.32 = (bf16[4,256,1408]{2,1,0:T(8,128)(2,1)}, bf16[4,256,1408]{2,1,0:T(8,128)(2,1)}, u32[]{:S(2)}, u32[]{:S(2)}) collective-permute-start(bf16[4,256,1408]{2,1,0:T(8,128)(2,1)} %shard_map.206), channel_id=1, source_target_pairs={{0,1},{1,0},{2,3},{3,2},{4,5},{5,4},{6,7},{7,6},{8,9},{9,8},{10,11... | collective-permute-start | bytes 8650760 | tf_op jit(solution)/shard_map/ppermute | solution.py:594
  185.0 18.9 %collective-permute-start.29 = (bf16[128,2048]{1,0:T(8,128)(2,1)}, bf16[128,2048]{1,0:T(8,128)(2,1)}, u32[]{:S(2)}, u32[]{:S(2)}) collective-permute-start(bf16[128,2048]{1,0:T(8,128)(2,1)} %get-tuple-element.433), channel_id=1, source_target_pairs={{0,16},{8,24},{16,0},{24,8},{1,17},{9,25},{17,1},{25,9},{2,18},{10... | collective-permute-start | bytes 1572872 | tf_op jit(solution)/shard_map/ppermute | solution.py:594
  197.2 2.7 collective-permute-start.15
  202.2 20.5 %collective-permute-start.30 = (bf16[128,2048]{1,0:T(8,128)(2,1)}, bf16[128,2048]{1,0:T(8,128)(2,1)}, u32[]{:S(2)}, u32[]{:S(2)}) collective-permute-start(bf16[128,2048]{1,0:T(8,128)(2,1)} %bitcast.45), channel_id=1, source_target_pairs={{0,16},{8,24},{16,0},{24,8},{1,17},{9,25},{17,1},{25,9},{2,18},{10... | collective-permute-start | bytes 1572872 | tf_op jit(solution)/shard_map/ppermute | solution.py:594
  221.0 71.5 %collective-permute-start.33 = (bf16[4,256,1408]{2,1,0:T(8,128)(2,1)}, bf16[4,256,1408]{2,1,0:T(8,128)(2,1)}, u32[]{:S(2)}, u32[]{:S(2)}) collective-permute-start(bf16[4,256,1408]{2,1,0:T(8,128)(2,1)} %shard_map.207), channel_id=1, source_target_pairs={{0,2},{2,0},{4,6},{6,4},{1,3},{3,1},{5,7},{7,5},{8,10},{10,8},{12,... | collective-permute-start | bytes 8650760 | tf_op jit(solution)/shard_map/ppermute | solution.py:594
  235.4 143.4 %collective-permute-start.37 = (bf16[4,256,1408]{2,1,0:T(8,128)(2,1)}, bf16[4,256,1408]{2,1,0:T(8,128)(2,1)}, u32[]{:S(2)}, u32[]{:S(2)}) collective-permute-start(bf16[4,256,1408]{2,1,0:T(8,128)(2,1)} %shard_map.208), channel_id=1, source_target_pairs={{0,1},{1,0},{2,3},{3,2},{4,5},{5,4},{6,7},{7,6},{8,9},{9,8},{10,11... | collective-permute-start | bytes 8650760 | tf_op jit(solution)/shard_map/ppermute | solution.py:594
  236.0 30.5 %collective-permute-start.31 = (bf16[128,2048]{1,0:T(8,128)(2,1)}, bf16[128,2048]{1,0:T(8,128)(2,1)}, u32[]{:S(2)}, u32[]{:S(2)}) collective-permute-start(bf16[128,2048]{1,0:T(8,128)(2,1)} %get-tuple-element.449), channel_id=1, source_target_pairs={{0,16},{8,24},{16,0},{24,8},{1,17},{9,25},{17,1},{25,9},{2,18},{10... | collective-permute-start | bytes 1572872 | tf_op jit(solution)/shard_map/ppermute | solution.py:594
  246.6 4.2 collective-permute-start.13
  254.3 48.3 %collective-permute-start.34 = (bf16[2,128,2048]{2,1,0:T(8,128)(2,1)}, bf16[2,128,2048]{2,1,0:T(8,128)(2,1)}, u32[]{:S(2)}, u32[]{:S(2)}) collective-permute-start(bf16[2,128,2048]{2,1,0:T(8,128)(2,1)} %get-tuple-element.455), channel_id=1, source_target_pairs={{0,16},{8,24},{16,0},{24,8},{1,17},{9,25},{17,1},{25,9},{2,18},{10... | collective-permute-start | bytes 3145736 | tf_op jit(solution)/shard_map/ppermute | solution.py:594
  285.8 101.7 %collective-permute-start.38 = (bf16[2,256,1408]{2,1,0:T(8,128)(2,1)}, bf16[2,256,1408]{2,1,0:T(8,128)(2,1)}, u32[]{:S(2)}, u32[]{:S(2)}) collective-permute-start(bf16[2,256,1408]{2,1,0:T(8,128)(2,1)} %get-tuple-element.462), channel_id=1, source_target_pairs={{0,2},{2,0},{4,6},{6,4},{1,3},{3,1},{5,7},{7,5},{8,10},{10,8},{12,... | collective-permute-start | bytes 4325384 | tf_op jit(solution)/shard_map/ppermute | solution.py:594
  301.1 89.8 %collective-permute-start.39 = (bf16[2,256,1408]{2,1,0:T(8,128)(2,1)}, bf16[2,256,1408]{2,1,0:T(8,128)(2,1)}, u32[]{:S(2)}, u32[]{:S(2)}) collective-permute-start(bf16[2,256,1408]{2,1,0:T(8,128)(2,1)} %get-tuple-element.464), channel_id=1, source_target_pairs={{0,1},{1,0},{2,3},{3,2},{4,5},{5,4},{6,7},{7,6},{8,9},{9,8},{10,11... | collective-permute-start | bytes 4325384 | tf_op jit(solution)/shard_map/ppermute | solution.py:594
  305.7 24.8 %collective-permute-start.35 = (bf16[2,128,2048]{2,1,0:T(8,128)(2,1)S(1)}, bf16[2,128,2048]{2,1,0:T(8,128)(2,1)}, u32[]{:S(2)}, u32[]{:S(2)}) collective-permute-start(bf16[2,128,2048]{2,1,0:T(8,128)(2,1)S(1)} %get-tuple-element.684.refs_0_), channel_id=1, source_target_pairs={{0,16},{8,24},{16,0},{24,8},{1,17},{9,25},{17,1},{25,9},{2,18},{10... | collective-permute-start | bytes 3145736 | tf_op jit(solution)/shard_map/ppermute | solution.py:594
  319.5 27.9 %collective-permute-start.36 = (bf16[2,2,128,512]{3,2,1,0:T(8,128)(2,1)}, bf16[2,2,128,512]{3,2,1,0:T(8,128)(2,1)}, u32[]{:S(2)}, u32[]{:S(2)}) collective-permute-start(bf16[2,2,128,512]{3,2,1,0:T(8,128)(2,1)} %get-tuple-element.473), channel_id=1, source_target_pairs={{0,2},{2,0},{4,6},{6,4},{1,3},{3,1},{5,7},{7,5},{8,10},{10,8},{12,... | collective-permute-start | bytes 1572872 | tf_op jit(solution)/shard_map/ppermute | solution.py:594
  330.5 2.8 collective-permute-start.4
  333.3 3.0 collective-permute-start.5
  346.8 97.0 %collective-permute-start.42 = (bf16[4,1024,256]{2,1,0:T(8,128)(2,1)}, bf16[4,1024,256]{2,1,0:T(8,128)(2,1)}, u32[]{:S(2)}, u32[]{:S(2)}) collective-permute-start(bf16[4,1024,256]{2,1,0:T(8,128)(2,1)} %shard_map.214), channel_id=1, source_target_pairs={{0,1},{1,0},{2,3},{3,2},{4,5},{5,4},{6,7},{7,6},{8,9},{9,8},{10,11... | collective-permute-start | bytes 6291464 | tf_op jit(solution)/shard_map/ppermute | solution.py:594
  349.6 47.7 %collective-permute-start.40 = (bf16[2,128,512]{2,1,0:T(8,128)(2,1)}, bf16[2,128,512]{2,1,0:T(8,128)(2,1)S(1)}, u32[]{:S(2)}, u32[]{:S(2)}) collective-permute-start(bf16[2,128,512]{2,1,0:T(8,128)(2,1)} %get-tuple-element.489), channel_id=1, source_target_pairs={{0,4},{2,6},{4,0},{6,2},{1,5},{3,7},{5,1},{7,3},{8,12},{10,14},{12... | collective-permute-start | bytes 786440 | tf_op jit(solution)/shard_map/ppermute | solution.py:594
  387.5 77.8 %collective-permute-start.46 = (bf16[2,256,1408]{2,1,0:T(8,128)(2,1)}, bf16[2,256,1408]{2,1,0:T(8,128)(2,1)}, u32[]{:S(2)}, u32[]{:S(2)}) collective-permute-start(bf16[2,256,1408]{2,1,0:T(8,128)(2,1)} %get-tuple-element.491), channel_id=1, source_target_pairs={{0,2},{2,0},{4,6},{6,4},{1,3},{3,1},{5,7},{7,5},{8,10},{10,8},{12,... | collective-permute-start | bytes 4325384 | tf_op jit(solution)/shard_map/ppermute | solution.py:594
  390.9 44.5 %collective-permute-start.41 = (bf16[256,1408]{1,0:T(8,128)(2,1)}, bf16[256,1408]{1,0:T(8,128)(2,1)}, u32[]{:S(2)}, u32[]{:S(2)}) collective-permute-start(bf16[256,1408]{1,0:T(8,128)(2,1)} %get-tuple-element.493), channel_id=1, source_target_pairs={{0,4},{2,6},{4,0},{6,2},{1,5},{3,7},{5,1},{7,3},{8,12},{10,14},{12... | collective-permute-start | bytes 2162696 | tf_op jit(solution)/shard_map/ppermute | solution.py:594
  394.4 61.9 %collective-permute-start.43 = (bf16[256,1408]{1,0:T(8,128)(2,1)}, bf16[256,1408]{1,0:T(8,128)(2,1)}, u32[]{:S(2)}, u32[]{:S(2)}) collective-permute-start(bf16[256,1408]{1,0:T(8,128)(2,1)} %get-tuple-element.497), channel_id=1, source_target_pairs={{0,4},{2,6},{4,0},{6,2},{1,5},{3,7},{5,1},{7,3},{8,12},{10,14},{12... | collective-permute-start | bytes 2162696 | tf_op jit(solution)/shard_map/ppermute | solution.py:594
  404.8 4.2 collective-permute-start.16
  411.1 48.1 %collective-permute-start.44 = (bf16[2,128,2048]{2,1,0:T(8,128)(2,1)}, bf16[2,128,2048]{2,1,0:T(8,128)(2,1)}, u32[]{:S(2)}, u32[]{:S(2)}) collective-permute-start(bf16[2,128,2048]{2,1,0:T(8,128)(2,1)} %get-tuple-element.501), channel_id=1, source_target_pairs={{0,16},{8,24},{16,0},{24,8},{1,17},{9,25},{17,1},{25,9},{2,18},{10... | collective-permute-start | bytes 3145736 | tf_op jit(solution)/shard_map/ppermute | solution.py:594
  442.2 26.4 %collective-permute-start.47 = (bf16[4,128,256]{2,1,0:T(8,128)(2,1)}, bf16[4,128,256]{2,1,0:T(8,128)(2,1)}, u32[]{:S(2)}, u32[]{:S(2)}) collective-permute-start(bf16[4,128,256]{2,1,0:T(8,128)(2,1)} %shard_map.219), channel_id=1, source_target_pairs={{0,1},{1,0},{2,3},{3,2},{4,5},{5,4},{6,7},{7,6},{8,9},{9,8},{10,11... | collective-permute-start | bytes 786440 | tf_op jit(solution)/shard_map/ppermute | solution.py:594
  451.2 55.7 %collective-permute-start.48 = (bf16[2,1024,256]{2,1,0:T(8,128)(2,1)}, bf16[2,1024,256]{2,1,0:T(8,128)(2,1)}, u32[]{:S(2)}, u32[]{:S(2)}) collective-permute-start(bf16[2,1024,256]{2,1,0:T(8,128)(2,1)} %get-tuple-element.507), channel_id=1, source_target_pairs={{0,2},{2,0},{4,6},{6,4},{1,3},{3,1},{5,7},{7,5},{8,10},{10,8},{12,... | collective-permute-start | bytes 3145736 | tf_op jit(solution)/shard_map/ppermute | solution.py:594
  464.3 54.3 %collective-permute-start.45 = (bf16[2,128,2048]{2,1,0:T(8,128)(2,1)}, bf16[2,128,2048]{2,1,0:T(8,128)(2,1)S(1)}, u32[]{:S(2)}, u32[]{:S(2)}) collective-permute-start(bf16[2,128,2048]{2,1,0:T(8,128)(2,1)} %get-tuple-element.513.refs_0_), channel_id=1, source_target_pairs={{0,16},{8,24},{16,0},{24,8},{1,17},{9,25},{17,1},{25,9},{2,18},{10... | collective-permute-start | bytes 3145736 | tf_op jit(solution)/shard_map/ppermute | solution.py:594
  468.6 41.1 %collective-permute-start.49 = (bf16[256,1408]{1,0:T(8,128)(2,1)}, bf16[256,1408]{1,0:T(8,128)(2,1)S(1)}, u32[]{:S(2)}, u32[]{:S(2)}) collective-permute-start(bf16[256,1408]{1,0:T(8,128)(2,1)} %get-tuple-element.516), channel_id=1, source_target_pairs={{0,4},{2,6},{4,0},{6,2},{1,5},{3,7},{5,1},{7,3},{8,12},{10,14},{12... | collective-permute-start | bytes 2162696 | tf_op jit(solution)/shard_map/ppermute | solution.py:594
  472.0 41.3 %collective-permute-start.50 = (bf16[2,128,256]{2,1,0:T(8,128)(2,1)}, bf16[2,128,256]{2,1,0:T(8,128)(2,1)S(1)}, u32[]{:S(2)}, u32[]{:S(2)}) collective-permute-start(bf16[2,128,256]{2,1,0:T(8,128)(2,1)} %get-tuple-element.521), channel_id=1, source_target_pairs={{0,2},{2,0},{4,6},{6,4},{1,3},{3,1},{5,7},{7,5},{8,10},{10,8},{12,... | collective-permute-start | bytes 393224 | tf_op jit(solution)/shard_map/ppermute | solution.py:594
  475.3 13.4 %collective-permute-start.7 = (f32[2,2048]{1,0:T(2,128)S(1)}, f32[2,2048]{1,0:T(2,128)S(1)}, u32[]{:S(2)}, u32[]{:S(2)}) collective-permute-start(f32[2,2048]{1,0:T(2,128)S(1)} %add.238), channel_id=1, source_target_pairs={{0,16},{8,24},{16,0},{24,8},{1,17},{9,25},{17,1},{25,9},{2,18},{10... | collective-permute-start | bytes 49160 | tf_op jit(solution)/shard_map/cond/branch_1_fun/ppermute | solution.py:594
  488.7 3.9 collective-permute-start.8
  492.6 9.8 %collective-permute-start.9 = (f32[2,2048]{1,0:T(2,128)S(1)}, f32[2,2048]{1,0:T(2,128)S(1)}, u32[]{:S(2)}, u32[]{:S(2)}) collective-permute-start(f32[2,2048]{1,0:T(2,128)S(1)} %add.240), channel_id=1, source_target_pairs={{0,4},{2,6},{4,0},{6,2},{1,5},{3,7},{5,1},{7,3},{8,12},{10,14},{12... | collective-permute-start | bytes 49160 | tf_op jit(solution)/shard_map/cond/branch_1_fun/ppermute | solution.py:594
  502.4 3.8 collective-permute-start.10
  509.7 29.8 %collective-permute-start.52 = (bf16[1024,256]{1,0:T(8,128)(2,1)}, bf16[1024,256]{1,0:T(8,128)(2,1)S(1)}, u32[]{:S(2)}, u32[]{:S(2)}) collective-permute-start(bf16[1024,256]{1,0:T(8,128)(2,1)} %get-tuple-element.525), channel_id=1, source_target_pairs={{0,4},{2,6},{4,0},{6,2},{1,5},{3,7},{5,1},{7,3},{8,12},{10,14},{12... | collective-permute-start | bytes 1572872 | tf_op jit(solution)/shard_map/ppermute | solution.py:594
  515.7 18.3 %collective-permute-start.51 = (bf16[128,256]{1,0:T(8,128)(2,1)}, bf16[128,256]{1,0:T(8,128)(2,1)S(1)}, u32[]{:S(2)}, u32[]{:S(2)}) collective-permute-start(bf16[128,256]{1,0:T(8,128)(2,1)} %get-tuple-element.528), channel_id=1, source_target_pairs={{0,4},{2,6},{4,0},{6,2},{1,5},{3,7},{5,1},{7,3},{8,12},{10,14},{12... | collective-permute-start | bytes 196616 | tf_op jit(solution)/shard_map/ppermute | solution.py:594
  518.6 3.0 collective-permute-start.11
  521.6 2.8 collective-permute-start.12
  (80 other events, 393.7 us)

commit v4 on v3

--- a/solution.py
+++ b/solution.py
@@ -240,24 +240,20 @@
     extra = jnp.where(row == 0, high, jnp.where(row == 1, middle, jnp.where(row == 2, low, 0.0)))
     rest = jnp.zeros((head - 2 * AUX, count), F32)
     da = jnp.concatenate([do, extra, rest], 0).astype(BF16)
-    for d in range(far_count + 1):
-
-        def part(d=d):
+    def run(blocks):
+        total = None
+        for d in range(blocks):
             scores = dot(ka_ref[d], qa, NN)
             probs = jnp.exp(causal(scores) if d == 0 else scores)
             d_scores = (probs * dot(va_ref[d], da, NN)).astype(BF16)
             dv_ref[d] += dot(probs.astype(BF16), da[:head], NT)
             dk_ref[d] += dot(d_scores, qa[:head], NT)
             update = dot(kt_ref[d], d_scores, NN)
-            if d == 0:
-                dq_acc[...] = update
-            else:
-                dq_acc[...] += update
-
-        if d == 0:
-            part()
-        else:
-            pl.when(d <= me)(part)
+            total = update if total is None else total + update
+        dq_acc[...] = total
+
+    for blocks in range(1, far_count + 2):
+        pl.when(me == blocks - 1)(functools.partial(run, blocks))
     score_scale = head ** (-0.5)
     dq = turn(dq_acc[...] * score_scale, cos_ref[...], sin_ref[...], -1.0).astype(BF16)
     for b, place in enumerate(here):
@@ -284,7 +280,7 @@
                     send_ref[place // 2] = part
 
 
-def attend_back(me, qa, do, full, kvs, segs, cos_rows, sine_rows, item):
+def attend_back(me, qa, do, full, kvs, segs, cos_rows, sine_rows, item, us):
     far_count = len(kvs) - 1
     heads, both, count = qa.shape
     head = both // 2
@@ -317,7 +313,7 @@
         out_shape=[jax.ShapeDtypeStruct((wide, count), BF16)]
         + [jax.ShapeDtypeStruct(((far_count + 1) // 2, both, count), BF16)] * 2,
         compiler_params=params(),
-        cost_estimate=COST,
+        cost_estimate=cost(us),
     )(me, qa, do, full, segs, cos_rows, sine_rows, *kvs)
 
 
@@ -478,6 +474,19 @@
     )(keep, recv)
 
 
+def add_pair_kernel(a_ref, b_ref, out_ref):
+    out_ref[...] = a_ref[...] + b_ref[...]
+
+
+def add_pair(a, b, us):
+    return pl.pallas_call(
+        add_pair_kernel,
+        out_shape=jax.ShapeDtypeStruct(a.shape, a.dtype),
+        compiler_params=params(),
+        cost_estimate=cost(us),
+    )(a, b)
+
+
 def add_last_kernel(turned, rest_ref, got_ref, *out_refs):
     row = 0
     for (count, flip), out_ref in zip(turned, out_refs):
@@ -671,11 +680,6 @@
     def spread(part):
         return swap(part, "tensor", n_tensor, 1)
 
-    def spread_more(part, got, pieces):
-        got = order.take(got)
-        block = order.mark(jnp.concatenate([part, got], 0))
-        return [swap(x, "tensor", n_tensor, 0) for x in cut(block, pieces)], block
-
     cts, d_hidden = [], []
     for s in each:
         cts.append(own_order(order.take(ct_rows), s))
@@ -706,10 +710,6 @@
 
     hidden, d_gate, d_up, h2 = ([None] * seqs for _ in range(4))
     got_b, kept_b = [None] * seqs, [None] * seqs
-
-    def whole(part, got):
-        got, block = spread_more(part, got, 1)
-        return order.mark(jnp.concatenate([block, *order.take_all(got)], 0))
 
     def back_sealed(s):
         def run(left, right):
@@ -745,31 +745,23 @@
     mix_job = Scatter(x_first, sizes, NN, fast)
     kv_job = Scatter(x_first, sizes, NN, fast)
 
-    downs = []
-
-    def feed_forward(rows, d_rows):
+    def feed_forward(part, got, d_rows):
+        rows = jnp.concatenate([part, got, *core_swaps(part, got)], 0)
         gate, up = dot(rows, w_gate, NN), dot(rows, w_up, NN)
         sig = jax.nn.sigmoid(gate)
         return (
+            rows,
             (gate * sig * up).astype(BF16),
             (d_rows * up * sig * (1.0 + gate * (1.0 - sig))).astype(BF16),
             (d_rows * gate * sig).astype(BF16),
         )
 
-    def add_down(s):
-        run = lambda rows: dot(rows, w_down, NN).astype(BF16)
-        downs.append(order.mark(sealed(run, order.take(hidden[s]))))
-
     for s in each:
-        h2[s] = whole(h2_own[s], got_h[s])
-        if s:
-            after_back(s - 1)
-        hidden[s], d_gate[s], d_up[s] = sealed(feed_forward, order.take(h2[s]), d_hidden[s])
+        h2[s], hidden[s], d_gate[s], d_up[s] = sealed(feed_forward, h2_own[s], order.take(got_h[s]), d_hidden[s])
         order.mark(d_up[s])
         if s + 1 < seqs:
             after_attention(s + 1)
             back_sealed(s)
-            add_down(s)
 
     d_low, dq_t, dkvs = [None] * seqs, [None] * seqs, [None] * seqs
 
@@ -782,9 +774,9 @@
         do_t[s], d_low[s] = sealed(run, d_low_own[s], order.take(got_d[s]))
         order.mark(do_t[s])
 
-    def attention_back(s):
+    def attention_back(s, us):
         dq_t[s], *dkvs[s] = attend_back(
-            at, qa[s], order.take(do_t[s]), full_o[s], kvs, segs, cos_rows, sine_rows, s
+            at, qa[s], order.take(do_t[s]), full_o[s], kvs, segs, cos_rows, sine_rows, s, us
         )
         order.mark(dq_t[s])
 
@@ -793,32 +785,39 @@
         return order.mark(place(at, [part, got, *far], dtype, us))
 
     last = seqs - 1
-    down_job.first(order, [(cts, hidden)])
+    down_job.first(order, [(cts, hidden)], 0)
+    for s in range(last):
+        after_back(s)
     back_sealed(last)
     unfolded(0)
-    up_job.first(order, [(h2, d_up)])
+    up_job.first(order, [(h2, d_up)], 20)
     after_back(last)
-    gate_job.first(order, [(h2, d_gate)], 12)
-    add_down(last)
-    send, kept_out = sealed(lambda *parts: fold_now(jnp.stack(parts)), *order.take_all(downs))
+    gate_job.first(order, [(h2, d_gate)], 0)
+
+    def down_partial(*parts):
+        total = dot(jnp.concatenate(parts, 0), w_down, NN).astype(BF16)
+        return fold_now(total.reshape(seqs, stretch, width))
+
+    send, kept_out = sealed(down_partial, *order.take_all(hidden))
     got_out = swap(order.mark(send), "tensor", n_tensor, 1)
-    attention_back(0)
+    down_job.second(order, 8)
+    attention_back(0, 20)
     unfolded(last)
-    down_job.second(order, 6)
-    up_job.second(order)
+    up_job.second(order, 12)
 
     def out_rows(got, kept, *rows):
         return (jnp.stack(rows) + kept + got.astype(F32)).astype(BF16)
 
     out_own = order.mark(sealed(out_rows, order.take(got_out), kept_out, *residual))
     got_out = spread(out_own)
-    attention_back(last)
+    attention_back(last, 0)
 
     keep_send = [x for s in each for x in dkvs[s]]
     kept_kv, send = sealed(lambda *xs: (jnp.stack(xs[0::2]), jnp.stack(xs[1::2])), *keep_send)
     got_kv = swap(order.mark(send), "context", n_context, 0)
-    layer_out = place_all(out_own, got_out, BF16)
-    mix_job.first(order, [(d_low, o_t), ([h1] * seqs, dq_t)])
+    down_job.third(order, 0)
+    layer_out = place_all(out_own, got_out, BF16, 0)
+    mix_job.first(order, [(d_low, o_t), ([h1] * seqs, dq_t)], 0)
 
     def add_kv(kept, got):
         total = kept.astype(F32) + got.astype(F32)
@@ -826,9 +825,7 @@
 
     kept_kv, send = sealed(add_kv, kept_kv, order.take(got_kv))
     got_kv = swap(order.mark(send), "context", n_context, 1)
-    gate_job.second(order)
-    down_job.third(order, 2)
-    up_job.third(order, 12)
+    gate_job.second(order, 0)
 
     def input_partial(kept, got, *parts):
         both = merge(at, kept, got, cos_rows, sine_rows)
@@ -838,10 +835,11 @@
 
     send, kept_x, *dkv_ts = sealed(input_partial, kept_kv, order.take(got_kv), *dq_t)
     got_x = swap(order.mark(send), "tensor", n_tensor, 1)
-    down_sum = down_job.final(order, [(BLOCK, True)], 2)
-    kv_job.first(order, [([h1] * seqs, dkv_ts)])
-    mix_job.second(order)
-    up_sum = up_job.final(order, [(BLOCK, False)], 4)
+    up_job.third(order, 0)
+    down_sum = down_job.final(order, [(BLOCK, True)], 16)
+    mix_job.second(order, 0)
+    gate_job.third(order, 0)
+    kv_job.first(order, [([h1] * seqs, dkv_ts)], 0)
 
     def input_grad(kept, got, sums_0, sums_1, *parts):
         back = kept + got.astype(F32)
@@ -849,29 +847,40 @@
         scale = lax.rsqrt(jnp.mean(streams * streams, -1, keepdims=True) + EPSILON)
         normed = streams * scale
         grad = res + norm_back(back, normed, scale, gain_1)
-        return grad.astype(BF16), jnp.stack([jnp.sum(back * normed, (0, 1)), sums_0 + sums_1])
-
-    grad_own, gain_sum = sealed(input_grad, kept_x, order.take(got_x), *gains_2, *stream, *d_res)
+        sums = jnp.stack([jnp.sum(back * normed, (0, 1)), sums_0 + sums_1])
+        return grad.astype(BF16), sums, core_swap(sums)
+
+    grad_own, gain_sum, got_gain = sealed(input_grad, kept_x, order.take(got_x), *gains_2, *stream, *d_res)
     got_grad = spread(order.mark(grad_own))
-    gate_job.third(order, 4)
-    kv_job.second(order, 8)
-
-    def all_sum(total):
-        for axis in ("tensor", "context", "dp"):
-            for bit in range((sizes[axis] - 1).bit_length()):
-                total = total + swap(total, axis, sizes[axis], bit)
-        return total
-
-    gain_sum = order.mark(sealed(all_sum, order.take(gain_sum)))
-    mix_job.third(order)
-    gate_sum = gate_job.final(order, [(BLOCK, False)])
-    kv_job.third(order)
-    grad_tokens = place_all(grad_own, got_grad, F32, 6)
+    hops = [(axis, bit) for axis in ("tensor", "context", "dp") for bit in range((sizes[axis] - 1).bit_length())]
+    hops.pop(0)
+
+    def hop(us=0):
+        nonlocal gain_sum, got_gain
+        gain_sum = order.mark(add_pair(gain_sum, order.take(got_gain), us))
+        if hops:
+            axis, bit = hops.pop(0)
+            got_gain = swap(gain_sum, axis, sizes[axis], bit)
+            return True
+        return False
+
+    up_sum = up_job.final(order, [(BLOCK, False)], 2)
+    kv_job.second(order, 2)
+    hop(0)
+    hop(0)
+    mix_job.third(order, 0)
+    kv_job.third(order, 0)
+    gate_sum = gate_job.final(order, [(BLOCK, False)], 0)
+    hop(4)
+    grad_tokens = place_all(grad_own, got_grad, F32, 0)
+    hop(0)
+    while hop():
+        pass
     per = width // blocks
     gain_sum = lax.dynamic_slice_in_dim(gain_sum, (me_c * n_dp + lax.axis_index("dp")) * per, per, 1)
 
     if fast:
-        key_sum, value_sum = kv_job.final(order, [(head, True), (head, True)])
+        key_sum, value_sum = kv_job.final(order, [(head, True), (head, True)], 1)
         output_sum, query_sum = mix_job.final(order, [(wide, False), (wide, True)])
     else:
 

time: 551 us -> 534 us (0.969)
  starting transfers between devices: 91.2 us -> 79.4 us
  other arithmetic: 54.9 us -> 44.7 us
  waiting for transfers between devices: 119 us -> 111 us
  Pallas kernels: 164 us -> 171 us
    ppermute x50 -> x52, starting transfers between devices: 80.4 us -> 68.7 us  [swap(): return lax.ppermute(x, axis, [(i, i ^ 1 << bit) for i in range(size)])]
    ppermute x50 -> x52, waiting for transfers between devices: 119 us -> 111 us  [swap(): return lax.ppermute(x, axis, [(i, i ^ 1 << bit) for i in range(size)])]
    concatenate x4 -> x0, other arithmetic: 6.97 us -> none  [the longest x2 4.59 us: whole(): return order.mark(jnp.concatenate([block, *order.take_all(got)], 0))]
    pallas_call x0 -> x5, Pallas kernels: none -> 6.71 us  [add_pair(): pl.pallas_call(add_pair_kernel, out_shape=jax.ShapeDtypeStruct(a.shape, a...]
    cond x30 -> x38, local copies, waits for them, and re-layouts: 1.65 us -> 7.76 us
    dot_general x16 -> x15, matrix products: 81.6 us -> 82.6 us  [dot(): lax.dot_general(left, right, (dims, ((), ())), preferred_element_type=F32)]
    unnamed x123 -> x135, local copies, waits for them, and re-layouts: 12.4 us -> 11.9 us
  transfers between devices with their start and end apart: 53 -> 55, of which waited for: 27 -> 26; matrix products, arithmetic and copies ran while one was open for 22% -> 26% of each run, Pallas kernels for 25% -> 29%
where the time goes in v4:
time: 534 us; the launch traced here: 526 us
  Pallas kernels  171 us (32%)
  waiting for transfers between devices  111 us (21%)
  matrix products  82.6 us (15%)
  starting transfers between devices  79.4 us (15%)
  other arithmetic  44.7 us (8%)
  local copies, waits for them, and re-layouts  35.5 us (7%)
    ppermute x52, waiting for transfers between devices, swap(): return lax.ppermute(x, axis, [(i, i ^ 1 << bit) for i in range(size)])  111 us
    dot_general x15, matrix products, dot(): lax.dot_general(left, right, (dims, ((), ())), preferred_element_type=F32)  82.6 us
    pallas_call x10, Pallas kernels, grad_blocks(): pl.pallas_call(functools.partial(grad_kernel, groups, recv is not None, s...  71.9 us
    ppermute x52, starting transfers between devices, swap(): return lax.ppermute(x, axis, [(i, i ^ 1 << bit) for i in range(size)])  68.7 us
    pallas_call x2, Pallas kernels, attend_back(): pl.pallas_call(functools.partial(back_kernel, far_count), grid_spec=pltpu...  21.3 us
    pallas_call x5, Pallas kernels, add_send(): pl.pallas_call(add_send_kernel, out_shape=[jax.ShapeDtypeStruct(shape, BF...  14.5 us
    pallas_call x2, Pallas kernels, attend(): pl.pallas_call(functools.partial(attend_kernel, far_count), grid_spec=plt...  14.2 us
    pallas_call x5, Pallas kernels, add_last(): pl.pallas_call(functools.partial(add_last_kernel, turned), out_shape=[jax...  13 us
  transfers between devices with their start and end apart: 55, of which 26 were waited for; matrix products, arithmetic and copies ran while one was open for 26% of the time, Pallas kernels for 29%

profile of v4, /device:TPU:0, one launch (start us, length us, event | category | flops | bytes accessed | tf_op | source)
XLA Modules:
  0.0 525.8 jit_solution(10335775014943764692)
XLA Ops:
  4.3 8.8 %shard_map.203 = (bf16[1024,2048]{1,0:T(8,128)(2,1)}, bf16[512,1024]{1,0:T(8,128)(2,1)}, bf16[128,1024]{1,0:T(8,128)(2,1)}) custom-call(s32[3]{0:T(128)S(1)} %pad_add_fusion.1.at_ref, bf16[1024,2048]{1,0:T(8,128)(2,1)} %bitcast.109, f32[1,2048]{1,0:T(1,128)} %bitcast.132, bf16[2048,512]{1,0:T(8,128)(2,1)} %wq_ref.1, ...), custom_call_target="tpu_custom_call" | custom-call | flops 1024 | bytes 1024 | tf_op jit(solution)/shard_map/pallas_call | solution.py:70
  13.1 4.9 collective-permute-start.17
  18.1 4.5 collective-permute-start.18
  26.9 7.8 %fusion.34 = f32[512,1408]{1,0:T(8,128)} fusion(bf16[1408,2048]{1,0:T(8,128)(2,1)} %param.54, bf16[128,2048]{1,0:T(8,128)(2,1)S(1)} %get-tuple-element.591, bf16[128,2048]{1,0:T(8,128)(2,1)S(1)} %get-tuple-element.592, bf16[128,2048]{1,0:T(8,128)(2,1)S(1)} %get-tuple-element.593, bf16[128,2048]{1,0:T(8,128)(2,1)S(1)} %get-tuple-element.590), kind=kOutput, calls=%fused_computation.150 | convolution fusion | flops 2961178624 | bytes 10747904 | tf_op jit(solution)/shard_map/dot_general | solution.py:31
  36.3 8.6 %fusion.33 = f32[512,1408]{1,0:T(8,128)} fusion(bf16[1408,2048]{1,0:T(8,128)(2,1)} %param.54, bf16[128,2048]{1,0:T(8,128)(2,1)S(1)} %get-tuple-element.587, bf16[128,2048]{1,0:T(8,128)(2,1)S(1)} %get-tuple-element.588, bf16[128,2048]{1,0:T(8,128)(2,1)S(1)} %get-tuple-element.589, bf16[128,2048]{1,0:T(8,128)(2,1)S(1)} %get-tuple-element.586), kind=kOutput, calls=%fused_computation.149 | convolution fusion | flops 2961178624 | bytes 10747904 | tf_op jit(solution)/shard_map/dot_general | solution.py:31
  47.1 7.3 %shard_map.204 = (bf16[8,128,512]{2,1,0:T(8,128)(2,1)}, bf16[512,512]{1,0:T(8,128)(2,1)}, f32[512,512]{1,0:T(8,128)}) custom-call(s32[3]{0:T(128)S(1)} %pad_add_fusion.1.at_ref, bf16[512,1024]{1,0:T(8,128)(2,1)} %get-tuple-element.407.q_ref, s32[2,4,512]{2,1,0:T(4,128)} %pad_add_fusion.seg_ref, bf16[128,1024]{1,0:T(8,128)(2,1)} %get-tuple-element.399.refs_0_, ...), custom_call_target="tpu_custom_call" | custom-call | flops 1024 | bytes 1024 | tf_op jit(solution)/shard_map/pallas_call | solution.py:186
  61.5 6.9 %shard_map.205 = (bf16[8,128,512]{2,1,0:T(8,128)(2,1)}, bf16[512,512]{1,0:T(8,128)(2,1)}, f32[512,512]{1,0:T(8,128)}) custom-call(s32[3]{0:T(128)S(1)} %pad_add_fusion.1.at_ref, bf16[512,1024]{1,0:T(8,128)(2,1)} %get-tuple-element.407.q_ref, s32[2,4,512]{2,1,0:T(4,128)} %pad_add_fusion.seg_ref, bf16[128,1024]{1,0:T(8,128)(2,1)} %get-tuple-element.399.refs_0_, ...), custom_call_target="tpu_custom_call" | custom-call | flops 1024 | bytes 1024 | tf_op jit(solution)/shard_map/pallas_call | solution.py:186
  68.4 5.5 %collective-permute-done.21 = bf16[128,2048]{1,0:T(8,128)(2,1)S(1)} collective-permute-done((bf16[128,2048]{1,0:T(8,128)(2,1)S(1)}, bf16[128,2048]{1,0:T(8,128)(2,1)S(1)}, u32[]{:S(2)}, u32[]{:S(2)}) %collective-permute-start.21) | collective-permute-done | bytes 524320 | tf_op jit(solution)/shard_map/ppermute | solution.py:603
  85.5 9.4 %collective-permute-done.23 = bf16[128,2048]{1,0:T(8,128)(2,1)S(1)} collective-permute-done((bf16[128,2048]{1,0:T(8,128)(2,1)S(1)}, bf16[128,2048]{1,0:T(8,128)(2,1)S(1)}, u32[]{:S(2)}, u32[]{:S(2)}) %collective-permute-start.23) | collective-permute-done | bytes 524320 | tf_op jit(solution)/shard_map/ppermute | solution.py:603
  94.9 18.9 %conditional.16 = (bf16[512,2048]{1,0:T(8,128)(2,1)}, bf16[512,1408]{1,0:T(8,128)(2,1)S(1)}, bf16[512,1408]{1,0:T(8,128)(2,1)S(1)}, bf16[512,1408]{1,0:T(8,128)(2,1)S(1)}) conditional(s32[]{:T(128)} %convert_element_type.181, () %tuple.204, (bf16[128,2048]{1,0:T(8,128)(2,1)S(1)}, bf16[128,2048]{1,0:T(8,128)(2,1)S(1)}, bf16[2048,1408]{1,0:T(8,128)(2,1)}, ...), branch_computations={%region_5.6_spmd, %region_6.7_spmd} | conditional | flops 5917114368 | bytes 65929404 | solution.py:532
  100.4 7.2 %fusion.40 = f32[512,1408]{1,0:T(8,128)S(1)} fusion(bf16[512,2048]{1,0:T(8,128)(2,1)} %constant_dynamic-update-slice_fusion, bf16[2048,1408]{1,0:T(8,128)(2,1)} %get-tuple-element.168), kind=kOutput, calls=%fused_computation.154 | convolution fusion | flops 2952790016 | bytes 10747904 | tf_op jit(solution)/shard_map/cond/branch_1_fun/dot_general | solution.py:31
  107.6 6.2 %multiply_convert_fusion = (bf16[512,1408]{1,0:T(8,128)(2,1)S(1)}, bf16[512,1408]{1,0:T(8,128)(2,1)S(1)}, bf16[512,1408]{1,0:T(8,128)(2,1)S(1)}) fusion(f32[512,1408]{1,0:T(8,128)S(1)} %copy-done.79, f32[512,1408]{1,0:T(8,128)S(1)} %fusion.40, bf16[512,2048]{1,0:T(8,128)(2,1)} %constant_dynamic-update-slice_fusion, bf16[2048,1408]{1,0:T(8,128)(2,1)S(1)} %bitcast.139), kind=kOutput, calls=%fused_computation | convolution fusion | flops 2964324352 | bytes 17956864 | tf_op jit(solution)/shard_map/cond/branch_1_fun/dot_general | solution.py:31
  120.5 13.4 %conditional.17 = (bf16[1,128,2048]{2,1,0:T(8,128)(2,1)}, f32[128,2048]{1,0:T(8,128)S(1)}) conditional(s32[]{:T(128)} %convert_element_type.181, () %tuple.213, (bf16[512,1408]{1,0:T(8,128)(2,1)S(1)}, bf16[2048,1408]{1,0:T(8,128)(2,1)}, bf16[512,1408]{1,0:T(8,128)(2,1)}, bf16[2048,1408]{1,0:T(8,128)(2,1)}) %tuple.368), branch_computations={%region_8.9_spmd, %region_9.10_spmd} | conditional | flops 5909250048 | bytes 67371120 | solution.py:532
  120.5 5.6 %fusion.41 = f32[512,2048]{1,0:T(8,128)S(1)} fusion(bf16[512,1408]{1,0:T(8,128)(2,1)S(1)} %get-tuple-element.170, bf16[2048,1408]{1,0:T(8,128)(2,1)} %get-tuple-element.171), kind=kOutput, calls=%fused_computation.155 | convolution fusion | flops 2952790016 | bytes 11403264 | tf_op jit(solution)/shard_map/cond/branch_1_fun/dot_general | solution.py:31
  139.1 21.0 %conditional.18 = (bf16[512,2048]{1,0:T(8,128)(2,1)}, bf16[512,1408]{1,0:T(8,128)(2,1)}, bf16[512,1408]{1,0:T(8,128)(2,1)S(1)}, bf16[512,1408]{1,0:T(8,128)(2,1)}) conditional(s32[]{:T(128)} %convert_element_type.181, () %tuple.212, (bf16[128,2048]{1,0:T(8,128)(2,1)S(1)}, bf16[128,2048]{1,0:T(8,128)(2,1)}, bf16[2048,1408]{1,0:T(8,128)(2,1)S(1)}, ...), branch_computations={%region_10.11_spmd, %region_11.12_spmd} | conditional | flops 5917114368 | bytes 48627852 | solution.py:532
  146.1 6.5 %fusion.42 = f32[512,1408]{1,0:T(8,128)S(1)} fusion(bf16[512,2048]{1,0:T(8,128)(2,1)} %constant_dynamic-update-slice_fusion.4, bf16[2048,1408]{1,0:T(8,128)(2,1)} %get-tuple-element.179), kind=kOutput, calls=%fused_computation.156 | convolution fusion | flops 2952790016 | bytes 10747904 | tf_op jit(solution)/shard_map/cond/branch_1_fun/dot_general | solution.py:31
  152.6 7.5 %multiply_convert_fusion.3 = (bf16[512,1408]{1,0:T(8,128)(2,1)}, bf16[512,1408]{1,0:T(8,128)(2,1)S(1)}, bf16[512,1408]{1,0:T(8,128)(2,1)}) fusion(f32[512,1408]{1,0:T(8,128)S(1)} %copy-done.78, f32[512,1408]{1,0:T(8,128)S(1)} %fusion.42, bf16[512,2048]{1,0:T(8,128)(2,1)} %constant_dynamic-update-slice_fusion.4, bf16[2048,1408]{1,0:T(8,128)(2,1)S(1)} %get-tuple-element.178), kind=kOutput, calls=%fused_computation.13 | convolution fusion | flops 2964324352 | bytes 17956864 | tf_op jit(solution)/shard_map/cond/branch_1_fun/dot_general | solution.py:31
  160.1 8.1 %shard_map.206 = bf16[4,256,1408]{2,1,0:T(8,128)(2,1)} custom-call(s32[4]{0:T(128)} %add_add_fusion.table_ref, bf16[512,1408]{1,0:T(8,128)(2,1)} %copy-done.13, bf16[512,2048]{1,0:T(8,128)(2,1)} %get-tuple-element.422.refs_1_.refs_2_, bf16[512,2048]{1,0:T(8,128)(2,1)} %get-tuple-element.422.refs_1_.refs_2_, bf16[512,1408]{1,0:T(8,128)(2,1)} %get-tuple-element.444.refs_3_, ...), custom_call_target="tpu_custom_call" | custom-call | flops 1024 | bytes 1024 | tf_op jit(solution)/shard_map/pallas_call | solution.py:453
  178.4 14.8 %conditional.20 = (bf16[1,128,2048]{2,1,0:T(8,128)(2,1)}, f32[128,2048]{1,0:T(8,128)S(1)}) conditional(s32[]{:T(128)} %convert_element_type.181, () %tuple.221, (bf16[512,1408]{1,0:T(8,128)(2,1)S(1)}, bf16[2048,1408]{1,0:T(8,128)(2,1)}, bf16[512,1408]{1,0:T(8,128)(2,1)}, bf16[2048,1408]{1,0:T(8,128)(2,1)}) %tuple.223), branch_computations={%region_16.17_spmd, %region_17.18_spmd} | conditional | flops 5909250048 | bytes 61603924 | solution.py:532
  178.4 5.6 %fusion.43 = f32[512,2048]{1,0:T(8,128)S(1)} fusion(bf16[512,1408]{1,0:T(8,128)(2,1)S(1)} %get-tuple-element.189, bf16[2048,1408]{1,0:T(8,128)(2,1)} %get-tuple-element.190), kind=kOutput, calls=%fused_computation.157 | convolution fusion | flops 2952790016 | bytes 11403264 | tf_op jit(solution)/shard_map/cond/branch_1_fun/dot_general | solution.py:31
  184.1 5.1 fusion.4
  194.5 9.3 %conditional.21 = ((bf16[512,512]{1,0:T(8,128)(2,1)}, bf16[512,2048]{1,0:T(8,128)(2,1)S(1)})) conditional(s32[]{:T(128)} %convert_element_type.181, () %tuple.210, (bf16[128,2048]{1,0:T(8,128)(2,1)}, bf16[128,2048]{1,0:T(8,128)(2,1)S(1)}, bf16[512,2048]{1,0:T(8,128)(2,1)}) %tuple.225), branch_computations={%region_18.19_spmd, %region_19.20_spmd} | conditional | flops 1024 | bytes 10486956 | solution.py:532
  203.8 8.0 %shard_map.207 = bf16[4,256,1408]{2,1,0:T(8,128)(2,1)} custom-call(s32[4]{0:T(128)} %add_add_fusion.1.table_ref, bf16[512,1408]{1,0:T(8,128)(2,1)} %copy-done.51, bf16[512,2048]{1,0:T(8,128)(2,1)} %get-tuple-element.441.refs_1_.refs_2_, bf16[512,2048]{1,0:T(8,128)(2,1)} %get-tuple-element.441.refs_1_.refs_2_, bf16[512,1408]{1,0:T(8,128)(2,1)} %get-tuple-element.430.refs_3_, ...), custom_call_target="tpu_custom_call" | custom-call | flops 23000000512 | bytes 1024 | tf_op jit(solution)/shard_map/pallas_call | solution.py:453
  218.7 7.4 %shard_map.208 = bf16[4,256,1408]{2,1,0:T(8,128)(2,1)} custom-call(s32[4]{0:T(128)} %add_add_fusion.table_ref, bf16[512,1408]{1,0:T(8,128)(2,1)S(1)} %get-tuple-element.417.refs_0_, bf16[512,2048]{1,0:T(8,128)(2,1)} %get-tuple-element.441.refs_1_.refs_2_, bf16[512,2048]{1,0:T(8,128)(2,1)} %get-tuple-element.441.refs_1_.refs_2_, bf16[512,1408]{1,0:T(8,128)(2,1)} %copy-done.4, ...), custom_call_target="tpu_custom_call" | custom-call | flops 1024 | bytes 1024 | tf_op jit(solution)/shard_map/pallas_call | solution.py:453
  226.7 17.7 %conditional.23 = (bf16[2,128,2048]{2,1,0:T(8,128)(2,1)}, f32[2,128,2048]{2,1,0:T(8,128)}) conditional(s32[]{:T(128)} %convert_element_type.181, () %tuple.208, (bf16[512,1408]{1,0:T(8,128)(2,1)S(1)}, bf16[512,1408]{1,0:T(8,128)(2,1)}, bf16[1408,2048]{1,0:T(8,128)(2,1)}) %tuple.358), branch_computations={%region_24.25_spmd, %region_25.26_spmd} | conditional | flops 5916590080 | bytes 40108088 | solution.py:532
  226.7 9.9 %convolution_convert_fusion = bf16[1024,2048]{1,0:T(8,128)(2,1)S(1)} fusion(bf16[1408,2048]{1,0:T(8,128)(2,1)} %get-tuple-element.208, bf16[512,1408]{1,0:T(8,128)(2,1)} %get-tuple-element.207, bf16[512,1408]{1,0:T(8,128)(2,1)S(1)} %get-tuple-element.206), kind=kOutput, calls=%fused_computation.45 | convolution fusion | flops 5913444352 | bytes 12845056 | tf_op jit(solution)/shard_map/cond/branch_1_fun/dot_general | solution.py:31
  245.5 9.3 %shard_map.209 = (bf16[2,256,1408]{2,1,0:T(8,128)(2,1)}, bf16[2,256,1408]{2,1,0:T(8,128)(2,1)}) custom-call(s32[4]{0:T(128)} %add_add_fusion.3.table_ref, bf16[512,1408]{1,0:T(8,128)(2,1)} %copy-done.13, bf16[512,2048]{1,0:T(8,128)(2,1)} %get-tuple-element.422.refs_1_.refs_2_, bf16[512,2048]{1,0:T(8,128)(2,1)} %get-tuple-element.422.refs_1_.refs_2_, ...), custom_call_target="tpu_custom_call" | custom-call | flops 9200001024 | bytes 1024 | tf_op jit(solution)/shard_map/pallas_call | solution.py:453
  255.1 10.6 %shard_map.210 = (bf16[512,512]{1,0:T(8,128)(2,1)}, bf16[2,128,512]{2,1,0:T(8,128)(2,1)}, bf16[2,128,512]{2,1,0:T(8,128)(2,1)}) custom-call(s32[3]{0:T(128)S(1)} %pad_add_fusion.1.at_ref, bf16[8,128,512]{2,1,0:T(8,128)(2,1)} %get-tuple-element.446.qa_ref, bf16[512,512]{1,0:T(8,128)(2,1)S(1)} %copy-done.54, f32[512,512]{1,0:T(8,128)} %get-tuple-element.451.full_ref, ...), custom_call_target="tpu_custom_call" | custom-call | flops 23000000512 | bytes 1024 | tf_op jit(solution)/shard_map/pallas_call | solution.py:288
  265.7 9.9 %conditional.24 = ((bf16[512,512]{1,0:T(8,128)(2,1)}, bf16[512,2048]{1,0:T(8,128)(2,1)})) conditional(s32[]{:T(128)} %convert_element_type.181, () %tuple.232, (bf16[128,2048]{1,0:T(8,128)(2,1)}, bf16[128,2048]{1,0:T(8,128)(2,1)}, bf16[512,2048]{1,0:T(8,128)(2,1)}) %tuple.236), branch_computations={%region_26.27_spmd, %region_27.28_spmd} | conditional | flops 1024 | bytes 8389776 | solution.py:532
  270.8 4.7 branch_1_fun.4
  275.6 7.1 %collective-permute-done.31.refs_6_ = bf16[4,256,1408]{2,1,0:T(8,128)(2,1)} collective-permute-done((bf16[4,256,1408]{2,1,0:T(8,128)(2,1)}, bf16[4,256,1408]{2,1,0:T(8,128)(2,1)}, u32[]{:S(2)}, u32[]{:S(2)}) %collective-permute-start.31) | collective-permute-done | bytes 2883616 | tf_op jit(solution)/shard_map/ppermute | solution.py:603
  282.7 9.5 %shard_map.211 = (bf16[2,256,1408]{2,1,0:T(8,128)(2,1)}, bf16[2,256,1408]{2,1,0:T(8,128)(2,1)}) custom-call(s32[4]{0:T(128)} %add_add_fusion.2.table_ref, bf16[512,1408]{1,0:T(8,128)(2,1)} %copy-done.51, bf16[512,2048]{1,0:T(8,128)(2,1)} %get-tuple-element.441.refs_1_.refs_2_, bf16[512,2048]{1,0:T(8,128)(2,1)} %get-tuple-element.441.refs_1_.refs_2_, ...), custom_call_target="tpu_custom_call" | custom-call | flops 13800001536 | bytes 1024 | tf_op jit(solution)/shard_map/pallas_call | solution.py:453
  297.7 10.7 %shard_map.212 = (bf16[512,512]{1,0:T(8,128)(2,1)}, bf16[2,128,512]{2,1,0:T(8,128)(2,1)}, bf16[2,128,512]{2,1,0:T(8,128)(2,1)}) custom-call(s32[3]{0:T(128)S(1)} %pad_add_fusion.1.at_ref, bf16[8,128,512]{2,1,0:T(8,128)(2,1)} %get-tuple-element.460.qa_ref, bf16[512,512]{1,0:T(8,128)(2,1)} %get-tuple-element.461.do_ref, ...), custom_call_target="tpu_custom_call" | custom-call | flops 1024 | bytes 1024 | tf_op jit(solution)/shard_map/pallas_call | solution.py:288
  310.8 6.7 %collective-permute-start.35 = (bf16[2,2,128,512]{3,2,1,0:T(8,128)(2,1)}, bf16[2,2,128,512]{3,2,1,0:T(8,128)(2,1)}, u32[]{:S(2)}, u32[]{:S(2)}) collective-permute-start(bf16[2,2,128,512]{3,2,1,0:T(8,128)(2,1)} %get-tuple-element.466), channel_id=1, source_target_pairs={{0,2},{2,0},{4,6},{6,4},{1,3},{3,1},{5,7},{7,5},{8,10},{10,8},{12,... | collective-permute-start | bytes 1572872 | tf_op jit(solution)/shard_map/ppermute | solution.py:603
  320.8 30.1 %collective-permute-start.39 = (bf16[256,1408]{1,0:T(8,128)(2,1)}, bf16[256,1408]{1,0:T(8,128)(2,1)}, u32[]{:S(2)}, u32[]{:S(2)}) collective-permute-start(bf16[256,1408]{1,0:T(8,128)(2,1)} %get-tuple-element.468), channel_id=1, source_target_pairs={{0,4},{2,6},{4,0},{6,2},{1,5},{3,7},{5,1},{7,3},{8,12},{10,14},{12... | collective-permute-start | bytes 2162696 | tf_op jit(solution)/shard_map/ppermute | solution.py:603
  350.9 5.8 %conditional.27 = (bf16[2,128,2048]{2,1,0:T(8,128)(2,1)}, bf16[2,128,2048]{2,1,0:T(8,128)(2,1)}) conditional(s32[]{:T(128)} %convert_element_type.181, () %tuple.240, (bf16[2,128,2048]{2,1,0:T(8,128)(2,1)S(1)}, bf16[2,128,2048]{2,1,0:T(8,128)(2,1)}) %tuple.360), branch_computations={%region_32.33_spmd, %region_33.34_spmd} | conditional | bytes 8388704 | solution.py:532
  356.7 4.5 shard_map.214
  361.2 6.5 %shard_map.215 = bf16[4,1024,256]{2,1,0:T(8,128)(2,1)} custom-call(s32[4]{0:T(128)} %add_add_fusion.table_ref, bf16[512,512]{1,0:T(8,128)(2,1)} %get-tuple-element.405.refs_0_, bf16[512,2048]{1,0:T(8,128)(2,1)S(1)} %get-tuple-element.478.refs_1_.refs_2_, bf16[512,2048]{1,0:T(8,128)(2,1)S(1)} %get-tuple-element.478.refs_1_.refs_2_, ...), custom_call_target="tpu_custom_call" | custom-call | flops 1024 | bytes 1024 | tf_op jit(solution)/shard_map/pallas_call | solution.py:453
  369.8 9.0 %shard_map.216 = (bf16[2,256,1408]{2,1,0:T(8,128)(2,1)}, bf16[2,256,1408]{2,1,0:T(8,128)(2,1)}) custom-call(s32[4]{0:T(128)} %add_add_fusion.3.table_ref, bf16[512,1408]{1,0:T(8,128)(2,1)S(1)} %get-tuple-element.417.refs_0_, bf16[512,2048]{1,0:T(8,128)(2,1)} %get-tuple-element.441.refs_1_.refs_2_, bf16[512,2048]{1,0:T(8,128)(2,1)} %get-tuple-element.441.refs_1_.refs_2_, ...), custom_call_target="tpu_custom_call" | custom-call | flops 1024 | bytes 1024 | tf_op jit(solution)/shard_map/pallas_call | solution.py:453
  378.9 14.6 %collective-permute-done.37 = bf16[2,128,512]{2,1,0:T(8,128)(2,1)S(1)} collective-permute-done((bf16[2,128,512]{2,1,0:T(8,128)(2,1)S(1)}, bf16[2,128,512]{2,1,0:T(8,128)(2,1)S(1)}, u32[]{:S(2)}, u32[]{:S(2)}) %collective-permute-start.37) | collective-permute-done | bytes 262176 | tf_op jit(solution)/shard_map/ppermute | solution.py:603
  393.5 14.4 %conditional.29 = (bf16[2,128,2048]{2,1,0:T(8,128)(2,1)}, f32[2,128,2048]{2,1,0:T(8,128)S(1)}, bf16[128,512]{1,0:T(8,128)(2,1)S(1)}, bf16[128,512]{1,0:T(8,128)(2,1)S(1)}) conditional(s32[]{:T(128)} %convert_element_type.181, () %tuple.248, (bf16[512,512]{1,0:T(8,128)(2,1)S(1)}, bf16[512,512]{1,0:T(8,128)(2,1)S(1)}, bf16[2048,512]{1,0:T(8,128)(2,1)}, ...), branch_computations={%region_36.37_spmd, %region_37.38_spmd} | conditional | flops 2694317056 | bytes 54789304 | solution.py:532
  415.8 7.2 %shard_map.219 = (bf16[2,1024,256]{2,1,0:T(8,128)(2,1)}, bf16[2,1024,256]{2,1,0:T(8,128)(2,1)}) custom-call(s32[4]{0:T(128)} %add_add_fusion.3.table_ref, bf16[512,512]{1,0:T(8,128)(2,1)} %get-tuple-element.405.refs_0_, bf16[512,2048]{1,0:T(8,128)(2,1)S(1)} %get-tuple-element.478.refs_1_.refs_2_, bf16[512,2048]{1,0:T(8,128)(2,1)S(1)} %get-tuple-element.478.refs_1_.refs_2_, ...), custom_call_target="tpu_custom_call" | custom-call | flops 1024 | bytes 1024 | tf_op jit(solution)/shard_map/pallas_call | solution.py:453
  435.1 4.5 conditional.30
  440.6 6.4 %collective-permute-done.44.got_ref = bf16[256,1408]{1,0:T(8,128)(2,1)} collective-permute-done((bf16[256,1408]{1,0:T(8,128)(2,1)}, bf16[256,1408]{1,0:T(8,128)(2,1)}, u32[]{:S(2)}, u32[]{:S(2)}) %collective-permute-start.44) | collective-permute-done | bytes 720928 | tf_op jit(solution)/shard_map/ppermute | solution.py:603
  455.5 10.1 %collective-permute-done.46.b_ref = f32[2,2048]{1,0:T(2,128)S(1)} collective-permute-done((f32[2,2048]{1,0:T(2,128)}, f32[2,2048]{1,0:T(2,128)S(1)}, u32[]{:S(2)}, u32[]{:S(2)}) %collective-permute-start.46) | collective-permute-done | bytes 16416 | tf_op jit(solution)/shard_map/ppermute | solution.py:603
  469.5 11.5 %collective-permute-done.47.recv_ref = bf16[2,1024,256]{2,1,0:T(8,128)(2,1)} collective-permute-done((bf16[2,1024,256]{2,1,0:T(8,128)(2,1)}, bf16[2,1024,256]{2,1,0:T(8,128)(2,1)}, u32[]{:S(2)}, u32[]{:S(2)}) %collective-permute-start.47) | collective-permute-done | bytes 1048608 | tf_op jit(solution)/shard_map/ppermute | solution.py:603
  493.7 5.8 %conditional.31 = (bf16[2,128,2048]{2,1,0:T(8,128)(2,1)}, bf16[2,128,2048]{2,1,0:T(8,128)(2,1)}) conditional(s32[]{:T(128)} %convert_element_type.181, () %tuple.263, (bf16[2,128,2048]{2,1,0:T(8,128)(2,1)}, bf16[2,128,2048]{2,1,0:T(8,128)(2,1)S(1)}) %tuple.273), branch_computations={%region_43.44_spmd, %region_44.45_spmd} | conditional | bytes 8388704 | solution.py:532
  499.5 5.6 %shard_map.230 = f32[2,512,2048]{2,1,0:T(8,128)} custom-call(s32[3]{0:T(128)S(1)} %pad_add_fusion.1.at_ref, bf16[2,128,2048]{2,1,0:T(8,128)(2,1)} %get-tuple-element.506.refs_0_, bf16[2,128,2048]{2,1,0:T(8,128)(2,1)S(1)} %collective-permute-done.43.refs_1_, bf16[2,128,2048]{2,1,0:T(8,128)(2,1)} %get-tuple-element.525.refs_2_, ...), custom_call_target="tpu_custom_call" | custom-call | flops 1024 | bytes 1024 | tf_op jit(solution)/shard_map/pallas_call | solution.py:591
  (376 shorter events, 233.2 us)
Async XLA Ops:
  13.1 32.5 %collective-permute-start.17 = (bf16[128,1024]{1,0:T(8,128)(2,1)}, bf16[128,1024]{1,0:T(8,128)(2,1)S(1)}, u32[]{:S(2)}, u32[]{:S(2)}) collective-permute-start(bf16[128,1024]{1,0:T(8,128)(2,1)} %get-tuple-element.399.refs_0_), channel_id=1, source_target_pairs={{0,2},{2,4},{4,6},{1,3},{3,5},{5,7},{8,10},{10,12},{12,14},{9,11},... | collective-permute-start | bytes 786440 | tf_op jit(solution)/shard_map/ppermute | solution.py:650
  18.1 27.5 %collective-permute-start.18 = (bf16[128,1024]{1,0:T(8,128)(2,1)}, bf16[128,1024]{1,0:T(8,128)(2,1)S(1)}, u32[]{:S(2)}, u32[]{:S(2)}) collective-permute-start(bf16[128,1024]{1,0:T(8,128)(2,1)} %get-tuple-element.399.refs_0_), channel_id=1, source_target_pairs={{0,4},{2,6},{1,5},{3,7},{8,12},{10,14},{9,13},{11,15},{16,20},{18,... | collective-permute-start | bytes 786440 | tf_op jit(solution)/shard_map/ppermute | solution.py:650
  22.6 23.1 %collective-permute-start.19 = (bf16[128,1024]{1,0:T(8,128)(2,1)}, bf16[128,1024]{1,0:T(8,128)(2,1)S(1)}, u32[]{:S(2)}, u32[]{:S(2)}) collective-permute-start(bf16[128,1024]{1,0:T(8,128)(2,1)} %get-tuple-element.399.refs_0_), channel_id=1, source_target_pairs={{0,6},{1,7},{8,14},{9,15},{16,22},{17,23},{24,30},{25,31}} | collective-permute-start | bytes 786440 | tf_op jit(solution)/shard_map/ppermute | solution.py:650
  56.8 2.7 collective-permute-start.20
  59.9 14.0 %collective-permute-start.21 = (bf16[128,2048]{1,0:T(8,128)(2,1)S(1)}, bf16[128,2048]{1,0:T(8,128)(2,1)S(1)}, u32[]{:S(2)}, u32[]{:S(2)}) collective-permute-start(bf16[128,2048]{1,0:T(8,128)(2,1)S(1)} %slice.167), channel_id=1, source_target_pairs={{0,16},{8,24},{16,0},{24,8},{1,17},{9,25},{17,1},{25,9},{2,18},{10... | collective-permute-start | bytes 1572872 | tf_op jit(solution)/shard_map/ppermute | solution.py:603
  80.1 2.7 collective-permute-start.22
  80.1 14.8 %collective-permute-start.23 = (bf16[128,2048]{1,0:T(8,128)(2,1)S(1)}, bf16[128,2048]{1,0:T(8,128)(2,1)S(1)}, u32[]{:S(2)}, u32[]{:S(2)}) collective-permute-start(bf16[128,2048]{1,0:T(8,128)(2,1)S(1)} %get-tuple-element.566), channel_id=1, source_target_pairs={{0,16},{8,24},{16,0},{24,8},{1,17},{9,25},{17,1},{25,9},{2,18},{10... | collective-permute-start | bytes 1572872 | tf_op jit(solution)/shard_map/ppermute | solution.py:603
  84.0 29.9 %collective-permute-start.24 = (bf16[128,2048]{1,0:T(8,128)(2,1)}, bf16[128,2048]{1,0:T(8,128)(2,1)}, u32[]{:S(2)}, u32[]{:S(2)}) collective-permute-start(bf16[128,2048]{1,0:T(8,128)(2,1)} %slice.166), channel_id=1, source_target_pairs={{0,16},{8,24},{16,0},{24,8},{1,17},{9,25},{17,1},{25,9},{2,18},{10... | collective-permute-start | bytes 1572872 | tf_op jit(solution)/shard_map/ppermute | solution.py:603
  118.3 20.4 %collective-permute-start.25 = (bf16[128,2048]{1,0:T(8,128)(2,1)S(1)}, bf16[128,2048]{1,0:T(8,128)(2,1)}, u32[]{:S(2)}, u32[]{:S(2)}) collective-permute-start(bf16[128,2048]{1,0:T(8,128)(2,1)S(1)} %get-tuple-element.562), channel_id=1, source_target_pairs={{0,16},{8,24},{16,0},{24,8},{1,17},{9,25},{17,1},{25,9},{2,18},{10... | collective-permute-start | bytes 1572872 | tf_op jit(solution)/shard_map/ppermute | solution.py:603
  130.0 2.7 collective-permute-start.11
  134.0 38.2 %collective-permute-start.26 = (bf16[128,2048]{1,0:T(8,128)(2,1)}, bf16[128,2048]{1,0:T(8,128)(2,1)S(1)}, u32[]{:S(2)}, u32[]{:S(2)}) collective-permute-start(bf16[128,2048]{1,0:T(8,128)(2,1)} %bitcast.42), channel_id=1, source_target_pairs={{0,16},{8,24},{16,0},{24,8},{1,17},{9,25},{17,1},{25,9},{2,18},{10... | collective-permute-start | bytes 1572872 | tf_op jit(solution)/shard_map/ppermute | solution.py:603
  141.3 4.0 collective-permute-start.13
  168.3 77.3 %collective-permute-start.29 = (bf16[4,256,1408]{2,1,0:T(8,128)(2,1)}, bf16[4,256,1408]{2,1,0:T(8,128)(2,1)}, u32[]{:S(2)}, u32[]{:S(2)}) collective-permute-start(bf16[4,256,1408]{2,1,0:T(8,128)(2,1)} %shard_map.206), channel_id=1, source_target_pairs={{0,1},{1,0},{2,3},{3,2},{4,5},{5,4},{6,7},{7,6},{8,9},{9,8},{10,11... | collective-permute-start | bytes 8650760 | tf_op jit(solution)/shard_map/ppermute | solution.py:603
  175.8 18.8 %collective-permute-start.27 = (bf16[128,2048]{1,0:T(8,128)(2,1)}, bf16[128,2048]{1,0:T(8,128)(2,1)S(1)}, u32[]{:S(2)}, u32[]{:S(2)}) collective-permute-start(bf16[128,2048]{1,0:T(8,128)(2,1)} %get-tuple-element.427), channel_id=1, source_target_pairs={{0,16},{8,24},{16,0},{24,8},{1,17},{9,25},{17,1},{25,9},{2,18},{10... | collective-permute-start | bytes 1572872 | tf_op jit(solution)/shard_map/ppermute | solution.py:603
  189.2 2.7 collective-permute-start.14
  193.3 18.5 %collective-permute-start.28 = (bf16[128,2048]{1,0:T(8,128)(2,1)}, bf16[128,2048]{1,0:T(8,128)(2,1)}, u32[]{:S(2)}, u32[]{:S(2)}) collective-permute-start(bf16[128,2048]{1,0:T(8,128)(2,1)} %bitcast.44), channel_id=1, source_target_pairs={{0,16},{8,24},{16,0},{24,8},{1,17},{9,25},{17,1},{25,9},{2,18},{10... | collective-permute-start | bytes 1572872 | tf_op jit(solution)/shard_map/ppermute | solution.py:603
  216.0 49.7 %collective-permute-start.30 = (bf16[128,2048]{1,0:T(8,128)(2,1)}, bf16[128,2048]{1,0:T(8,128)(2,1)}, u32[]{:S(2)}, u32[]{:S(2)}) collective-permute-start(bf16[128,2048]{1,0:T(8,128)(2,1)} %get-tuple-element.440), channel_id=1, source_target_pairs={{0,16},{8,24},{16,0},{24,8},{1,17},{9,25},{17,1},{25,9},{2,18},{10... | collective-permute-start | bytes 1572872 | tf_op jit(solution)/shard_map/ppermute | solution.py:603
  217.0 65.7 %collective-permute-start.31 = (bf16[4,256,1408]{2,1,0:T(8,128)(2,1)}, bf16[4,256,1408]{2,1,0:T(8,128)(2,1)}, u32[]{:S(2)}, u32[]{:S(2)}) collective-permute-start(bf16[4,256,1408]{2,1,0:T(8,128)(2,1)} %shard_map.207), channel_id=1, source_target_pairs={{0,2},{2,0},{4,6},{6,4},{1,3},{3,1},{5,7},{7,5},{8,10},{10,8},{12,... | collective-permute-start | bytes 8650760 | tf_op jit(solution)/shard_map/ppermute | solution.py:603
  226.1 143.7 %collective-permute-start.36 = (bf16[4,256,1408]{2,1,0:T(8,128)(2,1)}, bf16[4,256,1408]{2,1,0:T(8,128)(2,1)}, u32[]{:S(2)}, u32[]{:S(2)}) collective-permute-start(bf16[4,256,1408]{2,1,0:T(8,128)(2,1)} %shard_map.208), channel_id=1, source_target_pairs={{0,1},{1,0},{2,3},{3,2},{4,5},{5,4},{6,7},{7,6},{8,9},{9,8},{10,11... | collective-permute-start | bytes 8650760 | tf_op jit(solution)/shard_map/ppermute | solution.py:603
  236.8 4.2 collective-permute-start.15
  244.5 48.2 %collective-permute-start.32 = (bf16[2,128,2048]{2,1,0:T(8,128)(2,1)}, bf16[2,128,2048]{2,1,0:T(8,128)(2,1)}, u32[]{:S(2)}, u32[]{:S(2)}) collective-permute-start(bf16[2,128,2048]{2,1,0:T(8,128)(2,1)} %get-tuple-element.447), channel_id=1, source_target_pairs={{0,16},{8,24},{16,0},{24,8},{1,17},{9,25},{17,1},{25,9},{2,18},{10... | collective-permute-start | bytes 3145736 | tf_op jit(solution)/shard_map/ppermute | solution.py:603
  254.8 62.6 %collective-permute-start.34 = (bf16[2,256,1408]{2,1,0:T(8,128)(2,1)}, bf16[2,256,1408]{2,1,0:T(8,128)(2,1)}, u32[]{:S(2)}, u32[]{:S(2)}) collective-permute-start(bf16[2,256,1408]{2,1,0:T(8,128)(2,1)} %get-tuple-element.449), channel_id=1, source_target_pairs={{0,2},{2,0},{4,6},{6,4},{1,3},{3,1},{5,7},{7,5},{8,10},{10,8},{12,... | collective-permute-start | bytes 4325384 | tf_op jit(solution)/shard_map/ppermute | solution.py:603
  292.2 116.8 %collective-permute-start.38 = (bf16[2,256,1408]{2,1,0:T(8,128)(2,1)}, bf16[2,256,1408]{2,1,0:T(8,128)(2,1)}, u32[]{:S(2)}, u32[]{:S(2)}) collective-permute-start(bf16[2,256,1408]{2,1,0:T(8,128)(2,1)} %get-tuple-element.456), channel_id=1, source_target_pairs={{0,1},{1,0},{2,3},{3,2},{4,5},{5,4},{6,7},{7,6},{8,9},{9,8},{10,11... | collective-permute-start | bytes 4325384 | tf_op jit(solution)/shard_map/ppermute | solution.py:603
  296.7 54.2 %collective-permute-start.33 = (bf16[2,128,2048]{2,1,0:T(8,128)(2,1)}, bf16[2,128,2048]{2,1,0:T(8,128)(2,1)}, u32[]{:S(2)}, u32[]{:S(2)}) collective-permute-start(bf16[2,128,2048]{2,1,0:T(8,128)(2,1)} %get-tuple-element.685.refs_0_), channel_id=1, source_target_pairs={{0,16},{8,24},{16,0},{24,8},{1,17},{9,25},{17,1},{25,9},{2,18},{10... | collective-permute-start | bytes 3145736 | tf_op jit(solution)/shard_map/ppermute | solution.py:603
  310.8 57.6 %collective-permute-start.35 = (bf16[2,2,128,512]{3,2,1,0:T(8,128)(2,1)}, bf16[2,2,128,512]{3,2,1,0:T(8,128)(2,1)}, u32[]{:S(2)}, u32[]{:S(2)}) collective-permute-start(bf16[2,2,128,512]{3,2,1,0:T(8,128)(2,1)} %get-tuple-element.466), channel_id=1, source_target_pairs={{0,2},{2,0},{4,6},{6,4},{1,3},{3,1},{5,7},{7,5},{8,10},{10,8},{12,... | collective-permute-start | bytes 1572872 | tf_op jit(solution)/shard_map/ppermute | solution.py:603
  320.8 91.5 %collective-permute-start.39 = (bf16[256,1408]{1,0:T(8,128)(2,1)}, bf16[256,1408]{1,0:T(8,128)(2,1)}, u32[]{:S(2)}, u32[]{:S(2)}) collective-permute-start(bf16[256,1408]{1,0:T(8,128)(2,1)} %get-tuple-element.468), channel_id=1, source_target_pairs={{0,4},{2,6},{4,0},{6,2},{1,5},{3,7},{5,1},{7,3},{8,12},{10,14},{12... | collective-permute-start | bytes 2162696 | tf_op jit(solution)/shard_map/ppermute | solution.py:603
  350.9 2.8 collective-permute-start.4
  353.7 3.0 collective-permute-start.5
  367.8 48.1 %collective-permute-start.40 = (bf16[4,1024,256]{2,1,0:T(8,128)(2,1)}, bf16[4,1024,256]{2,1,0:T(8,128)(2,1)}, u32[]{:S(2)}, u32[]{:S(2)}) collective-permute-start(bf16[4,1024,256]{2,1,0:T(8,128)(2,1)} %shard_map.215), channel_id=1, source_target_pairs={{0,1},{1,0},{2,3},{3,2},{4,5},{5,4},{6,7},{7,6},{8,9},{9,8},{10,11... | collective-permute-start | bytes 6291464 | tf_op jit(solution)/shard_map/ppermute | solution.py:603
  369.6 23.8 %collective-permute-start.37 = (bf16[2,128,512]{2,1,0:T(8,128)(2,1)S(1)}, bf16[2,128,512]{2,1,0:T(8,128)(2,1)S(1)}, u32[]{:S(2)}, u32[]{:S(2)}) collective-permute-start(bf16[2,128,512]{2,1,0:T(8,128)(2,1)S(1)} %get-tuple-element.483), channel_id=1, source_target_pairs={{0,4},{2,6},{4,0},{6,2},{1,5},{3,7},{5,1},{7,3},{8,12},{10,14},{12... | collective-permute-start | bytes 786440 | tf_op jit(solution)/shard_map/ppermute | solution.py:603
  378.8 47.0 %collective-permute-start.41 = (bf16[2,256,1408]{2,1,0:T(8,128)(2,1)}, bf16[2,256,1408]{2,1,0:T(8,128)(2,1)}, u32[]{:S(2)}, u32[]{:S(2)}) collective-permute-start(bf16[2,256,1408]{2,1,0:T(8,128)(2,1)} %get-tuple-element.485), channel_id=1, source_target_pairs={{0,2},{2,0},{4,6},{6,4},{1,3},{3,1},{5,7},{7,5},{8,10},{10,8},{12,... | collective-permute-start | bytes 4325384 | tf_op jit(solution)/shard_map/ppermute | solution.py:603
  401.5 4.2 collective-permute-start.16
  407.9 27.1 %collective-permute-start.42 = (bf16[2,128,2048]{2,1,0:T(8,128)(2,1)}, bf16[2,128,2048]{2,1,0:T(8,128)(2,1)S(1)}, u32[]{:S(2)}, u32[]{:S(2)}) collective-permute-start(bf16[2,128,2048]{2,1,0:T(8,128)(2,1)} %get-tuple-element.491), channel_id=1, source_target_pairs={{0,16},{8,24},{16,0},{24,8},{1,17},{9,25},{17,1},{25,9},{2,18},{10... | collective-permute-start | bytes 3145736 | tf_op jit(solution)/shard_map/ppermute | solution.py:603
  412.3 34.6 %collective-permute-start.44 = (bf16[256,1408]{1,0:T(8,128)(2,1)}, bf16[256,1408]{1,0:T(8,128)(2,1)}, u32[]{:S(2)}, u32[]{:S(2)}) collective-permute-start(bf16[256,1408]{1,0:T(8,128)(2,1)} %get-tuple-element.493), channel_id=1, source_target_pairs={{0,4},{2,6},{4,0},{6,2},{1,5},{3,7},{5,1},{7,3},{8,12},{10,14},{12... | collective-permute-start | bytes 2162696 | tf_op jit(solution)/shard_map/ppermute | solution.py:603
  423.0 58.0 %collective-permute-start.47 = (bf16[2,1024,256]{2,1,0:T(8,128)(2,1)}, bf16[2,1024,256]{2,1,0:T(8,128)(2,1)}, u32[]{:S(2)}, u32[]{:S(2)}) collective-permute-start(bf16[2,1024,256]{2,1,0:T(8,128)(2,1)} %get-tuple-element.496), channel_id=1, source_target_pairs={{0,2},{2,0},{4,6},{6,4},{1,3},{3,1},{5,7},{7,5},{8,10},{10,8},{12,... | collective-permute-start | bytes 3145736 | tf_op jit(solution)/shard_map/ppermute | solution.py:603
  429.1 57.0 %collective-permute-start.49 = (bf16[256,1408]{1,0:T(8,128)(2,1)}, bf16[256,1408]{1,0:T(8,128)(2,1)}, u32[]{:S(2)}, u32[]{:S(2)}) collective-permute-start(bf16[256,1408]{1,0:T(8,128)(2,1)} %get-tuple-element.498), channel_id=1, source_target_pairs={{0,4},{2,6},{4,0},{6,2},{1,5},{3,7},{5,1},{7,3},{8,12},{10,14},{12... | collective-permute-start | bytes 2162696 | tf_op jit(solution)/shard_map/ppermute | solution.py:603
  432.7 17.0 %collective-permute-start.45 = (bf16[4,128,256]{2,1,0:T(8,128)(2,1)}, bf16[4,128,256]{2,1,0:T(8,128)(2,1)}, u32[]{:S(2)}, u32[]{:S(2)}) collective-permute-start(bf16[4,128,256]{2,1,0:T(8,128)(2,1)} %shard_map.221), channel_id=1, source_target_pairs={{0,1},{1,0},{2,3},{3,2},{4,5},{5,4},{6,7},{7,6},{8,9},{9,8},{10,11... | collective-permute-start | bytes 786440 | tf_op jit(solution)/shard_map/ppermute | solution.py:603
  436.7 2.9 collective-permute-start.8
  439.5 54.2 %collective-permute-start.43 = (bf16[2,128,2048]{2,1,0:T(8,128)(2,1)}, bf16[2,128,2048]{2,1,0:T(8,128)(2,1)S(1)}, u32[]{:S(2)}, u32[]{:S(2)}) collective-permute-start(bf16[2,128,2048]{2,1,0:T(8,128)(2,1)} %get-tuple-element.506.refs_0_), channel_id=1, source_target_pairs={{0,16},{8,24},{16,0},{24,8},{1,17},{9,25},{17,1},{25,9},{2,18},{10... | collective-permute-start | bytes 3145736 | tf_op jit(solution)/shard_map/ppermute | solution.py:603
  453.1 30.7 %collective-permute-start.48 = (bf16[2,128,256]{2,1,0:T(8,128)(2,1)}, bf16[2,128,256]{2,1,0:T(8,128)(2,1)S(1)}, u32[]{:S(2)}, u32[]{:S(2)}) collective-permute-start(bf16[2,128,256]{2,1,0:T(8,128)(2,1)} %get-tuple-element.511), channel_id=1, source_target_pairs={{0,2},{2,0},{4,6},{6,4},{1,3},{3,1},{5,7},{7,5},{8,10},{10,8},{12,... | collective-permute-start | bytes 393224 | tf_op jit(solution)/shard_map/ppermute | solution.py:603
  454.5 11.2 %collective-permute-start.46 = (f32[2,2048]{1,0:T(2,128)}, f32[2,2048]{1,0:T(2,128)S(1)}, u32[]{:S(2)}, u32[]{:S(2)}) collective-permute-start(f32[2,2048]{1,0:T(2,128)} %shard_map.224.a_ref), channel_id=1, source_target_pairs={{0,16},{8,24},{16,0},{24,8},{1,17},{9,25},{17,1},{25,9},{2,18},{10... | collective-permute-start | bytes 49160 | tf_op jit(solution)/shard_map/ppermute | solution.py:603
  467.6 21.3 %collective-permute-start.50 = (f32[2,2048]{1,0:T(2,128)}, f32[2,2048]{1,0:T(2,128)S(1)}, u32[]{:S(2)}, u32[]{:S(2)}) collective-permute-start(f32[2,2048]{1,0:T(2,128)} %shard_map.225.a_ref), channel_id=1, source_target_pairs={{0,2},{2,0},{4,6},{6,4},{1,3},{3,1},{5,7},{7,5},{8,10},{10,8},{12,... | collective-permute-start | bytes 49160 | tf_op jit(solution)/shard_map/ppermute | solution.py:603
  483.8 38.5 %collective-permute-start.54 = (bf16[1024,256]{1,0:T(8,128)(2,1)}, bf16[1024,256]{1,0:T(8,128)(2,1)S(1)}, u32[]{:S(2)}, u32[]{:S(2)}) collective-permute-start(bf16[1024,256]{1,0:T(8,128)(2,1)} %get-tuple-element.519), channel_id=1, source_target_pairs={{0,4},{2,6},{4,0},{6,2},{1,5},{3,7},{5,1},{7,3},{8,12},{10,14},{12... | collective-permute-start | bytes 1572872 | tf_op jit(solution)/shard_map/ppermute | solution.py:603
  490.8 16.7 %collective-permute-start.51 = (f32[2,2048]{1,0:T(2,128)}, f32[2,2048]{1,0:T(2,128)S(1)}, u32[]{:S(2)}, u32[]{:S(2)}) collective-permute-start(f32[2,2048]{1,0:T(2,128)} %shard_map.229.a_ref), channel_id=1, source_target_pairs={{0,4},{2,6},{4,0},{6,2},{1,5},{3,7},{5,1},{7,3},{8,12},{10,14},{12... | collective-permute-start | bytes 49160 | tf_op jit(solution)/shard_map/ppermute | solution.py:603
  493.7 3.0 collective-permute-start.6
  496.8 2.8 collective-permute-start.7
  509.4 3.9 collective-permute-start.52
  510.0 6.7 %collective-permute-start.53 = (bf16[128,256]{1,0:T(8,128)(2,1)S(1)}, bf16[128,256]{1,0:T(8,128)(2,1)S(1)}, u32[]{:S(2)}, u32[]{:S(2)}) collective-permute-start(bf16[128,256]{1,0:T(8,128)(2,1)S(1)} %copy-done.75), channel_id=1, source_target_pairs={{0,4},{2,6},{4,0},{6,2},{1,5},{3,7},{5,1},{7,3},{8,12},{10,14},{12... | collective-permute-start | bytes 196616 | tf_op jit(solution)/shard_map/ppermute | solution.py:603
  (89 other events, 555.9 us)

commit v5 on v4

--- a/solution.py
+++ b/solution.py
@@ -780,9 +780,14 @@
         )
         order.mark(dq_t[s])
 
-    def place_all(part, got, dtype, us=0):
-        far = sealed(core_swaps, part, order.take(got))
-        return order.mark(place(at, [part, got, *far], dtype, us))
+    def swap_quarters(part, got):
+        got = order.take(got)
+        far = sealed(core_swaps, part, got)
+        order.mark(far[1])
+        return [part, got, *far]
+
+    def put_quarters(quarters, dtype, us=0):
+        return order.mark(place(at, [order.take(quarters[0]), *quarters[1:]], dtype, us))
 
     last = seqs - 1
     down_job.first(order, [(cts, hidden)], 0)
@@ -816,7 +821,7 @@
     kept_kv, send = sealed(lambda *xs: (jnp.stack(xs[0::2]), jnp.stack(xs[1::2])), *keep_send)
     got_kv = swap(order.mark(send), "context", n_context, 0)
     down_job.third(order, 0)
-    layer_out = place_all(out_own, got_out, BF16, 0)
+    quarters = swap_quarters(out_own, got_out)
     mix_job.first(order, [(d_low, o_t), ([h1] * seqs, dq_t)], 0)
 
     def add_kv(kept, got):
@@ -825,7 +830,8 @@
 
     kept_kv, send = sealed(add_kv, kept_kv, order.take(got_kv))
     got_kv = swap(order.mark(send), "context", n_context, 1)
-    gate_job.second(order, 0)
+    gate_job.second(order)
+    layer_out = put_quarters(quarters, BF16)
 
     def input_partial(kept, got, *parts):
         both = merge(at, kept, got, cos_rows, sine_rows)
@@ -872,7 +878,7 @@
     kv_job.third(order, 0)
     gate_sum = gate_job.final(order, [(BLOCK, False)], 0)
     hop(4)
-    grad_tokens = place_all(grad_own, got_grad, F32, 0)
+    grad_tokens = put_quarters(swap_quarters(grad_own, got_grad), F32)
     hop(0)
     while hop():
         pass
@@ -880,7 +886,7 @@
     gain_sum = lax.dynamic_slice_in_dim(gain_sum, (me_c * n_dp + lax.axis_index("dp")) * per, per, 1)
 
     if fast:
-        key_sum, value_sum = kv_job.final(order, [(head, True), (head, True)], 1)
+        key_sum, value_sum = (x.T for x in kv_job.final(order, [(head, False), (head, False)], 1))
         output_sum, query_sum = mix_job.final(order, [(wide, False), (wide, True)])
     else:
 

time: 534 us -> 532 us (level)
    unnamed x135 -> x129, local copies, waits for them, and re-layouts: 11.9 us -> 9.44 us
  transfers between devices with their start and end apart: 55 -> 55, of which waited for: 26 -> 25; matrix products, arithmetic and copies ran while one was open for 26% -> 25% of each run, Pallas kernels for 29% -> 29%
where the time goes in v5:
time: 532 us; the launch traced here: 523 us
  Pallas kernels  171 us (32%)
  waiting for transfers between devices  111 us (21%)
  matrix products  82.6 us (16%)
  starting transfers between devices  79.6 us (15%)
  other arithmetic  44.7 us (8%)
  local copies, waits for them, and re-layouts  32.9 us (6%)
    ppermute x52, waiting for transfers between devices, swap(): return lax.ppermute(x, axis, [(i, i ^ 1 << bit) for i in range(size)])  111 us
    dot_general x15, matrix products, dot(): lax.dot_general(left, right, (dims, ((), ())), preferred_element_type=F32)  82.6 us
    pallas_call x10, Pallas kernels, grad_blocks(): pl.pallas_call(functools.partial(grad_kernel, groups, recv is not None, s...  72.3 us
    ppermute x52, starting transfers between devices, swap(): return lax.ppermute(x, axis, [(i, i ^ 1 << bit) for i in range(size)])  68.9 us
    pallas_call x2, Pallas kernels, attend_back(): pl.pallas_call(functools.partial(back_kernel, far_count), grid_spec=pltpu...  21.3 us
    pallas_call x5, Pallas kernels, add_send(): pl.pallas_call(add_send_kernel, out_shape=[jax.ShapeDtypeStruct(shape, BF...  14.5 us
    pallas_call x2, Pallas kernels, attend(): pl.pallas_call(functools.partial(attend_kernel, far_count), grid_spec=plt...  14.2 us
    pallas_call x5, Pallas kernels, add_last(): pl.pallas_call(functools.partial(add_last_kernel, turned), out_shape=[jax...  12.9 us
  transfers between devices with their start and end apart: 55, of which 25 were waited for; matrix products, arithmetic and copies ran while one was open for 25% of the time, Pallas kernels for 29%

profile of v5, /device:TPU:0, one launch (start us, length us, event | category | flops | bytes accessed | tf_op | source)
XLA Modules:
  0.0 523.4 jit_solution(9075977911054600949)
XLA Ops:
  4.2 8.8 %shard_map.203 = (bf16[1024,2048]{1,0:T(8,128)(2,1)}, bf16[512,1024]{1,0:T(8,128)(2,1)}, bf16[128,1024]{1,0:T(8,128)(2,1)}) custom-call(s32[3]{0:T(128)S(1)} %pad_add_fusion.1.at_ref, bf16[1024,2048]{1,0:T(8,128)(2,1)} %bitcast.111, f32[1,2048]{1,0:T(1,128)} %bitcast.134, bf16[2048,512]{1,0:T(8,128)(2,1)} %wq_ref.1, ...), custom_call_target="tpu_custom_call" | custom-call | flops 1024 | bytes 1024 | tf_op jit(solution)/shard_map/pallas_call | solution.py:70
  13.0 4.9 collective-permute-start.17
  17.9 4.5 collective-permute-start.18
  26.8 7.8 %fusion.34 = f32[512,1408]{1,0:T(8,128)} fusion(bf16[1408,2048]{1,0:T(8,128)(2,1)} %param.54, bf16[128,2048]{1,0:T(8,128)(2,1)S(1)} %get-tuple-element.584, bf16[128,2048]{1,0:T(8,128)(2,1)S(1)} %get-tuple-element.585, bf16[128,2048]{1,0:T(8,128)(2,1)S(1)} %get-tuple-element.586, bf16[128,2048]{1,0:T(8,128)(2,1)S(1)} %get-tuple-element.583), kind=kOutput, calls=%fused_computation.150 | convolution fusion | flops 2961178624 | bytes 10747904 | tf_op jit(solution)/shard_map/dot_general | solution.py:31
  36.3 8.6 %fusion.33 = f32[512,1408]{1,0:T(8,128)} fusion(bf16[1408,2048]{1,0:T(8,128)(2,1)} %param.54, bf16[128,2048]{1,0:T(8,128)(2,1)S(1)} %get-tuple-element.580, bf16[128,2048]{1,0:T(8,128)(2,1)S(1)} %get-tuple-element.581, bf16[128,2048]{1,0:T(8,128)(2,1)S(1)} %get-tuple-element.582, bf16[128,2048]{1,0:T(8,128)(2,1)S(1)} %get-tuple-element.579), kind=kOutput, calls=%fused_computation.149 | convolution fusion | flops 2961178624 | bytes 10747904 | tf_op jit(solution)/shard_map/dot_general | solution.py:31
  47.1 7.3 %shard_map.204 = (bf16[8,128,512]{2,1,0:T(8,128)(2,1)}, bf16[512,512]{1,0:T(8,128)(2,1)}, f32[512,512]{1,0:T(8,128)}) custom-call(s32[3]{0:T(128)S(1)} %pad_add_fusion.1.at_ref, bf16[512,1024]{1,0:T(8,128)(2,1)} %get-tuple-element.409.q_ref, s32[2,4,512]{2,1,0:T(4,128)} %pad_add_fusion.seg_ref, bf16[128,1024]{1,0:T(8,128)(2,1)} %get-tuple-element.401.refs_0_, ...), custom_call_target="tpu_custom_call" | custom-call | flops 1024 | bytes 1024 | tf_op jit(solution)/shard_map/pallas_call | solution.py:186
  61.5 6.9 %shard_map.205 = (bf16[8,128,512]{2,1,0:T(8,128)(2,1)}, bf16[512,512]{1,0:T(8,128)(2,1)}, f32[512,512]{1,0:T(8,128)}) custom-call(s32[3]{0:T(128)S(1)} %pad_add_fusion.1.at_ref, bf16[512,1024]{1,0:T(8,128)(2,1)} %get-tuple-element.409.q_ref, s32[2,4,512]{2,1,0:T(4,128)} %pad_add_fusion.seg_ref, bf16[128,1024]{1,0:T(8,128)(2,1)} %get-tuple-element.401.refs_0_, ...), custom_call_target="tpu_custom_call" | custom-call | flops 1024 | bytes 1024 | tf_op jit(solution)/shard_map/pallas_call | solution.py:186
  68.4 5.5 %collective-permute-done.21 = bf16[128,2048]{1,0:T(8,128)(2,1)S(1)} collective-permute-done((bf16[128,2048]{1,0:T(8,128)(2,1)S(1)}, bf16[128,2048]{1,0:T(8,128)(2,1)S(1)}, u32[]{:S(2)}, u32[]{:S(2)}) %collective-permute-start.21) | collective-permute-done | bytes 524320 | tf_op jit(solution)/shard_map/ppermute | solution.py:603
  85.5 9.4 %collective-permute-done.23 = bf16[128,2048]{1,0:T(8,128)(2,1)S(1)} collective-permute-done((bf16[128,2048]{1,0:T(8,128)(2,1)S(1)}, bf16[128,2048]{1,0:T(8,128)(2,1)S(1)}, u32[]{:S(2)}, u32[]{:S(2)}) %collective-permute-start.23) | collective-permute-done | bytes 524320 | tf_op jit(solution)/shard_map/ppermute | solution.py:603
  94.9 18.9 %conditional.16 = (bf16[512,2048]{1,0:T(8,128)(2,1)}, bf16[512,1408]{1,0:T(8,128)(2,1)S(1)}, bf16[512,1408]{1,0:T(8,128)(2,1)S(1)}, bf16[512,1408]{1,0:T(8,128)(2,1)S(1)}) conditional(s32[]{:T(128)} %convert_element_type.181, () %tuple.196, (bf16[128,2048]{1,0:T(8,128)(2,1)S(1)}, bf16[128,2048]{1,0:T(8,128)(2,1)S(1)}, bf16[2048,1408]{1,0:T(8,128)(2,1)}, ...), branch_computations={%region_5.6_spmd, %region_6.7_spmd} | conditional | flops 5917114368 | bytes 65929404 | solution.py:532
  100.4 7.2 %fusion.40 = f32[512,1408]{1,0:T(8,128)S(1)} fusion(bf16[512,2048]{1,0:T(8,128)(2,1)} %constant_dynamic-update-slice_fusion, bf16[2048,1408]{1,0:T(8,128)(2,1)} %get-tuple-element.168), kind=kOutput, calls=%fused_computation.154 | convolution fusion | flops 2952790016 | bytes 10747904 | tf_op jit(solution)/shard_map/cond/branch_1_fun/dot_general | solution.py:31
  107.6 6.2 %multiply_convert_fusion = (bf16[512,1408]{1,0:T(8,128)(2,1)S(1)}, bf16[512,1408]{1,0:T(8,128)(2,1)S(1)}, bf16[512,1408]{1,0:T(8,128)(2,1)S(1)}) fusion(f32[512,1408]{1,0:T(8,128)S(1)} %copy-done.77, f32[512,1408]{1,0:T(8,128)S(1)} %fusion.40, bf16[512,2048]{1,0:T(8,128)(2,1)} %constant_dynamic-update-slice_fusion, bf16[2048,1408]{1,0:T(8,128)(2,1)S(1)} %bitcast.141), kind=kOutput, calls=%fused_computation | convolution fusion | flops 2964324352 | bytes 17956864 | tf_op jit(solution)/shard_map/cond/branch_1_fun/dot_general | solution.py:31
  120.5 13.4 %conditional.17 = (bf16[1,128,2048]{2,1,0:T(8,128)(2,1)}, f32[128,2048]{1,0:T(8,128)S(1)}) conditional(s32[]{:T(128)} %convert_element_type.181, () %tuple.213, (bf16[512,1408]{1,0:T(8,128)(2,1)S(1)}, bf16[2048,1408]{1,0:T(8,128)(2,1)}, bf16[512,1408]{1,0:T(8,128)(2,1)}, bf16[2048,1408]{1,0:T(8,128)(2,1)}) %tuple.371), branch_computations={%region_8.9_spmd, %region_9.10_spmd} | conditional | flops 5909250048 | bytes 67371120 | solution.py:532
  120.5 5.6 %fusion.41 = f32[512,2048]{1,0:T(8,128)S(1)} fusion(bf16[512,1408]{1,0:T(8,128)(2,1)S(1)} %get-tuple-element.170, bf16[2048,1408]{1,0:T(8,128)(2,1)} %get-tuple-element.171), kind=kOutput, calls=%fused_computation.155 | convolution fusion | flops 2952790016 | bytes 11403264 | tf_op jit(solution)/shard_map/cond/branch_1_fun/dot_general | solution.py:31
  134.5 4.4 pad_maximum_fusion.4
  138.9 21.2 %conditional.18 = (bf16[512,2048]{1,0:T(8,128)(2,1)}, bf16[512,1408]{1,0:T(8,128)(2,1)}, bf16[512,1408]{1,0:T(8,128)(2,1)S(1)}, bf16[512,1408]{1,0:T(8,128)(2,1)}) conditional(s32[]{:T(128)} %convert_element_type.181, () %tuple.212, (bf16[128,2048]{1,0:T(8,128)(2,1)S(1)}, bf16[128,2048]{1,0:T(8,128)(2,1)}, bf16[2048,1408]{1,0:T(8,128)(2,1)S(1)}, ...), branch_computations={%region_10.11_spmd, %region_11.12_spmd} | conditional | flops 5917114368 | bytes 48627852 | solution.py:532
  146.1 6.5 %fusion.42 = f32[512,1408]{1,0:T(8,128)S(1)} fusion(bf16[512,2048]{1,0:T(8,128)(2,1)} %constant_dynamic-update-slice_fusion.4, bf16[2048,1408]{1,0:T(8,128)(2,1)} %get-tuple-element.179), kind=kOutput, calls=%fused_computation.156 | convolution fusion | flops 2952790016 | bytes 10747904 | tf_op jit(solution)/shard_map/cond/branch_1_fun/dot_general | solution.py:31
  152.6 7.5 %multiply_convert_fusion.3 = (bf16[512,1408]{1,0:T(8,128)(2,1)}, bf16[512,1408]{1,0:T(8,128)(2,1)S(1)}, bf16[512,1408]{1,0:T(8,128)(2,1)}) fusion(f32[512,1408]{1,0:T(8,128)S(1)} %copy-done.76, f32[512,1408]{1,0:T(8,128)S(1)} %fusion.42, bf16[512,2048]{1,0:T(8,128)(2,1)} %constant_dynamic-update-slice_fusion.4, bf16[2048,1408]{1,0:T(8,128)(2,1)S(1)} %get-tuple-element.178), kind=kOutput, calls=%fused_computation.13 | convolution fusion | flops 2964324352 | bytes 17956864 | tf_op jit(solution)/shard_map/cond/branch_1_fun/dot_general | solution.py:31
  160.1 8.2 %shard_map.206 = bf16[4,256,1408]{2,1,0:T(8,128)(2,1)} custom-call(s32[4]{0:T(128)} %add_add_fusion.2.table_ref, bf16[512,1408]{1,0:T(8,128)(2,1)} %copy-done.12, bf16[512,2048]{1,0:T(8,128)(2,1)} %get-tuple-element.424.refs_1_.refs_2_, bf16[512,2048]{1,0:T(8,128)(2,1)} %get-tuple-element.424.refs_1_.refs_2_, bf16[512,1408]{1,0:T(8,128)(2,1)} %get-tuple-element.447.refs_3_, ...), custom_call_target="tpu_custom_call" | custom-call | flops 1024 | bytes 1024 | tf_op jit(solution)/shard_map/pallas_call | solution.py:453
  178.5 14.8 %conditional.20 = (bf16[1,128,2048]{2,1,0:T(8,128)(2,1)}, f32[128,2048]{1,0:T(8,128)S(1)}) conditional(s32[]{:T(128)} %convert_element_type.181, () %tuple.221, (bf16[512,1408]{1,0:T(8,128)(2,1)S(1)}, bf16[2048,1408]{1,0:T(8,128)(2,1)}, bf16[512,1408]{1,0:T(8,128)(2,1)}, bf16[2048,1408]{1,0:T(8,128)(2,1)}) %tuple.223), branch_computations={%region_16.17_spmd, %region_17.18_spmd} | conditional | flops 5909250048 | bytes 61603924 | solution.py:532
  178.5 5.6 %fusion.43 = f32[512,2048]{1,0:T(8,128)S(1)} fusion(bf16[512,1408]{1,0:T(8,128)(2,1)S(1)} %get-tuple-element.189, bf16[2048,1408]{1,0:T(8,128)(2,1)} %get-tuple-element.190), kind=kOutput, calls=%fused_computation.157 | convolution fusion | flops 2952790016 | bytes 11403264 | tf_op jit(solution)/shard_map/cond/branch_1_fun/dot_general | solution.py:31
  184.1 5.0 fusion.4
  194.6 9.3 %conditional.21 = ((bf16[512,512]{1,0:T(8,128)(2,1)}, bf16[512,2048]{1,0:T(8,128)(2,1)S(1)})) conditional(s32[]{:T(128)} %convert_element_type.181, () %tuple.210, (bf16[128,2048]{1,0:T(8,128)(2,1)}, bf16[128,2048]{1,0:T(8,128)(2,1)S(1)}, bf16[512,2048]{1,0:T(8,128)(2,1)}) %tuple.225), branch_computations={%region_18.19_spmd, %region_19.20_spmd} | conditional | flops 1024 | bytes 10486956 | solution.py:532
  203.9 8.0 %shard_map.207 = bf16[4,256,1408]{2,1,0:T(8,128)(2,1)} custom-call(s32[4]{0:T(128)} %add_add_fusion.1.table_ref, bf16[512,1408]{1,0:T(8,128)(2,1)} %copy-done.48, bf16[512,2048]{1,0:T(8,128)(2,1)} %get-tuple-element.443.refs_1_.refs_2_, bf16[512,2048]{1,0:T(8,128)(2,1)} %get-tuple-element.443.refs_1_.refs_2_, bf16[512,1408]{1,0:T(8,128)(2,1)} %get-tuple-element.432.refs_3_, ...), custom_call_target="tpu_custom_call" | custom-call | flops 23000000512 | bytes 1024 | tf_op jit(solution)/shard_map/pallas_call | solution.py:453
  218.8 7.3 %shard_map.208 = bf16[4,256,1408]{2,1,0:T(8,128)(2,1)} custom-call(s32[4]{0:T(128)} %add_add_fusion.2.table_ref, bf16[512,1408]{1,0:T(8,128)(2,1)S(1)} %get-tuple-element.419.refs_0_, bf16[512,2048]{1,0:T(8,128)(2,1)} %get-tuple-element.443.refs_1_.refs_2_, bf16[512,2048]{1,0:T(8,128)(2,1)} %get-tuple-element.443.refs_1_.refs_2_, ...), custom_call_target="tpu_custom_call" | custom-call | flops 1024 | bytes 1024 | tf_op jit(solution)/shard_map/pallas_call | solution.py:453
  226.7 17.7 %conditional.23 = (bf16[2,128,2048]{2,1,0:T(8,128)(2,1)}, f32[2,128,2048]{2,1,0:T(8,128)}) conditional(s32[]{:T(128)} %convert_element_type.181, () %tuple.232, (bf16[512,1408]{1,0:T(8,128)(2,1)S(1)}, bf16[512,1408]{1,0:T(8,128)(2,1)}, bf16[1408,2048]{1,0:T(8,128)(2,1)}) %tuple.361), branch_computations={%region_24.25_spmd, %region_25.26_spmd} | conditional | flops 5916590080 | bytes 40108088 | solution.py:532
  226.7 9.9 %convolution_convert_fusion = bf16[1024,2048]{1,0:T(8,128)(2,1)S(1)} fusion(bf16[1408,2048]{1,0:T(8,128)(2,1)} %get-tuple-element.208, bf16[512,1408]{1,0:T(8,128)(2,1)} %get-tuple-element.207, bf16[512,1408]{1,0:T(8,128)(2,1)S(1)} %get-tuple-element.206), kind=kOutput, calls=%fused_computation.45 | convolution fusion | flops 5913444352 | bytes 12845056 | tf_op jit(solution)/shard_map/cond/branch_1_fun/dot_general | solution.py:31
  245.7 9.3 %shard_map.209 = (bf16[2,256,1408]{2,1,0:T(8,128)(2,1)}, bf16[2,256,1408]{2,1,0:T(8,128)(2,1)}) custom-call(s32[4]{0:T(128)} %add_add_fusion.table_ref, bf16[512,1408]{1,0:T(8,128)(2,1)} %copy-done.12, bf16[512,2048]{1,0:T(8,128)(2,1)} %get-tuple-element.424.refs_1_.refs_2_, bf16[512,2048]{1,0:T(8,128)(2,1)} %get-tuple-element.424.refs_1_.refs_2_, ...), custom_call_target="tpu_custom_call" | custom-call | flops 9200001024 | bytes 1024 | tf_op jit(solution)/shard_map/pallas_call | solution.py:453
  255.3 10.6 %shard_map.210 = (bf16[512,512]{1,0:T(8,128)(2,1)}, bf16[2,128,512]{2,1,0:T(8,128)(2,1)}, bf16[2,128,512]{2,1,0:T(8,128)(2,1)}) custom-call(s32[3]{0:T(128)S(1)} %pad_add_fusion.1.at_ref, bf16[8,128,512]{2,1,0:T(8,128)(2,1)} %get-tuple-element.445.qa_ref, bf16[512,512]{1,0:T(8,128)(2,1)S(1)} %copy-done.52, f32[512,512]{1,0:T(8,128)} %get-tuple-element.452.full_ref, ...), custom_call_target="tpu_custom_call" | custom-call | flops 23000000512 | bytes 1024 | tf_op jit(solution)/shard_map/pallas_call | solution.py:288
  265.9 9.9 %conditional.24 = ((bf16[512,512]{1,0:T(8,128)(2,1)}, bf16[512,2048]{1,0:T(8,128)(2,1)})) conditional(s32[]{:T(128)} %convert_element_type.181, () %tuple.238, (bf16[128,2048]{1,0:T(8,128)(2,1)}, bf16[128,2048]{1,0:T(8,128)(2,1)}, bf16[512,2048]{1,0:T(8,128)(2,1)}) %tuple.240), branch_computations={%region_26.27_spmd, %region_27.28_spmd} | conditional | flops 1024 | bytes 8389776 | solution.py:532
  271.0 4.7 branch_1_fun.4
  275.7 7.1 %collective-permute-done.31.refs_6_ = bf16[4,256,1408]{2,1,0:T(8,128)(2,1)} collective-permute-done((bf16[4,256,1408]{2,1,0:T(8,128)(2,1)}, bf16[4,256,1408]{2,1,0:T(8,128)(2,1)}, u32[]{:S(2)}, u32[]{:S(2)}) %collective-permute-start.31) | collective-permute-done | bytes 2883616 | tf_op jit(solution)/shard_map/ppermute | solution.py:603
  282.8 9.5 %shard_map.211 = (bf16[2,256,1408]{2,1,0:T(8,128)(2,1)}, bf16[2,256,1408]{2,1,0:T(8,128)(2,1)}) custom-call(s32[4]{0:T(128)} %add_add_fusion.3.table_ref, bf16[512,1408]{1,0:T(8,128)(2,1)} %copy-done.48, bf16[512,2048]{1,0:T(8,128)(2,1)} %get-tuple-element.443.refs_1_.refs_2_, bf16[512,2048]{1,0:T(8,128)(2,1)} %get-tuple-element.443.refs_1_.refs_2_, ...), custom_call_target="tpu_custom_call" | custom-call | flops 13800001536 | bytes 1024 | tf_op jit(solution)/shard_map/pallas_call | solution.py:453
  298.0 10.8 %shard_map.212 = (bf16[512,512]{1,0:T(8,128)(2,1)}, bf16[2,128,512]{2,1,0:T(8,128)(2,1)}, bf16[2,128,512]{2,1,0:T(8,128)(2,1)}) custom-call(s32[3]{0:T(128)S(1)} %pad_add_fusion.1.at_ref, bf16[8,128,512]{2,1,0:T(8,128)(2,1)} %get-tuple-element.454.qa_ref, bf16[512,512]{1,0:T(8,128)(2,1)} %get-tuple-element.462.do_ref, ...), custom_call_target="tpu_custom_call" | custom-call | flops 1024 | bytes 1024 | tf_op jit(solution)/shard_map/pallas_call | solution.py:288
  311.0 6.7 %collective-permute-start.35 = (bf16[2,2,128,512]{3,2,1,0:T(8,128)(2,1)}, bf16[2,2,128,512]{3,2,1,0:T(8,128)(2,1)}, u32[]{:S(2)}, u32[]{:S(2)}) collective-permute-start(bf16[2,2,128,512]{3,2,1,0:T(8,128)(2,1)} %get-tuple-element.469), channel_id=1, source_target_pairs={{0,2},{2,0},{4,6},{6,4},{1,3},{3,1},{5,7},{7,5},{8,10},{10,8},{12,... | collective-permute-start | bytes 1572872 | tf_op jit(solution)/shard_map/ppermute | solution.py:603
  321.1 29.9 %collective-permute-start.39 = (bf16[256,1408]{1,0:T(8,128)(2,1)}, bf16[256,1408]{1,0:T(8,128)(2,1)}, u32[]{:S(2)}, u32[]{:S(2)}) collective-permute-start(bf16[256,1408]{1,0:T(8,128)(2,1)} %get-tuple-element.471), channel_id=1, source_target_pairs={{0,4},{2,6},{4,0},{6,2},{1,5},{3,7},{5,1},{7,3},{8,12},{10,14},{12... | collective-permute-start | bytes 2162696 | tf_op jit(solution)/shard_map/ppermute | solution.py:603
  351.0 5.8 %conditional.27 = (bf16[2,128,2048]{2,1,0:T(8,128)(2,1)}, bf16[2,128,2048]{2,1,0:T(8,128)(2,1)}) conditional(s32[]{:T(128)} %convert_element_type.181, () %tuple.246, (bf16[2,128,2048]{2,1,0:T(8,128)(2,1)S(1)}, bf16[2,128,2048]{2,1,0:T(8,128)(2,1)}) %tuple.363), branch_computations={%region_32.33_spmd, %region_33.34_spmd} | conditional | bytes 8388704 | solution.py:532
  356.8 6.6 %shard_map.214 = bf16[4,1024,256]{2,1,0:T(8,128)(2,1)} custom-call(s32[4]{0:T(128)} %add_add_fusion.2.table_ref, bf16[512,512]{1,0:T(8,128)(2,1)} %get-tuple-element.407.refs_0_, bf16[512,2048]{1,0:T(8,128)(2,1)S(1)} %get-tuple-element.476.refs_1_.refs_2_, bf16[512,2048]{1,0:T(8,128)(2,1)S(1)} %get-tuple-element.476.refs_1_.refs_2_, ...), custom_call_target="tpu_custom_call" | custom-call | flops 1024 | bytes 1024 | tf_op jit(solution)/shard_map/pallas_call | solution.py:453
  365.4 9.4 %shard_map.215 = (bf16[2,256,1408]{2,1,0:T(8,128)(2,1)}, bf16[2,256,1408]{2,1,0:T(8,128)(2,1)}) custom-call(s32[4]{0:T(128)} %add_add_fusion.table_ref, bf16[512,1408]{1,0:T(8,128)(2,1)S(1)} %get-tuple-element.419.refs_0_, bf16[512,2048]{1,0:T(8,128)(2,1)} %get-tuple-element.443.refs_1_.refs_2_, bf16[512,2048]{1,0:T(8,128)(2,1)} %get-tuple-element.443.refs_1_.refs_2_, ...), custom_call_target="tpu_custom_call" | custom-call | flops 1024 | bytes 1024 | tf_op jit(solution)/shard_map/pallas_call | solution.py:453
  378.9 14.7 %collective-permute-done.37 = bf16[2,128,512]{2,1,0:T(8,128)(2,1)S(1)} collective-permute-done((bf16[2,128,512]{2,1,0:T(8,128)(2,1)S(1)}, bf16[2,128,512]{2,1,0:T(8,128)(2,1)S(1)}, u32[]{:S(2)}, u32[]{:S(2)}) %collective-permute-start.37) | collective-permute-done | bytes 262176 | tf_op jit(solution)/shard_map/ppermute | solution.py:603
  393.6 14.1 %conditional.29 = (bf16[2,128,2048]{2,1,0:T(8,128)(2,1)S(1)}, f32[2,128,2048]{2,1,0:T(8,128)S(1)}, bf16[128,512]{1,0:T(8,128)(2,1)S(1)}, bf16[128,512]{1,0:T(8,128)(2,1)S(1)}) conditional(s32[]{:T(128)} %convert_element_type.181, () %tuple.257, (bf16[512,512]{1,0:T(8,128)(2,1)S(1)}, bf16[512,512]{1,0:T(8,128)(2,1)S(1)}, ...), branch_computations={%region_36.37_spmd, %region_37.38_spmd} | conditional | flops 2694317056 | bytes 54789304 | solution.py:532
  416.2 7.2 %shard_map.219 = (bf16[2,1024,256]{2,1,0:T(8,128)(2,1)}, bf16[2,1024,256]{2,1,0:T(8,128)(2,1)}) custom-call(s32[4]{0:T(128)} %add_add_fusion.table_ref, bf16[512,512]{1,0:T(8,128)(2,1)} %get-tuple-element.407.refs_0_, bf16[512,2048]{1,0:T(8,128)(2,1)S(1)} %get-tuple-element.476.refs_1_.refs_2_, bf16[512,2048]{1,0:T(8,128)(2,1)S(1)} %get-tuple-element.476.refs_1_.refs_2_, ...), custom_call_target="tpu_custom_call" | custom-call | flops 1024 | bytes 1024 | tf_op jit(solution)/shard_map/pallas_call | solution.py:453
  435.7 4.5 conditional.30
  441.3 6.4 %collective-permute-done.43.got_ref = bf16[256,1408]{1,0:T(8,128)(2,1)} collective-permute-done((bf16[256,1408]{1,0:T(8,128)(2,1)}, bf16[256,1408]{1,0:T(8,128)(2,1)}, u32[]{:S(2)}, u32[]{:S(2)}) %collective-permute-start.43) | collective-permute-done | bytes 720928 | tf_op jit(solution)/shard_map/ppermute | solution.py:603
  456.3 10.0 %collective-permute-done.45.b_ref = f32[2,2048]{1,0:T(2,128)S(1)} collective-permute-done((f32[2,2048]{1,0:T(2,128)}, f32[2,2048]{1,0:T(2,128)S(1)}, u32[]{:S(2)}, u32[]{:S(2)}) %collective-permute-start.45) | collective-permute-done | bytes 16416 | tf_op jit(solution)/shard_map/ppermute | solution.py:603
  470.1 11.4 %collective-permute-done.46.recv_ref = bf16[2,1024,256]{2,1,0:T(8,128)(2,1)} collective-permute-done((bf16[2,1024,256]{2,1,0:T(8,128)(2,1)}, bf16[2,1024,256]{2,1,0:T(8,128)(2,1)}, u32[]{:S(2)}, u32[]{:S(2)}) %collective-permute-start.46) | collective-permute-done | bytes 1048608 | tf_op jit(solution)/shard_map/ppermute | solution.py:603
  494.3 5.8 %conditional.31 = (bf16[2,128,2048]{2,1,0:T(8,128)(2,1)}, bf16[2,128,2048]{2,1,0:T(8,128)(2,1)}) conditional(s32[]{:T(128)} %convert_element_type.181, () %tuple.255, (bf16[2,128,2048]{2,1,0:T(8,128)(2,1)}, bf16[2,128,2048]{2,1,0:T(8,128)(2,1)S(1)}) %tuple.276), branch_computations={%region_43.44_spmd, %region_44.45_spmd} | conditional | bytes 8388704 | solution.py:532
  500.1 5.6 %shard_map.230 = f32[2,512,2048]{2,1,0:T(8,128)} custom-call(s32[3]{0:T(128)S(1)} %pad_add_fusion.1.at_ref, bf16[2,128,2048]{2,1,0:T(8,128)(2,1)} %get-tuple-element.529.refs_0_, bf16[2,128,2048]{2,1,0:T(8,128)(2,1)S(1)} %collective-permute-done.50.refs_1_, bf16[2,128,2048]{2,1,0:T(8,128)(2,1)} %get-tuple-element.530.refs_2_, ...), custom_call_target="tpu_custom_call" | custom-call | flops 1024 | bytes 1024 | tf_op jit(solution)/shard_map/pallas_call | solution.py:591
  (370 shorter events, 230.8 us)
Async XLA Ops:
  13.0 32.6 %collective-permute-start.17 = (bf16[128,1024]{1,0:T(8,128)(2,1)}, bf16[128,1024]{1,0:T(8,128)(2,1)S(1)}, u32[]{:S(2)}, u32[]{:S(2)}) collective-permute-start(bf16[128,1024]{1,0:T(8,128)(2,1)} %get-tuple-element.401.refs_0_), channel_id=1, source_target_pairs={{0,2},{2,4},{4,6},{1,3},{3,5},{5,7},{8,10},{10,12},{12,14},{9,11},... | collective-permute-start | bytes 786440 | tf_op jit(solution)/shard_map/ppermute | solution.py:650
  17.9 27.6 %collective-permute-start.18 = (bf16[128,1024]{1,0:T(8,128)(2,1)}, bf16[128,1024]{1,0:T(8,128)(2,1)S(1)}, u32[]{:S(2)}, u32[]{:S(2)}) collective-permute-start(bf16[128,1024]{1,0:T(8,128)(2,1)} %get-tuple-element.401.refs_0_), channel_id=1, source_target_pairs={{0,4},{2,6},{1,5},{3,7},{8,12},{10,14},{9,13},{11,15},{16,20},{18,... | collective-permute-start | bytes 786440 | tf_op jit(solution)/shard_map/ppermute | solution.py:650
  22.4 23.2 %collective-permute-start.19 = (bf16[128,1024]{1,0:T(8,128)(2,1)}, bf16[128,1024]{1,0:T(8,128)(2,1)S(1)}, u32[]{:S(2)}, u32[]{:S(2)}) collective-permute-start(bf16[128,1024]{1,0:T(8,128)(2,1)} %get-tuple-element.401.refs_0_), channel_id=1, source_target_pairs={{0,6},{1,7},{8,14},{9,15},{16,22},{17,23},{24,30},{25,31}} | collective-permute-start | bytes 786440 | tf_op jit(solution)/shard_map/ppermute | solution.py:650
  56.8 2.7 collective-permute-start.20
  59.9 14.0 %collective-permute-start.21 = (bf16[128,2048]{1,0:T(8,128)(2,1)S(1)}, bf16[128,2048]{1,0:T(8,128)(2,1)S(1)}, u32[]{:S(2)}, u32[]{:S(2)}) collective-permute-start(bf16[128,2048]{1,0:T(8,128)(2,1)S(1)} %slice.167), channel_id=1, source_target_pairs={{0,16},{8,24},{16,0},{24,8},{1,17},{9,25},{17,1},{25,9},{2,18},{10... | collective-permute-start | bytes 1572872 | tf_op jit(solution)/shard_map/ppermute | solution.py:603
  80.1 2.7 collective-permute-start.22
  80.2 14.8 %collective-permute-start.23 = (bf16[128,2048]{1,0:T(8,128)(2,1)S(1)}, bf16[128,2048]{1,0:T(8,128)(2,1)S(1)}, u32[]{:S(2)}, u32[]{:S(2)}) collective-permute-start(bf16[128,2048]{1,0:T(8,128)(2,1)S(1)} %get-tuple-element.559), channel_id=1, source_target_pairs={{0,16},{8,24},{16,0},{24,8},{1,17},{9,25},{17,1},{25,9},{2,18},{10... | collective-permute-start | bytes 1572872 | tf_op jit(solution)/shard_map/ppermute | solution.py:603
  84.0 29.8 %collective-permute-start.24 = (bf16[128,2048]{1,0:T(8,128)(2,1)}, bf16[128,2048]{1,0:T(8,128)(2,1)}, u32[]{:S(2)}, u32[]{:S(2)}) collective-permute-start(bf16[128,2048]{1,0:T(8,128)(2,1)} %slice.166), channel_id=1, source_target_pairs={{0,16},{8,24},{16,0},{24,8},{1,17},{9,25},{17,1},{25,9},{2,18},{10... | collective-permute-start | bytes 1572872 | tf_op jit(solution)/shard_map/ppermute | solution.py:603
  118.3 20.6 %collective-permute-start.25 = (bf16[128,2048]{1,0:T(8,128)(2,1)S(1)}, bf16[128,2048]{1,0:T(8,128)(2,1)}, u32[]{:S(2)}, u32[]{:S(2)}) collective-permute-start(bf16[128,2048]{1,0:T(8,128)(2,1)S(1)} %get-tuple-element.555), channel_id=1, source_target_pairs={{0,16},{8,24},{16,0},{24,8},{1,17},{9,25},{17,1},{25,9},{2,18},{10... | collective-permute-start | bytes 1572872 | tf_op jit(solution)/shard_map/ppermute | solution.py:603
  129.9 2.7 collective-permute-start.11
  134.0 38.3 %collective-permute-start.26 = (bf16[128,2048]{1,0:T(8,128)(2,1)}, bf16[128,2048]{1,0:T(8,128)(2,1)S(1)}, u32[]{:S(2)}, u32[]{:S(2)}) collective-permute-start(bf16[128,2048]{1,0:T(8,128)(2,1)} %bitcast.44), channel_id=1, source_target_pairs={{0,16},{8,24},{16,0},{24,8},{1,17},{9,25},{17,1},{25,9},{2,18},{10... | collective-permute-start | bytes 1572872 | tf_op jit(solution)/shard_map/ppermute | solution.py:603
  141.2 4.0 collective-permute-start.13
  168.3 77.4 %collective-permute-start.29 = (bf16[4,256,1408]{2,1,0:T(8,128)(2,1)}, bf16[4,256,1408]{2,1,0:T(8,128)(2,1)}, u32[]{:S(2)}, u32[]{:S(2)}) collective-permute-start(bf16[4,256,1408]{2,1,0:T(8,128)(2,1)} %shard_map.206), channel_id=1, source_target_pairs={{0,1},{1,0},{2,3},{3,2},{4,5},{5,4},{6,7},{7,6},{8,9},{9,8},{10,11... | collective-permute-start | bytes 8650760 | tf_op jit(solution)/shard_map/ppermute | solution.py:603
  175.9 18.7 %collective-permute-start.27 = (bf16[128,2048]{1,0:T(8,128)(2,1)}, bf16[128,2048]{1,0:T(8,128)(2,1)S(1)}, u32[]{:S(2)}, u32[]{:S(2)}) collective-permute-start(bf16[128,2048]{1,0:T(8,128)(2,1)} %get-tuple-element.429), channel_id=1, source_target_pairs={{0,16},{8,24},{16,0},{24,8},{1,17},{9,25},{17,1},{25,9},{2,18},{10... | collective-permute-start | bytes 1572872 | tf_op jit(solution)/shard_map/ppermute | solution.py:603
  189.3 2.7 collective-permute-start.14
  193.3 18.6 %collective-permute-start.28 = (bf16[128,2048]{1,0:T(8,128)(2,1)}, bf16[128,2048]{1,0:T(8,128)(2,1)}, u32[]{:S(2)}, u32[]{:S(2)}) collective-permute-start(bf16[128,2048]{1,0:T(8,128)(2,1)} %bitcast.46), channel_id=1, source_target_pairs={{0,16},{8,24},{16,0},{24,8},{1,17},{9,25},{17,1},{25,9},{2,18},{10... | collective-permute-start | bytes 1572872 | tf_op jit(solution)/shard_map/ppermute | solution.py:603
  216.2 49.6 %collective-permute-start.30 = (bf16[128,2048]{1,0:T(8,128)(2,1)}, bf16[128,2048]{1,0:T(8,128)(2,1)}, u32[]{:S(2)}, u32[]{:S(2)}) collective-permute-start(bf16[128,2048]{1,0:T(8,128)(2,1)} %get-tuple-element.442), channel_id=1, source_target_pairs={{0,16},{8,24},{16,0},{24,8},{1,17},{9,25},{17,1},{25,9},{2,18},{10... | collective-permute-start | bytes 1572872 | tf_op jit(solution)/shard_map/ppermute | solution.py:603
  217.1 65.7 %collective-permute-start.31 = (bf16[4,256,1408]{2,1,0:T(8,128)(2,1)}, bf16[4,256,1408]{2,1,0:T(8,128)(2,1)}, u32[]{:S(2)}, u32[]{:S(2)}) collective-permute-start(bf16[4,256,1408]{2,1,0:T(8,128)(2,1)} %shard_map.207), channel_id=1, source_target_pairs={{0,2},{2,0},{4,6},{6,4},{1,3},{3,1},{5,7},{7,5},{8,10},{10,8},{12,... | collective-permute-start | bytes 8650760 | tf_op jit(solution)/shard_map/ppermute | solution.py:603
  226.1 139.3 %collective-permute-start.36 = (bf16[4,256,1408]{2,1,0:T(8,128)(2,1)}, bf16[4,256,1408]{2,1,0:T(8,128)(2,1)}, u32[]{:S(2)}, u32[]{:S(2)}) collective-permute-start(bf16[4,256,1408]{2,1,0:T(8,128)(2,1)} %shard_map.208), channel_id=1, source_target_pairs={{0,1},{1,0},{2,3},{3,2},{4,5},{5,4},{6,7},{7,6},{8,9},{9,8},{10,11... | collective-permute-start | bytes 8650760 | tf_op jit(solution)/shard_map/ppermute | solution.py:603
  236.8 4.2 collective-permute-start.15
  244.5 48.3 %collective-permute-start.32 = (bf16[2,128,2048]{2,1,0:T(8,128)(2,1)}, bf16[2,128,2048]{2,1,0:T(8,128)(2,1)}, u32[]{:S(2)}, u32[]{:S(2)}) collective-permute-start(bf16[2,128,2048]{2,1,0:T(8,128)(2,1)} %get-tuple-element.448), channel_id=1, source_target_pairs={{0,16},{8,24},{16,0},{24,8},{1,17},{9,25},{17,1},{25,9},{2,18},{10... | collective-permute-start | bytes 3145736 | tf_op jit(solution)/shard_map/ppermute | solution.py:603
  254.9 62.8 %collective-permute-start.33 = (bf16[2,256,1408]{2,1,0:T(8,128)(2,1)}, bf16[2,256,1408]{2,1,0:T(8,128)(2,1)}, u32[]{:S(2)}, u32[]{:S(2)}) collective-permute-start(bf16[2,256,1408]{2,1,0:T(8,128)(2,1)} %get-tuple-element.450), channel_id=1, source_target_pairs={{0,2},{2,0},{4,6},{6,4},{1,3},{3,1},{5,7},{7,5},{8,10},{10,8},{12,... | collective-permute-start | bytes 4325384 | tf_op jit(solution)/shard_map/ppermute | solution.py:603
  292.3 117.3 %collective-permute-start.38 = (bf16[2,256,1408]{2,1,0:T(8,128)(2,1)}, bf16[2,256,1408]{2,1,0:T(8,128)(2,1)}, u32[]{:S(2)}, u32[]{:S(2)}) collective-permute-start(bf16[2,256,1408]{2,1,0:T(8,128)(2,1)} %get-tuple-element.460), channel_id=1, source_target_pairs={{0,1},{1,0},{2,3},{3,2},{4,5},{5,4},{6,7},{7,6},{8,9},{9,8},{10,11... | collective-permute-start | bytes 4325384 | tf_op jit(solution)/shard_map/ppermute | solution.py:603
  296.8 54.2 %collective-permute-start.34 = (bf16[2,128,2048]{2,1,0:T(8,128)(2,1)}, bf16[2,128,2048]{2,1,0:T(8,128)(2,1)}, u32[]{:S(2)}, u32[]{:S(2)}) collective-permute-start(bf16[2,128,2048]{2,1,0:T(8,128)(2,1)} %get-tuple-element.678.refs_0_), channel_id=1, source_target_pairs={{0,16},{8,24},{16,0},{24,8},{1,17},{9,25},{17,1},{25,9},{2,18},{10... | collective-permute-start | bytes 3145736 | tf_op jit(solution)/shard_map/ppermute | solution.py:603
  311.0 53.0 %collective-permute-start.35 = (bf16[2,2,128,512]{3,2,1,0:T(8,128)(2,1)}, bf16[2,2,128,512]{3,2,1,0:T(8,128)(2,1)}, u32[]{:S(2)}, u32[]{:S(2)}) collective-permute-start(bf16[2,2,128,512]{3,2,1,0:T(8,128)(2,1)} %get-tuple-element.469), channel_id=1, source_target_pairs={{0,2},{2,0},{4,6},{6,4},{1,3},{3,1},{5,7},{7,5},{8,10},{10,8},{12,... | collective-permute-start | bytes 1572872 | tf_op jit(solution)/shard_map/ppermute | solution.py:603
  321.1 91.9 %collective-permute-start.39 = (bf16[256,1408]{1,0:T(8,128)(2,1)}, bf16[256,1408]{1,0:T(8,128)(2,1)}, u32[]{:S(2)}, u32[]{:S(2)}) collective-permute-start(bf16[256,1408]{1,0:T(8,128)(2,1)} %get-tuple-element.471), channel_id=1, source_target_pairs={{0,4},{2,6},{4,0},{6,2},{1,5},{3,7},{5,1},{7,3},{8,12},{10,14},{12... | collective-permute-start | bytes 2162696 | tf_op jit(solution)/shard_map/ppermute | solution.py:603
  351.0 2.8 collective-permute-start.4
  353.8 3.0 collective-permute-start.5
  363.4 52.8 %collective-permute-start.40 = (bf16[4,1024,256]{2,1,0:T(8,128)(2,1)}, bf16[4,1024,256]{2,1,0:T(8,128)(2,1)}, u32[]{:S(2)}, u32[]{:S(2)}) collective-permute-start(bf16[4,1024,256]{2,1,0:T(8,128)(2,1)} %shard_map.214), channel_id=1, source_target_pairs={{0,1},{1,0},{2,3},{3,2},{4,5},{5,4},{6,7},{7,6},{8,9},{9,8},{10,11... | collective-permute-start | bytes 6291464 | tf_op jit(solution)/shard_map/ppermute | solution.py:603
  365.2 28.4 %collective-permute-start.37 = (bf16[2,128,512]{2,1,0:T(8,128)(2,1)S(1)}, bf16[2,128,512]{2,1,0:T(8,128)(2,1)S(1)}, u32[]{:S(2)}, u32[]{:S(2)}) collective-permute-start(bf16[2,128,512]{2,1,0:T(8,128)(2,1)S(1)} %get-tuple-element.481), channel_id=1, source_target_pairs={{0,4},{2,6},{4,0},{6,2},{1,5},{3,7},{5,1},{7,3},{8,12},{10,14},{12... | collective-permute-start | bytes 786440 | tf_op jit(solution)/shard_map/ppermute | solution.py:603
  374.8 51.6 %collective-permute-start.41 = (bf16[2,256,1408]{2,1,0:T(8,128)(2,1)}, bf16[2,256,1408]{2,1,0:T(8,128)(2,1)}, u32[]{:S(2)}, u32[]{:S(2)}) collective-permute-start(bf16[2,256,1408]{2,1,0:T(8,128)(2,1)} %get-tuple-element.483), channel_id=1, source_target_pairs={{0,2},{2,0},{4,6},{6,4},{1,3},{3,1},{5,7},{7,5},{8,10},{10,8},{12,... | collective-permute-start | bytes 4325384 | tf_op jit(solution)/shard_map/ppermute | solution.py:603
  401.7 4.2 collective-permute-start.16
  408.7 26.9 %collective-permute-start.42 = (bf16[2,128,2048]{2,1,0:T(8,128)(2,1)}, bf16[2,128,2048]{2,1,0:T(8,128)(2,1)S(1)}, u32[]{:S(2)}, u32[]{:S(2)}) collective-permute-start(bf16[2,128,2048]{2,1,0:T(8,128)(2,1)} %copy-done.50), channel_id=1, source_target_pairs={{0,16},{8,24},{16,0},{24,8},{1,17},{9,25},{17,1},{25,9},{2,18},{10... | collective-permute-start | bytes 3145736 | tf_op jit(solution)/shard_map/ppermute | solution.py:603
  412.9 34.8 %collective-permute-start.43 = (bf16[256,1408]{1,0:T(8,128)(2,1)}, bf16[256,1408]{1,0:T(8,128)(2,1)}, u32[]{:S(2)}, u32[]{:S(2)}) collective-permute-start(bf16[256,1408]{1,0:T(8,128)(2,1)} %get-tuple-element.496), channel_id=1, source_target_pairs={{0,4},{2,6},{4,0},{6,2},{1,5},{3,7},{5,1},{7,3},{8,12},{10,14},{12... | collective-permute-start | bytes 2162696 | tf_op jit(solution)/shard_map/ppermute | solution.py:603
  423.4 58.1 %collective-permute-start.46 = (bf16[2,1024,256]{2,1,0:T(8,128)(2,1)}, bf16[2,1024,256]{2,1,0:T(8,128)(2,1)}, u32[]{:S(2)}, u32[]{:S(2)}) collective-permute-start(bf16[2,1024,256]{2,1,0:T(8,128)(2,1)} %get-tuple-element.499), channel_id=1, source_target_pairs={{0,2},{2,0},{4,6},{6,4},{1,3},{3,1},{5,7},{7,5},{8,10},{10,8},{12,... | collective-permute-start | bytes 3145736 | tf_op jit(solution)/shard_map/ppermute | solution.py:603
  429.7 56.9 %collective-permute-start.48 = (bf16[256,1408]{1,0:T(8,128)(2,1)}, bf16[256,1408]{1,0:T(8,128)(2,1)}, u32[]{:S(2)}, u32[]{:S(2)}) collective-permute-start(bf16[256,1408]{1,0:T(8,128)(2,1)} %get-tuple-element.501), channel_id=1, source_target_pairs={{0,4},{2,6},{4,0},{6,2},{1,5},{3,7},{5,1},{7,3},{8,12},{10,14},{12... | collective-permute-start | bytes 2162696 | tf_op jit(solution)/shard_map/ppermute | solution.py:603
  433.3 17.2 %collective-permute-start.44 = (bf16[4,128,256]{2,1,0:T(8,128)(2,1)}, bf16[4,128,256]{2,1,0:T(8,128)(2,1)}, u32[]{:S(2)}, u32[]{:S(2)}) collective-permute-start(bf16[4,128,256]{2,1,0:T(8,128)(2,1)} %shard_map.221), channel_id=1, source_target_pairs={{0,1},{1,0},{2,3},{3,2},{4,5},{5,4},{6,7},{7,6},{8,9},{9,8},{10,11... | collective-permute-start | bytes 786440 | tf_op jit(solution)/shard_map/ppermute | solution.py:603
  437.2 2.9 collective-permute-start.8
  440.1 54.2 %collective-permute-start.50 = (bf16[2,128,2048]{2,1,0:T(8,128)(2,1)}, bf16[2,128,2048]{2,1,0:T(8,128)(2,1)S(1)}, u32[]{:S(2)}, u32[]{:S(2)}) collective-permute-start(bf16[2,128,2048]{2,1,0:T(8,128)(2,1)} %get-tuple-element.529.refs_0_), channel_id=1, source_target_pairs={{0,16},{8,24},{16,0},{24,8},{1,17},{9,25},{17,1},{25,9},{2,18},{10... | collective-permute-start | bytes 3145736 | tf_op jit(solution)/shard_map/ppermute | solution.py:603
  453.9 30.4 %collective-permute-start.47 = (bf16[2,128,256]{2,1,0:T(8,128)(2,1)}, bf16[2,128,256]{2,1,0:T(8,128)(2,1)S(1)}, u32[]{:S(2)}, u32[]{:S(2)}) collective-permute-start(bf16[2,128,256]{2,1,0:T(8,128)(2,1)} %get-tuple-element.514), channel_id=1, source_target_pairs={{0,2},{2,0},{4,6},{6,4},{1,3},{3,1},{5,7},{7,5},{8,10},{10,8},{12,... | collective-permute-start | bytes 393224 | tf_op jit(solution)/shard_map/ppermute | solution.py:603
  455.2 11.0 %collective-permute-start.45 = (f32[2,2048]{1,0:T(2,128)}, f32[2,2048]{1,0:T(2,128)S(1)}, u32[]{:S(2)}, u32[]{:S(2)}) collective-permute-start(f32[2,2048]{1,0:T(2,128)} %shard_map.224.a_ref), channel_id=1, source_target_pairs={{0,16},{8,24},{16,0},{24,8},{1,17},{9,25},{17,1},{25,9},{2,18},{10... | collective-permute-start | bytes 49160 | tf_op jit(solution)/shard_map/ppermute | solution.py:603
  468.2 21.2 %collective-permute-start.49 = (f32[2,2048]{1,0:T(2,128)}, f32[2,2048]{1,0:T(2,128)S(1)}, u32[]{:S(2)}, u32[]{:S(2)}) collective-permute-start(f32[2,2048]{1,0:T(2,128)} %shard_map.225.a_ref), channel_id=1, source_target_pairs={{0,2},{2,0},{4,6},{6,4},{1,3},{3,1},{5,7},{7,5},{8,10},{10,8},{12,... | collective-permute-start | bytes 49160 | tf_op jit(solution)/shard_map/ppermute | solution.py:603
  484.3 35.6 %collective-permute-start.54 = (bf16[1024,256]{1,0:T(8,128)(2,1)}, bf16[1024,256]{1,0:T(8,128)(2,1)S(1)}, u32[]{:S(2)}, u32[]{:S(2)}) collective-permute-start(bf16[1024,256]{1,0:T(8,128)(2,1)} %get-tuple-element.522), channel_id=1, source_target_pairs={{0,4},{2,6},{4,0},{6,2},{1,5},{3,7},{5,1},{7,3},{8,12},{10,14},{12... | collective-permute-start | bytes 1572872 | tf_op jit(solution)/shard_map/ppermute | solution.py:603
  491.4 17.1 %collective-permute-start.51 = (f32[2,2048]{1,0:T(2,128)}, f32[2,2048]{1,0:T(2,128)S(1)}, u32[]{:S(2)}, u32[]{:S(2)}) collective-permute-start(f32[2,2048]{1,0:T(2,128)} %shard_map.229.a_ref), channel_id=1, source_target_pairs={{0,4},{2,6},{4,0},{6,2},{1,5},{3,7},{5,1},{7,3},{8,12},{10,14},{12... | collective-permute-start | bytes 49160 | tf_op jit(solution)/shard_map/ppermute | solution.py:603
  494.3 3.0 collective-permute-start.6
  497.3 2.8 collective-permute-start.7
  510.4 3.9 collective-permute-start.52
  510.9 6.7 %collective-permute-start.53 = (bf16[128,256]{1,0:T(8,128)(2,1)S(1)}, bf16[128,256]{1,0:T(8,128)(2,1)S(1)}, u32[]{:S(2)}, u32[]{:S(2)}) collective-permute-start(bf16[128,256]{1,0:T(8,128)(2,1)S(1)} %copy-done.73), channel_id=1, source_target_pairs={{0,4},{2,6},{4,0},{6,2},{1,5},{3,7},{5,1},{7,3},{8,12},{10,14},{12... | collective-permute-start | bytes 196616 | tf_op jit(solution)/shard_map/ppermute | solution.py:603
  (87 other events, 522.4 us)

commit v6 on v5

--- a/solution.py
+++ b/solution.py
@@ -820,7 +820,6 @@
     keep_send = [x for s in each for x in dkvs[s]]
     kept_kv, send = sealed(lambda *xs: (jnp.stack(xs[0::2]), jnp.stack(xs[1::2])), *keep_send)
     got_kv = swap(order.mark(send), "context", n_context, 0)
-    down_job.third(order, 0)
     quarters = swap_quarters(out_own, got_out)
     mix_job.first(order, [(d_low, o_t), ([h1] * seqs, dq_t)], 0)
 
@@ -831,6 +830,7 @@
     kept_kv, send = sealed(add_kv, kept_kv, order.take(got_kv))
     got_kv = swap(order.mark(send), "context", n_context, 1)
     gate_job.second(order)
+    down_job.third(order)
     layer_out = put_quarters(quarters, BF16)
 
     def input_partial(kept, got, *parts):

time: 532 us -> 556 us (1.045)
  waiting for transfers between devices: 111 us -> 135 us
    ppermute x52, waiting for transfers between devices: 111 us -> 135 us  [swap(): return lax.ppermute(x, axis, [(i, i ^ 1 << bit) for i in range(size)])]
  transfers between devices with their start and end apart: 55 -> 55, of which waited for: 25 -> 26; matrix products, arithmetic and copies ran while one was open for 25% -> 24% of each run, Pallas kernels for 29% -> 28%
where the time goes in v6:
time: 556 us; the launch traced here: 547 us
  Pallas kernels  171 us (31%)
  waiting for transfers between devices  135 us (24%)
  matrix products  82.5 us (15%)
  starting transfers between devices  78.8 us (14%)
  other arithmetic  44.6 us (8%)
  local copies, waits for them, and re-layouts  33.1 us (6%)
    ppermute x52, waiting for transfers between devices, swap(): return lax.ppermute(x, axis, [(i, i ^ 1 << bit) for i in range(size)])  135 us
    dot_general x15, matrix products, dot(): lax.dot_general(left, right, (dims, ((), ())), preferred_element_type=F32)  82.5 us
    pallas_call x10, Pallas kernels, grad_blocks(): pl.pallas_call(functools.partial(grad_kernel, groups, recv is not None, s...  72.1 us
    ppermute x52, starting transfers between devices, swap(): return lax.ppermute(x, axis, [(i, i ^ 1 << bit) for i in range(size)])  68 us
    pallas_call x2, Pallas kernels, attend_back(): pl.pallas_call(functools.partial(back_kernel, far_count), grid_spec=pltpu...  21.3 us
    pallas_call x5, Pallas kernels, add_send(): pl.pallas_call(add_send_kernel, out_shape=[jax.ShapeDtypeStruct(shape, BF...  14.6 us
    pallas_call x2, Pallas kernels, attend(): pl.pallas_call(functools.partial(attend_kernel, far_count), grid_spec=plt...  14.2 us
    pallas_call x5, Pallas kernels, add_last(): pl.pallas_call(functools.partial(add_last_kernel, turned), out_shape=[jax...  12.9 us
  transfers between devices with their start and end apart: 55, of which 26 were waited for; matrix products, arithmetic and copies ran while one was open for 24% of the time, Pallas kernels for 28%

profile of v6, /device:TPU:0, one launch (start us, length us, event | category | flops | bytes accessed | tf_op | source)
XLA Modules:
  0.0 547.0 jit_solution(11233599345917546876)
XLA Ops:
  4.2 8.8 %shard_map.203 = (bf16[1024,2048]{1,0:T(8,128)(2,1)}, bf16[512,1024]{1,0:T(8,128)(2,1)}, bf16[128,1024]{1,0:T(8,128)(2,1)}) custom-call(s32[3]{0:T(128)S(1)} %pad_add_fusion.1.at_ref, bf16[1024,2048]{1,0:T(8,128)(2,1)} %bitcast.111, f32[1,2048]{1,0:T(1,128)} %bitcast.134, bf16[2048,512]{1,0:T(8,128)(2,1)} %wq_ref.1, ...), custom_call_target="tpu_custom_call" | custom-call | flops 1024 | bytes 1024 | tf_op jit(solution)/shard_map/pallas_call | solution.py:70
  13.0 4.9 collective-permute-start.17
  17.9 4.5 collective-permute-start.18
  26.8 7.8 %fusion.34 = f32[512,1408]{1,0:T(8,128)} fusion(bf16[1408,2048]{1,0:T(8,128)(2,1)} %param.54, bf16[128,2048]{1,0:T(8,128)(2,1)S(1)} %get-tuple-element.584, bf16[128,2048]{1,0:T(8,128)(2,1)S(1)} %get-tuple-element.585, bf16[128,2048]{1,0:T(8,128)(2,1)S(1)} %get-tuple-element.586, bf16[128,2048]{1,0:T(8,128)(2,1)S(1)} %get-tuple-element.583), kind=kOutput, calls=%fused_computation.150 | convolution fusion | flops 2961178624 | bytes 10747904 | tf_op jit(solution)/shard_map/dot_general | solution.py:31
  36.2 8.6 %fusion.33 = f32[512,1408]{1,0:T(8,128)} fusion(bf16[1408,2048]{1,0:T(8,128)(2,1)} %param.54, bf16[128,2048]{1,0:T(8,128)(2,1)S(1)} %get-tuple-element.580, bf16[128,2048]{1,0:T(8,128)(2,1)S(1)} %get-tuple-element.581, bf16[128,2048]{1,0:T(8,128)(2,1)S(1)} %get-tuple-element.582, bf16[128,2048]{1,0:T(8,128)(2,1)S(1)} %get-tuple-element.579), kind=kOutput, calls=%fused_computation.149 | convolution fusion | flops 2961178624 | bytes 10747904 | tf_op jit(solution)/shard_map/dot_general | solution.py:31
  47.0 7.3 %shard_map.204 = (bf16[8,128,512]{2,1,0:T(8,128)(2,1)}, bf16[512,512]{1,0:T(8,128)(2,1)}, f32[512,512]{1,0:T(8,128)}) custom-call(s32[3]{0:T(128)S(1)} %pad_add_fusion.1.at_ref, bf16[512,1024]{1,0:T(8,128)(2,1)} %get-tuple-element.409.q_ref, s32[2,4,512]{2,1,0:T(4,128)} %pad_add_fusion.seg_ref, bf16[128,1024]{1,0:T(8,128)(2,1)} %get-tuple-element.401.refs_0_, ...), custom_call_target="tpu_custom_call" | custom-call | flops 1024 | bytes 1024 | tf_op jit(solution)/shard_map/pallas_call | solution.py:186
  61.4 6.9 %shard_map.205 = (bf16[8,128,512]{2,1,0:T(8,128)(2,1)}, bf16[512,512]{1,0:T(8,128)(2,1)}, f32[512,512]{1,0:T(8,128)}) custom-call(s32[3]{0:T(128)S(1)} %pad_add_fusion.1.at_ref, bf16[512,1024]{1,0:T(8,128)(2,1)} %get-tuple-element.409.q_ref, s32[2,4,512]{2,1,0:T(4,128)} %pad_add_fusion.seg_ref, bf16[128,1024]{1,0:T(8,128)(2,1)} %get-tuple-element.401.refs_0_, ...), custom_call_target="tpu_custom_call" | custom-call | flops 1024 | bytes 1024 | tf_op jit(solution)/shard_map/pallas_call | solution.py:186
  68.3 5.5 %collective-permute-done.21 = bf16[128,2048]{1,0:T(8,128)(2,1)S(1)} collective-permute-done((bf16[128,2048]{1,0:T(8,128)(2,1)S(1)}, bf16[128,2048]{1,0:T(8,128)(2,1)S(1)}, u32[]{:S(2)}, u32[]{:S(2)}) %collective-permute-start.21) | collective-permute-done | bytes 524320 | tf_op jit(solution)/shard_map/ppermute | solution.py:603
  85.4 9.4 %collective-permute-done.23 = bf16[128,2048]{1,0:T(8,128)(2,1)S(1)} collective-permute-done((bf16[128,2048]{1,0:T(8,128)(2,1)S(1)}, bf16[128,2048]{1,0:T(8,128)(2,1)S(1)}, u32[]{:S(2)}, u32[]{:S(2)}) %collective-permute-start.23) | collective-permute-done | bytes 524320 | tf_op jit(solution)/shard_map/ppermute | solution.py:603
  94.8 18.9 %conditional.16 = (bf16[512,2048]{1,0:T(8,128)(2,1)}, bf16[512,1408]{1,0:T(8,128)(2,1)S(1)}, bf16[512,1408]{1,0:T(8,128)(2,1)S(1)}, bf16[512,1408]{1,0:T(8,128)(2,1)S(1)}) conditional(s32[]{:T(128)} %convert_element_type.181, () %tuple.196, (bf16[128,2048]{1,0:T(8,128)(2,1)S(1)}, bf16[128,2048]{1,0:T(8,128)(2,1)S(1)}, bf16[2048,1408]{1,0:T(8,128)(2,1)}, ...), branch_computations={%region_5.6_spmd, %region_6.7_spmd} | conditional | flops 5917114368 | bytes 65929404 | solution.py:532
  100.3 7.2 %fusion.40 = f32[512,1408]{1,0:T(8,128)S(1)} fusion(bf16[512,2048]{1,0:T(8,128)(2,1)} %constant_dynamic-update-slice_fusion, bf16[2048,1408]{1,0:T(8,128)(2,1)} %get-tuple-element.168), kind=kOutput, calls=%fused_computation.154 | convolution fusion | flops 2952790016 | bytes 10747904 | tf_op jit(solution)/shard_map/cond/branch_1_fun/dot_general | solution.py:31
  107.5 6.2 %multiply_convert_fusion = (bf16[512,1408]{1,0:T(8,128)(2,1)S(1)}, bf16[512,1408]{1,0:T(8,128)(2,1)S(1)}, bf16[512,1408]{1,0:T(8,128)(2,1)S(1)}) fusion(f32[512,1408]{1,0:T(8,128)S(1)} %copy-done.76, f32[512,1408]{1,0:T(8,128)S(1)} %fusion.40, bf16[512,2048]{1,0:T(8,128)(2,1)} %constant_dynamic-update-slice_fusion, bf16[2048,1408]{1,0:T(8,128)(2,1)S(1)} %bitcast.141), kind=kOutput, calls=%fused_computation | convolution fusion | flops 2964324352 | bytes 17956864 | tf_op jit(solution)/shard_map/cond/branch_1_fun/dot_general | solution.py:31
  120.4 13.4 %conditional.17 = (bf16[1,128,2048]{2,1,0:T(8,128)(2,1)}, f32[128,2048]{1,0:T(8,128)S(1)}) conditional(s32[]{:T(128)} %convert_element_type.181, () %tuple.210, (bf16[512,1408]{1,0:T(8,128)(2,1)S(1)}, bf16[2048,1408]{1,0:T(8,128)(2,1)}, bf16[512,1408]{1,0:T(8,128)(2,1)}, bf16[2048,1408]{1,0:T(8,128)(2,1)}) %tuple.370), branch_computations={%region_8.9_spmd, %region_9.10_spmd} | conditional | flops 5909250048 | bytes 67371120 | solution.py:532
  120.4 5.6 %fusion.41 = f32[512,2048]{1,0:T(8,128)S(1)} fusion(bf16[512,1408]{1,0:T(8,128)(2,1)S(1)} %get-tuple-element.170, bf16[2048,1408]{1,0:T(8,128)(2,1)} %get-tuple-element.171), kind=kOutput, calls=%fused_computation.155 | convolution fusion | flops 2952790016 | bytes 11403264 | tf_op jit(solution)/shard_map/cond/branch_1_fun/dot_general | solution.py:31
  138.8 21.3 %conditional.18 = (bf16[512,2048]{1,0:T(8,128)(2,1)}, bf16[512,1408]{1,0:T(8,128)(2,1)}, bf16[512,1408]{1,0:T(8,128)(2,1)S(1)}, bf16[512,1408]{1,0:T(8,128)(2,1)}) conditional(s32[]{:T(128)} %convert_element_type.181, () %tuple.208, (bf16[128,2048]{1,0:T(8,128)(2,1)S(1)}, bf16[128,2048]{1,0:T(8,128)(2,1)}, bf16[2048,1408]{1,0:T(8,128)(2,1)S(1)}, ...), branch_computations={%region_10.11_spmd, %region_11.12_spmd} | conditional | flops 5917114368 | bytes 48627852 | solution.py:532
  146.0 6.5 %fusion.42 = f32[512,1408]{1,0:T(8,128)S(1)} fusion(bf16[512,2048]{1,0:T(8,128)(2,1)} %constant_dynamic-update-slice_fusion.4, bf16[2048,1408]{1,0:T(8,128)(2,1)} %get-tuple-element.179), kind=kOutput, calls=%fused_computation.156 | convolution fusion | flops 2952790016 | bytes 10747904 | tf_op jit(solution)/shard_map/cond/branch_1_fun/dot_general | solution.py:31
  152.6 7.5 %multiply_convert_fusion.3 = (bf16[512,1408]{1,0:T(8,128)(2,1)}, bf16[512,1408]{1,0:T(8,128)(2,1)S(1)}, bf16[512,1408]{1,0:T(8,128)(2,1)}) fusion(f32[512,1408]{1,0:T(8,128)S(1)} %copy-done.75, f32[512,1408]{1,0:T(8,128)S(1)} %fusion.42, bf16[512,2048]{1,0:T(8,128)(2,1)} %constant_dynamic-update-slice_fusion.4, bf16[2048,1408]{1,0:T(8,128)(2,1)S(1)} %get-tuple-element.178), kind=kOutput, calls=%fused_computation.13 | convolution fusion | flops 2964324352 | bytes 17956864 | tf_op jit(solution)/shard_map/cond/branch_1_fun/dot_general | solution.py:31
  160.1 8.1 %shard_map.206 = bf16[4,256,1408]{2,1,0:T(8,128)(2,1)} custom-call(s32[4]{0:T(128)} %add_add_fusion.1.table_ref, bf16[512,1408]{1,0:T(8,128)(2,1)} %copy-done.12, bf16[512,2048]{1,0:T(8,128)(2,1)} %get-tuple-element.424.refs_1_.refs_2_, bf16[512,2048]{1,0:T(8,128)(2,1)} %get-tuple-element.424.refs_1_.refs_2_, bf16[512,1408]{1,0:T(8,128)(2,1)} %get-tuple-element.446.refs_3_, ...), custom_call_target="tpu_custom_call" | custom-call | flops 1024 | bytes 1024 | tf_op jit(solution)/shard_map/pallas_call | solution.py:453
  178.5 14.8 %conditional.20 = (bf16[1,128,2048]{2,1,0:T(8,128)(2,1)}, f32[128,2048]{1,0:T(8,128)S(1)}) conditional(s32[]{:T(128)} %convert_element_type.181, () %tuple.222, (bf16[512,1408]{1,0:T(8,128)(2,1)S(1)}, bf16[2048,1408]{1,0:T(8,128)(2,1)}, bf16[512,1408]{1,0:T(8,128)(2,1)}, bf16[2048,1408]{1,0:T(8,128)(2,1)}) %tuple.224), branch_computations={%region_16.17_spmd, %region_17.18_spmd} | conditional | flops 5909250048 | bytes 61603924 | solution.py:532
  178.5 5.6 %fusion.43 = f32[512,2048]{1,0:T(8,128)S(1)} fusion(bf16[512,1408]{1,0:T(8,128)(2,1)S(1)} %get-tuple-element.189, bf16[2048,1408]{1,0:T(8,128)(2,1)} %get-tuple-element.190), kind=kOutput, calls=%fused_computation.157 | convolution fusion | flops 2952790016 | bytes 11403264 | tf_op jit(solution)/shard_map/cond/branch_1_fun/dot_general | solution.py:31
  184.1 5.1 fusion.4
  194.7 9.2 %conditional.21 = ((bf16[512,512]{1,0:T(8,128)(2,1)}, bf16[512,2048]{1,0:T(8,128)(2,1)S(1)})) conditional(s32[]{:T(128)} %convert_element_type.181, () %tuple.218, (bf16[128,2048]{1,0:T(8,128)(2,1)}, bf16[128,2048]{1,0:T(8,128)(2,1)S(1)}, bf16[512,2048]{1,0:T(8,128)(2,1)}) %tuple.226), branch_computations={%region_18.19_spmd, %region_19.20_spmd} | conditional | flops 1024 | bytes 10486956 | solution.py:532
  199.6 4.3 branch_1_fun.3
  203.9 8.0 %shard_map.207 = bf16[4,256,1408]{2,1,0:T(8,128)(2,1)} custom-call(s32[4]{0:T(128)} %add_add_fusion.2.table_ref, bf16[512,1408]{1,0:T(8,128)(2,1)} %copy-done.47, bf16[512,2048]{1,0:T(8,128)(2,1)} %get-tuple-element.443.refs_1_.refs_2_, bf16[512,2048]{1,0:T(8,128)(2,1)} %get-tuple-element.443.refs_1_.refs_2_, bf16[512,1408]{1,0:T(8,128)(2,1)} %get-tuple-element.432.refs_3_, ...), custom_call_target="tpu_custom_call" | custom-call | flops 23000000512 | bytes 1024 | tf_op jit(solution)/shard_map/pallas_call | solution.py:453
  218.8 7.3 %shard_map.208 = bf16[4,256,1408]{2,1,0:T(8,128)(2,1)} custom-call(s32[4]{0:T(128)} %add_add_fusion.1.table_ref, bf16[512,1408]{1,0:T(8,128)(2,1)S(1)} %get-tuple-element.419.refs_0_, bf16[512,2048]{1,0:T(8,128)(2,1)} %get-tuple-element.443.refs_1_.refs_2_, bf16[512,2048]{1,0:T(8,128)(2,1)} %get-tuple-element.443.refs_1_.refs_2_, ...), custom_call_target="tpu_custom_call" | custom-call | flops 1024 | bytes 1024 | tf_op jit(solution)/shard_map/pallas_call | solution.py:453
  226.7 17.8 %conditional.23 = (bf16[2,128,2048]{2,1,0:T(8,128)(2,1)}, f32[2,128,2048]{2,1,0:T(8,128)}) conditional(s32[]{:T(128)} %convert_element_type.181, () %tuple.216, (bf16[512,1408]{1,0:T(8,128)(2,1)S(1)}, bf16[512,1408]{1,0:T(8,128)(2,1)}, bf16[1408,2048]{1,0:T(8,128)(2,1)}) %tuple.361), branch_computations={%region_24.25_spmd, %region_25.26_spmd} | conditional | flops 5916590080 | bytes 40108088 | solution.py:532
  226.7 9.9 %convolution_convert_fusion = bf16[1024,2048]{1,0:T(8,128)(2,1)S(1)} fusion(bf16[1408,2048]{1,0:T(8,128)(2,1)} %get-tuple-element.208, bf16[512,1408]{1,0:T(8,128)(2,1)} %get-tuple-element.207, bf16[512,1408]{1,0:T(8,128)(2,1)S(1)} %get-tuple-element.206), kind=kOutput, calls=%fused_computation.45 | convolution fusion | flops 5913444352 | bytes 12845056 | tf_op jit(solution)/shard_map/cond/branch_1_fun/dot_general | solution.py:31
  245.7 9.3 %shard_map.209 = (bf16[2,256,1408]{2,1,0:T(8,128)(2,1)}, bf16[2,256,1408]{2,1,0:T(8,128)(2,1)}) custom-call(s32[4]{0:T(128)} %add_add_fusion.table_ref, bf16[512,1408]{1,0:T(8,128)(2,1)} %copy-done.12, bf16[512,2048]{1,0:T(8,128)(2,1)} %get-tuple-element.424.refs_1_.refs_2_, bf16[512,2048]{1,0:T(8,128)(2,1)} %get-tuple-element.424.refs_1_.refs_2_, ...), custom_call_target="tpu_custom_call" | custom-call | flops 9200001024 | bytes 1024 | tf_op jit(solution)/shard_map/pallas_call | solution.py:453
  255.3 10.5 %shard_map.210 = (bf16[512,512]{1,0:T(8,128)(2,1)}, bf16[2,128,512]{2,1,0:T(8,128)(2,1)}, bf16[2,128,512]{2,1,0:T(8,128)(2,1)}) custom-call(s32[3]{0:T(128)S(1)} %pad_add_fusion.1.at_ref, bf16[8,128,512]{2,1,0:T(8,128)(2,1)} %get-tuple-element.450.qa_ref, bf16[512,512]{1,0:T(8,128)(2,1)S(1)} %copy-done.51, f32[512,512]{1,0:T(8,128)} %get-tuple-element.453.full_ref, ...), custom_call_target="tpu_custom_call" | custom-call | flops 23000000512 | bytes 1024 | tf_op jit(solution)/shard_map/pallas_call | solution.py:288
  265.8 9.8 %conditional.24 = ((bf16[512,512]{1,0:T(8,128)(2,1)}, bf16[512,2048]{1,0:T(8,128)(2,1)})) conditional(s32[]{:T(128)} %convert_element_type.181, () %tuple.238, (bf16[128,2048]{1,0:T(8,128)(2,1)}, bf16[128,2048]{1,0:T(8,128)(2,1)}, bf16[512,2048]{1,0:T(8,128)(2,1)}) %tuple.240), branch_computations={%region_26.27_spmd, %region_27.28_spmd} | conditional | flops 1024 | bytes 8389776 | solution.py:532
  270.9 4.7 branch_1_fun.4
  275.6 7.1 %collective-permute-done.31.refs_6_ = bf16[4,256,1408]{2,1,0:T(8,128)(2,1)} collective-permute-done((bf16[4,256,1408]{2,1,0:T(8,128)(2,1)}, bf16[4,256,1408]{2,1,0:T(8,128)(2,1)}, u32[]{:S(2)}, u32[]{:S(2)}) %collective-permute-start.31) | collective-permute-done | bytes 2883616 | tf_op jit(solution)/shard_map/ppermute | solution.py:603
  282.7 9.5 %shard_map.211 = (bf16[2,256,1408]{2,1,0:T(8,128)(2,1)}, bf16[2,256,1408]{2,1,0:T(8,128)(2,1)}) custom-call(s32[4]{0:T(128)} %add_add_fusion.3.table_ref, bf16[512,1408]{1,0:T(8,128)(2,1)} %copy-done.47, bf16[512,2048]{1,0:T(8,128)(2,1)} %get-tuple-element.443.refs_1_.refs_2_, bf16[512,2048]{1,0:T(8,128)(2,1)} %get-tuple-element.443.refs_1_.refs_2_, ...), custom_call_target="tpu_custom_call" | custom-call | flops 13800001536 | bytes 1024 | tf_op jit(solution)/shard_map/pallas_call | solution.py:453
  297.9 10.8 %shard_map.212 = (bf16[512,512]{1,0:T(8,128)(2,1)}, bf16[2,128,512]{2,1,0:T(8,128)(2,1)}, bf16[2,128,512]{2,1,0:T(8,128)(2,1)}) custom-call(s32[3]{0:T(128)S(1)} %pad_add_fusion.1.at_ref, bf16[8,128,512]{2,1,0:T(8,128)(2,1)} %get-tuple-element.455.qa_ref, bf16[512,512]{1,0:T(8,128)(2,1)} %get-tuple-element.463.do_ref, ...), custom_call_target="tpu_custom_call" | custom-call | flops 1024 | bytes 1024 | tf_op jit(solution)/shard_map/pallas_call | solution.py:288
  310.9 6.7 %collective-permute-start.34 = (bf16[2,2,128,512]{3,2,1,0:T(8,128)(2,1)}, bf16[2,2,128,512]{3,2,1,0:T(8,128)(2,1)}, u32[]{:S(2)}, u32[]{:S(2)}) collective-permute-start(bf16[2,2,128,512]{3,2,1,0:T(8,128)(2,1)} %get-tuple-element.469), channel_id=1, source_target_pairs={{0,2},{2,0},{4,6},{6,4},{1,3},{3,1},{5,7},{7,5},{8,10},{10,8},{12,... | collective-permute-start | bytes 1572872 | tf_op jit(solution)/shard_map/ppermute | solution.py:603
  319.4 6.0 %conditional.27 = (bf16[2,128,2048]{2,1,0:T(8,128)(2,1)}, bf16[2,128,2048]{2,1,0:T(8,128)(2,1)}) conditional(s32[]{:T(128)} %convert_element_type.181, () %tuple.246, (bf16[2,128,2048]{2,1,0:T(8,128)(2,1)}, bf16[2,128,2048]{2,1,0:T(8,128)(2,1)}) %tuple.248), branch_computations={%region_32.33_spmd, %region_33.34_spmd} | conditional | bytes 8388704 | solution.py:532
  325.4 6.6 %shard_map.213 = bf16[4,1024,256]{2,1,0:T(8,128)(2,1)} custom-call(s32[4]{0:T(128)} %add_add_fusion.1.table_ref, bf16[512,512]{1,0:T(8,128)(2,1)} %get-tuple-element.407.refs_0_, bf16[512,2048]{1,0:T(8,128)(2,1)S(1)} %get-tuple-element.474.refs_1_.refs_2_, bf16[512,2048]{1,0:T(8,128)(2,1)S(1)} %get-tuple-element.474.refs_1_.refs_2_, ...), custom_call_target="tpu_custom_call" | custom-call | flops 1024 | bytes 1024 | tf_op jit(solution)/shard_map/pallas_call | solution.py:453
  333.3 9.2 %shard_map.214 = (bf16[2,256,1408]{2,1,0:T(8,128)(2,1)}, bf16[2,256,1408]{2,1,0:T(8,128)(2,1)}) custom-call(s32[4]{0:T(128)} %add_add_fusion.table_ref, bf16[512,1408]{1,0:T(8,128)(2,1)S(1)} %get-tuple-element.419.refs_0_, bf16[512,2048]{1,0:T(8,128)(2,1)} %get-tuple-element.443.refs_1_.refs_2_, bf16[512,2048]{1,0:T(8,128)(2,1)} %get-tuple-element.443.refs_1_.refs_2_, ...), custom_call_target="tpu_custom_call" | custom-call | flops 1024 | bytes 1024 | tf_op jit(solution)/shard_map/pallas_call | solution.py:453
  346.0 28.2 %collective-permute-start.39 = (bf16[256,1408]{1,0:T(8,128)(2,1)}, bf16[256,1408]{1,0:T(8,128)(2,1)}, u32[]{:S(2)}, u32[]{:S(2)}) collective-permute-start(bf16[256,1408]{1,0:T(8,128)(2,1)} %get-tuple-element.483), channel_id=1, source_target_pairs={{0,4},{2,6},{4,0},{6,2},{1,5},{3,7},{5,1},{7,3},{8,12},{10,14},{12... | collective-permute-start | bytes 2162696 | tf_op jit(solution)/shard_map/ppermute | solution.py:603
  379.9 37.2 %collective-permute-done.37 = bf16[2,128,512]{2,1,0:T(8,128)(2,1)S(1)} collective-permute-done((bf16[2,128,512]{2,1,0:T(8,128)(2,1)S(1)}, bf16[2,128,512]{2,1,0:T(8,128)(2,1)S(1)}, u32[]{:S(2)}, u32[]{:S(2)}) %collective-permute-start.37) | collective-permute-done | bytes 262176 | tf_op jit(solution)/shard_map/ppermute | solution.py:603
  417.1 14.1 %conditional.29 = (bf16[2,128,2048]{2,1,0:T(8,128)(2,1)S(1)}, f32[2,128,2048]{2,1,0:T(8,128)S(1)}, bf16[128,512]{1,0:T(8,128)(2,1)S(1)}, bf16[128,512]{1,0:T(8,128)(2,1)S(1)}) conditional(s32[]{:T(128)} %convert_element_type.181, () %tuple.257, (bf16[512,512]{1,0:T(8,128)(2,1)S(1)}, bf16[512,512]{1,0:T(8,128)(2,1)S(1)}, ...), branch_computations={%region_36.37_spmd, %region_37.38_spmd} | conditional | flops 2694317056 | bytes 54789304 | solution.py:532
  439.8 7.1 %shard_map.219 = (bf16[2,1024,256]{2,1,0:T(8,128)(2,1)}, bf16[2,1024,256]{2,1,0:T(8,128)(2,1)}) custom-call(s32[4]{0:T(128)} %add_add_fusion.table_ref, bf16[512,512]{1,0:T(8,128)(2,1)} %get-tuple-element.407.refs_0_, bf16[512,2048]{1,0:T(8,128)(2,1)S(1)} %get-tuple-element.474.refs_1_.refs_2_, bf16[512,2048]{1,0:T(8,128)(2,1)S(1)} %get-tuple-element.474.refs_1_.refs_2_, ...), custom_call_target="tpu_custom_call" | custom-call | flops 1024 | bytes 1024 | tf_op jit(solution)/shard_map/pallas_call | solution.py:453
  459.4 4.5 conditional.30
  465.0 6.4 %collective-permute-done.43.got_ref = bf16[256,1408]{1,0:T(8,128)(2,1)} collective-permute-done((bf16[256,1408]{1,0:T(8,128)(2,1)}, bf16[256,1408]{1,0:T(8,128)(2,1)}, u32[]{:S(2)}, u32[]{:S(2)}) %collective-permute-start.43) | collective-permute-done | bytes 720928 | tf_op jit(solution)/shard_map/ppermute | solution.py:603
  480.0 10.0 %collective-permute-done.45.b_ref = f32[2,2048]{1,0:T(2,128)S(1)} collective-permute-done((f32[2,2048]{1,0:T(2,128)}, f32[2,2048]{1,0:T(2,128)S(1)}, u32[]{:S(2)}, u32[]{:S(2)}) %collective-permute-start.45) | collective-permute-done | bytes 16416 | tf_op jit(solution)/shard_map/ppermute | solution.py:603
  493.7 11.5 %collective-permute-done.46.recv_ref = bf16[2,1024,256]{2,1,0:T(8,128)(2,1)} collective-permute-done((bf16[2,1024,256]{2,1,0:T(8,128)(2,1)}, bf16[2,1024,256]{2,1,0:T(8,128)(2,1)}, u32[]{:S(2)}, u32[]{:S(2)}) %collective-permute-start.46) | collective-permute-done | bytes 1048608 | tf_op jit(solution)/shard_map/ppermute | solution.py:603
  518.0 5.8 %conditional.31 = (bf16[2,128,2048]{2,1,0:T(8,128)(2,1)}, bf16[2,128,2048]{2,1,0:T(8,128)(2,1)}) conditional(s32[]{:T(128)} %convert_element_type.181, () %tuple.255, (bf16[2,128,2048]{2,1,0:T(8,128)(2,1)}, bf16[2,128,2048]{2,1,0:T(8,128)(2,1)S(1)}) %tuple.276), branch_computations={%region_43.44_spmd, %region_44.45_spmd} | conditional | bytes 8388704 | solution.py:532
  523.8 5.6 %shard_map.230 = f32[2,512,2048]{2,1,0:T(8,128)} custom-call(s32[3]{0:T(128)S(1)} %pad_add_fusion.1.at_ref, bf16[2,128,2048]{2,1,0:T(8,128)(2,1)} %get-tuple-element.529.refs_0_, bf16[2,128,2048]{2,1,0:T(8,128)(2,1)S(1)} %collective-permute-done.50.refs_1_, bf16[2,128,2048]{2,1,0:T(8,128)(2,1)} %get-tuple-element.530.refs_2_, ...), custom_call_target="tpu_custom_call" | custom-call | flops 1024 | bytes 1024 | tf_op jit(solution)/shard_map/pallas_call | solution.py:591
  (368 shorter events, 233.7 us)
Async XLA Ops:
  13.0 32.5 %collective-permute-start.17 = (bf16[128,1024]{1,0:T(8,128)(2,1)}, bf16[128,1024]{1,0:T(8,128)(2,1)S(1)}, u32[]{:S(2)}, u32[]{:S(2)}) collective-permute-start(bf16[128,1024]{1,0:T(8,128)(2,1)} %get-tuple-element.401.refs_0_), channel_id=1, source_target_pairs={{0,2},{2,4},{4,6},{1,3},{3,5},{5,7},{8,10},{10,12},{12,14},{9,11},... | collective-permute-start | bytes 786440 | tf_op jit(solution)/shard_map/ppermute | solution.py:650
  17.9 27.6 %collective-permute-start.18 = (bf16[128,1024]{1,0:T(8,128)(2,1)}, bf16[128,1024]{1,0:T(8,128)(2,1)S(1)}, u32[]{:S(2)}, u32[]{:S(2)}) collective-permute-start(bf16[128,1024]{1,0:T(8,128)(2,1)} %get-tuple-element.401.refs_0_), channel_id=1, source_target_pairs={{0,4},{2,6},{1,5},{3,7},{8,12},{10,14},{9,13},{11,15},{16,20},{18,... | collective-permute-start | bytes 786440 | tf_op jit(solution)/shard_map/ppermute | solution.py:650
  22.4 23.1 %collective-permute-start.19 = (bf16[128,1024]{1,0:T(8,128)(2,1)}, bf16[128,1024]{1,0:T(8,128)(2,1)S(1)}, u32[]{:S(2)}, u32[]{:S(2)}) collective-permute-start(bf16[128,1024]{1,0:T(8,128)(2,1)} %get-tuple-element.401.refs_0_), channel_id=1, source_target_pairs={{0,6},{1,7},{8,14},{9,15},{16,22},{17,23},{24,30},{25,31}} | collective-permute-start | bytes 786440 | tf_op jit(solution)/shard_map/ppermute | solution.py:650
  56.7 2.7 collective-permute-start.20
  59.8 14.0 %collective-permute-start.21 = (bf16[128,2048]{1,0:T(8,128)(2,1)S(1)}, bf16[128,2048]{1,0:T(8,128)(2,1)S(1)}, u32[]{:S(2)}, u32[]{:S(2)}) collective-permute-start(bf16[128,2048]{1,0:T(8,128)(2,1)S(1)} %slice.167), channel_id=1, source_target_pairs={{0,16},{8,24},{16,0},{24,8},{1,17},{9,25},{17,1},{25,9},{2,18},{10... | collective-permute-start | bytes 1572872 | tf_op jit(solution)/shard_map/ppermute | solution.py:603
  80.0 2.7 collective-permute-start.22
  80.0 14.8 %collective-permute-start.23 = (bf16[128,2048]{1,0:T(8,128)(2,1)S(1)}, bf16[128,2048]{1,0:T(8,128)(2,1)S(1)}, u32[]{:S(2)}, u32[]{:S(2)}) collective-permute-start(bf16[128,2048]{1,0:T(8,128)(2,1)S(1)} %get-tuple-element.559), channel_id=1, source_target_pairs={{0,16},{8,24},{16,0},{24,8},{1,17},{9,25},{17,1},{25,9},{2,18},{10... | collective-permute-start | bytes 1572872 | tf_op jit(solution)/shard_map/ppermute | solution.py:603
  83.9 29.8 %collective-permute-start.24 = (bf16[128,2048]{1,0:T(8,128)(2,1)}, bf16[128,2048]{1,0:T(8,128)(2,1)}, u32[]{:S(2)}, u32[]{:S(2)}) collective-permute-start(bf16[128,2048]{1,0:T(8,128)(2,1)} %slice.166), channel_id=1, source_target_pairs={{0,16},{8,24},{16,0},{24,8},{1,17},{9,25},{17,1},{25,9},{2,18},{10... | collective-permute-start | bytes 1572872 | tf_op jit(solution)/shard_map/ppermute | solution.py:603
  118.2 20.6 %collective-permute-start.25 = (bf16[128,2048]{1,0:T(8,128)(2,1)S(1)}, bf16[128,2048]{1,0:T(8,128)(2,1)}, u32[]{:S(2)}, u32[]{:S(2)}) collective-permute-start(bf16[128,2048]{1,0:T(8,128)(2,1)S(1)} %get-tuple-element.555), channel_id=1, source_target_pairs={{0,16},{8,24},{16,0},{24,8},{1,17},{9,25},{17,1},{25,9},{2,18},{10... | collective-permute-start | bytes 1572872 | tf_op jit(solution)/shard_map/ppermute | solution.py:603
  129.8 2.7 collective-permute-start.11
  133.9 38.2 %collective-permute-start.26 = (bf16[128,2048]{1,0:T(8,128)(2,1)}, bf16[128,2048]{1,0:T(8,128)(2,1)S(1)}, u32[]{:S(2)}, u32[]{:S(2)}) collective-permute-start(bf16[128,2048]{1,0:T(8,128)(2,1)} %bitcast.44), channel_id=1, source_target_pairs={{0,16},{8,24},{16,0},{24,8},{1,17},{9,25},{17,1},{25,9},{2,18},{10... | collective-permute-start | bytes 1572872 | tf_op jit(solution)/shard_map/ppermute | solution.py:603
  141.2 4.0 collective-permute-start.13
  168.2 77.4 %collective-permute-start.29 = (bf16[4,256,1408]{2,1,0:T(8,128)(2,1)}, bf16[4,256,1408]{2,1,0:T(8,128)(2,1)}, u32[]{:S(2)}, u32[]{:S(2)}) collective-permute-start(bf16[4,256,1408]{2,1,0:T(8,128)(2,1)} %shard_map.206), channel_id=1, source_target_pairs={{0,1},{1,0},{2,3},{3,2},{4,5},{5,4},{6,7},{7,6},{8,9},{9,8},{10,11... | collective-permute-start | bytes 8650760 | tf_op jit(solution)/shard_map/ppermute | solution.py:603
  175.9 18.8 %collective-permute-start.27 = (bf16[128,2048]{1,0:T(8,128)(2,1)}, bf16[128,2048]{1,0:T(8,128)(2,1)S(1)}, u32[]{:S(2)}, u32[]{:S(2)}) collective-permute-start(bf16[128,2048]{1,0:T(8,128)(2,1)} %get-tuple-element.429), channel_id=1, source_target_pairs={{0,16},{8,24},{16,0},{24,8},{1,17},{9,25},{17,1},{25,9},{2,18},{10... | collective-permute-start | bytes 1572872 | tf_op jit(solution)/shard_map/ppermute | solution.py:603
  189.3 2.7 collective-permute-start.14
  193.3 18.6 %collective-permute-start.28 = (bf16[128,2048]{1,0:T(8,128)(2,1)}, bf16[128,2048]{1,0:T(8,128)(2,1)}, u32[]{:S(2)}, u32[]{:S(2)}) collective-permute-start(bf16[128,2048]{1,0:T(8,128)(2,1)} %bitcast.46), channel_id=1, source_target_pairs={{0,16},{8,24},{16,0},{24,8},{1,17},{9,25},{17,1},{25,9},{2,18},{10... | collective-permute-start | bytes 1572872 | tf_op jit(solution)/shard_map/ppermute | solution.py:603
  216.2 49.6 %collective-permute-start.30 = (bf16[128,2048]{1,0:T(8,128)(2,1)}, bf16[128,2048]{1,0:T(8,128)(2,1)}, u32[]{:S(2)}, u32[]{:S(2)}) collective-permute-start(bf16[128,2048]{1,0:T(8,128)(2,1)} %get-tuple-element.442), channel_id=1, source_target_pairs={{0,16},{8,24},{16,0},{24,8},{1,17},{9,25},{17,1},{25,9},{2,18},{10... | collective-permute-start | bytes 1572872 | tf_op jit(solution)/shard_map/ppermute | solution.py:603
  217.1 65.7 %collective-permute-start.31 = (bf16[4,256,1408]{2,1,0:T(8,128)(2,1)}, bf16[4,256,1408]{2,1,0:T(8,128)(2,1)}, u32[]{:S(2)}, u32[]{:S(2)}) collective-permute-start(bf16[4,256,1408]{2,1,0:T(8,128)(2,1)} %shard_map.207), channel_id=1, source_target_pairs={{0,2},{2,0},{4,6},{6,4},{1,3},{3,1},{5,7},{7,5},{8,10},{10,8},{12,... | collective-permute-start | bytes 8650760 | tf_op jit(solution)/shard_map/ppermute | solution.py:603
  226.1 107.2 %collective-permute-start.35 = (bf16[4,256,1408]{2,1,0:T(8,128)(2,1)}, bf16[4,256,1408]{2,1,0:T(8,128)(2,1)}, u32[]{:S(2)}, u32[]{:S(2)}) collective-permute-start(bf16[4,256,1408]{2,1,0:T(8,128)(2,1)} %shard_map.208), channel_id=1, source_target_pairs={{0,1},{1,0},{2,3},{3,2},{4,5},{5,4},{6,7},{7,6},{8,9},{9,8},{10,11... | collective-permute-start | bytes 8650760 | tf_op jit(solution)/shard_map/ppermute | solution.py:603
  236.8 4.2 collective-permute-start.15
  244.5 47.7 %collective-permute-start.32 = (bf16[2,128,2048]{2,1,0:T(8,128)(2,1)}, bf16[2,128,2048]{2,1,0:T(8,128)(2,1)}, u32[]{:S(2)}, u32[]{:S(2)}) collective-permute-start(bf16[2,128,2048]{2,1,0:T(8,128)(2,1)} %get-tuple-element.447), channel_id=1, source_target_pairs={{0,16},{8,24},{16,0},{24,8},{1,17},{9,25},{17,1},{25,9},{2,18},{10... | collective-permute-start | bytes 3145736 | tf_op jit(solution)/shard_map/ppermute | solution.py:603
  254.9 87.6 %collective-permute-start.36 = (bf16[2,256,1408]{2,1,0:T(8,128)(2,1)}, bf16[2,256,1408]{2,1,0:T(8,128)(2,1)}, u32[]{:S(2)}, u32[]{:S(2)}) collective-permute-start(bf16[2,256,1408]{2,1,0:T(8,128)(2,1)} %get-tuple-element.451), channel_id=1, source_target_pairs={{0,2},{2,0},{4,6},{6,4},{1,3},{3,1},{5,7},{7,5},{8,10},{10,8},{12,... | collective-permute-start | bytes 4325384 | tf_op jit(solution)/shard_map/ppermute | solution.py:603
  296.2 23.2 %collective-permute-start.33 = (bf16[2,128,2048]{2,1,0:T(8,128)(2,1)}, bf16[2,128,2048]{2,1,0:T(8,128)(2,1)}, u32[]{:S(2)}, u32[]{:S(2)}) collective-permute-start(bf16[2,128,2048]{2,1,0:T(8,128)(2,1)} %get-tuple-element.678.refs_0_), channel_id=1, source_target_pairs={{0,16},{8,24},{16,0},{24,8},{1,17},{9,25},{17,1},{25,9},{2,18},{10... | collective-permute-start | bytes 3145736 | tf_op jit(solution)/shard_map/ppermute | solution.py:603
  297.4 135.7 %collective-permute-start.38 = (bf16[2,256,1408]{2,1,0:T(8,128)(2,1)}, bf16[2,256,1408]{2,1,0:T(8,128)(2,1)}, u32[]{:S(2)}, u32[]{:S(2)}) collective-permute-start(bf16[2,256,1408]{2,1,0:T(8,128)(2,1)} %get-tuple-element.461), channel_id=1, source_target_pairs={{0,1},{1,0},{2,3},{3,2},{4,5},{5,4},{6,7},{7,6},{8,9},{9,8},{10,11... | collective-permute-start | bytes 4325384 | tf_op jit(solution)/shard_map/ppermute | solution.py:603
  310.9 21.1 %collective-permute-start.34 = (bf16[2,2,128,512]{3,2,1,0:T(8,128)(2,1)}, bf16[2,2,128,512]{3,2,1,0:T(8,128)(2,1)}, u32[]{:S(2)}, u32[]{:S(2)}) collective-permute-start(bf16[2,2,128,512]{3,2,1,0:T(8,128)(2,1)} %get-tuple-element.469), channel_id=1, source_target_pairs={{0,2},{2,0},{4,6},{6,4},{1,3},{3,1},{5,7},{7,5},{8,10},{10,8},{12,... | collective-permute-start | bytes 1572872 | tf_op jit(solution)/shard_map/ppermute | solution.py:603
  319.4 3.0 collective-permute-start.4
  322.4 3.0 collective-permute-start.5
  346.0 90.6 %collective-permute-start.39 = (bf16[256,1408]{1,0:T(8,128)(2,1)}, bf16[256,1408]{1,0:T(8,128)(2,1)}, u32[]{:S(2)}, u32[]{:S(2)}) collective-permute-start(bf16[256,1408]{1,0:T(8,128)(2,1)} %get-tuple-element.483), channel_id=1, source_target_pairs={{0,4},{2,6},{4,0},{6,2},{1,5},{3,7},{5,1},{7,3},{8,12},{10,14},{12... | collective-permute-start | bytes 2162696 | tf_op jit(solution)/shard_map/ppermute | solution.py:603
  374.2 65.6 %collective-permute-start.40 = (bf16[4,1024,256]{2,1,0:T(8,128)(2,1)}, bf16[4,1024,256]{2,1,0:T(8,128)(2,1)}, u32[]{:S(2)}, u32[]{:S(2)}) collective-permute-start(bf16[4,1024,256]{2,1,0:T(8,128)(2,1)} %shard_map.213), channel_id=1, source_target_pairs={{0,1},{1,0},{2,3},{3,2},{4,5},{5,4},{6,7},{7,6},{8,9},{9,8},{10,11... | collective-permute-start | bytes 6291464 | tf_op jit(solution)/shard_map/ppermute | solution.py:603
  374.7 42.4 %collective-permute-start.37 = (bf16[2,128,512]{2,1,0:T(8,128)(2,1)S(1)}, bf16[2,128,512]{2,1,0:T(8,128)(2,1)S(1)}, u32[]{:S(2)}, u32[]{:S(2)}) collective-permute-start(bf16[2,128,512]{2,1,0:T(8,128)(2,1)S(1)} %get-tuple-element.479), channel_id=1, source_target_pairs={{0,4},{2,6},{4,0},{6,2},{1,5},{3,7},{5,1},{7,3},{8,12},{10,14},{12... | collective-permute-start | bytes 786440 | tf_op jit(solution)/shard_map/ppermute | solution.py:603
  374.7 75.4 %collective-permute-start.41 = (bf16[2,256,1408]{2,1,0:T(8,128)(2,1)}, bf16[2,256,1408]{2,1,0:T(8,128)(2,1)}, u32[]{:S(2)}, u32[]{:S(2)}) collective-permute-start(bf16[2,256,1408]{2,1,0:T(8,128)(2,1)} %get-tuple-element.481), channel_id=1, source_target_pairs={{0,2},{2,0},{4,6},{6,4},{1,3},{3,1},{5,7},{7,5},{8,10},{10,8},{12,... | collective-permute-start | bytes 4325384 | tf_op jit(solution)/shard_map/ppermute | solution.py:603
  425.2 4.2 collective-permute-start.16
  432.2 27.1 %collective-permute-start.42 = (bf16[2,128,2048]{2,1,0:T(8,128)(2,1)}, bf16[2,128,2048]{2,1,0:T(8,128)(2,1)S(1)}, u32[]{:S(2)}, u32[]{:S(2)}) collective-permute-start(bf16[2,128,2048]{2,1,0:T(8,128)(2,1)} %copy-done.49), channel_id=1, source_target_pairs={{0,16},{8,24},{16,0},{24,8},{1,17},{9,25},{17,1},{25,9},{2,18},{10... | collective-permute-start | bytes 3145736 | tf_op jit(solution)/shard_map/ppermute | solution.py:603
  436.5 34.9 %collective-permute-start.43 = (bf16[256,1408]{1,0:T(8,128)(2,1)}, bf16[256,1408]{1,0:T(8,128)(2,1)}, u32[]{:S(2)}, u32[]{:S(2)}) collective-permute-start(bf16[256,1408]{1,0:T(8,128)(2,1)} %get-tuple-element.496), channel_id=1, source_target_pairs={{0,4},{2,6},{4,0},{6,2},{1,5},{3,7},{5,1},{7,3},{8,12},{10,14},{12... | collective-permute-start | bytes 2162696 | tf_op jit(solution)/shard_map/ppermute | solution.py:603
  446.9 58.3 %collective-permute-start.46 = (bf16[2,1024,256]{2,1,0:T(8,128)(2,1)}, bf16[2,1024,256]{2,1,0:T(8,128)(2,1)}, u32[]{:S(2)}, u32[]{:S(2)}) collective-permute-start(bf16[2,1024,256]{2,1,0:T(8,128)(2,1)} %get-tuple-element.499), channel_id=1, source_target_pairs={{0,2},{2,0},{4,6},{6,4},{1,3},{3,1},{5,7},{7,5},{8,10},{10,8},{12,... | collective-permute-start | bytes 3145736 | tf_op jit(solution)/shard_map/ppermute | solution.py:603
  453.4 56.9 %collective-permute-start.48 = (bf16[256,1408]{1,0:T(8,128)(2,1)}, bf16[256,1408]{1,0:T(8,128)(2,1)}, u32[]{:S(2)}, u32[]{:S(2)}) collective-permute-start(bf16[256,1408]{1,0:T(8,128)(2,1)} %get-tuple-element.501), channel_id=1, source_target_pairs={{0,4},{2,6},{4,0},{6,2},{1,5},{3,7},{5,1},{7,3},{8,12},{10,14},{12... | collective-permute-start | bytes 2162696 | tf_op jit(solution)/shard_map/ppermute | solution.py:603
  457.0 17.1 %collective-permute-start.44 = (bf16[4,128,256]{2,1,0:T(8,128)(2,1)}, bf16[4,128,256]{2,1,0:T(8,128)(2,1)}, u32[]{:S(2)}, u32[]{:S(2)}) collective-permute-start(bf16[4,128,256]{2,1,0:T(8,128)(2,1)} %shard_map.221), channel_id=1, source_target_pairs={{0,1},{1,0},{2,3},{3,2},{4,5},{5,4},{6,7},{7,6},{8,9},{9,8},{10,11... | collective-permute-start | bytes 786440 | tf_op jit(solution)/shard_map/ppermute | solution.py:603
  461.0 2.9 collective-permute-start.8
  463.9 54.1 %collective-permute-start.50 = (bf16[2,128,2048]{2,1,0:T(8,128)(2,1)}, bf16[2,128,2048]{2,1,0:T(8,128)(2,1)S(1)}, u32[]{:S(2)}, u32[]{:S(2)}) collective-permute-start(bf16[2,128,2048]{2,1,0:T(8,128)(2,1)} %get-tuple-element.529.refs_0_), channel_id=1, source_target_pairs={{0,16},{8,24},{16,0},{24,8},{1,17},{9,25},{17,1},{25,9},{2,18},{10... | collective-permute-start | bytes 3145736 | tf_op jit(solution)/shard_map/ppermute | solution.py:603
  477.6 30.5 %collective-permute-start.47 = (bf16[2,128,256]{2,1,0:T(8,128)(2,1)}, bf16[2,128,256]{2,1,0:T(8,128)(2,1)S(1)}, u32[]{:S(2)}, u32[]{:S(2)}) collective-permute-start(bf16[2,128,256]{2,1,0:T(8,128)(2,1)} %get-tuple-element.514), channel_id=1, source_target_pairs={{0,2},{2,0},{4,6},{6,4},{1,3},{3,1},{5,7},{7,5},{8,10},{10,8},{12,... | collective-permute-start | bytes 393224 | tf_op jit(solution)/shard_map/ppermute | solution.py:603
  478.9 11.1 %collective-permute-start.45 = (f32[2,2048]{1,0:T(2,128)}, f32[2,2048]{1,0:T(2,128)S(1)}, u32[]{:S(2)}, u32[]{:S(2)}) collective-permute-start(f32[2,2048]{1,0:T(2,128)} %shard_map.224.a_ref), channel_id=1, source_target_pairs={{0,16},{8,24},{16,0},{24,8},{1,17},{9,25},{17,1},{25,9},{2,18},{10... | collective-permute-start | bytes 49160 | tf_op jit(solution)/shard_map/ppermute | solution.py:603
  492.0 21.2 %collective-permute-start.49 = (f32[2,2048]{1,0:T(2,128)}, f32[2,2048]{1,0:T(2,128)S(1)}, u32[]{:S(2)}, u32[]{:S(2)}) collective-permute-start(f32[2,2048]{1,0:T(2,128)} %shard_map.225.a_ref), channel_id=1, source_target_pairs={{0,2},{2,0},{4,6},{6,4},{1,3},{3,1},{5,7},{7,5},{8,10},{10,8},{12,... | collective-permute-start | bytes 49160 | tf_op jit(solution)/shard_map/ppermute | solution.py:603
  508.0 35.5 %collective-permute-start.54 = (bf16[1024,256]{1,0:T(8,128)(2,1)}, bf16[1024,256]{1,0:T(8,128)(2,1)S(1)}, u32[]{:S(2)}, u32[]{:S(2)}) collective-permute-start(bf16[1024,256]{1,0:T(8,128)(2,1)} %get-tuple-element.522), channel_id=1, source_target_pairs={{0,4},{2,6},{4,0},{6,2},{1,5},{3,7},{5,1},{7,3},{8,12},{10,14},{12... | collective-permute-start | bytes 1572872 | tf_op jit(solution)/shard_map/ppermute | solution.py:603
  515.1 17.0 %collective-permute-start.51 = (f32[2,2048]{1,0:T(2,128)}, f32[2,2048]{1,0:T(2,128)S(1)}, u32[]{:S(2)}, u32[]{:S(2)}) collective-permute-start(f32[2,2048]{1,0:T(2,128)} %shard_map.229.a_ref), channel_id=1, source_target_pairs={{0,4},{2,6},{4,0},{6,2},{1,5},{3,7},{5,1},{7,3},{8,12},{10,14},{12... | collective-permute-start | bytes 49160 | tf_op jit(solution)/shard_map/ppermute | solution.py:603
  518.0 3.0 collective-permute-start.6
  521.0 2.8 collective-permute-start.7
  534.0 3.9 collective-permute-start.52
  534.6 6.8 %collective-permute-start.53 = (bf16[128,256]{1,0:T(8,128)(2,1)S(1)}, bf16[128,256]{1,0:T(8,128)(2,1)S(1)}, u32[]{:S(2)}, u32[]{:S(2)}) collective-permute-start(bf16[128,256]{1,0:T(8,128)(2,1)S(1)} %copy-done.72), channel_id=1, source_target_pairs={{0,4},{2,6},{4,0},{6,2},{1,5},{3,7},{5,1},{7,3},{8,12},{10,14},{12... | collective-permute-start | bytes 196616 | tf_op jit(solution)/shard_map/ppermute | solution.py:603
  (86 other events, 618.0 us)
